TPU v7x, 32 devices: a whole 2x2x4 slice. The times are simulated.
32 devices in a mesh: dp: 8 (over y, x, core), ctx: 4 (over z).
Axes of the slice: x: 2, y: 2, z: 4, core: 2. Of those that a mesh axis runs over, the one named last changes fastest.
Arguments:
- tokens: bfloat16 [8, 1024, 8192], P('dp', 'ctx'), may hold values from -16 to 16
- positions: int32 [1024], replicated, may hold values from 0 to 1023, as said below
- query_weight: float32 [8192, 512], P(('dp', 'ctx')), may hold values from -0.5 to 0.5
- key_weight: float32 [8192, 128], P(('dp', 'ctx')), may hold values from -0.5 to 0.5
- value_weight: float32 [8192, 128], P(('dp', 'ctx')), may hold values from -0.0625 to 0.0625
- grad_output: bfloat16 [8, 1024, 512], P('dp', 'ctx'), may hold values from -6 to 6
Outputs:
- attention: bfloat16 [8, 1024, 512], P('dp', 'ctx')
- grad_tokens: bfloat16 [8, 1024, 8192], P('dp', 'ctx')
- query_grad: float32 [8192, 512], P(('dp', 'ctx'))
- key_grad: float32 [8192, 128], P(('dp', 'ctx'))
- value_grad: float32 [8192, 128], P(('dp', 'ctx'))
Inputs may be any that keep to these rules, and one draw needn't show every extreme that they name: Stored rows come in runs of 128; each run holds consecutive increasing positions starting at a multiple of 128; together the runs hold every position of the sequence once.
All inputs are finite; a program needn't handle non-finite values.
Results may differ from a plain program's by a relative error of at most 0.034.
Values may be sent and summed in bfloat16 or wider, within the bound.
No kernel may reach another device: no remote copies, remote signals or barrier semaphores. Data moves between devices by JAX's collectives and lax.ppermute only.
A program may use at most 192 MiB of HBM per device.

v0:
```python
import jax
import jax.numpy as jnp
from jax import lax
from jax.sharding import PartitionSpec as P

ROPE_BASE = 1000000.0
MASKED = -1e30


def rope_tables(positions_in, head_dim):
    half_width = head_dim // 2
    exponent = jnp.arange(half_width).astype(jnp.float32) * (2.0 / head_dim)
    frequency = jnp.power(ROPE_BASE, -exponent)
    angles = positions_in.astype(jnp.float32)[:, None] * frequency[None, :]
    angles = jnp.concatenate([angles, angles], axis=1)
    return (jnp.cos(angles), jnp.sin(angles))


def rotate(field, cos_table, sin_table):
    half_width = field.shape[-1] // 2
    turned = jnp.concatenate([-field[..., half_width:], field[..., :half_width]], axis=-1)
    return field * cos_table + turned * sin_table


def unrotate(field, cos_table, sin_table):
    half_width = field.shape[-1] // 2
    turned = jnp.concatenate([field[..., half_width:], -field[..., :half_width]], axis=-1)
    return field * cos_table + turned * sin_table


def body(tokens, positions, query_weight, key_weight, value_weight, grad_output):
    token_rows = tokens[0]
    local_rows = token_rows.shape[0]
    head_dim = key_weight.shape[1]
    query_width = query_weight.shape[1]
    head_count = query_width // head_dim
    score_scale = head_dim ** (-0.5)
    local_weights = jnp.concatenate([query_weight, key_weight, value_weight], axis=1).astype(
        jnp.bfloat16
    )
    weights_all = lax.all_gather(local_weights, ("dp", "ctx"), axis=0, tiled=True)
    projected = jnp.dot(token_rows, weights_all, preferred_element_type=jnp.float32)
    place_index = lax.axis_index("ctx")
    own_positions = lax.dynamic_slice_in_dim(positions, place_index * local_rows, local_rows)
    cos_table, sin_table = rope_tables(own_positions, head_dim)
    query = projected[:, :query_width].reshape(local_rows, head_count, head_dim)
    query_heads = rotate(query, cos_table[:, None, :], sin_table[:, None, :]).astype(jnp.bfloat16)
    key_rot = rotate(
        projected[:, query_width : query_width + head_dim], cos_table, sin_table
    ).astype(jnp.bfloat16)
    value_b = projected[:, query_width + head_dim :].astype(jnp.bfloat16)
    key_value = jnp.concatenate([key_rot, value_b], axis=1)
    key_piece = lax.all_gather(key_value, "ctx", axis=0, tiled=True)
    running_max = jnp.full((local_rows, head_count), MASKED, jnp.float32)
    allowed = positions[None, :] <= own_positions[:, None]
    scores = (
        jnp.einsum(
            "qhd,kd->qhk", query_heads, key_piece[:, :head_dim], preferred_element_type=jnp.float32
        )
        * score_scale
    )
    scores = jnp.where(allowed[:, None, :], scores, MASKED)
    new_max = jnp.maximum(running_max, jnp.max(scores, axis=-1))
    weight = jnp.where(allowed[:, None, :], jnp.exp(scores - new_max[..., None]), 0.0)
    denominator = jnp.sum(weight, axis=-1)
    weighted = jnp.einsum(
        "qhk,kd->qhd",
        weight.astype(jnp.bfloat16),
        key_piece[:, head_dim:],
        preferred_element_type=jnp.float32,
    )
    running_max, denominator, weighted = (new_max, denominator, weighted)
    keys_values = lax.all_gather(key_value, "ctx", axis=0, tiled=True)
    log_total = running_max + jnp.log(denominator)
    attention = (weighted / denominator[..., None]).astype(jnp.bfloat16)
    grad_heads = grad_output[0].reshape(local_rows, head_count, head_dim)
    row_delta = jnp.sum(grad_heads.astype(jnp.float32) * attention.astype(jnp.float32), axis=-1)
    key_all = keys_values[:, :head_dim]
    value_all = keys_values[:, head_dim:]
    allowed = positions[None, :] <= own_positions[:, None]
    scores = (
        jnp.einsum("qhd,kd->qhk", query_heads, key_all, preferred_element_type=jnp.float32)
        * score_scale
    )
    probs = jnp.where(allowed[:, None, :], jnp.exp(scores - log_total[..., None]), 0.0)
    grad_probs = jnp.einsum(
        "qhd,kd->qhk", grad_heads, value_all, preferred_element_type=jnp.float32
    )
    dscore = (probs * (grad_probs - row_delta[..., None])).astype(jnp.bfloat16)
    probs_b = probs.astype(jnp.bfloat16)
    grad_query_rot = (
        jnp.einsum("qhk,kd->qhd", dscore, key_all, preferred_element_type=jnp.float32) * score_scale
    )
    key_term = (
        jnp.einsum("qhk,qhd->kd", dscore, query_heads, preferred_element_type=jnp.float32)
        * score_scale
    )
    value_term = jnp.einsum("qhk,qhd->kd", probs_b, grad_heads, preferred_element_type=jnp.float32)
    keyval_term = jnp.concatenate([key_term, value_term], axis=1)
    keyval_grad = lax.psum_scatter(
        keyval_term.astype(jnp.bfloat16), "ctx", scatter_dimension=0, tiled=True
    ).astype(jnp.float32)
    grad_query = unrotate(grad_query_rot, cos_table[:, None, :], sin_table[:, None, :]).reshape(
        local_rows, query_width
    )
    grad_key = unrotate(keyval_grad[:, :head_dim], cos_table, sin_table)
    grad_proj = jnp.concatenate([grad_query, grad_key, keyval_grad[:, head_dim:]], axis=1).astype(
        jnp.bfloat16
    )
    grad_input = lax.dot_general(
        grad_proj, weights_all, (((1,), (1,)), ((), ())), preferred_element_type=jnp.float32
    ).astype(jnp.bfloat16)
    weight_grads = lax.psum_scatter(
        lax.dot_general(
            token_rows, grad_proj, (((0,), (0,)), ((), ())), preferred_element_type=jnp.float32
        ),
        ("dp", "ctx"),
        scatter_dimension=0,
        tiled=True,
    )
    query_grad = weight_grads[:, :query_width]
    key_grad = weight_grads[:, query_width : query_width + head_dim]
    value_grad = weight_grads[:, query_width + head_dim :]
    attention_rows = attention.reshape(local_rows, query_width)
    return (attention_rows[None], grad_input[None], query_grad, key_grad, value_grad)


def solution(mesh):
    in_specs = (
        P("dp", "ctx", None),
        P(),
        P(("dp", "ctx"), None),
        P(("dp", "ctx"), None),
        P(("dp", "ctx"), None),
        P("dp", "ctx", None),
    )
    out_specs = (
        P("dp", "ctx", None),
        P("dp", "ctx", None),
        P(("dp", "ctx"), None),
        P(("dp", "ctx"), None),
        P(("dp", "ctx"), None),
    )
    return jax.shard_map(body, mesh=mesh, in_specs=in_specs, out_specs=out_specs, check_vma=False)
```

profile of v0, /device:TPU:0, one launch (start us, length us, event | category | flops | bytes accessed | tf_op | source)
XLA Modules:
  0.0 432.4 jit_solution(13236212844909141665)
XLA Ops:
  7.2 0.0 all-gather.2.cloned.1.call-start
  7.2 0.9 convert.28
  8.1 0.9 convert.29
  9.0 1.1 convert.27
  10.1 0.8 pad_maximum_fusion.1
  10.9 0.0 all-gather.2.cloned.1.call-update
  10.9 0.0 reduce-scatter.3.cloned.1.call-start
  11.0 1.1 copy.13
  12.1 0.0 copy-start
  12.1 0.8 fusion.50
  12.9 0.1 broadcast_multiply_fusion.2
  13.0 0.9 broadcast_compare_fusion
  13.9 96.4 %all-gather.2.cloned.1.call-done = bf16[8192,768]{1,0:T(8,128)(2,1)} async-done(((bf16[256,768]{1,0:T(8,128)(2,1)}), bf16[8192,768]{1,0:T(8,128)(2,1)}) %all-gather.2.cloned.1.call-update) | async-done | bytes 12582928 | tf_op jit(solution)/shard_map/all_gather | solution.py:41
  110.2 7.7 %fusion.14 = f32[256,768]{0,1:T(8,128)S(1)} fusion(bf16[8192,768]{1,0:T(8,128)(2,1)} %all-gather.2.cloned.1.call-done, bf16[1,256,8192]{2,1,0:T(8,128)(2,1)} %param.6), kind=kOutput, calls=%fused_computation.18 | convolution fusion | flops 3221225472 | bytes 17563648 | tf_op jit(solution)/shard_map/dot_general | solution.py:42
  118.0 0.5 broadcast_multiply_fusion.1
  118.5 16.1 %all_gather.8 = bf16[1024,256]{0,1:T(8,128)(2,1)S(1)} all-gather(bf16[256,256]{0,1:T(8,128)(2,1)S(1)} %pad_maximum_fusion.6), channel_id=1, replica_groups=mesh['dp'=8,'ctx'=4] {'ctx'}, dimensions={0}, use_global_device_ids=true | all-gather | bytes 655360 | tf_op jit(solution)/shard_map/all_gather | solution.py:53
  134.6 0.1 fusion.32
  134.7 1.0 select_reduce_fusion
  135.7 1.5 fusion.6
  137.3 1.4 multiply_reduce_fusion
  138.7 0.0 copy-done
  138.7 1.2 fusion.21
  139.9 2.6 fusion.1
  142.5 0.5 fusion.24
  142.9 0.8 pad_maximum_fusion
  143.8 0.0 reduce-scatter.3.cloned.1.call-update
  143.8 0.2 reduce-scatter.5.cloned.1.call-start
  144.0 0.8 broadcast_multiply_fusion
  144.9 0.1 fusion.34
  145.0 18.6 %reduce-scatter.3.cloned.1.call-done = bf16[256,256]{0,1:T(8,128)(2,1)} async-done(((bf16[1024,256]{0,1:T(8,128)(2,1)}), bf16[256,256]{0,1:T(8,128)(2,1)}) %reduce-scatter.3.cloned.1.call-update) | async-done | bytes 131088 | tf_op jit(solution)/shard_map/reduce_scatter | solution.py:100
  163.6 0.9 convert_element_type.54
  164.5 0.8 slice.92
  165.3 0.5 fusion.38
  165.8 0.8 slice.94
  166.6 12.5 %convolution_bitcast_fusion = f32[8192,768]{0,1:T(8,128)} fusion(bf16[1,256,8192]{2,1,0:T(8,128)(2,1)} %param.6, bf16[256,128]{0,1:T(8,128)(2,1)S(1)} %slice.94, bf16[256,128]{0,1:T(8,128)(2,1)S(1)} %fusion.38, bf16[256,512]{0,1:T(8,128)(2,1)S(1)} %bitcast.57), kind=kOutput, calls=%fused_computation | convolution fusion | flops 3222405120 | bytes 29753344 | tf_op jit(solution)/shard_map/dot_general | solution.py:114
  179.2 0.0 reduce-scatter.5.cloned.1.call-update
  179.2 0.8 copy.17
  180.0 15.0 %fusion = bf16[1,256,8192]{2,1,0:T(8,128)(2,1)} fusion(bf16[8192,768]{1,0:T(8,128)(2,1)} %all-gather.2.cloned.1.call-done, bf16[256,128]{0,1:T(8,128)(2,1)S(1)} %slice.94, bf16[256,128]{0,1:T(8,128)(2,1)S(1)} %fusion.38, bf16[256,512]{0,1:T(8,128)(2,1)S(1)} %bitcast.58), kind=kOutput, calls=%fused_computation.2 | convolution fusion | flops 3224502272 | bytes 17170432 | tf_op jit(solution)/shard_map/dot_general | solution.py:110
  195.0 226.3 %reduce-scatter.5.cloned.1.call-done = f32[256,768]{0,1:T(8,128)} async-done(((f32[8192,768]{0,1:T(8,128)}), f32[256,768]{0,1:T(8,128)}) %reduce-scatter.5.cloned.1.call-update) | async-done | bytes 786448 | tf_op jit(solution)/shard_map/reduce_scatter | solution.py:113
  421.3 1.1 slice.95
  422.4 1.0 copy.18
  423.4 1.0 fusion.51
  424.4 0.8 copy.20
  425.2 0.8 copy.19
  (10 shorter events, 0.2 us)
Async XLA Ops:
  7.2 103.1 %all-gather.2.cloned.1.call-start = ((), (), s32[]{:S(2)}) async-start(), calls=%async_computation.2 | async-start | bytes 12976128 | tf_op jit(solution)/shard_map/all_gather | solution.py:41
  10.9 152.7 %reduce-scatter.3.cloned.1.call-start = ((), (), s32[]{:S(2)}) async-start(), calls=%async_computation.3 | async-start | bytes 655360 | tf_op jit(solution)/shard_map/reduce_scatter | solution.py:100
  12.1 126.7 %copy-start = (bf16[1,256,512]{1,2,0:T(8,128)(2,1)}, bf16[1,256,512]{1,2,0:T(8,128)(2,1)S(1)}, u32[]{:S(2)}) copy-start(bf16[1,256,512]{1,2,0:T(8,128)(2,1)S(1)} %copy.13) | copy-start | bytes 786436
  143.8 277.5 %reduce-scatter.5.cloned.1.call-start = ((), (), s32[]{:S(2)}) async-start(), calls=%async_computation.4 | async-start | bytes 25952256 | tf_op jit(solution)/shard_map/reduce_scatter | solution.py:113
Sparse Core Ops, SparseCore 0:
  11.5 98.7 all-gather.1
  143.9 19.6 reduce-scatter.2
  179.3 241.9 reduce-scatter.4
where the time goes:
time: 433 us; the launch traced here: 432 us
  waiting for transfers between devices  341 us (79%)
  matrix products  42.7 us (10%)
  blocking collectives  16.1 us (4%)
  between operations  13.9 us (3%)
  other arithmetic  10 us (2%)
  local copies, waits for them, and re-layouts  8.16 us (2%)
    reduce_scatter x1, waiting for transfers between devices, body(): lax.psum_scatter(lax.dot_general(token_rows, grad_proj, (((0,), (0,)), ((...  226 us
    all_gather x1, waiting for transfers between devices, body(): lax.all_gather(local_weights, ('dp', 'ctx'), axis=0, tiled=True)  96.4 us
    reduce_scatter x1, waiting for transfers between devices, body(): lax.psum_scatter(keyval_term.astype(jnp.bfloat16), 'ctx', scatter_dimensi...  18.6 us
    all_gather x1, blocking collectives, body(): key_piece = lax.all_gather(key_value, 'ctx', axis=0, tiled=True)  16.1 us
    dot_general x1, matrix products, body(): lax.dot_general(grad_proj, weights_all, (((1,), (1,)), ((), ())), preferr...  15 us
    dot_general x1, matrix products, body(): lax.dot_general(token_rows, grad_proj, (((0,), (0,)), ((), ())), preferre...  12.5 us
  transfers between devices with their start and end apart: 3, of which 3 were waited for; matrix products, arithmetic and copies ran while one was open for 5% of the time, Pallas kernels for 0%

commit v1 on v0

v1 whole, which is shorter than its diff:
```python
import functools

import jax
import jax.numpy as jnp
from jax import lax
from jax.experimental import pallas as pl
from jax.experimental.pallas import tpu as pltpu
from jax.sharding import Mesh, PartitionSpec as P

ROPE_BASE = 1000000.0
MASKED = -1e30


def rope_tables(positions_in, head_dim):
    half_width = head_dim // 2
    exponent = jnp.arange(half_width).astype(jnp.float32) * (2.0 / head_dim)
    frequency = jnp.power(ROPE_BASE, -exponent)
    angles = positions_in.astype(jnp.float32)[:, None] * frequency[None, :]
    angles = jnp.concatenate([angles, angles], axis=1)
    return (jnp.cos(angles), jnp.sin(angles))


def mm(a, b, dims):
    return lax.dot_general(a, b, (dims, ((), ())), preferred_element_type=jnp.float32)


def shift(block, axis, step):
    size = lax.axis_size(axis)
    return lax.ppermute(block, axis, [(i, (i + step) % size) for i in range(size)])


def after(block, *others):
    return lax.optimization_barrier((block, *others))[0]


def swap(block):
    return shift(block, "core", 1)


def gather_line(block):
    return [block] + [shift(block, "ctx", k) for k in range(1, lax.axis_size("ctx"))]


def along(block, axis):
    return [shift(block, axis, step) for step in range(1, lax.axis_size(axis))]


def gather_corners(sides_a, sides_b, way, *deps):
    corners = {}
    for da, side_a in enumerate(sides_a, 1):
        for db, side_b in enumerate(sides_b, 1):
            mid = side_a.shape[0] // 2
            if way == "b":
                corners[da, db] = [shift(after(side_a, *deps), "b", db)]
            elif way == "a":
                corners[da, db] = [shift(after(side_b, *deps), "a", da)]
            else:
                corners[da, db] = [
                    shift(after(side_a[:mid], *deps), "b", db),
                    shift(after(side_b[mid:], *deps), "a", da),
                ]
    return corners


def in_order(block, sides_a, sides_b, corners):
    slabs = [[block]] + [[side] for side in sides_b]
    for da, side in enumerate(sides_a, 1):
        slabs.append([side])
        slabs += [corners[da, db] for db in range(1, len(sides_b) + 1)]
    return slabs


def reduce_corners(make, way, split, *deps):
    size_b = lax.axis_size("b")
    whole, top, low = slice(None), slice(0, split), slice(split, None)
    came_a, came_b = {}, {}
    for da in range(1, lax.axis_size("a")):
        for db in range(1, size_b):
            i = da * size_b + db
            if way == "b":
                came_a[da, db] = shift(make(i, whole, deps), "b", -db)
            elif way == "a":
                came_b[da, db] = shift(make(i, whole, deps), "a", -da)
            else:
                came_a[da, db] = shift(make(i, top, deps), "b", -db)
                came_b[da, db] = shift(make(i, low, deps), "a", -da)
    return came_a, came_b


def reduce_sides(make, came, way, split, *deps):
    size_a, size_b = lax.axis_size("a"), lax.axis_size("b")
    whole, top, low = slice(None), slice(0, split), slice(split, None)

    def side(i, extra, part):
        if not extra:
            return make(i, whole, deps)
        if way != "both":
            return make(i, whole, deps, extra)
        halves = [make(i, rows, deps, extra if rows == part else []) for rows in (top, low)]
        return jnp.concatenate(halves, axis=0)

    arrived = []
    for da in range(1, size_a):
        extra = [piece for (at, _), piece in came[0].items() if at == da]
        arrived.append(shift(side(da * size_b, extra, top), "a", -da))
    for db in range(1, size_b):
        extra = [piece for (_, at), piece in came[1].items() if at == db]
        arrived.append(shift(side(db, extra, low), "b", -db))
    return arrived


def reduce_line(term, last=()):
    size = lax.axis_size("ctx")
    rows = term.shape[0] // size
    total = after(term[:rows], *last).astype(jnp.float32)
    for k in range(1, size):
        total = total + shift(term[k * rows : (k + 1) * rows], "ctx", -k).astype(jnp.float32)
    return total


def pick_kernel(slab_ref, piece_ref, source_ref, mine_ref, theirs_ref, *, block):
    for k in range(mine_ref.shape[1] // block):
        to = slice(k * block, (k + 1) * block)
        start = pl.multiple_of(piece_ref[0, k] * block, block)
        mine_ref[:, to] = source_ref[:, pl.ds(start, block)]
        start = pl.multiple_of(piece_ref[1, k] * block, block)
        theirs_ref[:, to] = source_ref[:, pl.ds(start, block)]


def slab_terms(grads, slabs, i):
    cuts = {0}
    for part in slabs:
        at = 0
        for piece in part[i]:
            at += piece.shape[0]
            cuts.add(at)
    cuts = sorted(cuts)
    for low, high in zip(cuts[:-1], cuts[1:]):
        total = None
        for grad, part in zip(grads, slabs):
            at = 0
            for piece in part[i]:
                if at <= low and high <= at + piece.shape[0]:
                    term = dot(grad, piece[low - at : high - at, :], 1, 1)
                    total = term if total is None else total + term
                at += piece.shape[0]
        yield low, total


def nest(refs, shape):
    refs = iter(refs)
    return [[[next(refs) for _ in range(count)] for count in part] for part in shape]


def grad_kernel(*refs, shape, plane):
    parts = len(shape)
    grads = [ref[...] for ref in refs[:parts]]
    slabs = nest(refs[parts:-1], shape)
    for i in range(len(shape[0])):
        for low, total in slab_terms(grads, slabs, i):
            start = i * plane + low
            refs[-1][:, start : start + total.shape[1]] = total.astype(jnp.bfloat16)


def grad_place_kernel(*refs, shape, plane, block):
    slab_ref, piece_ref, *refs = refs
    parts = len(shape)
    grads = [ref[...] for ref in refs[:parts]]
    slabs = nest(refs[parts:-2], shape)
    theirs_ref, target_ref = refs[-2:]
    for i in range(len(shape[0])):
        base = slab_ref[i] * (2 * plane)
        for k in range(plane // block):
            start = pl.multiple_of(base + piece_ref[1, k] * block, block)
            at = i * plane + k * block
            target_ref[:, pl.ds(start, block)] = theirs_ref[:, at : at + block]
        for low, total in slab_terms(grads, slabs, i):
            total = total.astype(jnp.bfloat16)
            for j in range(total.shape[1] // block):
                k = low // block + j
                start = pl.multiple_of(base + piece_ref[0, k] * block, block)
                target_ref[:, pl.ds(start, block)] = total[:, j * block : (j + 1) * block]


VMEM = pl.BlockSpec(memory_space=pltpu.VMEM)


def pieces_of(slabs, pieces, block):
    at = slabs[None, :, None] * pieces.size + pieces[:, None, :]
    return at[..., None] * block + jnp.arange(block)


def pick_columns(source, slabs, pieces, block):
    rows, width = source.shape
    count, depth = slabs.shape[0], pieces.shape[1]
    half = depth * block
    if block % 128:
        at = pieces_of(slabs, pieces, block).reshape(2, -1)
        return source[:, at[0]], source[:, at[1]]
    part = jax.ShapeDtypeStruct((rows, width // 2), source.dtype)
    return pl.pallas_call(
        functools.partial(pick_kernel, block=block),
        grid_spec=pltpu.PrefetchScalarGridSpec(
            num_scalar_prefetch=2,
            grid=(count,),
            in_specs=[pl.BlockSpec((rows, 2 * half), lambda i, slab, piece: (0, slab[i]))],
            out_specs=[pl.BlockSpec((rows, half), lambda i, slab, piece: (0, i))] * 2,
        ),
        out_shape=[part, part],
        cost_estimate=pl.CostEstimate(
            flops=0, bytes_accessed=4 * rows * width, transcendentals=0
        ),
        name="pick_columns",
    )(slabs, pieces, source)


def grad_columns(grads, slabs):
    rows = grads[0].shape[0]
    shape = [[len(slab) for slab in part] for part in slabs]
    flat = [piece for part in slabs for slab in part for piece in slab]
    plane = sum(piece.shape[0] for piece in slabs[0][0])
    width = plane * len(shape[0])
    return pl.pallas_call(
        functools.partial(grad_kernel, shape=shape, plane=plane),
        in_specs=[VMEM] * (len(grads) + len(flat)),
        out_specs=VMEM,
        out_shape=jax.ShapeDtypeStruct((rows, width), jnp.bfloat16),
        compiler_params=pltpu.CompilerParams(vmem_limit_bytes=40 * 1024 * 1024),
        cost_estimate=pl.CostEstimate(
            flops=2 * rows * sum(piece.size for piece in flat),
            bytes_accessed=2 * sum(piece.size for piece in flat) + 2 * rows * width,
            transcendentals=0,
        ),
        name="grad_columns",
    )(*grads, *flat)


def grad_place(grads, slabs, theirs, places, pieces, block):
    rows, width = theirs.shape[0], 2 * theirs.shape[1]
    shape = [[len(slab) for slab in part] for part in slabs]
    flat = [piece for part in slabs for slab in part for piece in slab]
    plane = sum(piece.shape[0] for piece in slabs[0][0])
    if block % 128:
        at = pieces_of(places, pieces, block).reshape(2, -1)
        target = jnp.zeros((rows, width), theirs.dtype)
        return target.at[:, at[0]].set(grad_columns(grads, slabs)).at[:, at[1]].set(theirs)
    return pl.pallas_call(
        functools.partial(grad_place_kernel, shape=shape, plane=plane, block=block),
        grid_spec=pltpu.PrefetchScalarGridSpec(
            num_scalar_prefetch=2,
            grid=(),
            in_specs=[VMEM] * (len(grads) + len(flat) + 1),
            out_specs=VMEM,
        ),
        out_shape=jax.ShapeDtypeStruct((rows, width), jnp.bfloat16),
        compiler_params=pltpu.CompilerParams(vmem_limit_bytes=40 * 1024 * 1024),
        cost_estimate=pl.CostEstimate(
            flops=2 * rows * sum(piece.size for piece in flat),
            bytes_accessed=2 * sum(piece.size for piece in flat) + 3 * rows * width,
            transcendentals=0,
        ),
        name="grad_place",
    )(places, pieces, *grads, *flat, theirs)


def dot(a, b, left, right):
    return lax.dot_general(
        a, b, (((left,), (right,)), ((), ())), preferred_element_type=jnp.float32
    )


def attend_kernel(*refs, group, parts, head_dim, scale, last):
    q_own, q_other, grads, cos_ref, sin_ref, row_pos, key_pos = refs[:7]
    pieces = refs[7 : 7 + parts]
    rest = refs[7 + parts :]
    if last:
        before, rest = rest[0], rest[1:]
    attention_ref, grad_ref = rest[:2]
    terms = rest[2:-1]
    held = rest[-1]
    rows = q_own.shape[0]
    for j in range(parts):
        held[j * rows : (j + 1) * rows, :] = pieces[j][...]
    keys, values = held[:, :head_dim], held[:, head_dim:]
    cos, sin = cos_ref[...], sin_ref[...]
    allowed = key_pos[...] <= row_pos[...]
    key_term = value_term = None
    for h in range(group):
        at = slice(h * head_dim, (h + 1) * head_dim)
        q = q_own[:, at] + q_other[:, at]
        q = (q * cos + pltpu.roll(q, head_dim // 2, 1) * sin).astype(jnp.bfloat16)
        scores = jnp.where(allowed, dot(q, keys, 1, 1) * scale, MASKED)
        weight = jnp.exp(scores - jnp.max(scores, axis=1, keepdims=True))
        inverse = 1.0 / jnp.sum(weight, axis=1, keepdims=True)
        attention = (dot(weight.astype(jnp.bfloat16), values, 1, 0) * inverse).astype(jnp.bfloat16)
        attention_ref[:, at] = attention
        grad = grads[:, at]
        delta = jnp.sum(
            grad.astype(jnp.float32) * attention.astype(jnp.float32), axis=1, keepdims=True
        )
        probs = weight * inverse
        dscore = (probs * (dot(grad, values, 1, 1) - delta)).astype(jnp.bfloat16)
        grad_q = dot(dscore, keys, 1, 0) * scale
        grad_q = grad_q * cos - pltpu.roll(grad_q, head_dim // 2, 1) * sin
        grad_ref[:, at] = grad_q.astype(jnp.bfloat16)
        key_new = dot(dscore, q, 0, 0) * scale
        value_new = dot(probs.astype(jnp.bfloat16), grad, 0, 0)
        key_term = key_new if h == 0 else key_term + key_new
        value_term = value_new if h == 0 else value_term + value_new
    if last:
        key_term = key_term + before[:, :head_dim]
        value_term = value_term + before[:, head_dim:]
        for j in range(parts):
            span = slice(j * rows, (j + 1) * rows)
            terms[j][:, :head_dim] = key_term[span].astype(terms[j].dtype)
            terms[j][:, head_dim:] = value_term[span].astype(terms[j].dtype)
    else:
        terms[0][:, :head_dim] = key_term
        terms[0][:, head_dim:] = value_term


def attend(q_own, q_other, grads, cos, sin, row_pos, key_pos, pieces, before, scale):
    rows, columns = q_own.shape
    head_dim = cos.shape[1]
    parts = len(pieces)
    last = before is not None
    keys = parts * rows
    group = columns // head_dim
    if last:
        terms = [jax.ShapeDtypeStruct((rows, 2 * head_dim), jnp.float32)]
        terms += [jax.ShapeDtypeStruct((rows, 2 * head_dim), jnp.bfloat16)] * (parts - 1)
    else:
        terms = [jax.ShapeDtypeStruct((keys, 2 * head_dim), jnp.float32)]
    out_shape = [jax.ShapeDtypeStruct((rows, columns), jnp.bfloat16)] * 2 + terms
    operands = [q_own, q_other, grads, cos, sin, row_pos, key_pos, *pieces]
    operands += [before] if last else []
    out = pl.pallas_call(
        functools.partial(
            attend_kernel, group=group, parts=parts, head_dim=head_dim, scale=scale, last=last
        ),
        in_specs=[VMEM] * len(operands),
        out_specs=[VMEM] * len(out_shape),
        out_shape=out_shape,
        scratch_shapes=[pltpu.VMEM((keys, 2 * head_dim), jnp.bfloat16)],
        compiler_params=pltpu.CompilerParams(vmem_limit_bytes=48 * 1024 * 1024),
        cost_estimate=pl.CostEstimate(
            flops=14 * rows * keys * columns,
            bytes_accessed=8 * keys * 2 * head_dim,
            transcendentals=rows * keys * group,
        ),
        name="attend",
    )(*operands)
    return out[0], out[1], out[2:]


def finish_kernel(own, other, cos_ref, sin_ref, out):
    head_dim = cos_ref.shape[1]
    total = own[...] + other[...]
    key = total[:, :head_dim]
    key = key * cos_ref[...] + pltpu.roll(key, head_dim // 2, 1) * sin_ref[...]
    out[:, :head_dim] = key.astype(jnp.bfloat16)
    out[:, head_dim:] = total[:, head_dim:].astype(jnp.bfloat16)


def finish_keys(own, other, cos, sin):
    return pl.pallas_call(
        finish_kernel,
        in_specs=[VMEM] * 4,
        out_specs=VMEM,
        out_shape=jax.ShapeDtypeStruct(own.shape, jnp.bfloat16),
        name="finish_keys",
    )(own, other, cos, sin)


def undo_kernel(*refs):
    pieces, (cos_ref, sin_ref, out) = refs[:-3], refs[-3:]
    head_dim = cos_ref.shape[1]
    total = pieces[0][...]
    for piece in pieces[1:]:
        total = total + piece[...].astype(jnp.float32)
    key = total[:, :head_dim]
    key = key * cos_ref[...] - pltpu.roll(key, head_dim // 2, 1) * sin_ref[...]
    out[:, :head_dim] = key.astype(jnp.bfloat16)
    out[:, head_dim:] = total[:, head_dim:].astype(jnp.bfloat16)


def undo_keys(pieces, cos, sin):
    return pl.pallas_call(
        undo_kernel,
        in_specs=[VMEM] * (len(pieces) + 2),
        out_specs=VMEM,
        out_shape=jax.ShapeDtypeStruct(pieces[0].shape, jnp.bfloat16),
        name="undo_keys",
    )(*pieces, cos, sin)


def body(tokens, positions, query_weight, key_weight, value_weight, grad_output):
    token_rows = tokens[0]
    rows, width = token_rows.shape
    head_dim = key_weight.shape[1]
    query_width = query_weight.shape[1]
    heads = query_width // head_dim
    group = heads // 2
    scale = head_dim ** (-0.5)
    size_a, size_b, ctx = lax.axis_size("a"), lax.axis_size("b"), lax.axis_size("ctx")
    at_a, at_b = lax.axis_index("a"), lax.axis_index("b")
    core, place = lax.axis_index("core"), lax.axis_index("ctx")
    block = query_weight.shape[0]
    plane = ctx * block

    kv_local = jnp.concatenate([key_weight, value_weight], axis=1).astype(jnp.bfloat16)
    q_local = [
        query_weight[:, g * group * head_dim : (g + 1) * group * head_dim].astype(jnp.bfloat16)
        for g in range(2)
    ]
    kv_line = jnp.concatenate(gather_line(kv_local), axis=0)
    q_line = [jnp.concatenate(gather_line(q_local[0]), axis=0)]
    kv_sides = along(kv_line, "a"), along(kv_line, "b")
    q_line.append(jnp.concatenate(gather_line(after(q_local[1], kv_line)), axis=0))
    stage = kv_sides[0] + kv_sides[1]
    kv_corners = gather_corners(*kv_sides, "b", *stage)
    q0_a = along(after(q_line[0], *stage), "a")
    stage = q0_a + [piece for corner in kv_corners.values() for piece in corner]
    q1_a = along(after(q_line[1], *stage), "a")
    q0_b = along(after(q_line[0], *stage), "b")
    kv_slabs = in_order(kv_line, *kv_sides, kv_corners)

    da, db = jnp.meshgrid(jnp.arange(size_a), jnp.arange(size_b), indexing="ij")
    slabs = ((at_a + size_a - da) % size_a) * size_b + (at_b + size_b - db) % size_b
    slabs = slabs.reshape(-1).astype(jnp.int32)
    line = (place + ctx - jnp.arange(ctx)) % ctx
    pieces = jnp.stack([core * ctx + line, (1 - core) * ctx + line]).astype(jnp.int32)
    mine, theirs = pick_columns(token_rows, slabs, pieces, block)
    theirs = swap(theirs)

    positions = after(positions, kv_line)
    own_positions = lax.dynamic_slice_in_dim(positions, place * rows, rows)
    cos_table, sin_table = rope_tables(own_positions, head_dim)
    sin_table = jnp.where(jnp.arange(head_dim) < head_dim // 2, -sin_table, sin_table)
    key_positions = jnp.concatenate(
        [
            lax.dynamic_slice_in_dim(positions, ((place + ctx - k) % ctx) * rows, rows)
            for k in range(ctx)
        ]
    )

    def product(columns, slabs):
        at, total = 0, None
        for piece in [piece for slab in slabs for piece in slab]:
            end = at + piece.shape[0]
            term = mm(columns[:, at:end], piece, ((1,), (0,)))
            total = term if total is None else total + term
            at = end
        return total

    def project(slabs):
        other = swap(product(theirs, slabs))
        return product(mine, slabs), other

    columns = jnp.concatenate([mine, theirs], axis=0)

    def terms_of(own, other):
        both = jnp.concatenate([own, other], axis=0)

        def make(i, part, deps=(), extra=()):
            start, stop, _ = part.indices(plane)
            at = slice(i * plane + start, i * plane + stop)
            term = mm(columns[:, at], after(both, *deps) if deps else both, ((0,), (0,)))
            for piece in extra:
                term = term + piece.astype(jnp.float32)
            return term.astype(jnp.bfloat16)

        return make

    key_value = finish_keys(*project(kv_slabs), cos_table, sin_table)
    stage = q1_a + q0_b + [key_value]
    q0_corners = gather_corners(q0_a, q0_b, "a", *stage)
    q1_b = along(after(q_line[1], *stage), "b")
    key_values = gather_line(key_value)
    stage = q1_b + [piece for corner in q0_corners.values() for piece in corner]
    q1_corners = gather_corners(q1_a, q1_b, "both", *stage)
    q_slabs = [
        in_order(q_line[0], q0_a, q0_b, q0_corners),
        in_order(q_line[1], q1_a, q1_b, q1_corners),
    ]
    attentions, gradients, made, came = [], [], [], []
    mid = plane // 2
    term = None
    for g in range(2):
        span = slice(g * group * head_dim, (g + 1) * group * head_dim)
        attention, grad_q, terms = attend(
            *project(q_slabs[g]),
            grad_output[0][:, span],
            cos_table,
            sin_table,
            own_positions[:, None],
            key_positions[None, :],
            key_values,
            term,
            scale,
        )
        term = terms[0]
        attentions.append(attention)
        grads = (grad_q, swap(grad_q))
        gradients.append(grads)
        made.append(terms_of(*grads))
        came.append(reduce_corners(made[g], "ba"[g], mid))
    summed = [terms[0]] + [shift(terms[k], "ctx", -k) for k in range(1, ctx)]
    first = [*came[0][0].values(), *came[0][1].values()]
    sides = [reduce_sides(made[0], came[0], "b", mid, *first)]
    grad_kv = undo_keys([after(summed[0], *first), *summed[1:]], cos_table, sin_table)
    gradients.append((grad_kv, swap(grad_kv)))
    made.append(terms_of(*gradients[2]))
    came.append(reduce_corners(made[2], "both", mid))
    line0 = made[0](0, slice(None), (), sides[0])
    q_sum = reduce_line(line0)
    sides.append(reduce_sides(made[1], came[1], "a", mid, *sides[0]))
    kv_sides = reduce_sides(made[2], came[2], "both", mid)
    kv_sum = reduce_line(made[2](0, slice(None), (), kv_sides))

    weights = [*q_slabs, kv_slabs]
    grad_theirs = grad_columns(
        [gradients[0][1], gradients[1][1], after(gradients[2][1], q_sum, *kv_sides)], weights
    )
    grad_theirs = swap(grad_theirs)
    line1 = made[1](0, slice(None), (), sides[1])
    grad_input = grad_place(
        [gradients[0][0], gradients[1][0], gradients[2][0]], weights, grad_theirs, slabs, pieces, block
    )
    q_grads = [q_sum, reduce_line(line1, (grad_input,))]
    kv_wgrad = kv_sum

    query_grad = jnp.concatenate(q_grads, axis=1)
    key_grad = kv_wgrad[:, :head_dim]
    value_grad = kv_wgrad[:, head_dim:]
    attention_rows = jnp.concatenate(attentions, axis=1)
    return (attention_rows[None], grad_input[None], query_grad, key_grad, value_grad)


def solution(mesh):
    dp, ctx = mesh.devices.shape
    fine = Mesh(mesh.devices.reshape(dp // 4, 2, 2, ctx), ("a", "b", "core", "ctx"))
    batch = P(("a", "b", "core"), "ctx", None)
    master = P(("a", "b", "core", "ctx"), None)
    in_specs = (batch, P(), master, master, master, batch)
    out_specs = (batch, batch, master, master, master)
    return jax.shard_map(body, mesh=fine, in_specs=in_specs, out_specs=out_specs, check_vma=False)
```

time: 433 us -> 218 us (0.50)
  waiting for transfers between devices: 341 us -> 77.1 us
  starting transfers between devices: 0.3 us -> 55.7 us
  Pallas kernels: 0 us -> 23.8 us
  blocking collectives: 16.1 us -> 0 us
  between operations: 13.9 us -> 1.82 us
    reduce_scatter x2 -> x0, waiting for transfers between devices: 245 us -> none  [the longest x1 226 us: body(): lax.psum_scatter(lax.dot_general(token_rows, grad_proj, (((0,), (0,)), ((...]
    all_gather x1 -> x0, waiting for transfers between devices: 96.4 us -> none  [body(): lax.all_gather(local_weights, ('dp', 'ctx'), axis=0, tiled=True)]
    ppermute x0 -> x52, waiting for transfers between devices: none -> 77.1 us  [shift(): lax.ppermute(block, axis, [(i, (i + step) % size) for i in range(size)])]
    ppermute x0 -> x52, starting transfers between devices: none -> 55.7 us  [shift(): lax.ppermute(block, axis, [(i, (i + step) % size) for i in range(size)])]
    pallas_call x0 -> x7, Pallas kernels: none -> 23.8 us  [the longest x1 5.84 us: grad_place(): pl.pallas_call(functools.partial(grad_place_kernel, shape=shape, plane=pl...]
    all_gather x1 -> x0, blocking collectives: 16.1 us -> none  [body(): key_piece = lax.all_gather(key_value, 'ctx', axis=0, tiled=True)]
    dot_general x9 -> x41, matrix products: 42.7 us -> 39.2 us  [mm(): lax.dot_general(a, b, (dims, ((), ())), preferred_element_type=jnp.float32)]
  transfers between devices with their start and end apart: 3 -> 52, of which waited for: 3 -> 21; matrix products, arithmetic and copies ran while one was open for 5% -> 22% of each run, Pallas kernels for 0% -> 9%
where the time goes in v1:
time: 218 us; the launch traced here: 217 us
  waiting for transfers between devices  77.1 us (35%)
  starting transfers between devices  55.7 us (26%)
  matrix products  39.2 us (18%)
  Pallas kernels  23.8 us (11%)
  local copies, waits for them, and re-layouts  10.8 us (5%)
  other arithmetic  8.33 us (4%)
    ppermute x52, waiting for transfers between devices, shift(): lax.ppermute(block, axis, [(i, (i + step) % size) for i in range(size)])  77.1 us
    ppermute x52, starting transfers between devices, shift(): lax.ppermute(block, axis, [(i, (i + step) % size) for i in range(size)])  55.7 us
    dot_general x41, matrix products, mm(): lax.dot_general(a, b, (dims, ((), ())), preferred_element_type=jnp.float32)  39.2 us
    pallas_call x1, Pallas kernels, grad_place(): pl.pallas_call(functools.partial(grad_place_kernel, shape=shape, plane=pl...  5.84 us
    pallas_call x1, Pallas kernels, pick_columns(): pl.pallas_call(functools.partial(pick_kernel, block=block), grid_spec=plt...  5.68 us
    pallas_call x2, Pallas kernels, attend(): pl.pallas_call(functools.partial(attend_kernel, group=group, parts=parts,...  5.4 us
    unnamed x118, local copies, waits for them, and re-layouts  4.76 us
  transfers between devices with their start and end apart: 52, of which 21 were waited for; matrix products, arithmetic and copies ran while one was open for 22% of the time, Pallas kernels for 9%

profile of v1, /device:TPU:0, one launch (start us, length us, event | category | flops | bytes accessed | tf_op | source)
XLA Modules:
  0.0 216.7 jit_solution(15907307198906648051)
XLA Ops:
  2.5 5.1 %collective-permute-start.5 = (bf16[256,256]{1,0:T(8,128)(2,1)S(1)}, bf16[256,256]{1,0:T(8,128)(2,1)S(1)}, u32[]{:S(2)}, u32[]{:S(2)}) collective-permute-start(bf16[256,256]{1,0:T(8,128)(2,1)S(1)} %pad_maximum_fusion.6), channel_id=1, source_target_pairs={{0,3},{1,0},{2,1},{3,2},{4,7},{5,4},{6,5},{7,6},{8,11},{9,8},{10,9... | collective-permute-start | bytes 393224 | tf_op jit(solution)/shard_map/ppermute | solution.py:29
  9.8 2.9 %collective-permute-start.2 = (bf16[256,256]{1,0:T(8,128)(2,1)S(1)}, bf16[256,256]{1,0:T(8,128)(2,1)S(1)}, u32[]{:S(2)}, u32[]{:S(2)}) collective-permute-start(bf16[256,256]{1,0:T(8,128)(2,1)S(1)} %get-tuple-element.75), channel_id=1, source_target_pairs={{0,3},{1,0},{2,1},{3,2},{4,7},{5,4},{6,5},{7,6},{8,11},{9,8},{10,9... | collective-permute-start | bytes 393224 | tf_op jit(solution)/shard_map/ppermute | solution.py:29
  15.9 5.7 %pick_columns.1 = (bf16[256,4096]{1,0:T(8,128)(2,1)}, bf16[256,4096]{1,0:T(8,128)(2,1)}) custom-call(s32[4]{0:T(128)} %fusion.86.slab_ref.refs_0_, s32[2,4]{1,0:T(2,128)} %pad_add_fusion.1.piece_ref.refs_1_, bf16[256,8192]{1,0:T(8,128)(2,1)} %bitcast.39), custom_call_target="tpu_custom_call" | custom-call | bytes 8388608 | tf_op jit(solution)/shard_map/pick_columns/pallas_call | solution.py:201
  21.6 3.1 %constant_dynamic-update-slice_fusion.5 = bf16[512,4096]{1,0:T(8,128)(2,1)} fusion(bf16[256,4096]{1,0:T(8,128)(2,1)} %get-tuple-element.31), kind=kLoop, calls=%fused_computation.126 | loop fusion | bytes 4194304
  25.0 3.1 %collective-permute-start.12 = (bf16[256,256]{1,0:T(8,128)(2,1)S(1)}, bf16[256,256]{1,0:T(8,128)(2,1)S(1)}, u32[]{:S(2)}, u32[]{:S(2)}) collective-permute-start(bf16[256,256]{1,0:T(8,128)(2,1)S(1)} %get-tuple-element.35), channel_id=1, source_target_pairs={{0,2},{1,3},{2,0},{3,1},{4,6},{5,7},{6,4},{7,5},{8,10},{9,11},{10,... | collective-permute-start | bytes 393224 | tf_op jit(solution)/shard_map/ppermute | solution.py:29
  28.3 1.3 negate_select_fusion
  29.5 1.3 collective-permute-start.11
  30.8 1.6 collective-permute-start.7
  32.6 1.5 collective-permute-start.6
  35.1 2.2 %collective-permute-done.11 = bf16[256,256]{1,0:T(8,128)(2,1)S(1)} collective-permute-done((bf16[256,256]{1,0:T(8,128)(2,1)S(1)}, bf16[256,256]{1,0:T(8,128)(2,1)S(1)}, u32[]{:S(2)}, u32[]{:S(2)}) %collective-permute-start.11) | collective-permute-done | bytes 131104 | tf_op jit(solution)/shard_map/ppermute | solution.py:29
  37.3 1.6 collective-permute-start.13
  39.0 5.7 %collective-permute-done.7.refs_13_.refs_15_ = bf16[1024,256]{1,0:T(8,128)(2,1)S(1)} collective-permute-done((bf16[1024,256]{1,0:T(8,128)(2,1)S(1)}, bf16[1024,256]{1,0:T(8,128)(2,1)S(1)}, u32[]{:S(2)}, u32[]{:S(2)}) %collective-permute-start.7) | collective-permute-done | bytes 524320 | tf_op jit(solution)/shard_map/ppermute | solution.py:29
  44.6 1.2 collective-permute-done.6.refs_14_.refs_16_
  45.9 1.5 collective-permute-start.8
  47.9 1.3 fusion.70
  49.3 1.4 fusion.64
  50.7 7.7 %collective-permute-done.8.refs_5_.refs_7_ = bf16[1024,256]{1,0:T(8,128)(2,1)S(1)} collective-permute-done((bf16[1024,256]{1,0:T(8,128)(2,1)}, bf16[1024,256]{1,0:T(8,128)(2,1)S(1)}, u32[]{:S(2)}, u32[]{:S(2)}) %collective-permute-start.8) | collective-permute-done | bytes 524320 | tf_op jit(solution)/shard_map/ppermute | solution.py:29
  63.2 8.4 %collective-permute-done.14.refs_9_.refs_11_ = bf16[1024,256]{1,0:T(8,128)(2,1)S(1)} collective-permute-done((bf16[1024,256]{1,0:T(8,128)(2,1)S(1)}, bf16[1024,256]{1,0:T(8,128)(2,1)S(1)}, u32[]{:S(2)}, u32[]{:S(2)}) %collective-permute-start.14) | collective-permute-done | bytes 524320 | tf_op jit(solution)/shard_map/ppermute | solution.py:29
  73.3 2.0 fusion.72
  75.4 1.3 fusion.41
  76.7 1.3 fusion.51
  78.1 1.3 fusion.57
  79.4 1.3 fusion.15
  80.8 2.2 %fusion.55 = f32[256,256]{1,0:T(8,128)} fusion(bf16[1024,256]{1,0:T(8,128)(2,1)} %collective-permute-done.10.refs_4_.refs_6_, bf16[256,4096]{1,0:T(8,128)(2,1)} %collective-permute-done.15), kind=kOutput, calls=%fused_computation.81 | convolution fusion | flops 134217728 | bytes 1310720 | tf_op jit(solution)/shard_map/dot_general | solution.py:24
  83.1 2.0 fusion.49
  85.8 1.9 finish_keys.1.refs_7_
  89.2 1.3 fusion.47
  90.6 3.3 %constant_dynamic-update-slice_fusion.4 = bf16[512,4096]{1,0:T(8,128)(2,1)} fusion(bf16[512,4096]{1,0:T(8,128)(2,1)} %constant_dynamic-update-slice_fusion.5, bf16[256,4096]{1,0:T(8,128)(2,1)} %collective-permute-done.15), kind=kLoop, calls=%fused_computation.125 | loop fusion | bytes 4194304 | tf_op jit(solution)/shard_map/concatenate | solution.py:460
  94.0 1.3 collective-permute-start.20
  95.2 1.9 collective-permute-start.19
  97.2 5.0 %collective-permute-done.17.refs_6_.refs_8_ = bf16[1024,256]{1,0:T(8,128)(2,1)S(1)} collective-permute-done((bf16[1024,256]{1,0:T(8,128)(2,1)}, bf16[1024,256]{1,0:T(8,128)(2,1)S(1)}, u32[]{:S(2)}, u32[]{:S(2)}) %collective-permute-start.17) | collective-permute-done | bytes 524320 | tf_op jit(solution)/shard_map/ppermute | solution.py:29
  102.5 1.3 collective-permute-start.24
  104.6 1.3 fusion.39
  106.3 1.3 fusion.17
  108.0 1.3 fusion.53
  111.4 1.3 fusion.79
  112.7 1.3 fusion.23
  114.7 2.6 %attend.2 = (bf16[256,256]{1,0:T(8,128)(2,1)S(1)}, bf16[256,256]{1,0:T(8,128)(2,1)S(1)}, f32[1024,256]{1,0:T(8,128)S(1)}) custom-call(f32[256,256]{1,0:T(8,128)S(1)} %fusion.11.refs_0_, f32[256,256]{1,0:T(8,128)S(1)} %collective-permute-done.18.refs_1_, bf16[256,256]{1,0:T(8,128)(2,1)S(1)} %copy-done.20, f32[256,128]{1,0:T(8,128)S(1)} %copy-done.9, ...), custom_call_target="tpu_custom_call" | custom-call | flops 939524096 | bytes 2097152 | tf_op jit(solution)/shard_map/attend/pallas_call | solution.py:337
  118.7 1.9 convolution_convert_fusion.3
  121.9 2.8 %attend.3 = (bf16[256,256]{1,0:T(8,128)(2,1)S(1)}, bf16[256,256]{1,0:T(8,128)(2,1)S(1)}, f32[256,256]{1,0:T(8,128)S(1)}, bf16[256,256]{1,0:T(8,128)(2,1)S(1)}, b...) custom-call(f32[256,256]{1,0:T(8,128)S(1)} %fusion.20.refs_0_, f32[256,256]{1,0:T(8,128)S(1)} %collective-permute-done.25.refs_1_, ...), custom_call_target="tpu_custom_call" | custom-call | flops 939524096 | bytes 2097152 | tf_op jit(solution)/shard_map/attend/pallas_call | solution.py:337
  125.9 1.9 collective-permute-start.30
  129.3 5.4 %collective-permute-done.27 = bf16[1024,256]{1,0:T(8,128)(2,1)S(1)} collective-permute-done((bf16[1024,256]{1,0:T(8,128)(2,1)S(1)}, bf16[1024,256]{1,0:T(8,128)(2,1)S(1)}, u32[]{:S(2)}, u32[]{:S(2)}) %collective-permute-start.27) | collective-permute-done | bytes 524320 | tf_op jit(solution)/shard_map/ppermute | solution.py:29
  134.6 3.2 %collective-permute-done.29.refs_2_ = bf16[256,256]{1,0:T(8,128)(2,1)S(1)} collective-permute-done((bf16[256,256]{1,0:T(8,128)(2,1)S(1)}, bf16[256,256]{1,0:T(8,128)(2,1)S(1)}, u32[]{:S(2)}, u32[]{:S(2)}) %collective-permute-start.29) | collective-permute-done | bytes 131104 | tf_op jit(solution)/shard_map/ppermute | solution.py:29
  138.5 2.0 undo_keys.1.refs_4_
  140.5 2.1 fusion.4
  142.6 1.7 convolution_convert_fusion.2
  145.3 1.5 collective-permute-start.34
  150.0 15.0 %collective-permute-done.38 = bf16[512,256]{1,0:T(8,128)(2,1)S(1)} collective-permute-done((bf16[512,256]{1,0:T(8,128)(2,1)S(1)}, bf16[512,256]{1,0:T(8,128)(2,1)S(1)}, u32[]{:S(2)}, u32[]{:S(2)}) %collective-permute-start.38) | collective-permute-done | bytes 262176 | tf_op jit(solution)/shard_map/ppermute | solution.py:29
  165.4 1.2 collective-permute-start.39
  167.0 1.3 collective-permute-start.41
  168.9 1.3 collective-permute-start.36
  170.2 2.8 %collective-permute-start.35 = (bf16[256,256]{1,0:T(8,128)(2,1)S(1)}, bf16[256,256]{1,0:T(8,128)(2,1)S(1)}, u32[]{:S(2)}, u32[]{:S(2)}) collective-permute-start(bf16[256,256]{1,0:T(8,128)(2,1)S(1)} %get-tuple-element.70), channel_id=1, source_target_pairs={{0,3},{1,0},{2,1},{3,2},{4,7},{5,4},{6,5},{7,6},{8,11},{9,8},{10,9... | collective-permute-start | bytes 393224 | tf_op jit(solution)/shard_map/ppermute | solution.py:29
  173.6 3.6 %collective-permute-done.37 = bf16[256,256]{1,0:T(8,128)(2,1)S(1)} collective-permute-done((bf16[256,256]{1,0:T(8,128)(2,1)S(1)}, bf16[256,256]{1,0:T(8,128)(2,1)S(1)}, u32[]{:S(2)}, u32[]{:S(2)}) %collective-permute-start.37) | collective-permute-done | bytes 131104 | tf_op jit(solution)/shard_map/ppermute | solution.py:29
  177.2 1.2 collective-permute-start.44
  178.4 2.3 %collective-permute-done.36 = bf16[256,256]{1,0:T(8,128)(2,1)S(1)} collective-permute-done((bf16[256,256]{1,0:T(8,128)(2,1)S(1)}, bf16[256,256]{1,0:T(8,128)(2,1)S(1)}, u32[]{:S(2)}, u32[]{:S(2)}) %collective-permute-start.36) | collective-permute-done | bytes 131104 | tf_op jit(solution)/shard_map/ppermute | solution.py:29
  180.9 3.0 %grad_columns.1 = bf16[256,4096]{1,0:T(8,128)(2,1)S(1)} custom-call(bf16[256,256]{1,0:T(8,128)(2,1)S(1)} %copy-done.15, bf16[256,256]{1,0:T(8,128)(2,1)S(1)} %collective-permute-done.31.refs_1_, bf16[256,256]{1,0:T(8,128)(2,1)S(1)} %collective-permute-done.32.refs_2_, bf16[1024,256]{1,0:T(8,128)(2,1)} %pad_maximum_fusion.refs_3_.refs_5_, ...), custom_call_target="tpu_custom_call" | custom-call | flops 1610612736 | bytes 8388608 | tf_op jit(solution)/shard_map/grad_columns/pallas_call | solution.py:223
  184.5 1.3 collective-permute-start.43
  185.8 6.3 %collective-permute-done.44 = bf16[1024,256]{1,0:T(8,128)(2,1)S(1)} collective-permute-done((bf16[1024,256]{1,0:T(8,128)(2,1)S(1)}, bf16[1024,256]{1,0:T(8,128)(2,1)S(1)}, u32[]{:S(2)}, u32[]{:S(2)}) %collective-permute-start.44) | collective-permute-done | bytes 524320 | tf_op jit(solution)/shard_map/ppermute | solution.py:29
  194.2 2.0 collective-permute-start.50
  196.2 5.0 %collective-permute-done.43 = bf16[1024,256]{1,0:T(8,128)(2,1)S(1)} collective-permute-done((bf16[1024,256]{1,0:T(8,128)(2,1)S(1)}, bf16[1024,256]{1,0:T(8,128)(2,1)S(1)}, u32[]{:S(2)}, u32[]{:S(2)}) %collective-permute-start.43) | collective-permute-done | bytes 524320 | tf_op jit(solution)/shard_map/ppermute | solution.py:29
  203.8 1.5 collective-permute-start.47
  205.3 1.7 collective-permute-start.46
  207.0 2.1 collective-permute-done.49
  209.9 5.8 %grad_place.1 = bf16[256,8192]{1,0:T(8,128)(2,1)} custom-call(s32[4]{0:T(128)S(1)} %copy-done.22, s32[2,4]{1,0:T(2,128)S(1)} %copy-done.21, bf16[256,256]{1,0:T(8,128)(2,1)S(1)} %copy-done.11, bf16[256,256]{1,0:T(8,128)(2,1)S(1)} %copy-done.13, bf16[256,256]{1,0:T(8,128)(2,1)S(1)} %copy-done.16, bf16[1024,256]{1,0:T(8,128)(2,1)} %pad_maximum_fusion.refs_3_.refs_5_, ...), custom_call_target="tpu_custom_call" | custom-call | flops 1610612736 | bytes 12582912 | tf_op jit(solution)/shard_map/grad_place/pallas_call | solution.py:247
  (247 shorter events, 41.6 us)
Async XLA Ops:
  0.6 13.4 %copy-start.34 = (bf16[1,256,512]{2,1,0:T(8,128)(2,1)S(1)}, bf16[1,256,512]{2,1,0:T(8,128)(2,1)}, u32[]{:S(2)}) copy-start(bf16[1,256,512]{2,1,0:T(8,128)(2,1)} %param.11) | copy-start | bytes 786436
  2.5 22.2 %collective-permute-start.5 = (bf16[256,256]{1,0:T(8,128)(2,1)S(1)}, bf16[256,256]{1,0:T(8,128)(2,1)S(1)}, u32[]{:S(2)}, u32[]{:S(2)}) collective-permute-start(bf16[256,256]{1,0:T(8,128)(2,1)S(1)} %pad_maximum_fusion.6), channel_id=1, source_target_pairs={{0,3},{1,0},{2,1},{3,2},{4,7},{5,4},{6,5},{7,6},{8,11},{9,8},{10,9... | collective-permute-start | bytes 393224 | tf_op jit(solution)/shard_map/ppermute | solution.py:29
  7.6 17.2 %collective-permute-start.4 = (bf16[256,256]{1,0:T(8,128)(2,1)S(1)}, bf16[256,256]{1,0:T(8,128)(2,1)S(1)}, u32[]{:S(2)}, u32[]{:S(2)}) collective-permute-start(bf16[256,256]{1,0:T(8,128)(2,1)S(1)} %pad_maximum_fusion.6), channel_id=1, source_target_pairs={{0,2},{1,3},{2,0},{3,1},{4,6},{5,7},{6,4},{7,5},{8,10},{9,11},{10,... | collective-permute-start | bytes 393224 | tf_op jit(solution)/shard_map/ppermute | solution.py:29
  7.6 17.3 %collective-permute-start.3 = (bf16[256,256]{1,0:T(8,128)(2,1)S(1)}, bf16[256,256]{1,0:T(8,128)(2,1)S(1)}, u32[]{:S(2)}, u32[]{:S(2)}) collective-permute-start(bf16[256,256]{1,0:T(8,128)(2,1)S(1)} %pad_maximum_fusion.6), channel_id=1, source_target_pairs={{0,1},{1,2},{2,3},{3,0},{4,5},{5,6},{6,7},{7,4},{8,9},{9,10},{10,1... | collective-permute-start | bytes 393224 | tf_op jit(solution)/shard_map/ppermute | solution.py:29
  9.7 24.3 %copy-start.27 = (bf16[256,256]{1,0:T(8,128)(2,1)}, bf16[256,256]{1,0:T(8,128)(2,1)S(1)}, u32[]{:S(2)}) copy-start(bf16[256,256]{1,0:T(8,128)(2,1)S(1)} %get-tuple-element.75) | copy-start | bytes 393220
  9.8 19.8 %collective-permute-start.2 = (bf16[256,256]{1,0:T(8,128)(2,1)S(1)}, bf16[256,256]{1,0:T(8,128)(2,1)S(1)}, u32[]{:S(2)}, u32[]{:S(2)}) collective-permute-start(bf16[256,256]{1,0:T(8,128)(2,1)S(1)} %get-tuple-element.75), channel_id=1, source_target_pairs={{0,3},{1,0},{2,1},{3,2},{4,7},{5,4},{6,5},{7,6},{8,11},{9,8},{10,9... | collective-permute-start | bytes 393224 | tf_op jit(solution)/shard_map/ppermute | solution.py:29
  12.6 18.2 %collective-permute-start.1 = (bf16[256,256]{1,0:T(8,128)(2,1)S(1)}, bf16[256,256]{1,0:T(8,128)(2,1)S(1)}, u32[]{:S(2)}, u32[]{:S(2)}) collective-permute-start(bf16[256,256]{1,0:T(8,128)(2,1)S(1)} %get-tuple-element.75), channel_id=1, source_target_pairs={{0,2},{1,3},{2,0},{3,1},{4,6},{5,7},{6,4},{7,5},{8,10},{9,11},{10,... | collective-permute-start | bytes 393224 | tf_op jit(solution)/shard_map/ppermute | solution.py:29
  24.7 19.9 %copy-start.40 = (bf16[256,256]{1,0:T(8,128)(2,1)}, bf16[256,256]{1,0:T(8,128)(2,1)S(1)}, u32[]{:S(2)}) copy-start(bf16[256,256]{1,0:T(8,128)(2,1)S(1)} %collective-permute-done.5) | copy-start | bytes 393220
  24.8 7.8 %collective-permute-start = (bf16[256,256]{1,0:T(8,128)(2,1)S(1)}, bf16[256,256]{1,0:T(8,128)(2,1)S(1)}, u32[]{:S(2)}, u32[]{:S(2)}) collective-permute-start(bf16[256,256]{1,0:T(8,128)(2,1)S(1)} %get-tuple-element.75), channel_id=1, source_target_pairs={{0,1},{1,2},{2,3},{3,0},{4,5},{5,6},{6,7},{7,4},{8,9},{9,10},{10,1... | collective-permute-start | bytes 393224 | tf_op jit(solution)/shard_map/ppermute | solution.py:29
  24.8 50.5 %collective-permute-start.15 = (bf16[256,4096]{1,0:T(8,128)(2,1)}, bf16[256,4096]{1,0:T(8,128)(2,1)}, u32[]{:S(2)}, u32[]{:S(2)}) collective-permute-start(bf16[256,4096]{1,0:T(8,128)(2,1)} %get-tuple-element.37), channel_id=1, source_target_pairs={{0,4},{4,0},{1,5},{5,1},{2,6},{6,2},{3,7},{7,3},{8,12},{12,8},{9,1... | collective-permute-start | bytes 6291464 | tf_op jit(solution)/shard_map/ppermute | solution.py:29
  25.0 25.7 %copy-start.4 = (bf16[1024,256]{1,0:T(8,128)(2,1)}, bf16[1024,256]{1,0:T(8,128)(2,1)S(1)}, u32[]{:S(2)}) copy-start(bf16[1024,256]{1,0:T(8,128)(2,1)S(1)} %pad_maximum_fusion.1.refs_12_.refs_14_) | copy-start | bytes 1572868
  25.0 13.9 %collective-permute-start.12 = (bf16[256,256]{1,0:T(8,128)(2,1)S(1)}, bf16[256,256]{1,0:T(8,128)(2,1)S(1)}, u32[]{:S(2)}, u32[]{:S(2)}) collective-permute-start(bf16[256,256]{1,0:T(8,128)(2,1)S(1)} %get-tuple-element.35), channel_id=1, source_target_pairs={{0,2},{1,3},{2,0},{3,1},{4,6},{5,7},{6,4},{7,5},{8,10},{9,11},{10,... | collective-permute-start | bytes 393224 | tf_op jit(solution)/shard_map/ppermute | solution.py:29
  29.5 15.1 %copy-start.36 = (bf16[256,256]{1,0:T(8,128)(2,1)}, bf16[256,256]{1,0:T(8,128)(2,1)S(1)}, u32[]{:S(2)}) copy-start(bf16[256,256]{1,0:T(8,128)(2,1)S(1)} %collective-permute-done.2) | copy-start | bytes 393220
  29.5 7.8 %collective-permute-start.11 = (bf16[256,256]{1,0:T(8,128)(2,1)S(1)}, bf16[256,256]{1,0:T(8,128)(2,1)S(1)}, u32[]{:S(2)}, u32[]{:S(2)}) collective-permute-start(bf16[256,256]{1,0:T(8,128)(2,1)S(1)} %get-tuple-element.35), channel_id=1, source_target_pairs={{0,1},{1,2},{2,3},{3,0},{4,5},{5,6},{6,7},{7,4},{8,9},{9,10},{10,1... | collective-permute-start | bytes 393224 | tf_op jit(solution)/shard_map/ppermute | solution.py:29
  30.8 13.8 %copy-start.38 = (bf16[256,256]{1,0:T(8,128)(2,1)}, bf16[256,256]{1,0:T(8,128)(2,1)S(1)}, u32[]{:S(2)}) copy-start(bf16[256,256]{1,0:T(8,128)(2,1)S(1)} %collective-permute-done.1) | copy-start | bytes 393220
  30.8 13.8 %collective-permute-start.7 = (bf16[1024,256]{1,0:T(8,128)(2,1)S(1)}, bf16[1024,256]{1,0:T(8,128)(2,1)S(1)}, u32[]{:S(2)}, u32[]{:S(2)}) collective-permute-start(bf16[1024,256]{1,0:T(8,128)(2,1)S(1)} %pad_maximum_fusion.1.refs_12_.refs_14_), channel_id=1, source_target_pairs={{0,8},{8,0},{1,9},{9,1},{2,10},{10,2},{3,11},{11,3},{4,12},{12,4},... | collective-permute-start | bytes 1572872 | tf_op jit(solution)/shard_map/ppermute | solution.py:29
  32.6 13.3 %copy-start.46 = (bf16[256,256]{1,0:T(8,128)(2,1)}, bf16[256,256]{1,0:T(8,128)(2,1)S(1)}, u32[]{:S(2)}) copy-start(bf16[256,256]{1,0:T(8,128)(2,1)S(1)} %collective-permute-done) | copy-start | bytes 393220
  32.6 13.3 %collective-permute-start.6 = (bf16[1024,256]{1,0:T(8,128)(2,1)S(1)}, bf16[1024,256]{1,0:T(8,128)(2,1)S(1)}, u32[]{:S(2)}, u32[]{:S(2)}) collective-permute-start(bf16[1024,256]{1,0:T(8,128)(2,1)S(1)} %pad_maximum_fusion.1.refs_12_.refs_14_), channel_id=1, source_target_pairs={{0,16},{16,0},{1,17},{17,1},{2,18},{18,2},{3,19},{19,3},{4,20},{20... | collective-permute-start | bytes 1572872 | tf_op jit(solution)/shard_map/ppermute | solution.py:29
  35.1 25.8 %copy-start.23 = (bf16[256,4096]{1,0:T(8,128)(2,1)S(1)}, bf16[256,4096]{1,0:T(8,128)(2,1)}, u32[]{:S(2)}) copy-start(bf16[256,4096]{1,0:T(8,128)(2,1)} %get-tuple-element.31) | copy-start | bytes 6291460
  37.3 10.6 %collective-permute-start.13 = (bf16[256,256]{1,0:T(8,128)(2,1)S(1)}, bf16[256,256]{1,0:T(8,128)(2,1)S(1)}, u32[]{:S(2)}, u32[]{:S(2)}) collective-permute-start(bf16[256,256]{1,0:T(8,128)(2,1)S(1)} %get-tuple-element.35), channel_id=1, source_target_pairs={{0,3},{1,0},{2,1},{3,2},{4,7},{5,4},{6,5},{7,6},{8,11},{9,8},{10,9... | collective-permute-start | bytes 393224 | tf_op jit(solution)/shard_map/ppermute | solution.py:29
  45.9 12.6 %collective-permute-start.8 = (bf16[1024,256]{1,0:T(8,128)(2,1)}, bf16[1024,256]{1,0:T(8,128)(2,1)S(1)}, u32[]{:S(2)}, u32[]{:S(2)}) collective-permute-start(bf16[1024,256]{1,0:T(8,128)(2,1)} %pad_maximum_fusion.refs_3_.refs_5_), channel_id=1, source_target_pairs={{0,16},{16,0},{1,17},{17,1},{2,18},{18,2},{3,19},{19,3},{4,20},{20... | collective-permute-start | bytes 1572872 | tf_op jit(solution)/shard_map/ppermute | solution.py:29
  47.4 12.1 %collective-permute-start.9 = (bf16[1024,256]{1,0:T(8,128)(2,1)S(1)}, bf16[1024,256]{1,0:T(8,128)(2,1)S(1)}, u32[]{:S(2)}, u32[]{:S(2)}) collective-permute-start(bf16[1024,256]{1,0:T(8,128)(2,1)S(1)} %collective-permute-done.6.refs_14_.refs_16_), channel_id=1, source_target_pairs={{0,8},{8,0},{1,9},{9,1},{2,10},{10,2},{3,11},{11,3},{4,12},{12,4},... | collective-permute-start | bytes 1572872 | tf_op jit(solution)/shard_map/ppermute | solution.py:29
  49.3 12.9 %copy-start.41 = (bf16[256,256]{1,0:T(8,128)(2,1)S(1)}, bf16[256,256]{1,0:T(8,128)(2,1)}, u32[]{:S(2)}) copy-start(bf16[256,256]{1,0:T(8,128)(2,1)} %copy-done.40) | copy-start | bytes 393220
  59.5 15.9 %copy-start = (bf16[1024,256]{1,0:T(8,128)(2,1)}, bf16[1024,256]{1,0:T(8,128)(2,1)S(1)}, u32[]{:S(2)}) copy-start(bf16[1024,256]{1,0:T(8,128)(2,1)S(1)} %collective-permute-done.9.refs_15_.refs_17_) | copy-start | bytes 1572868
  59.5 13.9 %collective-permute-start.10 = (bf16[1024,256]{1,0:T(8,128)(2,1)}, bf16[1024,256]{1,0:T(8,128)(2,1)}, u32[]{:S(2)}, u32[]{:S(2)}) collective-permute-start(bf16[1024,256]{1,0:T(8,128)(2,1)} %pad_maximum_fusion.refs_3_.refs_5_), channel_id=1, source_target_pairs={{0,8},{8,0},{1,9},{9,1},{2,10},{10,2},{3,11},{11,3},{4,12},{12,4},... | collective-permute-start | bytes 1572872 | tf_op jit(solution)/shard_map/ppermute | solution.py:29
  60.4 11.2 %collective-permute-start.14 = (bf16[1024,256]{1,0:T(8,128)(2,1)S(1)}, bf16[1024,256]{1,0:T(8,128)(2,1)S(1)}, u32[]{:S(2)}, u32[]{:S(2)}) collective-permute-start(bf16[1024,256]{1,0:T(8,128)(2,1)S(1)} %constant_dynamic-update-slice_fusion.refs_7_.refs_9_), channel_id=1, source_target_pairs={{0,16},{16,0},{1,17},{17,1},{2,18},{18,2},{3,19},{19,3},{4,20},{20... | collective-permute-start | bytes 1572872 | tf_op jit(solution)/shard_map/ppermute | solution.py:29
  80.8 4.3 %collective-permute-start.16 = (f32[256,256]{1,0:T(8,128)S(1)}, f32[256,256]{1,0:T(8,128)S(1)}, u32[]{:S(2)}, u32[]{:S(2)}) collective-permute-start(f32[256,256]{1,0:T(8,128)S(1)} %fusion.15), channel_id=1, source_target_pairs={{0,4},{4,0},{1,5},{5,1},{2,6},{6,2},{3,7},{7,3},{8,12},{12,8},{9,1... | collective-permute-start | bytes 786440 | tf_op jit(solution)/shard_map/ppermute | solution.py:29
  87.7 14.5 %collective-permute-start.17 = (bf16[1024,256]{1,0:T(8,128)(2,1)}, bf16[1024,256]{1,0:T(8,128)(2,1)S(1)}, u32[]{:S(2)}, u32[]{:S(2)}) collective-permute-start(bf16[1024,256]{1,0:T(8,128)(2,1)} %collective-permute-done.10.refs_4_.refs_6_), channel_id=1, source_target_pairs={{0,16},{16,0},{1,17},{17,1},{2,18},{18,2},{3,19},{19,3},{4,20},{20... | collective-permute-start | bytes 1572872 | tf_op jit(solution)/shard_map/ppermute | solution.py:29
  88.4 14.0 %collective-permute-start.22 = (bf16[1024,256]{1,0:T(8,128)(2,1)S(1)}, bf16[1024,256]{1,0:T(8,128)(2,1)S(1)}, u32[]{:S(2)}, u32[]{:S(2)}) collective-permute-start(bf16[1024,256]{1,0:T(8,128)(2,1)S(1)} %constant_dynamic-update-slice_fusion.refs_7_.refs_9_), channel_id=1, source_target_pairs={{0,8},{8,0},{1,9},{9,1},{2,10},{10,2},{3,11},{11,3},{4,12},{12,4},... | collective-permute-start | bytes 1572872 | tf_op jit(solution)/shard_map/ppermute | solution.py:29
  90.6 13.2 %copy-start.35 = (bf16[512,256]{1,0:T(8,128)(2,1)S(1)}, bf16[512,256]{1,0:T(8,128)(2,1)}, u32[]{:S(2)}) copy-start(bf16[512,256]{1,0:T(8,128)(2,1)} %slice.196) | copy-start | bytes 786436
  90.6 15.4 %copy-start.24 = (bf16[256,4096]{1,0:T(8,128)(2,1)S(1)}, bf16[256,4096]{1,0:T(8,128)(2,1)}, u32[]{:S(2)}) copy-start(bf16[256,4096]{1,0:T(8,128)(2,1)} %get-tuple-element.31) | copy-start | bytes 6291460
  93.9 20.7 %collective-permute-start.21 = (bf16[256,256]{1,0:T(8,128)(2,1)S(1)}, bf16[256,256]{1,0:T(8,128)(2,1)S(1)}, u32[]{:S(2)}, u32[]{:S(2)}) collective-permute-start(bf16[256,256]{1,0:T(8,128)(2,1)S(1)} %copy-done.18), channel_id=1, source_target_pairs={{0,3},{1,0},{2,1},{3,2},{4,7},{5,4},{6,5},{7,6},{8,11},{9,8},{10,9... | collective-permute-start | bytes 393224 | tf_op jit(solution)/shard_map/ppermute | solution.py:29
  94.0 20.6 %collective-permute-start.20 = (bf16[256,256]{1,0:T(8,128)(2,1)S(1)}, bf16[256,256]{1,0:T(8,128)(2,1)S(1)}, u32[]{:S(2)}, u32[]{:S(2)}) collective-permute-start(bf16[256,256]{1,0:T(8,128)(2,1)S(1)} %copy-done.18), channel_id=1, source_target_pairs={{0,2},{1,3},{2,0},{3,1},{4,6},{5,7},{6,4},{7,5},{8,10},{9,11},{10,... | collective-permute-start | bytes 393224 | tf_op jit(solution)/shard_map/ppermute | solution.py:29
  95.2 19.4 %collective-permute-start.19 = (bf16[256,256]{1,0:T(8,128)(2,1)S(1)}, bf16[256,256]{1,0:T(8,128)(2,1)S(1)}, u32[]{:S(2)}, u32[]{:S(2)}) collective-permute-start(bf16[256,256]{1,0:T(8,128)(2,1)S(1)} %copy-done.18), channel_id=1, source_target_pairs={{0,1},{1,2},{2,3},{3,0},{4,5},{5,6},{6,7},{7,4},{8,9},{9,10},{10,1... | collective-permute-start | bytes 393224 | tf_op jit(solution)/shard_map/ppermute | solution.py:29
  102.5 7.7 %collective-permute-start.24 = (bf16[512,256]{1,0:T(8,128)(2,1)S(1)}, bf16[512,256]{1,0:T(8,128)(2,1)S(1)}, u32[]{:S(2)}, u32[]{:S(2)}) collective-permute-start(bf16[512,256]{1,0:T(8,128)(2,1)S(1)} %slice.197), channel_id=1, source_target_pairs={{0,16},{16,0},{1,17},{17,1},{2,18},{18,2},{3,19},{19,3},{4,20},{20... | collective-permute-start | bytes 786440 | tf_op jit(solution)/shard_map/ppermute | solution.py:29
  103.8 7.6 %collective-permute-start.23 = (bf16[512,256]{1,0:T(8,128)(2,1)S(1)}, bf16[512,256]{1,0:T(8,128)(2,1)S(1)}, u32[]{:S(2)}, u32[]{:S(2)}) collective-permute-start(bf16[512,256]{1,0:T(8,128)(2,1)S(1)} %copy-done.35), channel_id=1, source_target_pairs={{0,8},{8,0},{1,9},{9,1},{2,10},{10,2},{3,11},{11,3},{4,12},{12,4},... | collective-permute-start | bytes 786440 | tf_op jit(solution)/shard_map/ppermute | solution.py:29
  110.2 4.4 %collective-permute-start.18 = (f32[256,256]{1,0:T(8,128)S(1)}, f32[256,256]{1,0:T(8,128)S(1)}, u32[]{:S(2)}, u32[]{:S(2)}) collective-permute-start(f32[256,256]{1,0:T(8,128)S(1)} %fusion.17), channel_id=1, source_target_pairs={{0,4},{4,0},{1,5},{5,1},{2,6},{6,2},{3,7},{7,3},{8,12},{12,8},{9,1... | collective-permute-start | bytes 786440 | tf_op jit(solution)/shard_map/ppermute | solution.py:29
  114.1 7.8 %collective-permute-start.25 = (f32[256,256]{1,0:T(8,128)S(1)}, f32[256,256]{1,0:T(8,128)S(1)}, u32[]{:S(2)}, u32[]{:S(2)}) collective-permute-start(f32[256,256]{1,0:T(8,128)S(1)} %fusion.23), channel_id=1, source_target_pairs={{0,4},{4,0},{1,5},{5,1},{2,6},{6,2},{3,7},{7,3},{8,12},{12,8},{9,1... | collective-permute-start | bytes 786440 | tf_op jit(solution)/shard_map/ppermute | solution.py:29
  117.3 1.4 collective-permute-start.26
  120.6 14.0 %collective-permute-start.27 = (bf16[1024,256]{1,0:T(8,128)(2,1)S(1)}, bf16[1024,256]{1,0:T(8,128)(2,1)S(1)}, u32[]{:S(2)}, u32[]{:S(2)}) collective-permute-start(bf16[1024,256]{1,0:T(8,128)(2,1)S(1)} %convolution_convert_fusion.3), channel_id=1, source_target_pairs={{0,8},{8,0},{1,9},{9,1},{2,10},{10,2},{3,11},{11,3},{4,12},{12,4},... | collective-permute-start | bytes 1572872 | tf_op jit(solution)/shard_map/ppermute | solution.py:29
  124.7 9.9 %collective-permute-start.28 = (bf16[256,256]{1,0:T(8,128)(2,1)S(1)}, bf16[256,256]{1,0:T(8,128)(2,1)S(1)}, u32[]{:S(2)}, u32[]{:S(2)}) collective-permute-start(bf16[256,256]{1,0:T(8,128)(2,1)S(1)} %get-tuple-element.50), channel_id=1, source_target_pairs={{0,3},{1,0},{2,1},{3,2},{4,7},{5,4},{6,5},{7,6},{8,11},{9,8},{10,9... | collective-permute-start | bytes 393224 | tf_op jit(solution)/shard_map/ppermute | solution.py:29
  124.8 13.0 %collective-permute-start.29 = (bf16[256,256]{1,0:T(8,128)(2,1)S(1)}, bf16[256,256]{1,0:T(8,128)(2,1)S(1)}, u32[]{:S(2)}, u32[]{:S(2)}) collective-permute-start(bf16[256,256]{1,0:T(8,128)(2,1)S(1)} %get-tuple-element.51), channel_id=1, source_target_pairs={{0,2},{1,3},{2,0},{3,1},{4,6},{5,7},{6,4},{7,5},{8,10},{9,11},{10,... | collective-permute-start | bytes 393224 | tf_op jit(solution)/shard_map/ppermute | solution.py:29
  125.9 12.5 %collective-permute-start.30 = (bf16[256,256]{1,0:T(8,128)(2,1)S(1)}, bf16[256,256]{1,0:T(8,128)(2,1)}, u32[]{:S(2)}, u32[]{:S(2)}) collective-permute-start(bf16[256,256]{1,0:T(8,128)(2,1)S(1)} %get-tuple-element.52), channel_id=1, source_target_pairs={{0,1},{1,2},{2,3},{3,0},{4,5},{5,6},{6,7},{7,4},{8,9},{9,10},{10,1... | collective-permute-start | bytes 393224 | tf_op jit(solution)/shard_map/ppermute | solution.py:29
  127.9 1.3 collective-permute-start.31
  140.5 6.3 %collective-permute-start.32 = (bf16[256,256]{1,0:T(8,128)(2,1)}, bf16[256,256]{1,0:T(8,128)(2,1)S(1)}, u32[]{:S(2)}, u32[]{:S(2)}) collective-permute-start(bf16[256,256]{1,0:T(8,128)(2,1)} %undo_keys.1.refs_4_), channel_id=1, source_target_pairs={{0,4},{4,0},{1,5},{5,1},{2,6},{6,2},{3,7},{7,3},{8,12},{12,8},{9,1... | collective-permute-start | bytes 393224 | tf_op jit(solution)/shard_map/ppermute | solution.py:29
  144.3 23.9 %collective-permute-start.33 = (bf16[1024,256]{1,0:T(8,128)(2,1)S(1)}, bf16[1024,256]{1,0:T(8,128)(2,1)S(1)}, u32[]{:S(2)}, u32[]{:S(2)}) collective-permute-start(bf16[1024,256]{1,0:T(8,128)(2,1)S(1)} %fusion.4), channel_id=1, source_target_pairs={{0,16},{16,0},{1,17},{17,1},{2,18},{18,2},{3,19},{19,3},{4,20},{20... | collective-permute-start | bytes 1572872 | tf_op jit(solution)/shard_map/ppermute | solution.py:29
  145.3 22.9 %collective-permute-start.34 = (bf16[1024,256]{1,0:T(8,128)(2,1)S(1)}, bf16[1024,256]{1,0:T(8,128)(2,1)S(1)}, u32[]{:S(2)}, u32[]{:S(2)}) collective-permute-start(bf16[1024,256]{1,0:T(8,128)(2,1)S(1)} %convolution_convert_fusion.2), channel_id=1, source_target_pairs={{0,8},{8,0},{1,9},{9,1},{2,10},{10,2},{3,11},{11,3},{4,12},{12,4},... | collective-permute-start | bytes 1572872 | tf_op jit(solution)/shard_map/ppermute | solution.py:29
  147.2 19.4 %collective-permute-start.40 = (bf16[512,256]{1,0:T(8,128)(2,1)S(1)}, bf16[512,256]{1,0:T(8,128)(2,1)S(1)}, u32[]{:S(2)}, u32[]{:S(2)}) collective-permute-start(bf16[512,256]{1,0:T(8,128)(2,1)S(1)} %convolution_convert_fusion.4), channel_id=1, source_target_pairs={{0,16},{16,0},{1,17},{17,1},{2,18},{18,2},{3,19},{19,3},{4,20},{20... | collective-permute-start | bytes 786440 | tf_op jit(solution)/shard_map/ppermute | solution.py:29
  148.4 16.6 %collective-permute-start.38 = (bf16[512,256]{1,0:T(8,128)(2,1)S(1)}, bf16[512,256]{1,0:T(8,128)(2,1)S(1)}, u32[]{:S(2)}, u32[]{:S(2)}) collective-permute-start(bf16[512,256]{1,0:T(8,128)(2,1)S(1)} %convolution_convert_fusion.7), channel_id=1, source_target_pairs={{0,8},{8,0},{1,9},{9,1},{2,10},{10,2},{3,11},{11,3},{4,12},{12,4},... | collective-permute-start | bytes 786440 | tf_op jit(solution)/shard_map/ppermute | solution.py:29
  165.4 15.4 %collective-permute-start.39 = (bf16[1024,256]{1,0:T(8,128)(2,1)S(1)}, bf16[1024,256]{1,0:T(8,128)(2,1)S(1)}, u32[]{:S(2)}, u32[]{:S(2)}) collective-permute-start(bf16[1024,256]{1,0:T(8,128)(2,1)S(1)} %pad_maximum_fusion.2), channel_id=1, source_target_pairs={{0,16},{16,0},{1,17},{17,1},{2,18},{18,2},{3,19},{19,3},{4,20},{20... | collective-permute-start | bytes 1572872 | tf_op jit(solution)/shard_map/ppermute | solution.py:29
  167.0 13.8 %collective-permute-start.41 = (bf16[1024,256]{1,0:T(8,128)(2,1)S(1)}, bf16[1024,256]{1,0:T(8,128)(2,1)S(1)}, u32[]{:S(2)}, u32[]{:S(2)}) collective-permute-start(bf16[1024,256]{1,0:T(8,128)(2,1)S(1)} %pad_maximum_fusion.3), channel_id=1, source_target_pairs={{0,8},{8,0},{1,9},{9,1},{2,10},{10,2},{3,11},{11,3},{4,12},{12,4},... | collective-permute-start | bytes 1572872 | tf_op jit(solution)/shard_map/ppermute | solution.py:29
  168.8 8.3 %collective-permute-start.37 = (bf16[256,256]{1,0:T(8,128)(2,1)S(1)}, bf16[256,256]{1,0:T(8,128)(2,1)S(1)}, u32[]{:S(2)}, u32[]{:S(2)}) collective-permute-start(bf16[256,256]{1,0:T(8,128)(2,1)S(1)} %get-tuple-element.68), channel_id=1, source_target_pairs={{0,1},{1,2},{2,3},{3,0},{4,5},{5,6},{6,7},{7,4},{8,9},{9,10},{10,1... | collective-permute-start | bytes 393224 | tf_op jit(solution)/shard_map/ppermute | solution.py:29
  168.9 11.8 %collective-permute-start.36 = (bf16[256,256]{1,0:T(8,128)(2,1)S(1)}, bf16[256,256]{1,0:T(8,128)(2,1)S(1)}, u32[]{:S(2)}, u32[]{:S(2)}) collective-permute-start(bf16[256,256]{1,0:T(8,128)(2,1)S(1)} %get-tuple-element.69), channel_id=1, source_target_pairs={{0,2},{1,3},{2,0},{3,1},{4,6},{5,7},{6,4},{7,5},{8,10},{9,11},{10,... | collective-permute-start | bytes 393224 | tf_op jit(solution)/shard_map/ppermute | solution.py:29
  170.2 10.5 %collective-permute-start.35 = (bf16[256,256]{1,0:T(8,128)(2,1)S(1)}, bf16[256,256]{1,0:T(8,128)(2,1)S(1)}, u32[]{:S(2)}, u32[]{:S(2)}) collective-permute-start(bf16[256,256]{1,0:T(8,128)(2,1)S(1)} %get-tuple-element.70), channel_id=1, source_target_pairs={{0,3},{1,0},{2,1},{3,2},{4,7},{5,4},{6,5},{7,6},{8,11},{9,8},{10,9... | collective-permute-start | bytes 393224 | tf_op jit(solution)/shard_map/ppermute | solution.py:29
  177.2 14.9 %collective-permute-start.44 = (bf16[1024,256]{1,0:T(8,128)(2,1)S(1)}, bf16[1024,256]{1,0:T(8,128)(2,1)S(1)}, u32[]{:S(2)}, u32[]{:S(2)}) collective-permute-start(bf16[1024,256]{1,0:T(8,128)(2,1)S(1)} %convolution_convert_fusion), channel_id=1, source_target_pairs={{0,16},{16,0},{1,17},{17,1},{2,18},{18,2},{3,19},{19,3},{4,20},{20... | collective-permute-start | bytes 1572872 | tf_op jit(solution)/shard_map/ppermute | solution.py:29
  183.9 26.0 %collective-permute-start.42 = (bf16[256,4096]{1,0:T(8,128)(2,1)S(1)}, bf16[256,4096]{1,0:T(8,128)(2,1)S(1)}, u32[]{:S(2)}, u32[]{:S(2)}) collective-permute-start(bf16[256,4096]{1,0:T(8,128)(2,1)S(1)} %grad_columns.1), channel_id=1, source_target_pairs={{0,4},{4,0},{1,5},{5,1},{2,6},{6,2},{3,7},{7,3},{8,12},{12,8},{9,1... | collective-permute-start | bytes 6291464 | tf_op jit(solution)/shard_map/ppermute | solution.py:29
  184.5 16.7 %collective-permute-start.43 = (bf16[1024,256]{1,0:T(8,128)(2,1)S(1)}, bf16[1024,256]{1,0:T(8,128)(2,1)S(1)}, u32[]{:S(2)}, u32[]{:S(2)}) collective-permute-start(bf16[1024,256]{1,0:T(8,128)(2,1)S(1)} %convolution_convert_fusion.1), channel_id=1, source_target_pairs={{0,16},{16,0},{1,17},{17,1},{2,18},{18,2},{3,19},{19,3},{4,20},{20... | collective-permute-start | bytes 1572872 | tf_op jit(solution)/shard_map/ppermute | solution.py:29
  192.5 10.0 %collective-permute-start.45 = (bf16[1024,256]{1,0:T(8,128)(2,1)S(1)}, bf16[1024,256]{1,0:T(8,128)(2,1)S(1)}, u32[]{:S(2)}, u32[]{:S(2)}) collective-permute-start(bf16[1024,256]{1,0:T(8,128)(2,1)S(1)} %fusion.6), channel_id=1, source_target_pairs={{0,8},{8,0},{1,9},{9,1},{2,10},{10,2},{3,11},{11,3},{4,12},{12,4},... | collective-permute-start | bytes 1572872 | tf_op jit(solution)/shard_map/ppermute | solution.py:29
  194.1 9.7 %collective-permute-start.51 = (bf16[256,256]{1,0:T(8,128)(2,1)S(1)}, bf16[256,256]{1,0:T(8,128)(2,1)S(1)}, u32[]{:S(2)}, u32[]{:S(2)}) collective-permute-start(bf16[256,256]{1,0:T(8,128)(2,1)S(1)} %get-tuple-element.60), channel_id=1, source_target_pairs={{0,1},{1,2},{2,3},{3,0},{4,5},{5,6},{6,7},{7,4},{8,9},{9,10},{10,1... | collective-permute-start | bytes 393224 | tf_op jit(solution)/shard_map/ppermute | solution.py:29
  194.2 11.1 %collective-permute-start.50 = (bf16[256,256]{1,0:T(8,128)(2,1)S(1)}, bf16[256,256]{1,0:T(8,128)(2,1)S(1)}, u32[]{:S(2)}, u32[]{:S(2)}) collective-permute-start(bf16[256,256]{1,0:T(8,128)(2,1)S(1)} %get-tuple-element.61), channel_id=1, source_target_pairs={{0,2},{1,3},{2,0},{3,1},{4,6},{5,7},{6,4},{7,5},{8,10},{9,11},{10,... | collective-permute-start | bytes 393224 | tf_op jit(solution)/shard_map/ppermute | solution.py:29
  201.1 8.0 %collective-permute-start.49 = (bf16[256,256]{1,0:T(8,128)(2,1)S(1)}, bf16[256,256]{1,0:T(8,128)(2,1)S(1)}, u32[]{:S(2)}, u32[]{:S(2)}) collective-permute-start(bf16[256,256]{1,0:T(8,128)(2,1)S(1)} %get-tuple-element.62), channel_id=1, source_target_pairs={{0,3},{1,0},{2,1},{3,2},{4,7},{5,4},{6,5},{7,6},{8,11},{9,8},{10,9... | collective-permute-start | bytes 393224 | tf_op jit(solution)/shard_map/ppermute | solution.py:29
  203.1 12.7 %collective-permute-start.48 = (bf16[256,256]{1,0:T(8,128)(2,1)S(1)}, bf16[256,256]{1,0:T(8,128)(2,1)S(1)}, u32[]{:S(2)}, u32[]{:S(2)}) collective-permute-start(bf16[256,256]{1,0:T(8,128)(2,1)S(1)} %get-tuple-element.64), channel_id=1, source_target_pairs={{0,1},{1,2},{2,3},{3,0},{4,5},{5,6},{6,7},{7,4},{8,9},{9,10},{10,1... | collective-permute-start | bytes 393224 | tf_op jit(solution)/shard_map/ppermute | solution.py:29
  203.8 12.0 %collective-permute-start.47 = (bf16[256,256]{1,0:T(8,128)(2,1)S(1)}, bf16[256,256]{1,0:T(8,128)(2,1)S(1)}, u32[]{:S(2)}, u32[]{:S(2)}) collective-permute-start(bf16[256,256]{1,0:T(8,128)(2,1)S(1)} %get-tuple-element.65), channel_id=1, source_target_pairs={{0,2},{1,3},{2,0},{3,1},{4,6},{5,7},{6,4},{7,5},{8,10},{9,11},{10,... | collective-permute-start | bytes 393224 | tf_op jit(solution)/shard_map/ppermute | solution.py:29
  205.3 10.5 %collective-permute-start.46 = (bf16[256,256]{1,0:T(8,128)(2,1)S(1)}, bf16[256,256]{1,0:T(8,128)(2,1)S(1)}, u32[]{:S(2)}, u32[]{:S(2)}) collective-permute-start(bf16[256,256]{1,0:T(8,128)(2,1)S(1)} %get-tuple-element.66), channel_id=1, source_target_pairs={{0,3},{1,0},{2,1},{3,2},{4,7},{5,4},{6,5},{7,6},{8,11},{9,8},{10,9... | collective-permute-start | bytes 393224 | tf_op jit(solution)/shard_map/ppermute | solution.py:29
  (44 other events, 297.5 us)

commit v2 on v1

--- a/solution.py
+++ b/solution.py
@@ -99,14 +99,16 @@
         halves = [make(i, rows, deps, extra if rows == part else []) for rows in (top, low)]
         return jnp.concatenate(halves, axis=0)
 
-    arrived = []
+    went, arrived = [], []
     for da in range(1, size_a):
         extra = [piece for (at, _), piece in came[0].items() if at == da]
-        arrived.append(shift(side(da * size_b, extra, top), "a", -da))
+        went.append(side(da * size_b, extra, top))
+        arrived.append(shift(went[-1], "a", -da))
     for db in range(1, size_b):
         extra = [piece for (_, at), piece in came[1].items() if at == db]
-        arrived.append(shift(side(db, extra, low), "b", -db))
-    return arrived
+        went.append(side(db, extra, low))
+        arrived.append(shift(went[-1], "b", -db))
+    return arrived, went
 
 
 def reduce_line(term, last=()):
@@ -225,7 +227,7 @@
         in_specs=[VMEM] * (len(grads) + len(flat)),
         out_specs=VMEM,
         out_shape=jax.ShapeDtypeStruct((rows, width), jnp.bfloat16),
-        compiler_params=pltpu.CompilerParams(vmem_limit_bytes=40 * 1024 * 1024),
+        compiler_params=pltpu.CompilerParams(vmem_limit_bytes=20 * 1024 * 1024),
         cost_estimate=pl.CostEstimate(
             flops=2 * rows * sum(piece.size for piece in flat),
             bytes_accessed=2 * sum(piece.size for piece in flat) + 2 * rows * width,
@@ -253,7 +255,7 @@
             out_specs=VMEM,
         ),
         out_shape=jax.ShapeDtypeStruct((rows, width), jnp.bfloat16),
-        compiler_params=pltpu.CompilerParams(vmem_limit_bytes=40 * 1024 * 1024),
+        compiler_params=pltpu.CompilerParams(vmem_limit_bytes=20 * 1024 * 1024),
         cost_estimate=pl.CostEstimate(
             flops=2 * rows * sum(piece.size for piece in flat),
             bytes_accessed=2 * sum(piece.size for piece in flat) + 3 * rows * width,
@@ -267,6 +269,35 @@
     return lax.dot_general(
         a, b, (((left,), (right,)), ((), ())), preferred_element_type=jnp.float32
     )
+
+
+def project_kernel(mine_ref, theirs_ref, *refs):
+    pieces, (own_ref, other_ref) = refs[:-2], refs[-2:]
+    for source, target in ((theirs_ref, other_ref), (mine_ref, own_ref)):
+        at, total = 0, None
+        for piece in pieces:
+            end = at + piece.shape[0]
+            term = dot(source[:, at:end], piece[...], 1, 0)
+            total = term if total is None else total + term
+            at = end
+        target[...] = total
+
+
+def project_rows(mine, theirs, pieces):
+    rows, columns = mine.shape[0], pieces[0].shape[1]
+    return pl.pallas_call(
+        project_kernel,
+        in_specs=[VMEM] * (len(pieces) + 2),
+        out_specs=[VMEM] * 2,
+        out_shape=[jax.ShapeDtypeStruct((rows, columns), jnp.float32)] * 2,
+        compiler_params=pltpu.CompilerParams(vmem_limit_bytes=20 * 1024 * 1024),
+        cost_estimate=pl.CostEstimate(
+            flops=4 * mine.size * columns,
+            bytes_accessed=4 * mine.size + 2 * mine.shape[1] * columns,
+            transcendentals=0,
+        ),
+        name="project_rows",
+    )(mine, theirs, *pieces)
 
 
 def attend_kernel(*refs, group, parts, head_dim, scale, last):
@@ -342,7 +373,7 @@
         out_specs=[VMEM] * len(out_shape),
         out_shape=out_shape,
         scratch_shapes=[pltpu.VMEM((keys, 2 * head_dim), jnp.bfloat16)],
-        compiler_params=pltpu.CompilerParams(vmem_limit_bytes=48 * 1024 * 1024),
+        compiler_params=pltpu.CompilerParams(vmem_limit_bytes=20 * 1024 * 1024),
         cost_estimate=pl.CostEstimate(
             flops=14 * rows * keys * columns,
             bytes_accessed=8 * keys * 2 * head_dim,
@@ -409,29 +440,30 @@
     plane = ctx * block
 
     kv_local = jnp.concatenate([key_weight, value_weight], axis=1).astype(jnp.bfloat16)
-    q_local = [
-        query_weight[:, g * group * head_dim : (g + 1) * group * head_dim].astype(jnp.bfloat16)
+    da, db = jnp.meshgrid(jnp.arange(size_a), jnp.arange(size_b), indexing="ij")
+    slabs = ((at_a + size_a - da) % size_a) * size_b + (at_b + size_b - db) % size_b
+    slabs = slabs.reshape(-1).astype(jnp.int32)
+    line = (place + ctx - jnp.arange(ctx)) % ctx
+    pieces = jnp.stack([core * ctx + line, (1 - core) * ctx + line]).astype(jnp.int32)
+    mine, theirs = pick_columns(token_rows, slabs, pieces, block)
+    pieces_kv = gather_line(kv_local)
+    kv_line = jnp.concatenate([after(pieces_kv[0], mine), *pieces_kv[1:]], axis=0)
+    theirs = swap(after(theirs, kv_line))
+
+    pieces_q = gather_line(after(query_weight, kv_line).astype(jnp.bfloat16))
+    half = query_width // 2
+    q_line = [
+        jnp.concatenate([piece[:, g * half : (g + 1) * half] for piece in pieces_q], axis=0)
         for g in range(2)
     ]
-    kv_line = jnp.concatenate(gather_line(kv_local), axis=0)
-    q_line = [jnp.concatenate(gather_line(q_local[0]), axis=0)]
     kv_sides = along(kv_line, "a"), along(kv_line, "b")
-    q_line.append(jnp.concatenate(gather_line(after(q_local[1], kv_line)), axis=0))
-    stage = kv_sides[0] + kv_sides[1]
+    stage = kv_sides[0] + kv_sides[1] + q_line
     kv_corners = gather_corners(*kv_sides, "b", *stage)
     q0_a = along(after(q_line[0], *stage), "a")
     stage = q0_a + [piece for corner in kv_corners.values() for piece in corner]
     q1_a = along(after(q_line[1], *stage), "a")
     q0_b = along(after(q_line[0], *stage), "b")
     kv_slabs = in_order(kv_line, *kv_sides, kv_corners)
-
-    da, db = jnp.meshgrid(jnp.arange(size_a), jnp.arange(size_b), indexing="ij")
-    slabs = ((at_a + size_a - da) % size_a) * size_b + (at_b + size_b - db) % size_b
-    slabs = slabs.reshape(-1).astype(jnp.int32)
-    line = (place + ctx - jnp.arange(ctx)) % ctx
-    pieces = jnp.stack([core * ctx + line, (1 - core) * ctx + line]).astype(jnp.int32)
-    mine, theirs = pick_columns(token_rows, slabs, pieces, block)
-    theirs = swap(theirs)
 
     positions = after(positions, kv_line)
     own_positions = lax.dynamic_slice_in_dim(positions, place * rows, rows)
@@ -444,20 +476,11 @@
         ]
     )
 
-    def product(columns, slabs):
-        at, total = 0, None
-        for piece in [piece for slab in slabs for piece in slab]:
-            end = at + piece.shape[0]
-            term = mm(columns[:, at:end], piece, ((1,), (0,)))
-            total = term if total is None else total + term
-            at = end
-        return total
-
     def project(slabs):
-        other = swap(product(theirs, slabs))
-        return product(mine, slabs), other
-
-    columns = jnp.concatenate([mine, theirs], axis=0)
+        own, other = project_rows(mine, theirs, [piece for slab in slabs for piece in slab])
+        return own, swap(other)
+
+    columns = jnp.concatenate([after(mine, *q0_a), theirs], axis=0)
 
     def terms_of(own, other):
         both = jnp.concatenate([own, other], axis=0)
@@ -477,7 +500,7 @@
     q0_corners = gather_corners(q0_a, q0_b, "a", *stage)
     q1_b = along(after(q_line[1], *stage), "b")
     key_values = gather_line(key_value)
-    stage = q1_b + [piece for corner in q0_corners.values() for piece in corner]
+    stage = q1_b + key_values + [piece for corner in q0_corners.values() for piece in corner]
     q1_corners = gather_corners(q1_a, q1_b, "both", *stage)
     q_slabs = [
         in_order(q_line[0], q0_a, q0_b, q0_corners),
@@ -507,28 +530,29 @@
         came.append(reduce_corners(made[g], "ba"[g], mid))
     summed = [terms[0]] + [shift(terms[k], "ctx", -k) for k in range(1, ctx)]
     first = [*came[0][0].values(), *came[0][1].values()]
-    sides = [reduce_sides(made[0], came[0], "b", mid, *first)]
-    grad_kv = undo_keys([after(summed[0], *first), *summed[1:]], cos_table, sin_table)
+    second = [*came[1][0].values(), *came[1][1].values()]
+    sides0, went0 = reduce_sides(made[0], came[0], "b", mid, *first, *summed[1:])
+    grad_kv = undo_keys(
+        [after(summed[0], *first, *second, *went0), *summed[1:]], cos_table, sin_table
+    )
     gradients.append((grad_kv, swap(grad_kv)))
     made.append(terms_of(*gradients[2]))
     came.append(reduce_corners(made[2], "both", mid))
-    line0 = made[0](0, slice(None), (), sides[0])
-    q_sum = reduce_line(line0)
-    sides.append(reduce_sides(made[1], came[1], "a", mid, *sides[0]))
-    kv_sides = reduce_sides(made[2], came[2], "both", mid)
-    kv_sum = reduce_line(made[2](0, slice(None), (), kv_sides))
+    sides1, went1 = reduce_sides(made[1], came[1], "a", mid, *sides0)
+    q_sum = reduce_line(made[0](0, slice(None), went1, sides0))
+    line1 = made[1](0, slice(None), (), sides1)
+    kv_sides, _ = reduce_sides(made[2], came[2], "both", mid, *sides1)
 
     weights = [*q_slabs, kv_slabs]
     grad_theirs = grad_columns(
-        [gradients[0][1], gradients[1][1], after(gradients[2][1], q_sum, *kv_sides)], weights
+        [gradients[0][1], gradients[1][1], after(gradients[2][1], q_sum, *sides1)], weights
     )
     grad_theirs = swap(grad_theirs)
-    line1 = made[1](0, slice(None), (), sides[1])
     grad_input = grad_place(
         [gradients[0][0], gradients[1][0], gradients[2][0]], weights, grad_theirs, slabs, pieces, block
     )
-    q_grads = [q_sum, reduce_line(line1, (grad_input,))]
-    kv_wgrad = kv_sum
+    q_grads = [q_sum, reduce_line(line1)]
+    kv_wgrad = reduce_line(made[2](0, slice(None), (), kv_sides), (grad_input,))
 
     query_grad = jnp.concatenate(q_grads, axis=1)
     key_grad = kv_wgrad[:, :head_dim]

time: 218 us -> 197 us (0.904)
  matrix products: 39.2 us -> 12.7 us
  Pallas kernels: 23.8 us -> 33.6 us
  waiting for transfers between devices: 77.1 us -> 71.9 us
  starting transfers between devices: 55.7 us -> 59.7 us
    dot_general x41 -> x15, matrix products: 39.2 us -> 12.7 us  [mm(): lax.dot_general(a, b, (dims, ((), ())), preferred_element_type=jnp.float32)]
    pallas_call x0 -> x3, Pallas kernels: none -> 9 us  [project_rows(): pl.pallas_call(project_kernel, in_specs=[VMEM] * (len(pieces) + 2), out_s...]
    ppermute x52 -> x49, waiting for transfers between devices: 77.1 us -> 71.9 us  [shift(): lax.ppermute(block, axis, [(i, (i + step) % size) for i in range(size)])]
    ppermute x52 -> x49, starting transfers between devices: 55.7 us -> 59.7 us  [shift(): lax.ppermute(block, axis, [(i, (i + step) % size) for i in range(size)])]
    unnamed x118 -> x104, local copies, waits for them, and re-layouts: 4.76 us -> 4.37 us
  transfers between devices with their start and end apart: 52 -> 49, of which waited for: 21 -> 24; matrix products, arithmetic and copies ran while one was open for 22% -> 11% of each run, Pallas kernels for 9% -> 17%
where the time goes in v2:
time: 197 us; the launch traced here: 196 us
  waiting for transfers between devices  71.9 us (36%)
  starting transfers between devices  59.7 us (30%)
  Pallas kernels  33.6 us (17%)
  matrix products  12.7 us (6%)
  local copies, waits for them, and re-layouts  10.4 us (5%)
  other arithmetic  6.52 us (3%)
    ppermute x49, waiting for transfers between devices, shift(): lax.ppermute(block, axis, [(i, (i + step) % size) for i in range(size)])  71.9 us
    ppermute x49, starting transfers between devices, shift(): lax.ppermute(block, axis, [(i, (i + step) % size) for i in range(size)])  59.7 us
    dot_general x15, matrix products, mm(): lax.dot_general(a, b, (dims, ((), ())), preferred_element_type=jnp.float32)  12.7 us
    pallas_call x3, Pallas kernels, project_rows(): pl.pallas_call(project_kernel, in_specs=[VMEM] * (len(pieces) + 2), out_s...  9 us
    pallas_call x1, Pallas kernels, grad_place(): pl.pallas_call(functools.partial(grad_place_kernel, shape=shape, plane=pl...  6.16 us
    pallas_call x1, Pallas kernels, pick_columns(): pl.pallas_call(functools.partial(pick_kernel, block=block), grid_spec=plt...  5.77 us
    pallas_call x2, Pallas kernels, attend(): pl.pallas_call(functools.partial(attend_kernel, group=group, parts=parts,...  5.46 us
    unnamed x104, local copies, waits for them, and re-layouts  4.37 us
  transfers between devices with their start and end apart: 49, of which 24 were waited for; matrix products, arithmetic and copies ran while one was open for 11% of the time, Pallas kernels for 17%

profile of v2, /device:TPU:0, one launch (start us, length us, event | category | flops | bytes accessed | tf_op | source)
XLA Modules:
  0.0 196.4 jit_solution(9846127127821028390)
XLA Ops:
  2.5 5.1 %collective-permute-start.2 = (bf16[256,256]{1,0:T(8,128)(2,1)S(1)}, bf16[256,256]{1,0:T(8,128)(2,1)S(1)}, u32[]{:S(2)}, u32[]{:S(2)}) collective-permute-start(bf16[256,256]{1,0:T(8,128)(2,1)S(1)} %pad_maximum_fusion.6), channel_id=1, source_target_pairs={{0,3},{1,0},{2,1},{3,2},{4,7},{5,4},{6,5},{7,6},{8,11},{9,8},{10,9... | collective-permute-start | bytes 393224 | tf_op jit(solution)/shard_map/ppermute | solution.py:29
  10.1 5.8 %pick_columns.1 = (bf16[256,4096]{1,0:T(8,128)(2,1)}, bf16[256,4096]{1,0:T(8,128)(2,1)}) custom-call(s32[4]{0:T(128)} %fusion.26.slab_ref.refs_0_, s32[2,4]{1,0:T(2,128)} %pad_add_fusion.1.piece_ref.refs_1_, bf16[256,8192]{1,0:T(8,128)(2,1)} %bitcast.21), custom_call_target="tpu_custom_call" | custom-call | bytes 8388608 | tf_op jit(solution)/shard_map/pick_columns/pallas_call | solution.py:203
  17.7 1.2 collective-permute-done.1
  20.2 1.7 collective-permute-start.6
  21.9 1.8 collective-permute-start.5
  23.7 1.9 collective-permute-start.4
  25.7 1.5 collective-permute-start.8
  27.2 1.8 collective-permute-done.6
  29.0 1.5 collective-permute-start.7
  30.5 16.9 %collective-permute-done.5 = bf16[256,512]{1,0:T(8,128)(2,1)S(1)} collective-permute-done((bf16[256,512]{1,0:T(8,128)(2,1)S(1)}, bf16[256,512]{1,0:T(8,128)(2,1)S(1)}, u32[]{:S(2)}, u32[]{:S(2)}) %collective-permute-start.5) | collective-permute-done | bytes 262176 | tf_op jit(solution)/shard_map/ppermute | solution.py:29
  47.6 1.6 collective-permute-start.9
  49.2 1.5 collective-permute-start.10
  51.5 9.9 %collective-permute-done.9.refs_2_.refs_5_.refs_7_ = bf16[1024,256]{1,0:T(8,128)(2,1)S(1)} collective-permute-done((bf16[1024,256]{1,0:T(8,128)(2,1)S(1)}, bf16[1024,256]{1,0:T(8,128)(2,1)S(1)}, u32[]{:S(2)}, u32[]{:S(2)}) %collective-permute-start.9) | collective-permute-done | bytes 524320 | tf_op jit(solution)/shard_map/ppermute | solution.py:29
  61.4 1.2 collective-permute-done.10.refs_3_.refs_15_.refs_17_
  62.6 1.5 collective-permute-start.11
  64.7 2.9 %project_rows.3 = (f32[256,256]{1,0:T(8,128)S(1)}, f32[256,256]{1,0:T(8,128)S(1)}) custom-call(bf16[256,4096]{1,0:T(8,128)(2,1)S(1)} %copy-done, bf16[256,4096]{1,0:T(8,128)(2,1)} %collective-permute-done.3.theirs_ref, bf16[1024,256]{1,0:T(8,128)(2,1)} %constant_dynamic-update-slice_fusion.refs_0_.refs_12_.refs_14_, ...), custom_call_target="tpu_custom_call" | custom-call | flops 1073741824 | bytes 6291456 | tf_op jit(solution)/shard_map/project_rows/pallas_call | solution.py:288
  68.4 1.2 negate_select_fusion
  70.5 1.9 finish_keys.1.refs_7_
  72.4 2.9 %collective-permute-done.11.refs_1_.refs_4_.refs_6_ = bf16[1024,256]{1,0:T(8,128)(2,1)} collective-permute-done((bf16[1024,256]{1,0:T(8,128)(2,1)S(1)}, bf16[1024,256]{1,0:T(8,128)(2,1)}, u32[]{:S(2)}, u32[]{:S(2)}) %collective-permute-start.11) | collective-permute-done | bytes 524320 | tf_op jit(solution)/shard_map/ppermute | solution.py:29
  75.3 1.2 collective-permute-done.12.refs_2_.refs_9_.refs_11_
  78.0 1.2 collective-permute-start.17
  79.2 2.0 %collective-permute-start.16 = (bf16[256,256]{1,0:T(8,128)(2,1)}, bf16[256,256]{1,0:T(8,128)(2,1)S(1)}, u32[]{:S(2)}, u32[]{:S(2)}) collective-permute-start(bf16[256,256]{1,0:T(8,128)(2,1)} %finish_keys.1.refs_7_), channel_id=1, source_target_pairs={{0,1},{1,2},{2,3},{3,0},{4,5},{5,6},{6,7},{7,4},{8,9},{9,10},{10,1... | collective-permute-start | bytes 393224 | tf_op jit(solution)/shard_map/ppermute | solution.py:29
  82.9 5.3 %collective-permute-done.14.refs_3_.refs_6_.refs_8_ = bf16[1024,256]{1,0:T(8,128)(2,1)} collective-permute-done((bf16[1024,256]{1,0:T(8,128)(2,1)}, bf16[1024,256]{1,0:T(8,128)(2,1)}, u32[]{:S(2)}, u32[]{:S(2)}) %collective-permute-start.14) | collective-permute-done | bytes 524320 | tf_op jit(solution)/shard_map/ppermute | solution.py:29
  88.2 3.1 %project_rows.4 = (f32[256,256]{1,0:T(8,128)S(1)}, f32[256,256]{1,0:T(8,128)S(1)}) custom-call(bf16[256,4096]{1,0:T(8,128)(2,1)S(1)} %copy-done, bf16[256,4096]{1,0:T(8,128)(2,1)} %collective-permute-done.3.theirs_ref, bf16[1024,256]{1,0:T(8,128)(2,1)S(1)} %pad_maximum_fusion.refs_0_.refs_3_.refs_5_, ...), custom_call_target="tpu_custom_call" | custom-call | flops 1073741824 | bytes 6291456 | tf_op jit(solution)/shard_map/project_rows/pallas_call | solution.py:288
  91.8 1.3 collective-permute-start.21
  93.6 1.7 constant_dynamic-update-slice_fusion.4
  95.5 2.6 %attend.2 = (bf16[256,256]{1,0:T(8,128)(2,1)S(1)}, bf16[256,256]{1,0:T(8,128)(2,1)S(1)}, f32[1024,256]{1,0:T(8,128)S(1)}) custom-call(f32[256,256]{1,0:T(8,128)S(1)} %get-tuple-element.55.refs_0_, f32[256,256]{1,0:T(8,128)S(1)} %collective-permute-done.15.refs_1_, bf16[256,256]{1,0:T(8,128)(2,1)S(1)} %copy-done.32, f32[256,128]{1,0:T(8,128)S(1)} %copy-done.16, ...), custom_call_target="tpu_custom_call" | custom-call | flops 939524096 | bytes 2097152 | tf_op jit(solution)/shard_map/attend/pallas_call | solution.py:368
  98.7 1.5 collective-permute-done.21.refs_4_.refs_11_.refs_13_
  100.8 3.0 %project_rows.5 = (f32[256,256]{1,0:T(8,128)S(1)}, f32[256,256]{1,0:T(8,128)S(1)}) custom-call(bf16[256,4096]{1,0:T(8,128)(2,1)S(1)} %copy-done, bf16[256,4096]{1,0:T(8,128)(2,1)} %collective-permute-done.3.theirs_ref, bf16[1024,256]{1,0:T(8,128)(2,1)S(1)} %pad_maximum_fusion.1.refs_0_.refs_7_.refs_9_, ...), custom_call_target="tpu_custom_call" | custom-call | flops 1073741824 | bytes 6291456 | tf_op jit(solution)/shard_map/project_rows/pallas_call | solution.py:288
  105.4 2.9 %attend.3 = (bf16[256,256]{1,0:T(8,128)(2,1)S(1)}, bf16[256,256]{1,0:T(8,128)(2,1)S(1)}, f32[256,256]{1,0:T(8,128)S(1)}, bf16[256,256]{1,0:T(8,128)(2,1)S(1)}, b...) custom-call(f32[256,256]{1,0:T(8,128)S(1)} %get-tuple-element.61.refs_0_, ...), custom_call_target="tpu_custom_call" | custom-call | flops 939524096 | bytes 2097152 | tf_op jit(solution)/shard_map/attend/pallas_call | solution.py:368
  108.5 1.7 collective-permute-start.27
  110.2 1.7 collective-permute-start.29
  112.5 1.3 collective-permute-start.26
  113.7 1.6 collective-permute-done.27.refs_1_
  115.3 7.0 %collective-permute-done.28.refs_2_ = bf16[256,256]{1,0:T(8,128)(2,1)S(1)} collective-permute-done((bf16[256,256]{1,0:T(8,128)(2,1)S(1)}, bf16[256,256]{1,0:T(8,128)(2,1)S(1)}, u32[]{:S(2)}, u32[]{:S(2)}) %collective-permute-start.28) | collective-permute-done | bytes 131104 | tf_op jit(solution)/shard_map/ppermute | solution.py:29
  122.3 1.3 convolution_convert_fusion.1
  123.7 1.3 fusion.3
  125.0 1.3 collective-permute-start.31
  126.3 1.2 collective-permute-start.32
  127.5 2.0 %undo_keys.1.refs_4_ = bf16[256,256]{1,0:T(8,128)(2,1)} custom-call(f32[256,256]{1,0:T(8,128)} %copy-done.24, bf16[256,256]{1,0:T(8,128)(2,1)} %copy-done.40, bf16[256,256]{1,0:T(8,128)(2,1)} %copy-done.41, bf16[256,256]{1,0:T(8,128)(2,1)} %copy-done.42, f32[256,128]{1,0:T(8,128)} %get-tuple-element.106.cos_ref.refs_3_.refs_4_, ...), custom_call_target="tpu_custom_call" | custom-call | tf_op jit(solution)/shard_map/undo_keys/pallas_call | solution.py:419
  129.4 1.6 collective-permute-done.30.refs_2_
  131.0 1.4 convolution_convert_fusion.7
  132.4 6.1 %collective-permute-done.31 = bf16[1024,256]{1,0:T(8,128)(2,1)S(1)} collective-permute-done((bf16[1024,256]{1,0:T(8,128)(2,1)}, bf16[1024,256]{1,0:T(8,128)(2,1)S(1)}, u32[]{:S(2)}, u32[]{:S(2)}) %collective-permute-start.31) | collective-permute-done | bytes 524320 | tf_op jit(solution)/shard_map/ppermute | solution.py:29
  138.5 1.4 collective-permute-done.32
  139.9 1.7 convolution_convert_fusion
  142.7 1.5 fusion.4
  144.3 1.2 collective-permute-start.37
  145.5 1.7 fusion.5
  148.2 2.1 %collective-permute-start.34 = (bf16[256,256]{1,0:T(8,128)(2,1)S(1)}, bf16[256,256]{1,0:T(8,128)(2,1)S(1)}, u32[]{:S(2)}, u32[]{:S(2)}) collective-permute-start(bf16[256,256]{1,0:T(8,128)(2,1)S(1)} %get-tuple-element.91), channel_id=1, source_target_pairs={{0,2},{1,3},{2,0},{3,1},{4,6},{5,7},{6,4},{7,5},{8,10},{9,11},{10,... | collective-permute-start | bytes 393224 | tf_op jit(solution)/shard_map/ppermute | solution.py:29
  150.3 2.8 %collective-permute-start.33 = (bf16[256,256]{1,0:T(8,128)(2,1)S(1)}, bf16[256,256]{1,0:T(8,128)(2,1)S(1)}, u32[]{:S(2)}, u32[]{:S(2)}) collective-permute-start(bf16[256,256]{1,0:T(8,128)(2,1)S(1)} %get-tuple-element.92), channel_id=1, source_target_pairs={{0,3},{1,0},{2,1},{3,2},{4,7},{5,4},{6,5},{7,6},{8,11},{9,8},{10,9... | collective-permute-start | bytes 393224 | tf_op jit(solution)/shard_map/ppermute | solution.py:29
  153.5 2.0 %collective-permute-done.35 = bf16[256,256]{1,0:T(8,128)(2,1)S(1)} collective-permute-done((bf16[256,256]{1,0:T(8,128)(2,1)S(1)}, bf16[256,256]{1,0:T(8,128)(2,1)S(1)}, u32[]{:S(2)}, u32[]{:S(2)}) %collective-permute-start.35) | collective-permute-done | bytes 131104 | tf_op jit(solution)/shard_map/ppermute | solution.py:29
  155.5 1.1 collective-permute-start.44
  156.6 2.6 %collective-permute-done.34 = bf16[256,256]{1,0:T(8,128)(2,1)S(1)} collective-permute-done((bf16[256,256]{1,0:T(8,128)(2,1)S(1)}, bf16[256,256]{1,0:T(8,128)(2,1)S(1)}, u32[]{:S(2)}, u32[]{:S(2)}) %collective-permute-start.34) | collective-permute-done | bytes 131104 | tf_op jit(solution)/shard_map/ppermute | solution.py:29
  160.7 3.4 %grad_columns.1 = bf16[256,4096]{1,0:T(8,128)(2,1)S(1)} custom-call(bf16[256,256]{1,0:T(8,128)(2,1)S(1)} %copy-done.22, bf16[256,256]{1,0:T(8,128)(2,1)S(1)} %collective-permute-done.25.refs_1_, bf16[256,256]{1,0:T(8,128)(2,1)S(1)} %collective-permute-done.30.refs_2_, bf16[1024,256]{1,0:T(8,128)(2,1)S(1)} %pad_maximum_fusion.refs_0_.refs_3_.refs_5_, ...), custom_call_target="tpu_custom_call" | custom-call | flops 1610612736 | bytes 8388608 | tf_op jit(solution)/shard_map/grad_columns/pallas_call | solution.py:225
  164.7 1.7 collective-permute-start.41
  166.8 1.1 collective-permute-start.45
  168.7 1.2 collective-permute-start.43
  169.9 3.4 %collective-permute-start.40 = (bf16[256,256]{1,0:T(8,128)(2,1)S(1)}, bf16[256,256]{1,0:T(8,128)(2,1)S(1)}, u32[]{:S(2)}, u32[]{:S(2)}) collective-permute-start(bf16[256,256]{1,0:T(8,128)(2,1)S(1)} %get-tuple-element.87), channel_id=1, source_target_pairs={{0,2},{1,3},{2,0},{3,1},{4,6},{5,7},{6,4},{7,5},{8,10},{9,11},{10,... | collective-permute-start | bytes 393224 | tf_op jit(solution)/shard_map/ppermute | solution.py:29
  173.3 1.7 collective-permute-start.39
  175.8 4.4 %collective-permute-done.40 = bf16[256,256]{1,0:T(8,128)(2,1)S(1)} collective-permute-done((bf16[256,256]{1,0:T(8,128)(2,1)S(1)}, bf16[256,256]{1,0:T(8,128)(2,1)S(1)}, u32[]{:S(2)}, u32[]{:S(2)}) %collective-permute-start.40) | collective-permute-done | bytes 131104 | tf_op jit(solution)/shard_map/ppermute | solution.py:29
  183.0 2.3 %collective-permute-start.48 = (bf16[256,256]{1,0:T(8,128)(2,1)S(1)}, bf16[256,256]{1,0:T(8,128)(2,1)S(1)}, u32[]{:S(2)}, u32[]{:S(2)}) collective-permute-start(bf16[256,256]{1,0:T(8,128)(2,1)S(1)} %get-tuple-element.82), channel_id=1, source_target_pairs={{0,1},{1,2},{2,3},{3,0},{4,5},{5,6},{6,7},{7,4},{8,9},{9,10},{10,1... | collective-permute-start | bytes 393224 | tf_op jit(solution)/shard_map/ppermute | solution.py:29
  185.4 1.4 collective-permute-start.47
  186.8 2.6 %collective-permute-start.46 = (bf16[256,256]{1,0:T(8,128)(2,1)S(1)}, bf16[256,256]{1,0:T(8,128)(2,1)S(1)}, u32[]{:S(2)}, u32[]{:S(2)}) collective-permute-start(bf16[256,256]{1,0:T(8,128)(2,1)S(1)} %get-tuple-element.84), channel_id=1, source_target_pairs={{0,3},{1,0},{2,1},{3,2},{4,7},{5,4},{6,5},{7,6},{8,11},{9,8},{10,9... | collective-permute-start | bytes 393224 | tf_op jit(solution)/shard_map/ppermute | solution.py:29
  189.4 6.2 %grad_place.1 = bf16[256,8192]{1,0:T(8,128)(2,1)} custom-call(s32[4]{0:T(128)S(1)} %copy-done.34, s32[2,4]{1,0:T(2,128)S(1)} %copy-done.33, bf16[256,256]{1,0:T(8,128)(2,1)S(1)} %copy-done.18, bf16[256,256]{1,0:T(8,128)(2,1)S(1)} %copy-done.20, bf16[256,256]{1,0:T(8,128)(2,1)S(1)} %copy-done.14, ...), custom_call_target="tpu_custom_call" | custom-call | flops 1610612736 | bytes 12582912 | tf_op jit(solution)/shard_map/grad_place/pallas_call | solution.py:249
  (208 shorter events, 28.4 us)
Async XLA Ops:
  0.6 19.5 %copy-start.37 = (f32[256,512]{1,0:T(8,128)S(1)}, f32[256,512]{1,0:T(8,128)}, u32[]{:S(2)}) copy-start(f32[256,512]{1,0:T(8,128)} %param.8) | copy-start | bytes 1572868
  2.5 17.0 %collective-permute-start.2 = (bf16[256,256]{1,0:T(8,128)(2,1)S(1)}, bf16[256,256]{1,0:T(8,128)(2,1)S(1)}, u32[]{:S(2)}, u32[]{:S(2)}) collective-permute-start(bf16[256,256]{1,0:T(8,128)(2,1)S(1)} %pad_maximum_fusion.6), channel_id=1, source_target_pairs={{0,3},{1,0},{2,1},{3,2},{4,7},{5,4},{6,5},{7,6},{8,11},{9,8},{10,9... | collective-permute-start | bytes 393224 | tf_op jit(solution)/shard_map/ppermute | solution.py:29
  7.6 11.2 %collective-permute-start.1 = (bf16[256,256]{1,0:T(8,128)(2,1)S(1)}, bf16[256,256]{1,0:T(8,128)(2,1)S(1)}, u32[]{:S(2)}, u32[]{:S(2)}) collective-permute-start(bf16[256,256]{1,0:T(8,128)(2,1)S(1)} %pad_maximum_fusion.6), channel_id=1, source_target_pairs={{0,2},{1,3},{2,0},{3,1},{4,6},{5,7},{6,4},{7,5},{8,10},{9,11},{10,... | collective-permute-start | bytes 393224 | tf_op jit(solution)/shard_map/ppermute | solution.py:29
  7.6 9.4 %collective-permute-start = (bf16[256,256]{1,0:T(8,128)(2,1)S(1)}, bf16[256,256]{1,0:T(8,128)(2,1)S(1)}, u32[]{:S(2)}, u32[]{:S(2)}) collective-permute-start(bf16[256,256]{1,0:T(8,128)(2,1)S(1)} %pad_maximum_fusion.6), channel_id=1, source_target_pairs={{0,1},{1,2},{2,3},{3,0},{4,5},{5,6},{6,7},{7,4},{8,9},{9,10},{10,1... | collective-permute-start | bytes 393224 | tf_op jit(solution)/shard_map/ppermute | solution.py:29
  10.1 40.6 %copy-start.39 = (bf16[1,256,512]{2,1,0:T(8,128)(2,1)S(1)}, bf16[1,256,512]{2,1,0:T(8,128)(2,1)}, u32[]{:S(2)}) copy-start(bf16[1,256,512]{2,1,0:T(8,128)(2,1)} %param.11) | copy-start | bytes 786436
  15.9 35.5 %copy-start.47 = (s32[1024]{0:T(1024)S(1)}, s32[1024]{0:T(1024)}, u32[]{:S(2)}) copy-start(s32[1024]{0:T(1024)} %param.7) | copy-start | bytes 12292
  15.9 48.8 %copy-start = (bf16[256,4096]{1,0:T(8,128)(2,1)S(1)}, bf16[256,4096]{1,0:T(8,128)(2,1)}, u32[]{:S(2)}) copy-start(bf16[256,4096]{1,0:T(8,128)(2,1)} %get-tuple-element.68.mine_ref) | copy-start | bytes 6291460
  20.2 44.5 %collective-permute-start.3 = (bf16[256,4096]{1,0:T(8,128)(2,1)}, bf16[256,4096]{1,0:T(8,128)(2,1)}, u32[]{:S(2)}, u32[]{:S(2)}) collective-permute-start(bf16[256,4096]{1,0:T(8,128)(2,1)} %get-tuple-element.45), channel_id=1, source_target_pairs={{0,4},{4,0},{1,5},{5,1},{2,6},{6,2},{3,7},{7,3},{8,12},{12,8},{9,1... | collective-permute-start | bytes 6291464 | tf_op jit(solution)/shard_map/ppermute | solution.py:29
  20.2 8.8 %collective-permute-start.6 = (bf16[256,512]{1,0:T(8,128)(2,1)S(1)}, bf16[256,512]{1,0:T(8,128)(2,1)S(1)}, u32[]{:S(2)}, u32[]{:S(2)}) collective-permute-start(bf16[256,512]{1,0:T(8,128)(2,1)S(1)} %convert_element_type.125), channel_id=1, source_target_pairs={{0,3},{1,0},{2,1},{3,2},{4,7},{5,4},{6,5},{7,6},{8,11},{9,8},{10,9... | collective-permute-start | bytes 786440 | tf_op jit(solution)/shard_map/ppermute | solution.py:29
  21.9 25.5 %collective-permute-start.5 = (bf16[256,512]{1,0:T(8,128)(2,1)S(1)}, bf16[256,512]{1,0:T(8,128)(2,1)S(1)}, u32[]{:S(2)}, u32[]{:S(2)}) collective-permute-start(bf16[256,512]{1,0:T(8,128)(2,1)S(1)} %convert_element_type.125), channel_id=1, source_target_pairs={{0,2},{1,3},{2,0},{3,1},{4,6},{5,7},{6,4},{7,5},{8,10},{9,11},{10,... | collective-permute-start | bytes 786440 | tf_op jit(solution)/shard_map/ppermute | solution.py:29
  23.7 23.7 %collective-permute-start.4 = (bf16[256,512]{1,0:T(8,128)(2,1)S(1)}, bf16[256,512]{1,0:T(8,128)(2,1)S(1)}, u32[]{:S(2)}, u32[]{:S(2)}) collective-permute-start(bf16[256,512]{1,0:T(8,128)(2,1)S(1)} %convert_element_type.125), channel_id=1, source_target_pairs={{0,1},{1,2},{2,3},{3,0},{4,5},{5,6},{6,7},{7,4},{8,9},{9,10},{10,1... | collective-permute-start | bytes 786440 | tf_op jit(solution)/shard_map/ppermute | solution.py:29
  25.7 21.9 %collective-permute-start.8 = (bf16[1024,256]{1,0:T(8,128)(2,1)}, bf16[1024,256]{1,0:T(8,128)(2,1)S(1)}, u32[]{:S(2)}, u32[]{:S(2)}) collective-permute-start(bf16[1024,256]{1,0:T(8,128)(2,1)} %constant_dynamic-update-slice_fusion.refs_0_.refs_12_.refs_14_), channel_id=1, source_target_pairs={{0,8},{8,0},{1,9},{9,1},{2,10},{10,2},{3,11},{11,3},{4,12},{12,4},... | collective-permute-start | bytes 1572872 | tf_op jit(solution)/shard_map/ppermute | solution.py:29
  29.0 18.6 %collective-permute-start.7 = (bf16[1024,256]{1,0:T(8,128)(2,1)}, bf16[1024,256]{1,0:T(8,128)(2,1)S(1)}, u32[]{:S(2)}, u32[]{:S(2)}) collective-permute-start(bf16[1024,256]{1,0:T(8,128)(2,1)} %constant_dynamic-update-slice_fusion.refs_0_.refs_12_.refs_14_), channel_id=1, source_target_pairs={{0,16},{16,0},{1,17},{17,1},{2,18},{18,2},{3,19},{19,3},{4,20},{20... | collective-permute-start | bytes 1572872 | tf_op jit(solution)/shard_map/ppermute | solution.py:29
  47.6 17.1 %copy-start.3 = (bf16[1024,256]{1,0:T(8,128)(2,1)}, bf16[1024,256]{1,0:T(8,128)(2,1)S(1)}, u32[]{:S(2)}) copy-start(bf16[1024,256]{1,0:T(8,128)(2,1)S(1)} %collective-permute-done.8.refs_1_.refs_13_.refs_15_) | copy-start | bytes 1572868
  47.6 20.0 %copy-start.5 = (bf16[1024,256]{1,0:T(8,128)(2,1)}, bf16[1024,256]{1,0:T(8,128)(2,1)S(1)}, u32[]{:S(2)}) copy-start(bf16[1024,256]{1,0:T(8,128)(2,1)S(1)} %collective-permute-done.7.refs_2_.refs_14_.refs_16_) | copy-start | bytes 1572868
  47.6 13.8 %collective-permute-start.9 = (bf16[1024,256]{1,0:T(8,128)(2,1)S(1)}, bf16[1024,256]{1,0:T(8,128)(2,1)S(1)}, u32[]{:S(2)}, u32[]{:S(2)}) collective-permute-start(bf16[1024,256]{1,0:T(8,128)(2,1)S(1)} %pad_maximum_fusion.refs_0_.refs_3_.refs_5_), channel_id=1, source_target_pairs={{0,16},{16,0},{1,17},{17,1},{2,18},{18,2},{3,19},{19,3},{4,20},{20... | collective-permute-start | bytes 1572872 | tf_op jit(solution)/shard_map/ppermute | solution.py:29
  49.2 13.5 %collective-permute-start.10 = (bf16[1024,256]{1,0:T(8,128)(2,1)S(1)}, bf16[1024,256]{1,0:T(8,128)(2,1)S(1)}, u32[]{:S(2)}, u32[]{:S(2)}) collective-permute-start(bf16[1024,256]{1,0:T(8,128)(2,1)S(1)} %collective-permute-done.7.refs_2_.refs_14_.refs_16_), channel_id=1, source_target_pairs={{0,8},{8,0},{1,9},{9,1},{2,10},{10,2},{3,11},{11,3},{4,12},{12,4},... | collective-permute-start | bytes 1572872 | tf_op jit(solution)/shard_map/ppermute | solution.py:29
  62.6 12.7 %collective-permute-start.11 = (bf16[1024,256]{1,0:T(8,128)(2,1)S(1)}, bf16[1024,256]{1,0:T(8,128)(2,1)}, u32[]{:S(2)}, u32[]{:S(2)}) collective-permute-start(bf16[1024,256]{1,0:T(8,128)(2,1)S(1)} %pad_maximum_fusion.refs_0_.refs_3_.refs_5_), channel_id=1, source_target_pairs={{0,8},{8,0},{1,9},{9,1},{2,10},{10,2},{3,11},{11,3},{4,12},{12,4},... | collective-permute-start | bytes 1572872 | tf_op jit(solution)/shard_map/ppermute | solution.py:29
  64.1 12.4 %collective-permute-start.12 = (bf16[1024,256]{1,0:T(8,128)(2,1)S(1)}, bf16[1024,256]{1,0:T(8,128)(2,1)}, u32[]{:S(2)}, u32[]{:S(2)}) collective-permute-start(bf16[1024,256]{1,0:T(8,128)(2,1)S(1)} %pad_maximum_fusion.1.refs_0_.refs_7_.refs_9_), channel_id=1, source_target_pairs={{0,16},{16,0},{1,17},{17,1},{2,18},{18,2},{3,19},{19,3},{4,20},{20... | collective-permute-start | bytes 1572872 | tf_op jit(solution)/shard_map/ppermute | solution.py:29
  68.3 1.5 collective-permute-start.13
  76.5 11.7 %collective-permute-start.14 = (bf16[1024,256]{1,0:T(8,128)(2,1)}, bf16[1024,256]{1,0:T(8,128)(2,1)}, u32[]{:S(2)}, u32[]{:S(2)}) collective-permute-start(bf16[1024,256]{1,0:T(8,128)(2,1)} %collective-permute-done.11.refs_1_.refs_4_.refs_6_), channel_id=1, source_target_pairs={{0,16},{16,0},{1,17},{17,1},{2,18},{18,2},{3,19},{19,3},{4,20},{20... | collective-permute-start | bytes 1572872 | tf_op jit(solution)/shard_map/ppermute | solution.py:29
  78.0 13.4 %collective-permute-start.18 = (bf16[256,256]{1,0:T(8,128)(2,1)}, bf16[256,256]{1,0:T(8,128)(2,1)S(1)}, u32[]{:S(2)}, u32[]{:S(2)}) collective-permute-start(bf16[256,256]{1,0:T(8,128)(2,1)} %finish_keys.1.refs_7_), channel_id=1, source_target_pairs={{0,3},{1,0},{2,1},{3,2},{4,7},{5,4},{6,5},{7,6},{8,11},{9,8},{10,9... | collective-permute-start | bytes 393224 | tf_op jit(solution)/shard_map/ppermute | solution.py:29
  78.0 13.4 %collective-permute-start.17 = (bf16[256,256]{1,0:T(8,128)(2,1)}, bf16[256,256]{1,0:T(8,128)(2,1)S(1)}, u32[]{:S(2)}, u32[]{:S(2)}) collective-permute-start(bf16[256,256]{1,0:T(8,128)(2,1)} %finish_keys.1.refs_7_), channel_id=1, source_target_pairs={{0,2},{1,3},{2,0},{3,1},{4,6},{5,7},{6,4},{7,5},{8,10},{9,11},{10,... | collective-permute-start | bytes 393224 | tf_op jit(solution)/shard_map/ppermute | solution.py:29
  79.2 12.2 %collective-permute-start.16 = (bf16[256,256]{1,0:T(8,128)(2,1)}, bf16[256,256]{1,0:T(8,128)(2,1)S(1)}, u32[]{:S(2)}, u32[]{:S(2)}) collective-permute-start(bf16[256,256]{1,0:T(8,128)(2,1)} %finish_keys.1.refs_7_), channel_id=1, source_target_pairs={{0,1},{1,2},{2,3},{3,0},{4,5},{5,6},{6,7},{7,4},{8,9},{9,10},{10,1... | collective-permute-start | bytes 393224 | tf_op jit(solution)/shard_map/ppermute | solution.py:29
  81.2 10.5 %collective-permute-start.19 = (bf16[1024,256]{1,0:T(8,128)(2,1)S(1)}, bf16[1024,256]{1,0:T(8,128)(2,1)S(1)}, u32[]{:S(2)}, u32[]{:S(2)}) collective-permute-start(bf16[1024,256]{1,0:T(8,128)(2,1)S(1)} %pad_maximum_fusion.1.refs_0_.refs_7_.refs_9_), channel_id=1, source_target_pairs={{0,8},{8,0},{1,9},{9,1},{2,10},{10,2},{3,11},{11,3},{4,12},{12,4},... | collective-permute-start | bytes 1572872 | tf_op jit(solution)/shard_map/ppermute | solution.py:29
  91.3 4.1 %collective-permute-start.15 = (f32[256,256]{1,0:T(8,128)S(1)}, f32[256,256]{1,0:T(8,128)S(1)}, u32[]{:S(2)}, u32[]{:S(2)}) collective-permute-start(f32[256,256]{1,0:T(8,128)S(1)} %get-tuple-element.56), channel_id=1, source_target_pairs={{0,4},{4,0},{1,5},{5,1},{2,6},{6,2},{3,7},{7,3},{8,12},{12,8},{9,1... | collective-permute-start | bytes 786440 | tf_op jit(solution)/shard_map/ppermute | solution.py:29
  91.8 8.4 %collective-permute-start.21 = (bf16[512,256]{1,0:T(8,128)(2,1)S(1)}, bf16[512,256]{1,0:T(8,128)(2,1)S(1)}, u32[]{:S(2)}, u32[]{:S(2)}) collective-permute-start(bf16[512,256]{1,0:T(8,128)(2,1)S(1)} %slice.159), channel_id=1, source_target_pairs={{0,16},{16,0},{1,17},{17,1},{2,18},{18,2},{3,19},{19,3},{4,20},{20... | collective-permute-start | bytes 786440 | tf_op jit(solution)/shard_map/ppermute | solution.py:29
  93.1 7.7 %collective-permute-start.20 = (bf16[512,256]{1,0:T(8,128)(2,1)S(1)}, bf16[512,256]{1,0:T(8,128)(2,1)S(1)}, u32[]{:S(2)}, u32[]{:S(2)}) collective-permute-start(bf16[512,256]{1,0:T(8,128)(2,1)S(1)} %slice.158), channel_id=1, source_target_pairs={{0,8},{8,0},{1,9},{9,1},{2,10},{10,2},{3,11},{11,3},{4,12},{12,4},... | collective-permute-start | bytes 786440 | tf_op jit(solution)/shard_map/ppermute | solution.py:29
  95.4 29.6 %copy-start.35 = (bf16[512,4096]{1,0:T(8,128)(2,1)}, bf16[512,4096]{1,0:T(8,128)(2,1)S(1)}, u32[]{:S(2)}) copy-start(bf16[512,4096]{1,0:T(8,128)(2,1)S(1)} %constant_dynamic-update-slice_fusion.4) | copy-start | bytes 12582916
  98.7 5.2 %collective-permute-start.23 = (bf16[256,256]{1,0:T(8,128)(2,1)S(1)}, bf16[256,256]{1,0:T(8,128)(2,1)S(1)}, u32[]{:S(2)}, u32[]{:S(2)}) collective-permute-start(bf16[256,256]{1,0:T(8,128)(2,1)S(1)} %get-tuple-element.65.refs_2_), channel_id=1, source_target_pairs={{0,4},{4,0},{1,5},{5,1},{2,6},{6,2},{3,7},{7,3},{8,12},{12,8},{9,1... | collective-permute-start | bytes 393224 | tf_op jit(solution)/shard_map/ppermute | solution.py:29
  103.8 1.6 collective-permute-start.22
  103.9 19.7 %copy-start.43 = (bf16[512,256]{1,0:T(8,128)(2,1)}, bf16[512,256]{1,0:T(8,128)(2,1)S(1)}, u32[]{:S(2)}) copy-start(bf16[512,256]{1,0:T(8,128)(2,1)S(1)} %constant_dynamic-update-slice_fusion.6) | copy-start | bytes 786436
  104.5 17.9 %collective-permute-start.24 = (bf16[1024,256]{1,0:T(8,128)(2,1)S(1)}, bf16[1024,256]{1,0:T(8,128)(2,1)S(1)}, u32[]{:S(2)}, u32[]{:S(2)}) collective-permute-start(bf16[1024,256]{1,0:T(8,128)(2,1)S(1)} %convolution_convert_fusion.3), channel_id=1, source_target_pairs={{0,8},{8,0},{1,9},{9,1},{2,10},{10,2},{3,11},{11,3},{4,12},{12,4},... | collective-permute-start | bytes 1572872 | tf_op jit(solution)/shard_map/ppermute | solution.py:29
  108.3 16.7 %copy-start.19 = (bf16[256,256]{1,0:T(8,128)(2,1)}, bf16[256,256]{1,0:T(8,128)(2,1)S(1)}, u32[]{:S(2)}) copy-start(bf16[256,256]{1,0:T(8,128)(2,1)S(1)} %get-tuple-element.66.refs_3_) | copy-start | bytes 393220
  108.3 16.7 %copy-start.24 = (f32[256,256]{1,0:T(8,128)}, f32[256,256]{1,0:T(8,128)S(1)}, u32[]{:S(2)}) copy-start(f32[256,256]{1,0:T(8,128)S(1)} %get-tuple-element.73.refs_0_) | copy-start | bytes 786436
  108.3 3.6 %collective-permute-start.25 = (bf16[256,256]{1,0:T(8,128)(2,1)S(1)}, bf16[256,256]{1,0:T(8,128)(2,1)S(1)}, u32[]{:S(2)}, u32[]{:S(2)}) collective-permute-start(bf16[256,256]{1,0:T(8,128)(2,1)S(1)} %get-tuple-element.66.refs_3_), channel_id=1, source_target_pairs={{0,4},{4,0},{1,5},{5,1},{2,6},{6,2},{3,7},{7,3},{8,12},{12,8},{9,1... | collective-permute-start | bytes 393224 | tf_op jit(solution)/shard_map/ppermute | solution.py:29
  108.5 6.8 %collective-permute-start.27 = (bf16[256,256]{1,0:T(8,128)(2,1)S(1)}, bf16[256,256]{1,0:T(8,128)(2,1)S(1)}, u32[]{:S(2)}, u32[]{:S(2)}) collective-permute-start(bf16[256,256]{1,0:T(8,128)(2,1)S(1)} %get-tuple-element.69), channel_id=1, source_target_pairs={{0,3},{1,0},{2,1},{3,2},{4,7},{5,4},{6,5},{7,6},{8,11},{9,8},{10,9... | collective-permute-start | bytes 393224 | tf_op jit(solution)/shard_map/ppermute | solution.py:29
  110.2 12.1 %collective-permute-start.28 = (bf16[256,256]{1,0:T(8,128)(2,1)S(1)}, bf16[256,256]{1,0:T(8,128)(2,1)S(1)}, u32[]{:S(2)}, u32[]{:S(2)}) collective-permute-start(bf16[256,256]{1,0:T(8,128)(2,1)S(1)} %get-tuple-element.70), channel_id=1, source_target_pairs={{0,2},{1,3},{2,0},{3,1},{4,6},{5,7},{6,4},{7,5},{8,10},{9,11},{10,... | collective-permute-start | bytes 393224 | tf_op jit(solution)/shard_map/ppermute | solution.py:29
  110.2 12.1 %collective-permute-start.29 = (bf16[256,256]{1,0:T(8,128)(2,1)S(1)}, bf16[256,256]{1,0:T(8,128)(2,1)S(1)}, u32[]{:S(2)}, u32[]{:S(2)}) collective-permute-start(bf16[256,256]{1,0:T(8,128)(2,1)S(1)} %get-tuple-element.71), channel_id=1, source_target_pairs={{0,1},{1,2},{2,3},{3,0},{4,5},{5,6},{6,7},{7,4},{8,9},{9,10},{10,1... | collective-permute-start | bytes 393224 | tf_op jit(solution)/shard_map/ppermute | solution.py:29
  111.9 30.7 %copy-start.45 = (bf16[512,256]{1,0:T(8,128)(2,1)}, bf16[512,256]{1,0:T(8,128)(2,1)S(1)}, u32[]{:S(2)}) copy-start(bf16[512,256]{1,0:T(8,128)(2,1)S(1)} %constant_dynamic-update-slice_fusion.8) | copy-start | bytes 786436
  112.5 15.0 %collective-permute-start.26 = (bf16[1024,256]{1,0:T(8,128)(2,1)S(1)}, bf16[1024,256]{1,0:T(8,128)(2,1)}, u32[]{:S(2)}, u32[]{:S(2)}) collective-permute-start(bf16[1024,256]{1,0:T(8,128)(2,1)S(1)} %convolution_convert_fusion.2), channel_id=1, source_target_pairs={{0,16},{16,0},{1,17},{17,1},{2,18},{18,2},{3,19},{19,3},{4,20},{20... | collective-permute-start | bytes 1572872 | tf_op jit(solution)/shard_map/ppermute | solution.py:29
  125.0 13.5 %collective-permute-start.31 = (bf16[1024,256]{1,0:T(8,128)(2,1)}, bf16[1024,256]{1,0:T(8,128)(2,1)S(1)}, u32[]{:S(2)}, u32[]{:S(2)}) collective-permute-start(bf16[1024,256]{1,0:T(8,128)(2,1)} %fusion.3), channel_id=1, source_target_pairs={{0,16},{16,0},{1,17},{17,1},{2,18},{18,2},{3,19},{19,3},{4,20},{20... | collective-permute-start | bytes 1572872 | tf_op jit(solution)/shard_map/ppermute | solution.py:29
  126.3 13.7 %collective-permute-start.32 = (bf16[1024,256]{1,0:T(8,128)(2,1)}, bf16[1024,256]{1,0:T(8,128)(2,1)}, u32[]{:S(2)}, u32[]{:S(2)}) collective-permute-start(bf16[1024,256]{1,0:T(8,128)(2,1)} %convolution_convert_fusion.1), channel_id=1, source_target_pairs={{0,8},{8,0},{1,9},{9,1},{2,10},{10,2},{3,11},{11,3},{4,12},{12,4},... | collective-permute-start | bytes 1572872 | tf_op jit(solution)/shard_map/ppermute | solution.py:29
  129.4 1.6 collective-permute-start.30
  141.7 18.5 %collective-permute-start.36 = (bf16[1024,256]{1,0:T(8,128)(2,1)S(1)}, bf16[1024,256]{1,0:T(8,128)(2,1)S(1)}, u32[]{:S(2)}, u32[]{:S(2)}) collective-permute-start(bf16[1024,256]{1,0:T(8,128)(2,1)S(1)} %convolution_convert_fusion), channel_id=1, source_target_pairs={{0,16},{16,0},{1,17},{17,1},{2,18},{18,2},{3,19},{19,3},{4,20},{20... | collective-permute-start | bytes 1572872 | tf_op jit(solution)/shard_map/ppermute | solution.py:29
  144.3 15.9 %collective-permute-start.37 = (bf16[1024,256]{1,0:T(8,128)(2,1)S(1)}, bf16[1024,256]{1,0:T(8,128)(2,1)S(1)}, u32[]{:S(2)}, u32[]{:S(2)}) collective-permute-start(bf16[1024,256]{1,0:T(8,128)(2,1)S(1)} %fusion.4), channel_id=1, source_target_pairs={{0,8},{8,0},{1,9},{9,1},{2,10},{10,2},{3,11},{11,3},{4,12},{12,4},... | collective-permute-start | bytes 1572872 | tf_op jit(solution)/shard_map/ppermute | solution.py:29
  147.3 8.2 %collective-permute-start.35 = (bf16[256,256]{1,0:T(8,128)(2,1)S(1)}, bf16[256,256]{1,0:T(8,128)(2,1)S(1)}, u32[]{:S(2)}, u32[]{:S(2)}) collective-permute-start(bf16[256,256]{1,0:T(8,128)(2,1)S(1)} %get-tuple-element.90), channel_id=1, source_target_pairs={{0,1},{1,2},{2,3},{3,0},{4,5},{5,6},{6,7},{7,4},{8,9},{9,10},{10,1... | collective-permute-start | bytes 393224 | tf_op jit(solution)/shard_map/ppermute | solution.py:29
  148.2 10.9 %collective-permute-start.34 = (bf16[256,256]{1,0:T(8,128)(2,1)S(1)}, bf16[256,256]{1,0:T(8,128)(2,1)S(1)}, u32[]{:S(2)}, u32[]{:S(2)}) collective-permute-start(bf16[256,256]{1,0:T(8,128)(2,1)S(1)} %get-tuple-element.91), channel_id=1, source_target_pairs={{0,2},{1,3},{2,0},{3,1},{4,6},{5,7},{6,4},{7,5},{8,10},{9,11},{10,... | collective-permute-start | bytes 393224 | tf_op jit(solution)/shard_map/ppermute | solution.py:29
  150.3 9.8 %collective-permute-start.33 = (bf16[256,256]{1,0:T(8,128)(2,1)S(1)}, bf16[256,256]{1,0:T(8,128)(2,1)S(1)}, u32[]{:S(2)}, u32[]{:S(2)}) collective-permute-start(bf16[256,256]{1,0:T(8,128)(2,1)S(1)} %get-tuple-element.92), channel_id=1, source_target_pairs={{0,3},{1,0},{2,1},{3,2},{4,7},{5,4},{6,5},{7,6},{8,11},{9,8},{10,9... | collective-permute-start | bytes 393224 | tf_op jit(solution)/shard_map/ppermute | solution.py:29
  155.5 10.9 %collective-permute-start.44 = (bf16[512,256]{1,0:T(8,128)(2,1)S(1)}, bf16[512,256]{1,0:T(8,128)(2,1)S(1)}, u32[]{:S(2)}, u32[]{:S(2)}) collective-permute-start(bf16[512,256]{1,0:T(8,128)(2,1)S(1)} %convolution_convert_fusion.4), channel_id=1, source_target_pairs={{0,16},{16,0},{1,17},{17,1},{2,18},{18,2},{3,19},{19,3},{4,20},{20... | collective-permute-start | bytes 786440 | tf_op jit(solution)/shard_map/ppermute | solution.py:29
  159.1 9.1 %collective-permute-start.42 = (bf16[512,256]{1,0:T(8,128)(2,1)S(1)}, bf16[512,256]{1,0:T(8,128)(2,1)S(1)}, u32[]{:S(2)}, u32[]{:S(2)}) collective-permute-start(bf16[512,256]{1,0:T(8,128)(2,1)S(1)} %convolution_convert_fusion.7), channel_id=1, source_target_pairs={{0,8},{8,0},{1,9},{9,1},{2,10},{10,2},{3,11},{11,3},{4,12},{12,4},... | collective-permute-start | bytes 786440 | tf_op jit(solution)/shard_map/ppermute | solution.py:29
  164.0 25.4 %collective-permute-start.38 = (bf16[256,4096]{1,0:T(8,128)(2,1)S(1)}, bf16[256,4096]{1,0:T(8,128)(2,1)S(1)}, u32[]{:S(2)}, u32[]{:S(2)}) collective-permute-start(bf16[256,4096]{1,0:T(8,128)(2,1)S(1)} %grad_columns.1), channel_id=1, source_target_pairs={{0,4},{4,0},{1,5},{5,1},{2,6},{6,2},{3,7},{7,3},{8,12},{12,8},{9,1... | collective-permute-start | bytes 6291464 | tf_op jit(solution)/shard_map/ppermute | solution.py:29
  164.7 8.6 %collective-permute-start.41 = (bf16[256,256]{1,0:T(8,128)(2,1)S(1)}, bf16[256,256]{1,0:T(8,128)(2,1)S(1)}, u32[]{:S(2)}, u32[]{:S(2)}) collective-permute-start(bf16[256,256]{1,0:T(8,128)(2,1)S(1)} %get-tuple-element.86), channel_id=1, source_target_pairs={{0,1},{1,2},{2,3},{3,0},{4,5},{5,6},{6,7},{7,4},{8,9},{9,10},{10,1... | collective-permute-start | bytes 393224 | tf_op jit(solution)/shard_map/ppermute | solution.py:29
  166.8 14.9 %collective-permute-start.45 = (bf16[1024,256]{1,0:T(8,128)(2,1)S(1)}, bf16[1024,256]{1,0:T(8,128)(2,1)S(1)}, u32[]{:S(2)}, u32[]{:S(2)}) collective-permute-start(bf16[1024,256]{1,0:T(8,128)(2,1)S(1)} %pad_maximum_fusion.4), channel_id=1, source_target_pairs={{0,8},{8,0},{1,9},{9,1},{2,10},{10,2},{3,11},{11,3},{4,12},{12,4},... | collective-permute-start | bytes 1572872 | tf_op jit(solution)/shard_map/ppermute | solution.py:29
  168.6 20.8 %copy-start.18 = (bf16[256,256]{1,0:T(8,128)(2,1)S(1)}, bf16[256,256]{1,0:T(8,128)(2,1)}, u32[]{:S(2)}) copy-start(bf16[256,256]{1,0:T(8,128)(2,1)} %copy-done.17) | copy-start | bytes 393220
  168.6 20.8 %copy-start.20 = (bf16[256,256]{1,0:T(8,128)(2,1)S(1)}, bf16[256,256]{1,0:T(8,128)(2,1)}, u32[]{:S(2)}) copy-start(bf16[256,256]{1,0:T(8,128)(2,1)} %copy-done.19) | copy-start | bytes 393220
  168.6 20.8 %copy-start.33 = (s32[2,4]{1,0:T(2,128)S(1)}, s32[2,4]{1,0:T(2,128)}, u32[]{:S(2)}) copy-start(s32[2,4]{1,0:T(2,128)} %pad_add_fusion.1.piece_ref.refs_1_) | copy-start | bytes 100
  168.6 20.8 %copy-start.34 = (s32[4]{0:T(128)S(1)}, s32[4]{0:T(128)}, u32[]{:S(2)}) copy-start(s32[4]{0:T(128)} %fusion.26.slab_ref.refs_0_) | copy-start | bytes 52
  168.7 13.8 %collective-permute-start.43 = (bf16[1024,256]{1,0:T(8,128)(2,1)S(1)}, bf16[1024,256]{1,0:T(8,128)(2,1)S(1)}, u32[]{:S(2)}, u32[]{:S(2)}) collective-permute-start(bf16[1024,256]{1,0:T(8,128)(2,1)S(1)} %pad_maximum_fusion.3), channel_id=1, source_target_pairs={{0,16},{16,0},{1,17},{17,1},{2,18},{18,2},{3,19},{19,3},{4,20},{20... | collective-permute-start | bytes 1572872 | tf_op jit(solution)/shard_map/ppermute | solution.py:29
  169.9 10.2 %collective-permute-start.40 = (bf16[256,256]{1,0:T(8,128)(2,1)S(1)}, bf16[256,256]{1,0:T(8,128)(2,1)S(1)}, u32[]{:S(2)}, u32[]{:S(2)}) collective-permute-start(bf16[256,256]{1,0:T(8,128)(2,1)S(1)} %get-tuple-element.87), channel_id=1, source_target_pairs={{0,2},{1,3},{2,0},{3,1},{4,6},{5,7},{6,4},{7,5},{8,10},{9,11},{10,... | collective-permute-start | bytes 393224 | tf_op jit(solution)/shard_map/ppermute | solution.py:29
  173.3 7.4 %collective-permute-start.39 = (bf16[256,256]{1,0:T(8,128)(2,1)S(1)}, bf16[256,256]{1,0:T(8,128)(2,1)S(1)}, u32[]{:S(2)}, u32[]{:S(2)}) collective-permute-start(bf16[256,256]{1,0:T(8,128)(2,1)S(1)} %get-tuple-element.88), channel_id=1, source_target_pairs={{0,3},{1,0},{2,1},{3,2},{4,7},{5,4},{6,5},{7,6},{8,11},{9,8},{10,9... | collective-permute-start | bytes 393224 | tf_op jit(solution)/shard_map/ppermute | solution.py:29
  183.0 12.6 %collective-permute-start.48 = (bf16[256,256]{1,0:T(8,128)(2,1)S(1)}, bf16[256,256]{1,0:T(8,128)(2,1)S(1)}, u32[]{:S(2)}, u32[]{:S(2)}) collective-permute-start(bf16[256,256]{1,0:T(8,128)(2,1)S(1)} %get-tuple-element.82), channel_id=1, source_target_pairs={{0,1},{1,2},{2,3},{3,0},{4,5},{5,6},{6,7},{7,4},{8,9},{9,10},{10,1... | collective-permute-start | bytes 393224 | tf_op jit(solution)/shard_map/ppermute | solution.py:29
  185.4 10.3 %collective-permute-start.47 = (bf16[256,256]{1,0:T(8,128)(2,1)S(1)}, bf16[256,256]{1,0:T(8,128)(2,1)S(1)}, u32[]{:S(2)}, u32[]{:S(2)}) collective-permute-start(bf16[256,256]{1,0:T(8,128)(2,1)S(1)} %get-tuple-element.83), channel_id=1, source_target_pairs={{0,2},{1,3},{2,0},{3,1},{4,6},{5,7},{6,4},{7,5},{8,10},{9,11},{10,... | collective-permute-start | bytes 393224 | tf_op jit(solution)/shard_map/ppermute | solution.py:29
  186.8 8.9 %collective-permute-start.46 = (bf16[256,256]{1,0:T(8,128)(2,1)S(1)}, bf16[256,256]{1,0:T(8,128)(2,1)S(1)}, u32[]{:S(2)}, u32[]{:S(2)}) collective-permute-start(bf16[256,256]{1,0:T(8,128)(2,1)S(1)} %get-tuple-element.84), channel_id=1, source_target_pairs={{0,3},{1,0},{2,1},{3,2},{4,7},{5,4},{6,5},{7,6},{8,11},{9,8},{10,9... | collective-permute-start | bytes 393224 | tf_op jit(solution)/shard_map/ppermute | solution.py:29
  (34 other events, 344.2 us)

commit v3 on v2

--- a/solution.py
+++ b/solution.py
@@ -33,12 +33,27 @@
     return lax.optimization_barrier((block, *others))[0]
 
 
+def stage(*arrays):
+    return list(lax.optimization_barrier(arrays))
+
+
+def after_all(blocks, *others):
+    return [after(block, *others) for block in blocks]
+
+
 def swap(block):
     return shift(block, "core", 1)
 
 
 def gather_line(block):
-    return [block] + [shift(block, "ctx", k) for k in range(1, lax.axis_size("ctx"))]
+    copies = jnp.broadcast_to(block[None], (lax.axis_size("ctx"), *block.shape))
+    return lax.all_to_all(copies, "ctx", 0, 0).reshape(-1, block.shape[1])
+
+
+def scatter_line(term):
+    size = lax.axis_size("ctx")
+    blocks = term.reshape(size, term.shape[0] // size, term.shape[1])
+    return lax.all_to_all(blocks, "ctx", 0, 0)
 
 
 def along(block, axis):
@@ -70,21 +85,19 @@
     return slabs
 
 
-def reduce_corners(make, way, split, *deps):
+def reduce_corners(make, way, split):
     size_b = lax.axis_size("b")
     whole, top, low = slice(None), slice(0, split), slice(split, None)
-    came_a, came_b = {}, {}
+    came_a, came_b, went = {}, {}, []
     for da in range(1, lax.axis_size("a")):
         for db in range(1, size_b):
             i = da * size_b + db
-            if way == "b":
-                came_a[da, db] = shift(make(i, whole, deps), "b", -db)
-            elif way == "a":
-                came_b[da, db] = shift(make(i, whole, deps), "a", -da)
-            else:
-                came_a[da, db] = shift(make(i, top, deps), "b", -db)
-                came_b[da, db] = shift(make(i, low, deps), "a", -da)
-    return came_a, came_b
+            went += [make(i, rows) for rows in ((top, low) if way == "both" else (whole,))]
+            if way != "a":
+                came_a[da, db] = shift(went[-2 if way == "both" else -1], "b", -db)
+            if way != "b":
+                came_b[da, db] = shift(went[-1], "a", -da)
+    return came_a, came_b, went
 
 
 def reduce_sides(make, came, way, split, *deps):
@@ -92,12 +105,12 @@
     whole, top, low = slice(None), slice(0, split), slice(split, None)
 
     def side(i, extra, part):
-        if not extra:
-            return make(i, whole, deps)
-        if way != "both":
-            return make(i, whole, deps, extra)
-        halves = [make(i, rows, deps, extra if rows == part else []) for rows in (top, low)]
-        return jnp.concatenate(halves, axis=0)
+        if not extra or way != "both":
+            term = make(i, whole, extra)
+        else:
+            halves = [make(i, rows, extra if rows == part else []) for rows in (top, low)]
+            term = jnp.concatenate(halves, axis=0)
+        return after(term, *deps) if deps else term
 
     went, arrived = [], []
     for da in range(1, size_a):
@@ -112,12 +125,7 @@
 
 
 def reduce_line(term, last=()):
-    size = lax.axis_size("ctx")
-    rows = term.shape[0] // size
-    total = after(term[:rows], *last).astype(jnp.float32)
-    for k in range(1, size):
-        total = total + shift(term[k * rows : (k + 1) * rows], "ctx", -k).astype(jnp.float32)
-    return total
+    return jnp.sum(after(scatter_line(term), *last).astype(jnp.float32), axis=0)
 
 
 def pick_kernel(slab_ref, piece_ref, source_ref, mine_ref, theirs_ref, *, block):
@@ -271,47 +279,58 @@
     )
 
 
-def project_kernel(mine_ref, theirs_ref, *refs):
-    pieces, (own_ref, other_ref) = refs[:-2], refs[-2:]
-    for source, target in ((theirs_ref, other_ref), (mine_ref, own_ref)):
-        at, total = 0, None
-        for piece in pieces:
-            end = at + piece.shape[0]
-            term = dot(source[:, at:end], piece[...], 1, 0)
-            total = term if total is None else total + term
-            at = end
+def project_kernel(*refs, counts, more):
+    count = 2 * len(counts)
+    sources, refs = refs[:count], refs[count:]
+    pieces, (own_ref, other_ref) = refs[: sum(counts)], refs[-2:]
+    for half, target in ((1, other_ref), (0, own_ref)):
+        total = refs[sum(counts) + half][...] if more else None
+        left = iter(pieces)
+        for i, number in enumerate(counts):
+            source, at = sources[2 * i + half], 0
+            for _ in range(number):
+                piece = next(left)
+                end = at + piece.shape[0]
+                term = dot(source[:, at:end], piece[...], 1, 0)
+                total = term if total is None else total + term
+                at = end
         target[...] = total
 
 
-def project_rows(mine, theirs, pieces):
-    rows, columns = mine.shape[0], pieces[0].shape[1]
-    return pl.pallas_call(
-        project_kernel,
-        in_specs=[VMEM] * (len(pieces) + 2),
-        out_specs=[VMEM] * 2,
+def project_rows(mine, theirs, slabs, before=()):
+    rows = mine.shape[0]
+    flat = [piece for slab in slabs.values() for piece in slab]
+    columns = flat[0].shape[1]
+    operands, in_specs = [], []
+    for i, slab in slabs.items():
+        plane = sum(piece.shape[0] for piece in slab)
+        operands += [mine, theirs]
+        in_specs += [pl.BlockSpec((rows, plane), lambda _, i=i: (0, i))] * 2
+    whole = [*flat, *before]
+    in_specs += [pl.BlockSpec(array.shape, lambda _: (0, 0)) for array in whole]
+    area = sum(piece.size for piece in flat)
+    return pl.pallas_call(
+        functools.partial(
+            project_kernel, counts=[len(slab) for slab in slabs.values()], more=bool(before)
+        ),
+        grid=(1,),
+        in_specs=in_specs,
+        out_specs=[pl.BlockSpec((rows, columns), lambda _: (0, 0))] * 2,
         out_shape=[jax.ShapeDtypeStruct((rows, columns), jnp.float32)] * 2,
-        compiler_params=pltpu.CompilerParams(vmem_limit_bytes=20 * 1024 * 1024),
+        compiler_params=pltpu.CompilerParams(vmem_limit_bytes=24 * 1024 * 1024),
         cost_estimate=pl.CostEstimate(
-            flops=4 * mine.size * columns,
-            bytes_accessed=4 * mine.size + 2 * mine.shape[1] * columns,
+            flops=4 * rows * area,
+            bytes_accessed=2 * area + 4 * rows * area // columns,
             transcendentals=0,
         ),
         name="project_rows",
-    )(mine, theirs, *pieces)
-
-
-def attend_kernel(*refs, group, parts, head_dim, scale, last):
-    q_own, q_other, grads, cos_ref, sin_ref, row_pos, key_pos = refs[:7]
-    pieces = refs[7 : 7 + parts]
-    rest = refs[7 + parts :]
-    if last:
-        before, rest = rest[0], rest[1:]
-    attention_ref, grad_ref = rest[:2]
-    terms = rest[2:-1]
-    held = rest[-1]
-    rows = q_own.shape[0]
-    for j in range(parts):
-        held[j * rows : (j + 1) * rows, :] = pieces[j][...]
+    )(*operands, *whole)
+
+
+def attend_kernel(*refs, group, head_dim, scale, last):
+    q_own, q_other, grads, cos_ref, sin_ref, row_pos, key_pos, held = refs[:8]
+    before = refs[8]
+    attention_ref, grad_ref, term_ref = refs[-3:]
     keys, values = held[:, :head_dim], held[:, head_dim:]
     cos, sin = cos_ref[...], sin_ref[...]
     allowed = key_pos[...] <= row_pos[...]
@@ -341,38 +360,27 @@
     if last:
         key_term = key_term + before[:, :head_dim]
         value_term = value_term + before[:, head_dim:]
-        for j in range(parts):
-            span = slice(j * rows, (j + 1) * rows)
-            terms[j][:, :head_dim] = key_term[span].astype(terms[j].dtype)
-            terms[j][:, head_dim:] = value_term[span].astype(terms[j].dtype)
-    else:
-        terms[0][:, :head_dim] = key_term
-        terms[0][:, head_dim:] = value_term
-
-
-def attend(q_own, q_other, grads, cos, sin, row_pos, key_pos, pieces, before, scale):
+    term_ref[:, :head_dim] = key_term.astype(term_ref.dtype)
+    term_ref[:, head_dim:] = value_term.astype(term_ref.dtype)
+
+
+def attend(q_own, q_other, grads, cos, sin, row_pos, key_pos, key_values, before, scale):
     rows, columns = q_own.shape
     head_dim = cos.shape[1]
-    parts = len(pieces)
+    keys = key_values.shape[0]
+    group = columns // head_dim
     last = before is not None
-    keys = parts * rows
-    group = columns // head_dim
-    if last:
-        terms = [jax.ShapeDtypeStruct((rows, 2 * head_dim), jnp.float32)]
-        terms += [jax.ShapeDtypeStruct((rows, 2 * head_dim), jnp.bfloat16)] * (parts - 1)
-    else:
-        terms = [jax.ShapeDtypeStruct((keys, 2 * head_dim), jnp.float32)]
-    out_shape = [jax.ShapeDtypeStruct((rows, columns), jnp.bfloat16)] * 2 + terms
-    operands = [q_own, q_other, grads, cos, sin, row_pos, key_pos, *pieces]
+    operands = [q_own, q_other, grads, cos, sin, row_pos, key_pos, key_values]
     operands += [before] if last else []
-    out = pl.pallas_call(
-        functools.partial(
-            attend_kernel, group=group, parts=parts, head_dim=head_dim, scale=scale, last=last
-        ),
+    return pl.pallas_call(
+        functools.partial(attend_kernel, group=group, head_dim=head_dim, scale=scale, last=last),
         in_specs=[VMEM] * len(operands),
-        out_specs=[VMEM] * len(out_shape),
-        out_shape=out_shape,
-        scratch_shapes=[pltpu.VMEM((keys, 2 * head_dim), jnp.bfloat16)],
+        out_specs=[VMEM] * 3,
+        out_shape=[
+            jax.ShapeDtypeStruct((rows, columns), jnp.bfloat16),
+            jax.ShapeDtypeStruct((rows, columns), jnp.bfloat16),
+            jax.ShapeDtypeStruct(key_values.shape, jnp.bfloat16 if last else jnp.float32),
+        ],
         compiler_params=pltpu.CompilerParams(vmem_limit_bytes=20 * 1024 * 1024),
         cost_estimate=pl.CostEstimate(
             flops=14 * rows * keys * columns,
@@ -381,7 +389,6 @@
         ),
         name="attend",
     )(*operands)
-    return out[0], out[1], out[2:]
 
 
 def finish_kernel(own, other, cos_ref, sin_ref, out):
@@ -403,12 +410,11 @@
     )(own, other, cos, sin)
 
 
-def undo_kernel(*refs):
-    pieces, (cos_ref, sin_ref, out) = refs[:-3], refs[-3:]
+def undo_kernel(pieces, cos_ref, sin_ref, out):
     head_dim = cos_ref.shape[1]
-    total = pieces[0][...]
-    for piece in pieces[1:]:
-        total = total + piece[...].astype(jnp.float32)
+    total = pieces[0].astype(jnp.float32)
+    for k in range(1, pieces.shape[0]):
+        total = total + pieces[k].astype(jnp.float32)
     key = total[:, :head_dim]
     key = key * cos_ref[...] - pltpu.roll(key, head_dim // 2, 1) * sin_ref[...]
     out[:, :head_dim] = key.astype(jnp.bfloat16)
@@ -418,11 +424,11 @@
 def undo_keys(pieces, cos, sin):
     return pl.pallas_call(
         undo_kernel,
-        in_specs=[VMEM] * (len(pieces) + 2),
+        in_specs=[VMEM] * 3,
         out_specs=VMEM,
-        out_shape=jax.ShapeDtypeStruct(pieces[0].shape, jnp.bfloat16),
+        out_shape=jax.ShapeDtypeStruct(pieces.shape[1:], jnp.bfloat16),
         name="undo_keys",
-    )(*pieces, cos, sin)
+    )(pieces, cos, sin)
 
 
 def body(tokens, positions, query_weight, key_weight, value_weight, grad_output):
@@ -443,41 +449,37 @@
     da, db = jnp.meshgrid(jnp.arange(size_a), jnp.arange(size_b), indexing="ij")
     slabs = ((at_a + size_a - da) % size_a) * size_b + (at_b + size_b - db) % size_b
     slabs = slabs.reshape(-1).astype(jnp.int32)
-    line = (place + ctx - jnp.arange(ctx)) % ctx
+    line = jnp.arange(ctx)
     pieces = jnp.stack([core * ctx + line, (1 - core) * ctx + line]).astype(jnp.int32)
     mine, theirs = pick_columns(token_rows, slabs, pieces, block)
-    pieces_kv = gather_line(kv_local)
-    kv_line = jnp.concatenate([after(pieces_kv[0], mine), *pieces_kv[1:]], axis=0)
+    kv_line, _ = stage(gather_line(kv_local), mine)
     theirs = swap(after(theirs, kv_line))
-
-    pieces_q = gather_line(after(query_weight, kv_line).astype(jnp.bfloat16))
     half = query_width // 2
-    q_line = [
-        jnp.concatenate([piece[:, g * half : (g + 1) * half] for piece in pieces_q], axis=0)
-        for g in range(2)
-    ]
-    kv_sides = along(kv_line, "a"), along(kv_line, "b")
-    stage = kv_sides[0] + kv_sides[1] + q_line
-    kv_corners = gather_corners(*kv_sides, "b", *stage)
-    q0_a = along(after(q_line[0], *stage), "a")
-    stage = q0_a + [piece for corner in kv_corners.values() for piece in corner]
-    q1_a = along(after(q_line[1], *stage), "a")
-    q0_b = along(after(q_line[0], *stage), "b")
-    kv_slabs = in_order(kv_line, *kv_sides, kv_corners)
+    q_local = [query_weight[:, g * half : (g + 1) * half].astype(jnp.bfloat16) for g in range(2)]
+
+    count_a, count_b = size_a - 1, size_b - 1
+    kv_sides = along(kv_line, "a") + along(kv_line, "b")
+    there = stage(*kv_sides, gather_line(after(q_local[0], kv_line)))
+    kv_a, kv_b, q_line = there[:count_a], there[count_a:-1], there[-1:]
+    kv_corners = gather_corners(kv_a, kv_b, "b")
+    q0_a = along(q_line[0], "a")
+    corners = [piece for corner in kv_corners.values() for piece in corner]
+    there = stage(*q0_a, *corners, gather_line(after(q_local[1], *kv_a)))
+    q0_a = there[:count_a]
+    q_line.append(there[-1])
+    q1_a = along(q_line[1], "a")
+    q0_b = along(after(q_line[0], *q0_a), "b")
+    kv_slabs = in_order(kv_line, kv_a, kv_b, kv_corners)
 
     positions = after(positions, kv_line)
     own_positions = lax.dynamic_slice_in_dim(positions, place * rows, rows)
     cos_table, sin_table = rope_tables(own_positions, head_dim)
     sin_table = jnp.where(jnp.arange(head_dim) < head_dim // 2, -sin_table, sin_table)
-    key_positions = jnp.concatenate(
-        [
-            lax.dynamic_slice_in_dim(positions, ((place + ctx - k) % ctx) * rows, rows)
-            for k in range(ctx)
-        ]
-    )
-
     def project(slabs):
-        own, other = project_rows(mine, theirs, [piece for slab in slabs for piece in slab])
+        early = {i: slab for i, slab in enumerate(slabs) if (i // size_b) * (i % size_b) == 0}
+        late = {i: slab for i, slab in enumerate(slabs) if i not in early}
+        part = project_rows(mine, theirs, early)
+        own, other = project_rows(mine, theirs, late, part)
         return own, swap(other)
 
     columns = jnp.concatenate([after(mine, *q0_a), theirs], axis=0)
@@ -485,23 +487,27 @@
     def terms_of(own, other):
         both = jnp.concatenate([own, other], axis=0)
 
-        def make(i, part, deps=(), extra=()):
+        def make(i, part, extra=()):
             start, stop, _ = part.indices(plane)
             at = slice(i * plane + start, i * plane + stop)
-            term = mm(columns[:, at], after(both, *deps) if deps else both, ((0,), (0,)))
+            term = mm(columns[:, at], both, ((0,), (0,)))
             for piece in extra:
                 term = term + piece.astype(jnp.float32)
             return term.astype(jnp.bfloat16)
 
         return make
 
-    key_value = finish_keys(*project(kv_slabs), cos_table, sin_table)
-    stage = q1_a + q0_b + [key_value]
-    q0_corners = gather_corners(q0_a, q0_b, "a", *stage)
-    q1_b = along(after(q_line[1], *stage), "b")
+    own, other = project_rows(mine, theirs, dict(enumerate(kv_slabs)))
+    key_value = finish_keys(own, swap(other), cos_table, sin_table)
+    key_value, *there = stage(key_value, *q1_a, *q0_b)
+    q1_a, q0_b = there[:count_a], there[count_a:]
+    q0_corners = gather_corners(q0_a, q0_b, "a")
+    q1_b = along(after(q_line[1], key_value), "b")
     key_values = gather_line(key_value)
-    stage = q1_b + key_values + [piece for corner in q0_corners.values() for piece in corner]
-    q1_corners = gather_corners(q1_a, q1_b, "both", *stage)
+    corners = [piece for corner in q0_corners.values() for piece in corner]
+    there = stage(*q1_b, *corners, key_values)
+    q1_b, key_values = there[:count_b], there[-1]
+    q1_corners = gather_corners(after_all(q1_a, *there), q1_b, "both")
     q_slabs = [
         in_order(q_line[0], q0_a, q0_b, q0_corners),
         in_order(q_line[1], q1_a, q1_b, q1_corners),
@@ -511,48 +517,48 @@
     term = None
     for g in range(2):
         span = slice(g * group * head_dim, (g + 1) * group * head_dim)
-        attention, grad_q, terms = attend(
+        attention, grad_q, term = attend(
             *project(q_slabs[g]),
             grad_output[0][:, span],
             cos_table,
             sin_table,
             own_positions[:, None],
-            key_positions[None, :],
+            positions[None, :],
             key_values,
             term,
             scale,
         )
-        term = terms[0]
         attentions.append(attention)
         grads = (grad_q, swap(grad_q))
         gradients.append(grads)
         made.append(terms_of(*grads))
         came.append(reduce_corners(made[g], "ba"[g], mid))
-    summed = [terms[0]] + [shift(terms[k], "ctx", -k) for k in range(1, ctx)]
+    summed = scatter_line(after(term, *came[1][2]))
     first = [*came[0][0].values(), *came[0][1].values()]
     second = [*came[1][0].values(), *came[1][1].values()]
-    sides0, went0 = reduce_sides(made[0], came[0], "b", mid, *first, *summed[1:])
-    grad_kv = undo_keys(
-        [after(summed[0], *first, *second, *went0), *summed[1:]], cos_table, sin_table
-    )
+    sides0, went0 = reduce_sides(made[0], came[0], "b", mid, *first, summed)
+    grad_kv = undo_keys(after(summed, *first, *second, *went0), cos_table, sin_table)
     gradients.append((grad_kv, swap(grad_kv)))
     made.append(terms_of(*gradients[2]))
     came.append(reduce_corners(made[2], "both", mid))
-    sides1, went1 = reduce_sides(made[1], came[1], "a", mid, *sides0)
-    q_sum = reduce_line(made[0](0, slice(None), went1, sides0))
-    line1 = made[1](0, slice(None), (), sides1)
-    kv_sides, _ = reduce_sides(made[2], came[2], "both", mid, *sides1)
+    third = [*came[2][0].values(), *came[2][1].values()]
+    sides1, went1 = reduce_sides(made[1], came[1], "a", mid, *sides0, *third)
+    line0 = after(made[0](0, slice(None), sides0), *went1)
+    q_grads = [reduce_line(line0, sides1)]
+    line1 = made[1](0, slice(None), sides1)
+    kv_sides, _ = reduce_sides(made[2], came[2], "both", mid, *sides1, q_grads[0])
+    q_grads.append(reduce_line(line1, kv_sides))
 
     weights = [*q_slabs, kv_slabs]
     grad_theirs = grad_columns(
-        [gradients[0][1], gradients[1][1], after(gradients[2][1], q_sum, *sides1)], weights
+        [gradients[0][1], gradients[1][1], after(gradients[2][1], *third)], weights
     )
     grad_theirs = swap(grad_theirs)
     grad_input = grad_place(
         [gradients[0][0], gradients[1][0], gradients[2][0]], weights, grad_theirs, slabs, pieces, block
     )
-    q_grads = [q_sum, reduce_line(line1)]
-    kv_wgrad = reduce_line(made[2](0, slice(None), (), kv_sides), (grad_input,))
+    kv_line = after(made[2](0, slice(None), kv_sides), q_grads[1])
+    kv_wgrad = reduce_line(kv_line, (grad_input,))
 
     query_grad = jnp.concatenate(q_grads, axis=1)
     key_grad = kv_wgrad[:, :head_dim]

time: 197 us -> 251 us (1.27)
  matrix products: 12.7 us -> 28.5 us
  local copies, waits for them, and re-layouts: 10.4 us -> 21 us
  Pallas kernels: 33.6 us -> 43.6 us
  other arithmetic: 6.52 us -> 15.6 us
  waiting for transfers between devices: 71.9 us -> 78.1 us
    all_to_all x0 -> x8, starting transfers between devices: none -> 37 us  [the longest x4 18.8 us: gather_line(): return lax.all_to_all(copies, 'ctx', 0, 0).reshape(-1, block.shape[1])]
    ppermute x49 -> x28, starting transfers between devices: 59.7 us -> 23.7 us  [shift(): lax.ppermute(block, axis, [(i, (i + step) % size) for i in range(size)])]
    all_to_all x0 -> x8, waiting for transfers between devices: none -> 24 us  [the longest x4 16.7 us: scatter_line(): return lax.all_to_all(blocks, 'ctx', 0, 0)]
    ppermute x49 -> x28, waiting for transfers between devices: 71.9 us -> 54.1 us  [shift(): lax.ppermute(block, axis, [(i, (i + step) % size) for i in range(size)])]
    dot_general x15, matrix products: 12.7 us -> 28.5 us  [mm(): lax.dot_general(a, b, (dims, ((), ())), preferred_element_type=jnp.float32)]
    pallas_call x6 -> x8, Pallas kernels: 16.4 us -> 23.3 us  [the longest x5 12.6 us: project_rows(): pl.pallas_call(functools.partial(project_kernel, counts=[len(slab) for sl...]
    unnamed x104 -> x87, local copies, waits for them, and re-layouts: 4.37 us -> 9.53 us
    reduce_sum x0 -> x3, other arithmetic: none -> 4.86 us  [reduce_line(): return jnp.sum(after(scatter_line(term), *last).astype(jnp.float32), axis=0)]
  transfers between devices with their start and end apart: 49 -> 36, of which waited for: 24 -> 20; matrix products, arithmetic and copies ran while one was open for 11% -> 20% of each run, Pallas kernels for 17% -> 15%
where the time goes in v3:
time: 251 us; the launch traced here: 249 us
  waiting for transfers between devices  78.1 us (31%)
  starting transfers between devices  60.7 us (24%)
  Pallas kernels  43.6 us (17%)
  matrix products  28.5 us (11%)
  local copies, waits for them, and re-layouts  21 us (8%)
  other arithmetic  15.6 us (6%)
    ppermute x28, waiting for transfers between devices, shift(): lax.ppermute(block, axis, [(i, (i + step) % size) for i in range(size)])  54.1 us
    dot_general x15, matrix products, mm(): lax.dot_general(a, b, (dims, ((), ())), preferred_element_type=jnp.float32)  28.5 us
    ppermute x28, starting transfers between devices, shift(): lax.ppermute(block, axis, [(i, (i + step) % size) for i in range(size)])  23.7 us
    all_to_all x4, starting transfers between devices, gather_line(): return lax.all_to_all(copies, 'ctx', 0, 0).reshape(-1, block.shape[1])  18.8 us
    all_to_all x4, starting transfers between devices, scatter_line(): return lax.all_to_all(blocks, 'ctx', 0, 0)  18.2 us
    all_to_all x4, waiting for transfers between devices, scatter_line(): return lax.all_to_all(blocks, 'ctx', 0, 0)  16.7 us
    pallas_call x5, Pallas kernels, project_rows(): pl.pallas_call(functools.partial(project_kernel, counts=[len(slab) for sl...  12.6 us
    unnamed x87, local copies, waits for them, and re-layouts  9.53 us
  transfers between devices with their start and end apart: 36, of which 20 were waited for; matrix products, arithmetic and copies ran while one was open for 20% of the time, Pallas kernels for 15%

profile of v3, /device:TPU:0, one launch (start us, length us, event | category | flops | bytes accessed | tf_op | source)
XLA Modules:
  0.0 248.8 jit_solution(18288590460301966758)
XLA Ops:
  3.4 6.3 %all-to-all-start = ((bf16[4,256,256]{2,1,0:T(8,128)(2,1)}), bf16[4,256,256]{2,1,0:T(8,128)(2,1)S(1)}, u32[]{:S(2)}, u32[]{:S(2)}) async-start(bf16[4,256,256]{2,1,0:T(8,128)(2,1)} %broadcast_in_dim.58), calls=%async_computation | async-start | bytes 1048576 | tf_op jit(solution)/shard_map/all_to_all | solution.py:50
  11.0 5.8 %pick_columns.1 = (bf16[256,4096]{1,0:T(8,128)(2,1)}, bf16[256,4096]{1,0:T(8,128)(2,1)}) custom-call(s32[4]{0:T(128)} %fusion.26.slab_ref.refs_0_, s32[2,4]{1,0:T(2,128)} %pad_add_fusion.piece_ref.refs_1_, bf16[256,8192]{1,0:T(8,128)(2,1)} %bitcast.40), custom_call_target="tpu_custom_call" | custom-call | bytes 8388608 | tf_op jit(solution)/shard_map/pick_columns/pallas_call | solution.py:211
  16.9 7.3 %all-to-all-done = bf16[4,256,256]{2,1,0:T(8,128)(2,1)S(1)} async-done(((bf16[4,256,256]{2,1,0:T(8,128)(2,1)}), bf16[4,256,256]{2,1,0:T(8,128)(2,1)S(1)}, u32[]{:S(2)}, u32[]{:S(2)}) %all-to-all-start) | async-done | bytes 524320 | tf_op jit(solution)/shard_map/all_to_all | solution.py:50
  25.1 3.5 %all-to-all-start.1 = ((bf16[4,256,256]{2,1,0:T(8,128)(2,1)}), bf16[4,256,256]{2,1,0:T(8,128)(2,1)S(1)}, u32[]{:S(2)}, u32[]{:S(2)}) async-start(bf16[4,256,256]{2,1,0:T(8,128)(2,1)} %broadcast_in_dim.59), calls=%async_computation.1 | async-start | bytes 1048576 | tf_op jit(solution)/shard_map/all_to_all | solution.py:50
  28.6 1.6 collective-permute-start.2
  30.2 1.5 collective-permute-start.1
  31.7 11.3 %collective-permute-done.2.refs_9_.refs_13_.refs_15_ = bf16[1024,256]{1,0:T(8,128)(2,1)S(1)} collective-permute-done((bf16[1024,256]{1,0:T(8,128)(2,1)S(1)}, bf16[1024,256]{1,0:T(8,128)(2,1)S(1)}, u32[]{:S(2)}, u32[]{:S(2)}) %collective-permute-start.2) | collective-permute-done | bytes 524320 | tf_op jit(solution)/shard_map/ppermute | solution.py:29
  45.1 4.7 %all-to-all-start.2 = ((bf16[4,256,256]{2,1,0:T(8,128)(2,1)}), bf16[4,256,256]{2,1,0:T(8,128)(2,1)S(1)}, u32[]{:S(2)}, u32[]{:S(2)}) async-start(bf16[4,256,256]{2,1,0:T(8,128)(2,1)} %broadcast_in_dim.61), calls=%async_computation.2 | async-start | bytes 1048576 | tf_op jit(solution)/shard_map/all_to_all | solution.py:50
  50.8 1.5 collective-permute-start.5
  52.4 10.3 %collective-permute-done.3.refs_11_.refs_15_.refs_17_ = bf16[1024,256]{1,0:T(8,128)(2,1)} collective-permute-done((bf16[1024,256]{1,0:T(8,128)(2,1)}, bf16[1024,256]{1,0:T(8,128)(2,1)}, u32[]{:S(2)}, u32[]{:S(2)}) %collective-permute-start.3) | collective-permute-done | bytes 524320 | tf_op jit(solution)/shard_map/ppermute | solution.py:29
  63.6 1.3 collective-permute-start.7
  64.9 1.5 collective-permute-start.6
  68.5 3.1 %project_rows.5 = (f32[256,256]{1,0:T(8,128)S(1)}, f32[256,256]{1,0:T(8,128)S(1)}) custom-call(bf16[256,4096]{1,0:T(8,128)(2,1)S(1)} %copy-done, bf16[256,4096]{1,0:T(8,128)(2,1)} %collective-permute-done.refs_1_.refs_3_.refs_5_.refs_7_, bf16[256,4096]{1,0:T(8,128)(2,1)S(1)} %copy-done, ...), custom_call_target="tpu_custom_call" | custom-call | flops 1073741824 | bytes 6291456 | tf_op jit(solution)/shard_map/project_rows/pallas_call | solution.py:312
  71.8 1.3 negate_select_fusion
  74.0 1.9 finish_keys.1
  77.6 1.7 broadcast_in_dim.64
  79.3 4.3 %all-to-all-start.3 = ((bf16[4,256,256]{2,1,0:T(8,128)(2,1)}), bf16[4,256,256]{2,1,0:T(8,128)(2,1)}, u32[]{:S(2)}, u32[]{:S(2)}) async-start(bf16[4,256,256]{2,1,0:T(8,128)(2,1)} %broadcast_in_dim.64), calls=%async_computation.3 | async-start | bytes 1048576 | tf_op jit(solution)/shard_map/all_to_all | solution.py:50
  83.7 1.6 collective-permute-start.8
  85.9 1.7 fusion.32
  88.3 2.7 %project_rows.6 = (f32[256,256]{1,0:T(8,128)S(1)}, f32[256,256]{1,0:T(8,128)S(1)}) custom-call(bf16[256,4096]{1,0:T(8,128)(2,1)S(1)} %copy-done, bf16[256,4096]{1,0:T(8,128)(2,1)} %collective-permute-done.refs_1_.refs_3_.refs_5_.refs_7_, bf16[256,4096]{1,0:T(8,128)(2,1)S(1)} %copy-done, ...), custom_call_target="tpu_custom_call" | custom-call | flops 805306368 | bytes 4718592 | tf_op jit(solution)/shard_map/project_rows/pallas_call | solution.py:312
  91.0 5.4 %collective-permute-done.8.refs_2_.refs_6_.refs_8_ = bf16[1024,256]{1,0:T(8,128)(2,1)} collective-permute-done((bf16[1024,256]{1,0:T(8,128)(2,1)}, bf16[1024,256]{1,0:T(8,128)(2,1)}, u32[]{:S(2)}, u32[]{:S(2)}) %collective-permute-start.8) | collective-permute-done | bytes 524320 | tf_op jit(solution)/shard_map/ppermute | solution.py:29
  96.5 2.4 project_rows.7
  105.9 3.7 %attend.2 = (bf16[256,256]{1,0:T(8,128)(2,1)S(1)}, bf16[256,256]{1,0:T(8,128)(2,1)S(1)}, f32[1024,256]{1,0:T(8,128)S(1)}) custom-call(f32[256,256]{1,0:T(8,128)S(1)} %copy-done.32, f32[256,256]{1,0:T(8,128)} %collective-permute-done.9.refs_1_, bf16[256,256]{1,0:T(8,128)(2,1)S(1)} %copy-done.27, f32[256,128]{1,0:T(8,128)S(1)} %copy-done.10, ...), custom_call_target="tpu_custom_call" | custom-call | flops 939524096 | bytes 2097152 | tf_op jit(solution)/shard_map/attend/pallas_call | solution.py:375
  110.3 2.7 %project_rows.8 = (f32[256,256]{1,0:T(8,128)S(1)}, f32[256,256]{1,0:T(8,128)S(1)}) custom-call(bf16[256,4096]{1,0:T(8,128)(2,1)S(1)} %copy-done, bf16[256,4096]{1,0:T(8,128)(2,1)} %collective-permute-done.refs_1_.refs_3_.refs_5_.refs_7_, bf16[256,4096]{1,0:T(8,128)(2,1)S(1)} %copy-done, ...), custom_call_target="tpu_custom_call" | custom-call | flops 805306368 | bytes 4718592 | tf_op jit(solution)/shard_map/project_rows/pallas_call | solution.py:312
  113.1 1.7 project_rows.9
  115.3 1.8 constant_dynamic-update-slice_fusion
  117.3 5.1 %attend.3 = (bf16[256,256]{1,0:T(8,128)(2,1)S(1)}, bf16[256,256]{1,0:T(8,128)(2,1)S(1)}, bf16[1024,256]{1,0:T(8,128)(2,1)}) custom-call(f32[256,256]{1,0:T(8,128)S(1)} %get-tuple-element.85.refs_0_, f32[256,256]{1,0:T(8,128)S(1)} %collective-permute-done.13.refs_1_, bf16[256,256]{1,0:T(8,128)(2,1)S(1)} %copy-done.26, f32[256,128]{1,0:T(8,128)S(1)} %copy-done.11, ...), custom_call_target="tpu_custom_call" | custom-call | flops 939524096 | bytes 2097152 | tf_op jit(solution)/shard_map/attend/pallas_call | solution.py:375
  122.4 1.3 convolution_convert_fusion.2
  123.7 1.4 collective-permute-start.16
  125.1 1.3 convolution_convert_fusion.3
  126.5 4.5 %all-to-all-start.4 = ((bf16[4,256,256]{2,1,0:T(8,128)(2,1)}), bf16[4,256,256]{2,1,0:T(8,128)(2,1)S(1)}, u32[]{:S(2)}, u32[]{:S(2)}) async-start(bf16[4,256,256]{2,1,0:T(8,128)(2,1)} %bitcast.9), calls=%async_computation.4 | async-start | bytes 1048576 | tf_op jit(solution)/shard_map/all_to_all | solution.py:56
  131.0 2.5 %convolution_convert_fusion.1 = bf16[1024,256]{1,0:T(8,128)(2,1)} fusion(bf16[512,256]{1,0:T(8,128)(2,1)S(1)} %constant_dynamic-update-slice_fusion.4, bf16[512,4096]{1,0:T(8,128)(2,1)} %copy-done.35), kind=kOutput, calls=%fused_computation.9 | convolution fusion | flops 268697600 | bytes 1835008 | tf_op jit(solution)/shard_map/dot_general | solution.py:24
  134.8 3.4 %collective-permute-done.16 = bf16[1024,256]{1,0:T(8,128)(2,1)S(1)} collective-permute-done((bf16[1024,256]{1,0:T(8,128)(2,1)}, bf16[1024,256]{1,0:T(8,128)(2,1)S(1)}, u32[]{:S(2)}, u32[]{:S(2)}) %collective-permute-start.16) | collective-permute-done | bytes 524320 | tf_op jit(solution)/shard_map/ppermute | solution.py:29
  138.2 2.5 %fusion.3 = bf16[1024,256]{1,0:T(8,128)(2,1)} fusion(bf16[512,256]{1,0:T(8,128)(2,1)S(1)} %constant_dynamic-update-slice_fusion.4, bf16[1024,256]{1,0:T(8,128)(2,1)S(1)} %collective-permute-done.16, bf16[512,4096]{1,0:T(8,128)(2,1)} %copy-done.35), kind=kOutput, calls=%fused_computation.12 | convolution fusion | flops 269221888 | bytes 2359296 | tf_op jit(solution)/shard_map/dot_general | solution.py:24
  140.7 2.5 %convolution_convert_fusion = bf16[1024,256]{1,0:T(8,128)(2,1)} fusion(bf16[512,256]{1,0:T(8,128)(2,1)S(1)} %constant_dynamic-update-slice_fusion.2, bf16[512,4096]{1,0:T(8,128)(2,1)} %copy-done.35), kind=kOutput, calls=%fused_computation.8 | convolution fusion | flops 268697600 | bytes 1835008 | tf_op jit(solution)/shard_map/dot_general | solution.py:24
  143.3 2.6 %all-to-all-done.4.pieces = bf16[4,256,256]{2,1,0:T(8,128)(2,1)S(1)} async-done(((bf16[4,256,256]{2,1,0:T(8,128)(2,1)}), bf16[4,256,256]{2,1,0:T(8,128)(2,1)S(1)}, u32[]{:S(2)}, u32[]{:S(2)}) %all-to-all-start.4) | async-done | bytes 524320 | tf_op jit(solution)/shard_map/all_to_all | solution.py:56
  145.9 1.6 collective-permute-done.17
  148.3 1.9 undo_keys.1.refs_4_
  150.3 2.8 %fusion.5 = bf16[1024,256]{1,0:T(8,128)(2,1)} fusion(bf16[512,256]{1,0:T(8,128)(2,1)S(1)} %constant_dynamic-update-slice_fusion.2, bf16[1024,256]{1,0:T(8,128)(2,1)} %copy-done.41, bf16[512,4096]{1,0:T(8,128)(2,1)} %copy-done.35), kind=kOutput, calls=%fused_computation.14 | convolution fusion | flops 269221888 | bytes 2359296 | tf_op jit(solution)/shard_map/dot_general | solution.py:24
  155.6 1.4 convolution_convert_fusion.7
  157.9 1.4 convolution_convert_fusion.6
  162.3 12.1 %collective-permute-done.19 = bf16[512,256]{1,0:T(8,128)(2,1)} collective-permute-done((bf16[512,256]{1,0:T(8,128)(2,1)S(1)}, bf16[512,256]{1,0:T(8,128)(2,1)}, u32[]{:S(2)}, u32[]{:S(2)}) %collective-permute-start.19) | collective-permute-done | bytes 262176 | tf_op jit(solution)/shard_map/ppermute | solution.py:29
  174.4 5.2 %grad_columns.1 = bf16[256,4096]{1,0:T(8,128)(2,1)} custom-call(bf16[256,256]{1,0:T(8,128)(2,1)S(1)} %copy-done.18, bf16[256,256]{1,0:T(8,128)(2,1)S(1)} %collective-permute-done.14.refs_1_, bf16[256,256]{1,0:T(8,128)(2,1)S(1)} %collective-permute-done.18.refs_2_, bf16[1024,256]{1,0:T(8,128)(2,1)S(1)} %bitcast.26, ...), custom_call_target="tpu_custom_call" | custom-call | flops 1610612736 | bytes 8388608 | tf_op jit(solution)/shard_map/grad_columns/pallas_call | solution.py:233
  181.4 1.3 fusion.4
  182.7 4.6 %all-to-all-start.5 = ((bf16[4,256,256]{2,1,0:T(8,128)(2,1)}), bf16[4,256,256]{2,1,0:T(8,128)(2,1)S(1)}, u32[]{:S(2)}, u32[]{:S(2)}) async-start(bf16[4,256,256]{2,1,0:T(8,128)(2,1)} %bitcast.43), calls=%async_computation.5 | async-start | bytes 1048576 | tf_op jit(solution)/shard_map/all_to_all | solution.py:56
  187.3 1.5 fusion.8
  188.8 1.8 pad_maximum_fusion
  190.6 2.2 fusion.9
  192.8 1.5 collective-permute-done.25
  195.2 2.8 %fusion.6 = bf16[1024,256]{1,0:T(8,128)(2,1)} fusion(bf16[512,256]{1,0:T(8,128)(2,1)S(1)} %copy-done.40, bf16[1024,256]{1,0:T(8,128)(2,1)} %collective-permute-done.25, bf16[1024,256]{1,0:T(8,128)(2,1)} %collective-permute-done.24, bf16[512,4096]{1,0:T(8,128)(2,1)} %copy-done.35), kind=kOutput, calls=%fused_computation.15 | convolution fusion | flops 269746176 | bytes 2883584 | tf_op jit(solution)/shard_map/dot_general | solution.py:24
  198.0 3.9 %all-to-all-done.5 = bf16[4,256,256]{2,1,0:T(8,128)(2,1)S(1)} async-done(((bf16[4,256,256]{2,1,0:T(8,128)(2,1)}), bf16[4,256,256]{2,1,0:T(8,128)(2,1)S(1)}, u32[]{:S(2)}, u32[]{:S(2)}) %all-to-all-start.5) | async-done | bytes 524320 | tf_op jit(solution)/shard_map/all_to_all | solution.py:56
  202.7 4.3 %all-to-all-start.6 = ((bf16[4,256,256]{2,1,0:T(8,128)(2,1)}), bf16[4,256,256]{2,1,0:T(8,128)(2,1)}, u32[]{:S(2)}, u32[]{:S(2)}) async-start(bf16[4,256,256]{2,1,0:T(8,128)(2,1)} %bitcast.44), calls=%async_computation.6 | async-start | bytes 1048576 | tf_op jit(solution)/shard_map/all_to_all | solution.py:56
  207.0 1.9 pad_maximum_fusion.1
  208.8 1.9 convert_reduce_fusion.2
  210.7 1.5 collective-permute-start.26
  213.1 7.9 %all-to-all-done.6 = bf16[4,256,256]{2,1,0:T(8,128)(2,1)} async-done(((bf16[4,256,256]{2,1,0:T(8,128)(2,1)}), bf16[4,256,256]{2,1,0:T(8,128)(2,1)}, u32[]{:S(2)}, u32[]{:S(2)}) %all-to-all-start.6) | async-done | bytes 524320 | tf_op jit(solution)/shard_map/all_to_all | solution.py:56
  221.0 2.9 %collective-permute-done.26 = bf16[1024,256]{1,0:T(8,128)(2,1)} collective-permute-done((bf16[1024,256]{1,0:T(8,128)(2,1)}, bf16[1024,256]{1,0:T(8,128)(2,1)}, u32[]{:S(2)}, u32[]{:S(2)}) %collective-permute-start.26) | collective-permute-done | bytes 524320 | tf_op jit(solution)/shard_map/ppermute | solution.py:29
  223.9 1.2 collective-permute-done.27
  225.2 1.8 convert_reduce_fusion.1
  227.0 2.8 %fusion.7 = bf16[1024,256]{1,0:T(8,128)(2,1)} fusion(bf16[1024,256]{1,0:T(8,128)(2,1)} %collective-permute-done.27, bf16[1024,256]{1,0:T(8,128)(2,1)} %collective-permute-done.26, bf16[512,4096]{1,0:T(8,128)(2,1)} %copy-done.35, bf16[256,256]{1,0:T(8,128)(2,1)S(1)} %collective-permute-done.18.refs_2_, bf16[256,256]{1,0:T(8,128)(2,1)S(1)} %copy-done.12), kind=kOutput, calls=%fused_computation.16 | convolution fusion | flops 270270464 | bytes 2883584 | tf_op jit(solution)/shard_map/dot_general | solution.py:24
  229.8 4.8 %all-to-all-start.7 = ((bf16[4,256,256]{2,1,0:T(8,128)(2,1)}), bf16[4,256,256]{2,1,0:T(8,128)(2,1)}, u32[]{:S(2)}, u32[]{:S(2)}) async-start(bf16[4,256,256]{2,1,0:T(8,128)(2,1)} %bitcast.42), calls=%async_computation.7 | async-start | bytes 1048576 | tf_op jit(solution)/shard_map/all_to_all | solution.py:56
  235.3 1.9 pad_maximum_fusion.2
  237.2 7.4 %grad_place.1 = bf16[256,8192]{1,0:T(8,128)(2,1)} custom-call(s32[4]{0:T(128)S(1)} %copy-done.29, s32[2,4]{1,0:T(2,128)S(1)} %copy-done.28, bf16[256,256]{1,0:T(8,128)(2,1)S(1)} %copy-done.14, bf16[256,256]{1,0:T(8,128)(2,1)S(1)} %copy-done.16, bf16[256,256]{1,0:T(8,128)(2,1)S(1)} %copy-done.12, bf16[1024,256]{1,0:T(8,128)(2,1)S(1)} %bitcast.27, ...), custom_call_target="tpu_custom_call" | custom-call | flops 1610612736 | bytes 12582912 | tf_op jit(solution)/shard_map/grad_place/pallas_call | solution.py:257
  244.6 2.3 all-to-all-done.7
  (160 shorter events, 39.1 us)
Async XLA Ops:
  0.6 23.6 %copy-start.37 = (f32[256,512]{1,0:T(8,128)S(1)}, f32[256,512]{1,0:T(8,128)}, u32[]{:S(2)}) copy-start(f32[256,512]{1,0:T(8,128)} %param.8) | copy-start | bytes 1572868
  3.4 20.8 %all-to-all-start = ((bf16[4,256,256]{2,1,0:T(8,128)(2,1)}), bf16[4,256,256]{2,1,0:T(8,128)(2,1)S(1)}, u32[]{:S(2)}, u32[]{:S(2)}) async-start(bf16[4,256,256]{2,1,0:T(8,128)(2,1)} %broadcast_in_dim.58), calls=%async_computation | async-start | bytes 1048576 | tf_op jit(solution)/shard_map/all_to_all | solution.py:50
  11.0 41.3 %copy-start.30 = (s32[1024]{0:T(1024)S(1)}, s32[1024]{0:T(1024)}, u32[]{:S(2)}) copy-start(s32[1024]{0:T(1024)} %param.7) | copy-start | bytes 12292
  16.9 49.5 %copy-start = (bf16[256,4096]{1,0:T(8,128)(2,1)S(1)}, bf16[256,4096]{1,0:T(8,128)(2,1)}, u32[]{:S(2)}) copy-start(bf16[256,4096]{1,0:T(8,128)(2,1)} %get-tuple-element.92.refs_0_.refs_2_.refs_4_.refs_6_) | copy-start | bytes 6291460
  24.2 20.9 %copy-start.1 = (bf16[4,256,256]{2,1,0:T(8,128)(2,1)}, bf16[4,256,256]{2,1,0:T(8,128)(2,1)S(1)}, u32[]{:S(2)}) copy-start(bf16[4,256,256]{2,1,0:T(8,128)(2,1)S(1)} %all-to-all-done) | copy-start | bytes 1572868
  24.2 42.2 %collective-permute-start = (bf16[256,4096]{1,0:T(8,128)(2,1)}, bf16[256,4096]{1,0:T(8,128)(2,1)}, u32[]{:S(2)}, u32[]{:S(2)}) collective-permute-start(bf16[256,4096]{1,0:T(8,128)(2,1)} %get-tuple-element.59), channel_id=1, source_target_pairs={{0,4},{4,0},{1,5},{5,1},{2,6},{6,2},{3,7},{7,3},{8,12},{12,8},{9,1... | collective-permute-start | bytes 6291464 | tf_op jit(solution)/shard_map/ppermute | solution.py:29
  25.1 19.1 %all-to-all-start.1 = ((bf16[4,256,256]{2,1,0:T(8,128)(2,1)}), bf16[4,256,256]{2,1,0:T(8,128)(2,1)S(1)}, u32[]{:S(2)}, u32[]{:S(2)}) async-start(bf16[4,256,256]{2,1,0:T(8,128)(2,1)} %broadcast_in_dim.59), calls=%async_computation.1 | async-start | bytes 1048576 | tf_op jit(solution)/shard_map/all_to_all | solution.py:50
  28.6 14.3 %collective-permute-start.2 = (bf16[1024,256]{1,0:T(8,128)(2,1)S(1)}, bf16[1024,256]{1,0:T(8,128)(2,1)S(1)}, u32[]{:S(2)}, u32[]{:S(2)}) collective-permute-start(bf16[1024,256]{1,0:T(8,128)(2,1)S(1)} %bitcast.33), channel_id=1, source_target_pairs={{0,8},{8,0},{1,9},{9,1},{2,10},{10,2},{3,11},{11,3},{4,12},{12,4},... | collective-permute-start | bytes 1572872 | tf_op jit(solution)/shard_map/ppermute | solution.py:29
  30.2 14.1 %collective-permute-start.1 = (bf16[1024,256]{1,0:T(8,128)(2,1)S(1)}, bf16[1024,256]{1,0:T(8,128)(2,1)}, u32[]{:S(2)}, u32[]{:S(2)}) collective-permute-start(bf16[1024,256]{1,0:T(8,128)(2,1)S(1)} %bitcast.34), channel_id=1, source_target_pairs={{0,16},{16,0},{1,17},{17,1},{2,18},{18,2},{3,19},{19,3},{4,20},{20... | collective-permute-start | bytes 1572872 | tf_op jit(solution)/shard_map/ppermute | solution.py:29
  45.1 18.5 %all-to-all-start.2 = ((bf16[4,256,256]{2,1,0:T(8,128)(2,1)}), bf16[4,256,256]{2,1,0:T(8,128)(2,1)S(1)}, u32[]{:S(2)}, u32[]{:S(2)}) async-start(bf16[4,256,256]{2,1,0:T(8,128)(2,1)} %broadcast_in_dim.61), calls=%async_computation.2 | async-start | bytes 1048576 | tf_op jit(solution)/shard_map/all_to_all | solution.py:50
  49.8 12.9 %collective-permute-start.3 = (bf16[1024,256]{1,0:T(8,128)(2,1)}, bf16[1024,256]{1,0:T(8,128)(2,1)}, u32[]{:S(2)}, u32[]{:S(2)}) collective-permute-start(bf16[1024,256]{1,0:T(8,128)(2,1)} %collective-permute-done.1.refs_10_.refs_14_.refs_16_), channel_id=1, source_target_pairs={{0,8},{8,0},{1,9},{9,1},{2,10},{10,2},{3,11},{11,3},{4,12},{12,4},... | collective-permute-start | bytes 1572872 | tf_op jit(solution)/shard_map/ppermute | solution.py:29
  50.8 12.8 %collective-permute-start.5 = (bf16[1024,256]{1,0:T(8,128)(2,1)S(1)}, bf16[1024,256]{1,0:T(8,128)(2,1)}, u32[]{:S(2)}, u32[]{:S(2)}) collective-permute-start(bf16[1024,256]{1,0:T(8,128)(2,1)S(1)} %bitcast.23), channel_id=1, source_target_pairs={{0,16},{16,0},{1,17},{17,1},{2,18},{18,2},{3,19},{19,3},{4,20},{20... | collective-permute-start | bytes 1572872 | tf_op jit(solution)/shard_map/ppermute | solution.py:29
  63.6 12.9 %collective-permute-start.7 = (bf16[1024,256]{1,0:T(8,128)(2,1)S(1)}, bf16[1024,256]{1,0:T(8,128)(2,1)}, u32[]{:S(2)}, u32[]{:S(2)}) collective-permute-start(bf16[1024,256]{1,0:T(8,128)(2,1)S(1)} %bitcast.24), channel_id=1, source_target_pairs={{0,8},{8,0},{1,9},{9,1},{2,10},{10,2},{3,11},{11,3},{4,12},{12,4},... | collective-permute-start | bytes 1572872 | tf_op jit(solution)/shard_map/ppermute | solution.py:29
  64.9 12.7 %collective-permute-start.6 = (bf16[1024,256]{1,0:T(8,128)(2,1)S(1)}, bf16[1024,256]{1,0:T(8,128)(2,1)}, u32[]{:S(2)}, u32[]{:S(2)}) collective-permute-start(bf16[1024,256]{1,0:T(8,128)(2,1)S(1)} %bitcast.28), channel_id=1, source_target_pairs={{0,16},{16,0},{1,17},{17,1},{2,18},{18,2},{3,19},{19,3},{4,20},{20... | collective-permute-start | bytes 1572872 | tf_op jit(solution)/shard_map/ppermute | solution.py:29
  71.7 1.6 collective-permute-start.4
  79.3 20.2 %all-to-all-start.3 = ((bf16[4,256,256]{2,1,0:T(8,128)(2,1)}), bf16[4,256,256]{2,1,0:T(8,128)(2,1)}, u32[]{:S(2)}, u32[]{:S(2)}) async-start(bf16[4,256,256]{2,1,0:T(8,128)(2,1)} %broadcast_in_dim.64), calls=%async_computation.3 | async-start | bytes 1048576 | tf_op jit(solution)/shard_map/all_to_all | solution.py:50
  83.7 12.8 %collective-permute-start.8 = (bf16[1024,256]{1,0:T(8,128)(2,1)}, bf16[1024,256]{1,0:T(8,128)(2,1)}, u32[]{:S(2)}, u32[]{:S(2)}) collective-permute-start(bf16[1024,256]{1,0:T(8,128)(2,1)} %collective-permute-done.7.refs_7_.refs_4_.refs_6_), channel_id=1, source_target_pairs={{0,16},{16,0},{1,17},{17,1},{2,18},{18,2},{3,19},{19,3},{4,20},{20... | collective-permute-start | bytes 1572872 | tf_op jit(solution)/shard_map/ppermute | solution.py:29
  85.2 14.3 %collective-permute-start.10 = (bf16[1024,256]{1,0:T(8,128)(2,1)S(1)}, bf16[1024,256]{1,0:T(8,128)(2,1)}, u32[]{:S(2)}, u32[]{:S(2)}) collective-permute-start(bf16[1024,256]{1,0:T(8,128)(2,1)S(1)} %bitcast.29), channel_id=1, source_target_pairs={{0,8},{8,0},{1,9},{9,1},{2,10},{10,2},{3,11},{11,3},{4,12},{12,4},... | collective-permute-start | bytes 1572872 | tf_op jit(solution)/shard_map/ppermute | solution.py:29
  96.4 6.7 %copy-start.9 = (f32[256,128]{1,0:T(8,128)S(1)}, f32[256,128]{1,0:T(8,128)}, u32[]{:S(2)}) copy-start(f32[256,128]{1,0:T(8,128)} %get-tuple-element.115.sin_ref.refs_4_) | copy-start | bytes 393220
  99.6 3.6 %collective-permute-start.9 = (f32[256,256]{1,0:T(8,128)}, f32[256,256]{1,0:T(8,128)}, u32[]{:S(2)}, u32[]{:S(2)}) collective-permute-start(f32[256,256]{1,0:T(8,128)} %get-tuple-element.75), channel_id=1, source_target_pairs={{0,4},{4,0},{1,5},{5,1},{2,6},{6,2},{3,7},{7,3},{8,12},{12,8},{9,1... | collective-permute-start | bytes 786440 | tf_op jit(solution)/shard_map/ppermute | solution.py:29
  99.6 3.6 %copy-start.32 = (f32[256,256]{1,0:T(8,128)S(1)}, f32[256,256]{1,0:T(8,128)}, u32[]{:S(2)}) copy-start(f32[256,256]{1,0:T(8,128)} %copy-done.31) | copy-start | bytes 786436
  101.6 11.4 %collective-permute-start.12 = (bf16[512,256]{1,0:T(8,128)(2,1)S(1)}, bf16[512,256]{1,0:T(8,128)(2,1)S(1)}, u32[]{:S(2)}, u32[]{:S(2)}) collective-permute-start(bf16[512,256]{1,0:T(8,128)(2,1)S(1)} %slice.65), channel_id=1, source_target_pairs={{0,16},{16,0},{1,17},{17,1},{2,18},{18,2},{3,19},{19,3},{4,20},{20... | collective-permute-start | bytes 786440 | tf_op jit(solution)/shard_map/ppermute | solution.py:29
  102.4 10.6 %collective-permute-start.11 = (bf16[512,256]{1,0:T(8,128)(2,1)S(1)}, bf16[512,256]{1,0:T(8,128)(2,1)S(1)}, u32[]{:S(2)}, u32[]{:S(2)}) collective-permute-start(bf16[512,256]{1,0:T(8,128)(2,1)S(1)} %slice.64), channel_id=1, source_target_pairs={{0,8},{8,0},{1,9},{9,1},{2,10},{10,2},{3,11},{11,3},{4,12},{12,4},... | collective-permute-start | bytes 786440 | tf_op jit(solution)/shard_map/ppermute | solution.py:29
  110.3 6.9 %copy-start.13 = (bf16[256,256]{1,0:T(8,128)(2,1)}, bf16[256,256]{1,0:T(8,128)(2,1)S(1)}, u32[]{:S(2)}) copy-start(bf16[256,256]{1,0:T(8,128)(2,1)S(1)} %get-tuple-element.89.refs_2_) | copy-start | bytes 393220
  110.3 6.9 %collective-permute-start.15 = (bf16[256,256]{1,0:T(8,128)(2,1)S(1)}, bf16[256,256]{1,0:T(8,128)(2,1)S(1)}, u32[]{:S(2)}, u32[]{:S(2)}) collective-permute-start(bf16[256,256]{1,0:T(8,128)(2,1)S(1)} %get-tuple-element.89.refs_2_), channel_id=1, source_target_pairs={{0,4},{4,0},{1,5},{5,1},{2,6},{6,2},{3,7},{7,3},{8,12},{12,8},{9,1... | collective-permute-start | bytes 393224 | tf_op jit(solution)/shard_map/ppermute | solution.py:29
  113.0 4.1 %copy-start.7 = (bf16[512,256]{1,0:T(8,128)(2,1)}, bf16[512,256]{1,0:T(8,128)(2,1)S(1)}, u32[]{:S(2)}) copy-start(bf16[512,256]{1,0:T(8,128)(2,1)S(1)} %collective-permute-done.11.refs_2_.refs_10_.refs_12_) | copy-start | bytes 786436
  113.0 4.2 %copy-start.11 = (f32[256,128]{1,0:T(8,128)S(1)}, f32[256,128]{1,0:T(8,128)}, u32[]{:S(2)}) copy-start(f32[256,128]{1,0:T(8,128)} %get-tuple-element.116.cos_ref.refs_3_) | copy-start | bytes 393220
  113.1 4.2 %copy-start.21 = (s32[256,1]{1,0:T(8,128)S(1)}, s32[256,1]{1,0:T(8,128)}, u32[]{:S(2)}) copy-start(s32[256,1]{1,0:T(8,128)} %copy.11.refs_5_) | copy-start | bytes 3076
  113.1 4.2 %copy-start.26 = (bf16[256,256]{1,0:T(8,128)(2,1)S(1)}, bf16[256,256]{1,0:T(8,128)(2,1)}, u32[]{:S(2)}) copy-start(bf16[256,256]{1,0:T(8,128)(2,1)} %get-tuple-element.112.refs_2_) | copy-start | bytes 393220
  114.8 2.5 collective-permute-start.13
  117.2 9.3 %copy-start.35 = (bf16[512,4096]{1,0:T(8,128)(2,1)}, bf16[512,4096]{1,0:T(8,128)(2,1)S(1)}, u32[]{:S(2)}) copy-start(bf16[512,4096]{1,0:T(8,128)(2,1)S(1)} %constant_dynamic-update-slice_fusion) | copy-start | bytes 12582916
  117.2 9.3 %copy-start.17 = (bf16[256,256]{1,0:T(8,128)(2,1)}, bf16[256,256]{1,0:T(8,128)(2,1)S(1)}, u32[]{:S(2)}) copy-start(bf16[256,256]{1,0:T(8,128)(2,1)S(1)} %collective-permute-done.15.refs_0_) | copy-start | bytes 393220
  122.3 4.1 %copy-start.24 = (bf16[256,256]{1,0:T(8,128)(2,1)}, bf16[256,256]{1,0:T(8,128)(2,1)S(1)}, u32[]{:S(2)}) copy-start(bf16[256,256]{1,0:T(8,128)(2,1)S(1)} %get-tuple-element.88) | copy-start | bytes 393220
  122.3 2.8 %collective-permute-start.14 = (bf16[256,256]{1,0:T(8,128)(2,1)S(1)}, bf16[256,256]{1,0:T(8,128)(2,1)S(1)}, u32[]{:S(2)}, u32[]{:S(2)}) collective-permute-start(bf16[256,256]{1,0:T(8,128)(2,1)S(1)} %get-tuple-element.90.refs_3_), channel_id=1, source_target_pairs={{0,4},{4,0},{1,5},{5,1},{2,6},{6,2},{3,7},{7,3},{8,12},{12,8},{9,1... | collective-permute-start | bytes 393224 | tf_op jit(solution)/shard_map/ppermute | solution.py:29
  123.7 14.5 %collective-permute-start.16 = (bf16[1024,256]{1,0:T(8,128)(2,1)}, bf16[1024,256]{1,0:T(8,128)(2,1)S(1)}, u32[]{:S(2)}, u32[]{:S(2)}) collective-permute-start(bf16[1024,256]{1,0:T(8,128)(2,1)} %convolution_convert_fusion.2), channel_id=1, source_target_pairs={{0,8},{8,0},{1,9},{9,1},{2,10},{10,2},{3,11},{11,3},{4,12},{12,4},... | collective-permute-start | bytes 1572872 | tf_op jit(solution)/shard_map/ppermute | solution.py:29
  125.1 25.2 %copy-start.39 = (bf16[512,256]{1,0:T(8,128)(2,1)}, bf16[512,256]{1,0:T(8,128)(2,1)S(1)}, u32[]{:S(2)}) copy-start(bf16[512,256]{1,0:T(8,128)(2,1)S(1)} %constant_dynamic-update-slice_fusion.2) | copy-start | bytes 786436
  126.5 19.4 %all-to-all-start.4 = ((bf16[4,256,256]{2,1,0:T(8,128)(2,1)}), bf16[4,256,256]{2,1,0:T(8,128)(2,1)S(1)}, u32[]{:S(2)}, u32[]{:S(2)}) async-start(bf16[4,256,256]{2,1,0:T(8,128)(2,1)} %bitcast.9), calls=%async_computation.4 | async-start | bytes 1048576 | tf_op jit(solution)/shard_map/all_to_all | solution.py:56
  133.5 14.0 %collective-permute-start.17 = (bf16[1024,256]{1,0:T(8,128)(2,1)}, bf16[1024,256]{1,0:T(8,128)(2,1)S(1)}, u32[]{:S(2)}, u32[]{:S(2)}) collective-permute-start(bf16[1024,256]{1,0:T(8,128)(2,1)} %convolution_convert_fusion.3), channel_id=1, source_target_pairs={{0,16},{16,0},{1,17},{17,1},{2,18},{18,2},{3,19},{19,3},{4,20},{20... | collective-permute-start | bytes 1572872 | tf_op jit(solution)/shard_map/ppermute | solution.py:29
  150.2 7.7 %copy-start.12 = (bf16[256,256]{1,0:T(8,128)(2,1)S(1)}, bf16[256,256]{1,0:T(8,128)(2,1)}, u32[]{:S(2)}) copy-start(bf16[256,256]{1,0:T(8,128)(2,1)} %undo_keys.1.refs_4_) | copy-start | bytes 393220
  150.2 9.9 %copy-start.36 = (bf16[512,4096]{1,0:T(8,128)(2,1)S(1)}, bf16[512,4096]{1,0:T(8,128)(2,1)}, u32[]{:S(2)}) copy-start(bf16[512,4096]{1,0:T(8,128)(2,1)} %copy-done.35) | copy-start | bytes 12582916
  150.2 24.2 %copy-start.3 = (bf16[4,256,256]{2,1,0:T(8,128)(2,1)S(1)}, bf16[4,256,256]{2,1,0:T(8,128)(2,1)}, u32[]{:S(2)}) copy-start(bf16[4,256,256]{2,1,0:T(8,128)(2,1)} %copy-done.1) | copy-start | bytes 1572868
  150.2 24.2 %copy-start.6 = (bf16[1024,256]{1,0:T(8,128)(2,1)S(1)}, bf16[1024,256]{1,0:T(8,128)(2,1)}, u32[]{:S(2)}) copy-start(bf16[1024,256]{1,0:T(8,128)(2,1)} %copy-done.4) | copy-start | bytes 1572868
  150.2 24.2 %copy-start.8 = (bf16[512,256]{1,0:T(8,128)(2,1)S(1)}, bf16[512,256]{1,0:T(8,128)(2,1)}, u32[]{:S(2)}) copy-start(bf16[512,256]{1,0:T(8,128)(2,1)} %copy-done.7) | copy-start | bytes 786436
  150.2 24.2 %copy-start.18 = (bf16[256,256]{1,0:T(8,128)(2,1)S(1)}, bf16[256,256]{1,0:T(8,128)(2,1)}, u32[]{:S(2)}) copy-start(bf16[256,256]{1,0:T(8,128)(2,1)} %copy-done.17) | copy-start | bytes 393220
  150.3 5.3 %collective-permute-start.18 = (bf16[256,256]{1,0:T(8,128)(2,1)}, bf16[256,256]{1,0:T(8,128)(2,1)S(1)}, u32[]{:S(2)}, u32[]{:S(2)}) collective-permute-start(bf16[256,256]{1,0:T(8,128)(2,1)} %undo_keys.1.refs_4_), channel_id=1, source_target_pairs={{0,4},{4,0},{1,5},{5,1},{2,6},{6,2},{3,7},{7,3},{8,12},{12,8},{9,1... | collective-permute-start | bytes 393224 | tf_op jit(solution)/shard_map/ppermute | solution.py:29
  153.2 26.5 %collective-permute-start.22 = (bf16[1024,256]{1,0:T(8,128)(2,1)}, bf16[1024,256]{1,0:T(8,128)(2,1)S(1)}, u32[]{:S(2)}, u32[]{:S(2)}) collective-permute-start(bf16[1024,256]{1,0:T(8,128)(2,1)} %fusion.3), channel_id=1, source_target_pairs={{0,16},{16,0},{1,17},{17,1},{2,18},{18,2},{3,19},{19,3},{4,20},{20... | collective-permute-start | bytes 1572872 | tf_op jit(solution)/shard_map/ppermute | solution.py:29
  154.4 25.3 %collective-permute-start.23 = (bf16[1024,256]{1,0:T(8,128)(2,1)}, bf16[1024,256]{1,0:T(8,128)(2,1)S(1)}, u32[]{:S(2)}, u32[]{:S(2)}) collective-permute-start(bf16[1024,256]{1,0:T(8,128)(2,1)} %convolution_convert_fusion.1), channel_id=1, source_target_pairs={{0,8},{8,0},{1,9},{9,1},{2,10},{10,2},{3,11},{11,3},{4,12},{12,4},... | collective-permute-start | bytes 1572872 | tf_op jit(solution)/shard_map/ppermute | solution.py:29
  157.0 17.4 %collective-permute-start.19 = (bf16[512,256]{1,0:T(8,128)(2,1)S(1)}, bf16[512,256]{1,0:T(8,128)(2,1)}, u32[]{:S(2)}, u32[]{:S(2)}) collective-permute-start(bf16[512,256]{1,0:T(8,128)(2,1)S(1)} %convolution_convert_fusion.7), channel_id=1, source_target_pairs={{0,8},{8,0},{1,9},{9,1},{2,10},{10,2},{3,11},{11,3},{4,12},{12,4},... | collective-permute-start | bytes 786440 | tf_op jit(solution)/shard_map/ppermute | solution.py:29
  159.3 15.1 %collective-permute-start.20 = (bf16[512,256]{1,0:T(8,128)(2,1)S(1)}, bf16[512,256]{1,0:T(8,128)(2,1)}, u32[]{:S(2)}, u32[]{:S(2)}) collective-permute-start(bf16[512,256]{1,0:T(8,128)(2,1)S(1)} %convolution_convert_fusion.6), channel_id=1, source_target_pairs={{0,16},{16,0},{1,17},{17,1},{2,18},{18,2},{3,19},{19,3},{4,20},{20... | collective-permute-start | bytes 786440 | tf_op jit(solution)/shard_map/ppermute | solution.py:29
  179.6 57.6 %collective-permute-start.21 = (bf16[256,4096]{1,0:T(8,128)(2,1)}, bf16[256,4096]{1,0:T(8,128)(2,1)}, u32[]{:S(2)}, u32[]{:S(2)}) collective-permute-start(bf16[256,4096]{1,0:T(8,128)(2,1)} %grad_columns.1), channel_id=1, source_target_pairs={{0,4},{4,0},{1,5},{5,1},{2,6},{6,2},{3,7},{7,3},{8,12},{12,8},{9,1... | collective-permute-start | bytes 6291464 | tf_op jit(solution)/shard_map/ppermute | solution.py:29
  179.6 14.7 %collective-permute-start.25 = (bf16[1024,256]{1,0:T(8,128)(2,1)}, bf16[1024,256]{1,0:T(8,128)(2,1)}, u32[]{:S(2)}, u32[]{:S(2)}) collective-permute-start(bf16[1024,256]{1,0:T(8,128)(2,1)} %fusion.5), channel_id=1, source_target_pairs={{0,8},{8,0},{1,9},{9,1},{2,10},{10,2},{3,11},{11,3},{4,12},{12,4},... | collective-permute-start | bytes 1572872 | tf_op jit(solution)/shard_map/ppermute | solution.py:29
  180.9 14.3 %collective-permute-start.24 = (bf16[1024,256]{1,0:T(8,128)(2,1)}, bf16[1024,256]{1,0:T(8,128)(2,1)}, u32[]{:S(2)}, u32[]{:S(2)}) collective-permute-start(bf16[1024,256]{1,0:T(8,128)(2,1)} %convolution_convert_fusion), channel_id=1, source_target_pairs={{0,16},{16,0},{1,17},{17,1},{2,18},{18,2},{3,19},{19,3},{4,20},{20... | collective-permute-start | bytes 1572872 | tf_op jit(solution)/shard_map/ppermute | solution.py:29
  182.7 19.2 %all-to-all-start.5 = ((bf16[4,256,256]{2,1,0:T(8,128)(2,1)}), bf16[4,256,256]{2,1,0:T(8,128)(2,1)S(1)}, u32[]{:S(2)}, u32[]{:S(2)}) async-start(bf16[4,256,256]{2,1,0:T(8,128)(2,1)} %bitcast.43), calls=%async_computation.5 | async-start | bytes 1048576 | tf_op jit(solution)/shard_map/all_to_all | solution.py:56
  187.3 7.9 %copy-start.40 = (bf16[512,256]{1,0:T(8,128)(2,1)S(1)}, bf16[512,256]{1,0:T(8,128)(2,1)}, u32[]{:S(2)}) copy-start(bf16[512,256]{1,0:T(8,128)(2,1)} %copy-done.39) | copy-start | bytes 786436
  202.7 31.9 %copy-start.23 = (bf16[256,256]{1,0:T(8,128)(2,1)S(1)}, bf16[256,256]{1,0:T(8,128)(2,1)}, u32[]{:S(2)}) copy-start(bf16[256,256]{1,0:T(8,128)(2,1)} %copy-done.22) | copy-start | bytes 393220
  202.7 31.9 %copy-start.25 = (bf16[256,256]{1,0:T(8,128)(2,1)S(1)}, bf16[256,256]{1,0:T(8,128)(2,1)}, u32[]{:S(2)}) copy-start(bf16[256,256]{1,0:T(8,128)(2,1)} %copy-done.24) | copy-start | bytes 393220
  202.7 18.3 %all-to-all-start.6 = ((bf16[4,256,256]{2,1,0:T(8,128)(2,1)}), bf16[4,256,256]{2,1,0:T(8,128)(2,1)}, u32[]{:S(2)}, u32[]{:S(2)}) async-start(bf16[4,256,256]{2,1,0:T(8,128)(2,1)} %bitcast.44), calls=%async_computation.6 | async-start | bytes 1048576 | tf_op jit(solution)/shard_map/all_to_all | solution.py:56
  208.8 28.4 %copy-start.14 = (bf16[256,256]{1,0:T(8,128)(2,1)S(1)}, bf16[256,256]{1,0:T(8,128)(2,1)}, u32[]{:S(2)}) copy-start(bf16[256,256]{1,0:T(8,128)(2,1)} %copy-done.13) | copy-start | bytes 393220
  208.8 28.4 %copy-start.16 = (bf16[256,256]{1,0:T(8,128)(2,1)S(1)}, bf16[256,256]{1,0:T(8,128)(2,1)}, u32[]{:S(2)}) copy-start(bf16[256,256]{1,0:T(8,128)(2,1)} %copy-done.15) | copy-start | bytes 393220
  208.8 28.4 %copy-start.28 = (s32[2,4]{1,0:T(2,128)S(1)}, s32[2,4]{1,0:T(2,128)}, u32[]{:S(2)}) copy-start(s32[2,4]{1,0:T(2,128)} %pad_add_fusion.piece_ref.refs_1_) | copy-start | bytes 100
  208.8 28.4 %copy-start.29 = (s32[4]{0:T(128)S(1)}, s32[4]{0:T(128)}, u32[]{:S(2)}) copy-start(s32[4]{0:T(128)} %fusion.26.slab_ref.refs_0_) | copy-start | bytes 52
  210.7 13.2 %collective-permute-start.26 = (bf16[1024,256]{1,0:T(8,128)(2,1)}, bf16[1024,256]{1,0:T(8,128)(2,1)}, u32[]{:S(2)}, u32[]{:S(2)}) collective-permute-start(bf16[1024,256]{1,0:T(8,128)(2,1)} %pad_maximum_fusion), channel_id=1, source_target_pairs={{0,16},{16,0},{1,17},{17,1},{2,18},{18,2},{3,19},{19,3},{4,20},{20... | collective-permute-start | bytes 1572872 | tf_op jit(solution)/shard_map/ppermute | solution.py:29
  212.2 12.9 %collective-permute-start.27 = (bf16[1024,256]{1,0:T(8,128)(2,1)}, bf16[1024,256]{1,0:T(8,128)(2,1)}, u32[]{:S(2)}, u32[]{:S(2)}) collective-permute-start(bf16[1024,256]{1,0:T(8,128)(2,1)} %pad_maximum_fusion.1), channel_id=1, source_target_pairs={{0,8},{8,0},{1,9},{9,1},{2,10},{10,2},{3,11},{11,3},{4,12},{12,4},... | collective-permute-start | bytes 1572872 | tf_op jit(solution)/shard_map/ppermute | solution.py:29
  229.8 17.1 %all-to-all-start.7 = ((bf16[4,256,256]{2,1,0:T(8,128)(2,1)}), bf16[4,256,256]{2,1,0:T(8,128)(2,1)}, u32[]{:S(2)}, u32[]{:S(2)}) async-start(bf16[4,256,256]{2,1,0:T(8,128)(2,1)} %bitcast.42), calls=%async_computation.7 | async-start | bytes 1048576 | tf_op jit(solution)/shard_map/all_to_all | solution.py:56
  (14 other events, 16.0 us)

commit v4 on v2

--- a/solution.py
+++ b/solution.py
@@ -31,6 +31,10 @@
 
 def after(block, *others):
     return lax.optimization_barrier((block, *others))[0]
+
+
+def after_all(blocks, *others):
+    return [after(block, *others) for block in blocks]
 
 
 def swap(block):
@@ -70,21 +74,19 @@
     return slabs
 
 
-def reduce_corners(make, way, split, *deps):
+def reduce_corners(make, way, split):
     size_b = lax.axis_size("b")
     whole, top, low = slice(None), slice(0, split), slice(split, None)
-    came_a, came_b = {}, {}
+    came_a, came_b, went = {}, {}, []
     for da in range(1, lax.axis_size("a")):
         for db in range(1, size_b):
             i = da * size_b + db
-            if way == "b":
-                came_a[da, db] = shift(make(i, whole, deps), "b", -db)
-            elif way == "a":
-                came_b[da, db] = shift(make(i, whole, deps), "a", -da)
-            else:
-                came_a[da, db] = shift(make(i, top, deps), "b", -db)
-                came_b[da, db] = shift(make(i, low, deps), "a", -da)
-    return came_a, came_b
+            went += [make(i, rows) for rows in ((top, low) if way == "both" else (whole,))]
+            if way != "a":
+                came_a[da, db] = shift(went[-2 if way == "both" else -1], "b", -db)
+            if way != "b":
+                came_b[da, db] = shift(went[-1], "a", -da)
+    return came_a, came_b, went
 
 
 def reduce_sides(make, came, way, split, *deps):
@@ -92,12 +94,12 @@
     whole, top, low = slice(None), slice(0, split), slice(split, None)
 
     def side(i, extra, part):
-        if not extra:
-            return make(i, whole, deps)
-        if way != "both":
-            return make(i, whole, deps, extra)
-        halves = [make(i, rows, deps, extra if rows == part else []) for rows in (top, low)]
-        return jnp.concatenate(halves, axis=0)
+        if not extra or way != "both":
+            term = make(i, whole, extra)
+        else:
+            halves = [make(i, rows, extra if rows == part else []) for rows in (top, low)]
+            term = jnp.concatenate(halves, axis=0)
+        return after(term, *deps) if deps else term
 
     went, arrived = [], []
     for da in range(1, size_a):
@@ -271,33 +273,52 @@
     )
 
 
-def project_kernel(mine_ref, theirs_ref, *refs):
-    pieces, (own_ref, other_ref) = refs[:-2], refs[-2:]
-    for source, target in ((theirs_ref, other_ref), (mine_ref, own_ref)):
-        at, total = 0, None
-        for piece in pieces:
-            end = at + piece.shape[0]
-            term = dot(source[:, at:end], piece[...], 1, 0)
-            total = term if total is None else total + term
-            at = end
+def project_kernel(*refs, counts, more):
+    count = 2 * len(counts)
+    sources, refs = refs[:count], refs[count:]
+    pieces, (own_ref, other_ref) = refs[: sum(counts)], refs[-2:]
+    for half, target in ((1, other_ref), (0, own_ref)):
+        total = refs[sum(counts) + half][...] if more else None
+        left = iter(pieces)
+        for i, number in enumerate(counts):
+            source, at = sources[2 * i + half], 0
+            for _ in range(number):
+                piece = next(left)
+                end = at + piece.shape[0]
+                term = dot(source[:, at:end], piece[...], 1, 0)
+                total = term if total is None else total + term
+                at = end
         target[...] = total
 
 
-def project_rows(mine, theirs, pieces):
-    rows, columns = mine.shape[0], pieces[0].shape[1]
+def project_rows(mine, theirs, slabs, before=()):
+    rows = mine.shape[0]
+    flat = [piece for slab in slabs.values() for piece in slab]
+    columns = flat[0].shape[1]
+    operands, in_specs = [], []
+    for i, slab in slabs.items():
+        plane = sum(piece.shape[0] for piece in slab)
+        operands += [mine, theirs]
+        in_specs += [pl.BlockSpec((rows, plane), lambda _, i=i: (0, i))] * 2
+    whole = [*flat, *before]
+    in_specs += [pl.BlockSpec(array.shape, lambda _: (0, 0)) for array in whole]
+    area = sum(piece.size for piece in flat)
     return pl.pallas_call(
-        project_kernel,
-        in_specs=[VMEM] * (len(pieces) + 2),
-        out_specs=[VMEM] * 2,
+        functools.partial(
+            project_kernel, counts=[len(slab) for slab in slabs.values()], more=bool(before)
+        ),
+        grid=(1,),
+        in_specs=in_specs,
+        out_specs=[pl.BlockSpec((rows, columns), lambda _: (0, 0))] * 2,
         out_shape=[jax.ShapeDtypeStruct((rows, columns), jnp.float32)] * 2,
-        compiler_params=pltpu.CompilerParams(vmem_limit_bytes=20 * 1024 * 1024),
+        compiler_params=pltpu.CompilerParams(vmem_limit_bytes=24 * 1024 * 1024),
         cost_estimate=pl.CostEstimate(
-            flops=4 * mine.size * columns,
-            bytes_accessed=4 * mine.size + 2 * mine.shape[1] * columns,
+            flops=4 * rows * area,
+            bytes_accessed=2 * area + 4 * rows * area // columns,
             transcendentals=0,
         ),
         name="project_rows",
-    )(mine, theirs, *pieces)
+    )(*operands, *whole)
 
 
 def attend_kernel(*refs, group, parts, head_dim, scale, last):
@@ -446,18 +467,16 @@
     line = (place + ctx - jnp.arange(ctx)) % ctx
     pieces = jnp.stack([core * ctx + line, (1 - core) * ctx + line]).astype(jnp.int32)
     mine, theirs = pick_columns(token_rows, slabs, pieces, block)
+    half = query_width // 2
+    q_local = [query_weight[:, g * half : (g + 1) * half].astype(jnp.bfloat16) for g in range(2)]
     pieces_kv = gather_line(kv_local)
     kv_line = jnp.concatenate([after(pieces_kv[0], mine), *pieces_kv[1:]], axis=0)
     theirs = swap(after(theirs, kv_line))
 
-    pieces_q = gather_line(after(query_weight, kv_line).astype(jnp.bfloat16))
-    half = query_width // 2
-    q_line = [
-        jnp.concatenate([piece[:, g * half : (g + 1) * half] for piece in pieces_q], axis=0)
-        for g in range(2)
-    ]
+    q_local = [after(local, theirs) for local in q_local]
+    q_line = [jnp.concatenate(gather_line(local), axis=0) for local in q_local]
     kv_sides = along(kv_line, "a"), along(kv_line, "b")
-    stage = kv_sides[0] + kv_sides[1] + q_line
+    stage = kv_sides[0] + kv_sides[1] + q_line[:1]
     kv_corners = gather_corners(*kv_sides, "b", *stage)
     q0_a = along(after(q_line[0], *stage), "a")
     stage = q0_a + [piece for corner in kv_corners.values() for piece in corner]
@@ -476,29 +495,37 @@
         ]
     )
 
-    def project(slabs):
-        own, other = project_rows(mine, theirs, [piece for slab in slabs for piece in slab])
+    def project(slabs, early_part):
+        late = {i: slab for i, slab in enumerate(slabs) if (i // size_b) * (i % size_b) > 0}
+        own, other = project_rows(mine, theirs, late, early_part)
         return own, swap(other)
+
+    def project_early(slabs, *deps):
+        early = {i: slab for i, slab in enumerate(slabs) if (i // size_b) * (i % size_b) == 0}
+        early[0] = after_all(early[0], *deps) if deps else early[0]
+        return project_rows(mine, theirs, early)
 
     columns = jnp.concatenate([after(mine, *q0_a), theirs], axis=0)
 
     def terms_of(own, other):
         both = jnp.concatenate([own, other], axis=0)
 
-        def make(i, part, deps=(), extra=()):
+        def make(i, part, extra=()):
             start, stop, _ = part.indices(plane)
             at = slice(i * plane + start, i * plane + stop)
-            term = mm(columns[:, at], after(both, *deps) if deps else both, ((0,), (0,)))
+            term = mm(columns[:, at], both, ((0,), (0,)))
             for piece in extra:
                 term = term + piece.astype(jnp.float32)
             return term.astype(jnp.bfloat16)
 
         return make
 
-    key_value = finish_keys(*project(kv_slabs), cos_table, sin_table)
+    own, other = project_rows(mine, theirs, dict(enumerate(kv_slabs)))
+    key_value = finish_keys(own, swap(other), cos_table, sin_table)
     stage = q1_a + q0_b + [key_value]
     q0_corners = gather_corners(q0_a, q0_b, "a", *stage)
     q1_b = along(after(q_line[1], *stage), "b")
+    part = project_early(in_order(q_line[0], q0_a, q0_b, q0_corners))
     key_values = gather_line(key_value)
     stage = q1_b + key_values + [piece for corner in q0_corners.values() for piece in corner]
     q1_corners = gather_corners(q1_a, q1_b, "both", *stage)
@@ -511,8 +538,14 @@
     term = None
     for g in range(2):
         span = slice(g * group * head_dim, (g + 1) * group * head_dim)
+        if g == 1:
+            part = project_early(q_slabs[1], term)
+        own, other = project(q_slabs[g], part)
+        if g == 1:
+            own = after(own, *came[0][2])
         attention, grad_q, terms = attend(
-            *project(q_slabs[g]),
+            own,
+            other,
             grad_output[0][:, span],
             cos_table,
             sin_table,
@@ -538,21 +571,24 @@
     gradients.append((grad_kv, swap(grad_kv)))
     made.append(terms_of(*gradients[2]))
     came.append(reduce_corners(made[2], "both", mid))
-    sides1, went1 = reduce_sides(made[1], came[1], "a", mid, *sides0)
-    q_sum = reduce_line(made[0](0, slice(None), went1, sides0))
-    line1 = made[1](0, slice(None), (), sides1)
-    kv_sides, _ = reduce_sides(made[2], came[2], "both", mid, *sides1)
+    third = [*came[2][0].values(), *came[2][1].values()]
+    sides1, went1 = reduce_sides(made[1], came[1], "a", mid, *sides0, *third)
+    line0 = after(made[0](0, slice(None), sides0), *went1)
+    q_grads = [reduce_line(line0, sides1)]
+    line1 = made[1](0, slice(None), sides1)
+    kv_sides, _ = reduce_sides(made[2], came[2], "both", mid, *sides1, q_grads[0])
+    q_grads.append(reduce_line(line1, kv_sides))
 
     weights = [*q_slabs, kv_slabs]
     grad_theirs = grad_columns(
-        [gradients[0][1], gradients[1][1], after(gradients[2][1], q_sum, *sides1)], weights
+        [gradients[0][1], gradients[1][1], after(gradients[2][1], *third)], weights
     )
     grad_theirs = swap(grad_theirs)
     grad_input = grad_place(
         [gradients[0][0], gradients[1][0], gradients[2][0]], weights, grad_theirs, slabs, pieces, block
     )
-    q_grads = [q_sum, reduce_line(line1)]
-    kv_wgrad = reduce_line(made[2](0, slice(None), (), kv_sides), (grad_input,))
+    kv_line = after(made[2](0, slice(None), kv_sides), q_grads[1])
+    kv_wgrad = reduce_line(kv_line, (grad_input,))
 
     query_grad = jnp.concatenate(q_grads, axis=1)
     key_grad = kv_wgrad[:, :head_dim]

time: 197 us -> 189 us (0.959)
  waiting for transfers between devices: 71.9 us -> 61.5 us
  local copies, waits for them, and re-layouts: 10.4 us -> 13.5 us
    ppermute x49 -> x52, waiting for transfers between devices: 71.9 us -> 61.5 us  [shift(): lax.ppermute(block, axis, [(i, (i + step) % size) for i in range(size)])]
    unnamed x104 -> x110, local copies, waits for them, and re-layouts: 4.37 us -> 9.58 us
    pallas_call x3 -> x5, Pallas kernels: 9 us -> 7.97 us  [project_rows(): pl.pallas_call(functools.partial(project_kernel, counts=[len(slab) for sl...]
    ppermute x49 -> x52, starting transfers between devices: 59.7 us -> 58.7 us  [shift(): lax.ppermute(block, axis, [(i, (i + step) % size) for i in range(size)])]
  transfers between devices with their start and end apart: 49 -> 52, of which waited for: 24 -> 17; matrix products, arithmetic and copies ran while one was open for 11% -> 13% of each run, Pallas kernels for 17% -> 16%
where the time goes in v4:
time: 189 us; the launch traced here: 188 us
  waiting for transfers between devices  61.5 us (33%)
  starting transfers between devices  58.7 us (31%)
  Pallas kernels  32.4 us (17%)
  local copies, waits for them, and re-layouts  13.5 us (7%)
  matrix products  12.7 us (7%)
  other arithmetic  7.99 us (4%)
    ppermute x52, waiting for transfers between devices, shift(): lax.ppermute(block, axis, [(i, (i + step) % size) for i in range(size)])  61.5 us
    ppermute x52, starting transfers between devices, shift(): lax.ppermute(block, axis, [(i, (i + step) % size) for i in range(size)])  58.7 us
    dot_general x15, matrix products, mm(): lax.dot_general(a, b, (dims, ((), ())), preferred_element_type=jnp.float32)  12.7 us
    unnamed x110, local copies, waits for them, and re-layouts  9.58 us
    pallas_call x5, Pallas kernels, project_rows(): pl.pallas_call(functools.partial(project_kernel, counts=[len(slab) for sl...  7.97 us
    pallas_call x1, Pallas kernels, grad_place(): pl.pallas_call(functools.partial(grad_place_kernel, shape=shape, plane=pl...  6.15 us
    pallas_call x1, Pallas kernels, pick_columns(): pl.pallas_call(functools.partial(pick_kernel, block=block), grid_spec=plt...  5.69 us
    pallas_call x2, Pallas kernels, attend(): pl.pallas_call(functools.partial(attend_kernel, group=group, parts=parts,...  5.41 us
  transfers between devices with their start and end apart: 52, of which 17 were waited for; matrix products, arithmetic and copies ran while one was open for 13% of the time, Pallas kernels for 16%

profile of v4, /device:TPU:0, one launch (start us, length us, event | category | flops | bytes accessed | tf_op | source)
XLA Modules:
  0.0 188.4 jit_solution(12220026264519642928)
XLA Ops:
  0.6 1.0 convert.10
  1.6 0.9 convert.11
  2.6 3.1 %collective-permute-start = (bf16[256,256]{1,0:T(8,128)(2,1)S(1)}, bf16[256,256]{1,0:T(8,128)(2,1)}, u32[]{:S(2)}, u32[]{:S(2)}) collective-permute-start(bf16[256,256]{1,0:T(8,128)(2,1)S(1)} %pad_maximum_fusion.4), channel_id=1, source_target_pairs={{0,1},{1,2},{2,3},{3,0},{4,5},{5,6},{6,7},{7,4},{8,9},{9,10},{10,1... | collective-permute-start | bytes 393224 | tf_op jit(solution)/shard_map/ppermute | solution.py:29
  5.6 2.6 %collective-permute-start.1 = (bf16[256,256]{1,0:T(8,128)(2,1)S(1)}, bf16[256,256]{1,0:T(8,128)(2,1)S(1)}, u32[]{:S(2)}, u32[]{:S(2)}) collective-permute-start(bf16[256,256]{1,0:T(8,128)(2,1)S(1)} %pad_maximum_fusion.4), channel_id=1, source_target_pairs={{0,2},{1,3},{2,0},{3,1},{4,6},{5,7},{6,4},{7,5},{8,10},{9,11},{10,... | collective-permute-start | bytes 393224 | tf_op jit(solution)/shard_map/ppermute | solution.py:29
  8.2 1.3 collective-permute-start.2
  10.9 5.7 %pick_columns.1 = (bf16[256,4096]{1,0:T(8,128)(2,1)}, bf16[256,4096]{1,0:T(8,128)(2,1)}) custom-call(s32[4]{0:T(128)} %fusion.26.slab_ref.refs_0_, s32[2,4]{1,0:T(2,128)} %pad_add_fusion.1.piece_ref.refs_1_, bf16[256,8192]{1,0:T(8,128)(2,1)} %bitcast.17), custom_call_target="tpu_custom_call" | custom-call | bytes 8388608 | tf_op jit(solution)/shard_map/pick_columns/pallas_call | solution.py:205
  16.6 1.1 constant_dynamic-update-slice_fusion.2
  18.0 1.7 fusion.37
  19.6 1.5 collective-permute-start.7
  21.2 1.5 collective-permute-start.8
  22.7 1.3 copy-done.1
  24.0 2.4 %collective-permute-start.4 = (bf16[256,256]{1,0:T(8,128)(2,1)S(1)}, bf16[256,256]{1,0:T(8,128)(2,1)S(1)}, u32[]{:S(2)}, u32[]{:S(2)}) collective-permute-start(bf16[256,256]{1,0:T(8,128)(2,1)S(1)} %get-tuple-element.59), channel_id=1, source_target_pairs={{0,1},{1,2},{2,3},{3,0},{4,5},{5,6},{6,7},{7,4},{8,9},{9,10},{10,1... | collective-permute-start | bytes 393224 | tf_op jit(solution)/shard_map/ppermute | solution.py:29
  26.4 1.7 collective-permute-start.5
  28.0 0.9 collective-permute-start.6
  28.9 3.3 %collective-permute-done.4 = bf16[256,256]{1,0:T(8,128)(2,1)S(1)} collective-permute-done((bf16[256,256]{1,0:T(8,128)(2,1)S(1)}, bf16[256,256]{1,0:T(8,128)(2,1)S(1)}, u32[]{:S(2)}, u32[]{:S(2)}) %collective-permute-start.4) | collective-permute-done | bytes 131104 | tf_op jit(solution)/shard_map/ppermute | solution.py:29
  32.7 5.1 %collective-permute-done.5 = bf16[256,256]{1,0:T(8,128)(2,1)S(1)} collective-permute-done((bf16[256,256]{1,0:T(8,128)(2,1)S(1)}, bf16[256,256]{1,0:T(8,128)(2,1)S(1)}, u32[]{:S(2)}, u32[]{:S(2)}) %collective-permute-start.5) | collective-permute-done | bytes 131104 | tf_op jit(solution)/shard_map/ppermute | solution.py:29
  37.9 1.1 collective-permute-start.9
  39.0 1.5 collective-permute-start.10
  40.6 4.2 %collective-permute-start.13 = (bf16[256,256]{1,0:T(8,128)(2,1)S(1)}, bf16[256,256]{1,0:T(8,128)(2,1)S(1)}, u32[]{:S(2)}, u32[]{:S(2)}) collective-permute-start(bf16[256,256]{1,0:T(8,128)(2,1)S(1)} %get-tuple-element.63), channel_id=1, source_target_pairs={{0,2},{1,3},{2,0},{3,1},{4,6},{5,7},{6,4},{7,5},{8,10},{9,11},{10,... | collective-permute-start | bytes 393224 | tf_op jit(solution)/shard_map/ppermute | solution.py:29
  45.5 3.4 %collective-permute-start.14 = (bf16[256,256]{1,0:T(8,128)(2,1)S(1)}, bf16[256,256]{1,0:T(8,128)(2,1)S(1)}, u32[]{:S(2)}, u32[]{:S(2)}) collective-permute-start(bf16[256,256]{1,0:T(8,128)(2,1)S(1)} %get-tuple-element.63), channel_id=1, source_target_pairs={{0,3},{1,0},{2,1},{3,2},{4,7},{5,4},{6,5},{7,6},{8,11},{9,8},{10,9... | collective-permute-start | bytes 393224 | tf_op jit(solution)/shard_map/ppermute | solution.py:29
  50.2 1.2 collective-permute-done.14
  52.9 1.2 collective-permute-start.11
  54.1 0.9 collective-permute-start.15
  55.8 1.6 copy-done.2
  57.4 1.0 copy-done.8
  58.4 2.7 %project_rows.5 = (f32[256,256]{1,0:T(8,128)S(1)}, f32[256,256]{1,0:T(8,128)S(1)}) custom-call(bf16[256,4096]{1,0:T(8,128)(2,1)S(1)} %copy-done, bf16[256,4096]{1,0:T(8,128)(2,1)S(1)} %copy-done.2, bf16[256,4096]{1,0:T(8,128)(2,1)S(1)} %copy-done, bf16[256,4096]{1,0:T(8,128)(2,1)S(1)} %copy-done.2, bf16[256,4096]{1,0:T(8,128)(2,1)S(1)} %copy-done, ...), custom_call_target="tpu_custom_call" | custom-call | flops 1073741824 | bytes 6291456 | tf_op jit(solution)/shard_map/project_rows/pallas_call | solution.py:306
  62.0 2.2 %negate_select_fusion = (f32[256,128]{1,0:T(8,128)}, f32[256,128]{1,0:T(8,128)}) fusion(f32[256,64]{1,0:T(8,128)} %broadcast_multiply_fusion, pred[128]{0:T(512)(128)(4,1)S(1)} %iota_compare_fusion), kind=kLoop, calls=%fused_computation.48 | loop fusion | flops 98304 | bytes 327808 | tf_op jit(solution)/shard_map/jit(_where)/select_n | solution.py:490
  64.2 1.9 finish_keys.1.refs_7_
  66.1 5.5 %collective-permute-start.19 = (bf16[256,256]{1,0:T(8,128)(2,1)}, bf16[256,256]{1,0:T(8,128)(2,1)S(1)}, u32[]{:S(2)}, u32[]{:S(2)}) collective-permute-start(bf16[256,256]{1,0:T(8,128)(2,1)} %finish_keys.1.refs_7_), channel_id=1, source_target_pairs={{0,1},{1,2},{2,3},{3,0},{4,5},{5,6},{6,7},{7,4},{8,9},{9,10},{10,1... | collective-permute-start | bytes 393224 | tf_op jit(solution)/shard_map/ppermute | solution.py:29
  72.1 1.9 %collective-permute-start.21 = (bf16[256,256]{1,0:T(8,128)(2,1)}, bf16[256,256]{1,0:T(8,128)(2,1)S(1)}, u32[]{:S(2)}, u32[]{:S(2)}) collective-permute-start(bf16[256,256]{1,0:T(8,128)(2,1)} %finish_keys.1.refs_7_), channel_id=1, source_target_pairs={{0,3},{1,0},{2,1},{3,2},{4,7},{5,4},{6,5},{7,6},{8,11},{9,8},{10,9... | collective-permute-start | bytes 393224 | tf_op jit(solution)/shard_map/ppermute | solution.py:29
  74.1 1.1 collective-permute-start.17
  76.0 2.2 %project_rows.6 = (f32[256,256]{1,0:T(8,128)S(1)}, f32[256,256]{1,0:T(8,128)S(1)}) custom-call(bf16[256,4096]{1,0:T(8,128)(2,1)S(1)} %copy-done, bf16[256,4096]{1,0:T(8,128)(2,1)S(1)} %copy-done.3, bf16[256,4096]{1,0:T(8,128)(2,1)S(1)} %copy-done, bf16[256,4096]{1,0:T(8,128)(2,1)S(1)} %copy-done.3, bf16[256,4096]{1,0:T(8,128)(2,1)S(1)} %copy-done, ...), custom_call_target="tpu_custom_call" | custom-call | flops 805306368 | bytes 4718592 | tf_op jit(solution)/shard_map/project_rows/pallas_call | solution.py:306
  78.2 9.9 %collective-permute-done.17.refs_2_.refs_6_.refs_8_ = bf16[1024,256]{1,0:T(8,128)(2,1)S(1)} collective-permute-done((bf16[1024,256]{1,0:T(8,128)(2,1)}, bf16[1024,256]{1,0:T(8,128)(2,1)S(1)}, u32[]{:S(2)}, u32[]{:S(2)}) %collective-permute-start.17) | collective-permute-done | bytes 524320 | tf_op jit(solution)/shard_map/ppermute | solution.py:29
  88.9 1.0 collective-permute-start.24
  90.8 2.6 %attend.2 = (bf16[256,256]{1,0:T(8,128)(2,1)S(1)}, bf16[256,256]{1,0:T(8,128)(2,1)S(1)}, f32[1024,256]{1,0:T(8,128)S(1)}) custom-call(f32[256,256]{1,0:T(8,128)S(1)} %get-tuple-element.71.refs_0_, f32[256,256]{1,0:T(8,128)S(1)} %collective-permute-done.18.refs_1_, bf16[256,256]{1,0:T(8,128)(2,1)S(1)} %copy-done.30, f32[256,128]{1,0:T(8,128)S(1)} %copy-done.20, ...), custom_call_target="tpu_custom_call" | custom-call | flops 939524096 | bytes 2097152 | tf_op jit(solution)/shard_map/attend/pallas_call | solution.py:389
  94.0 2.2 %project_rows.8 = (f32[256,256]{1,0:T(8,128)S(1)}, f32[256,256]{1,0:T(8,128)S(1)}) custom-call(bf16[256,4096]{1,0:T(8,128)(2,1)S(1)} %copy-done, bf16[256,4096]{1,0:T(8,128)(2,1)S(1)} %copy-done.3, bf16[256,4096]{1,0:T(8,128)(2,1)S(1)} %copy-done, bf16[256,4096]{1,0:T(8,128)(2,1)S(1)} %copy-done.3, bf16[256,4096]{1,0:T(8,128)(2,1)S(1)} %copy-done, ...), custom_call_target="tpu_custom_call" | custom-call | flops 805306368 | bytes 4718592 | tf_op jit(solution)/shard_map/project_rows/pallas_call | solution.py:306
  96.2 1.2 collective-permute-done.24.refs_3_.refs_11_.refs_13_
  99.3 0.9 collective-permute-done.26.refs_1_
  100.3 2.8 %attend.3 = (bf16[256,256]{1,0:T(8,128)(2,1)S(1)}, bf16[256,256]{1,0:T(8,128)(2,1)S(1)}, f32[256,256]{1,0:T(8,128)S(1)}, bf16[256,256]{1,0:T(8,128)(2,1)S(1)}, b...) custom-call(f32[256,256]{1,0:T(8,128)S(1)} %get-tuple-element.84.refs_0_, ...), custom_call_target="tpu_custom_call" | custom-call | flops 939524096 | bytes 2097152 | tf_op jit(solution)/shard_map/attend/pallas_call | solution.py:389
  103.4 1.3 convolution_convert_fusion.1
  105.2 1.7 collective-permute-start.30
  109.3 1.3 convolution_convert_fusion
  110.8 8.7 %collective-permute-done.31.refs_2_ = bf16[256,256]{1,0:T(8,128)(2,1)S(1)} collective-permute-done((bf16[256,256]{1,0:T(8,128)(2,1)S(1)}, bf16[256,256]{1,0:T(8,128)(2,1)S(1)}, u32[]{:S(2)}, u32[]{:S(2)}) %collective-permute-start.31) | collective-permute-done | bytes 131104 | tf_op jit(solution)/shard_map/ppermute | solution.py:29
  119.6 1.3 fusion.3
  122.3 2.0 %undo_keys.1.refs_4_ = bf16[256,256]{1,0:T(8,128)(2,1)} custom-call(f32[256,256]{1,0:T(8,128)} %copy-done.27, bf16[256,256]{1,0:T(8,128)(2,1)} %copy-done.40, bf16[256,256]{1,0:T(8,128)(2,1)} %copy-done.41, bf16[256,256]{1,0:T(8,128)(2,1)} %copy-done.42, f32[256,128]{1,0:T(8,128)} %get-tuple-element.126.cos_ref.refs_3_.refs_4_, ...), custom_call_target="tpu_custom_call" | custom-call | tf_op jit(solution)/shard_map/undo_keys/pallas_call | solution.py:440
  124.4 2.0 %fusion.5 = bf16[1024,256]{1,0:T(8,128)(2,1)S(1)} fusion(bf16[512,256]{1,0:T(8,128)(2,1)S(1)} %constant_dynamic-update-slice_fusion.16, bf16[1024,256]{1,0:T(8,128)(2,1)} %collective-permute-done.29, bf16[512,4096]{1,0:T(8,128)(2,1)} %copy-done.37), kind=kOutput, calls=%fused_computation.14 | convolution fusion | flops 269221888 | bytes 2359296 | tf_op jit(solution)/shard_map/dot_general | solution.py:24
  126.4 1.4 convolution_convert_fusion.6
  127.8 1.2 collective-permute-start.35
  129.5 1.5 collective-permute-start.34
  131.8 4.3 %collective-permute-done.38 = bf16[1024,256]{1,0:T(8,128)(2,1)} collective-permute-done((bf16[1024,256]{1,0:T(8,128)(2,1)}, bf16[1024,256]{1,0:T(8,128)(2,1)}, u32[]{:S(2)}, u32[]{:S(2)}) %collective-permute-start.38) | collective-permute-done | bytes 524320 | tf_op jit(solution)/shard_map/ppermute | solution.py:29
  136.6 1.7 fusion.4
  138.3 2.1 %collective-permute-done.35 = bf16[512,256]{1,0:T(8,128)(2,1)S(1)} collective-permute-done((bf16[512,256]{1,0:T(8,128)(2,1)S(1)}, bf16[512,256]{1,0:T(8,128)(2,1)S(1)}, u32[]{:S(2)}, u32[]{:S(2)}) %collective-permute-start.35) | collective-permute-done | bytes 262176 | tf_op jit(solution)/shard_map/ppermute | solution.py:29
  141.2 1.2 collective-permute-start.40
  142.4 1.6 collective-permute-start.41
  144.9 3.3 %grad_columns.1 = bf16[256,4096]{1,0:T(8,128)(2,1)S(1)} custom-call(bf16[256,256]{1,0:T(8,128)(2,1)S(1)} %copy-done.24, bf16[256,256]{1,0:T(8,128)(2,1)S(1)} %collective-permute-done.28.refs_1_, bf16[256,256]{1,0:T(8,128)(2,1)S(1)} %collective-permute-done.33.refs_2_, bf16[1024,256]{1,0:T(8,128)(2,1)S(1)} %copy-done.6, ...), custom_call_target="tpu_custom_call" | custom-call | flops 1610612736 | bytes 8388608 | tf_op jit(solution)/shard_map/grad_columns/pallas_call | solution.py:227
  149.1 3.5 %collective-permute-done.39 = bf16[1024,256]{1,0:T(8,128)(2,1)S(1)} collective-permute-done((bf16[1024,256]{1,0:T(8,128)(2,1)S(1)}, bf16[1024,256]{1,0:T(8,128)(2,1)S(1)}, u32[]{:S(2)}, u32[]{:S(2)}) %collective-permute-start.39) | collective-permute-done | bytes 524320 | tf_op jit(solution)/shard_map/ppermute | solution.py:29
  152.6 1.2 collective-permute-start.43
  153.9 5.5 %collective-permute-done.43 = bf16[256,256]{1,0:T(8,128)(2,1)S(1)} collective-permute-done((bf16[256,256]{1,0:T(8,128)(2,1)S(1)}, bf16[256,256]{1,0:T(8,128)(2,1)S(1)}, u32[]{:S(2)}, u32[]{:S(2)}) %collective-permute-start.43) | collective-permute-done | bytes 131104 | tf_op jit(solution)/shard_map/ppermute | solution.py:29
  160.3 1.2 collective-permute-start.44
  162.1 1.1 collective-permute-start.47
  163.2 6.4 %collective-permute-done.45 = bf16[1024,256]{1,0:T(8,128)(2,1)S(1)} collective-permute-done((bf16[1024,256]{1,0:T(8,128)(2,1)S(1)}, bf16[1024,256]{1,0:T(8,128)(2,1)S(1)}, u32[]{:S(2)}, u32[]{:S(2)}) %collective-permute-start.45) | collective-permute-done | bytes 524320 | tf_op jit(solution)/shard_map/ppermute | solution.py:29
  170.4 7.4 %collective-permute-done.48 = bf16[256,256]{1,0:T(8,128)(2,1)S(1)} collective-permute-done((bf16[256,256]{1,0:T(8,128)(2,1)S(1)}, bf16[256,256]{1,0:T(8,128)(2,1)S(1)}, u32[]{:S(2)}, u32[]{:S(2)}) %collective-permute-start.48) | collective-permute-done | bytes 131104 | tf_op jit(solution)/shard_map/ppermute | solution.py:29
  178.6 1.9 %collective-permute-start.51 = (bf16[256,256]{1,0:T(8,128)(2,1)S(1)}, bf16[256,256]{1,0:T(8,128)(2,1)S(1)}, u32[]{:S(2)}, u32[]{:S(2)}) collective-permute-start(bf16[256,256]{1,0:T(8,128)(2,1)S(1)} %get-tuple-element.108), channel_id=1, source_target_pairs={{0,1},{1,2},{2,3},{3,0},{4,5},{5,6},{6,7},{7,4},{8,9},{9,10},{10,1... | collective-permute-start | bytes 393224 | tf_op jit(solution)/shard_map/ppermute | solution.py:29
  181.4 6.2 %grad_place.1 = bf16[256,8192]{1,0:T(8,128)(2,1)} custom-call(s32[4]{0:T(128)S(1)} %copy-done.36, s32[2,4]{1,0:T(2,128)S(1)} %copy-done.35, bf16[256,256]{1,0:T(8,128)(2,1)S(1)} %copy-done.22, bf16[256,256]{1,0:T(8,128)(2,1)S(1)} %get-tuple-element.87.refs_3_, bf16[256,256]{1,0:T(8,128)(2,1)S(1)} %copy-done.25, bf16[1024,256]{1,0:T(8,128)(2,1)S(1)} %copy-done.6, ...), custom_call_target="tpu_custom_call" | custom-call | flops 1610612736 | bytes 12582912 | tf_op jit(solution)/shard_map/grad_place/pallas_call | solution.py:251
  (218 shorter events, 26.3 us)
Async XLA Ops:
  0.6 17.2 %copy-start.39 = (f32[256,512]{1,0:T(8,128)S(1)}, f32[256,512]{1,0:T(8,128)}, u32[]{:S(2)}) copy-start(f32[256,512]{1,0:T(8,128)} %param.8) | copy-start | bytes 1572868
  2.5 38.0 %copy-start.47 = (s32[1024]{0:T(1024)S(1)}, s32[1024]{0:T(1024)}, u32[]{:S(2)}) copy-start(s32[1024]{0:T(1024)} %param.7) | copy-start | bytes 12292
  2.6 14.1 %collective-permute-start = (bf16[256,256]{1,0:T(8,128)(2,1)S(1)}, bf16[256,256]{1,0:T(8,128)(2,1)}, u32[]{:S(2)}, u32[]{:S(2)}) collective-permute-start(bf16[256,256]{1,0:T(8,128)(2,1)S(1)} %pad_maximum_fusion.4), channel_id=1, source_target_pairs={{0,1},{1,2},{2,3},{3,0},{4,5},{5,6},{6,7},{7,4},{8,9},{9,10},{10,1... | collective-permute-start | bytes 393224 | tf_op jit(solution)/shard_map/ppermute | solution.py:29
  5.6 12.1 %collective-permute-start.1 = (bf16[256,256]{1,0:T(8,128)(2,1)S(1)}, bf16[256,256]{1,0:T(8,128)(2,1)S(1)}, u32[]{:S(2)}, u32[]{:S(2)}) collective-permute-start(bf16[256,256]{1,0:T(8,128)(2,1)S(1)} %pad_maximum_fusion.4), channel_id=1, source_target_pairs={{0,2},{1,3},{2,0},{3,1},{4,6},{5,7},{6,4},{7,5},{8,10},{9,11},{10,... | collective-permute-start | bytes 393224 | tf_op jit(solution)/shard_map/ppermute | solution.py:29
  8.2 9.5 %collective-permute-start.2 = (bf16[256,256]{1,0:T(8,128)(2,1)S(1)}, bf16[256,256]{1,0:T(8,128)(2,1)S(1)}, u32[]{:S(2)}, u32[]{:S(2)}) collective-permute-start(bf16[256,256]{1,0:T(8,128)(2,1)S(1)} %pad_maximum_fusion.4), channel_id=1, source_target_pairs={{0,3},{1,0},{2,1},{3,2},{4,7},{5,4},{6,5},{7,6},{8,11},{9,8},{10,9... | collective-permute-start | bytes 393224 | tf_op jit(solution)/shard_map/ppermute | solution.py:29
  16.6 39.1 %copy-start = (bf16[256,4096]{1,0:T(8,128)(2,1)S(1)}, bf16[256,4096]{1,0:T(8,128)(2,1)}, u32[]{:S(2)}) copy-start(bf16[256,4096]{1,0:T(8,128)(2,1)} %get-tuple-element.82.refs_0_.refs_2_.refs_4_.refs_6_) | copy-start | bytes 6291460
  17.8 35.1 %copy-start.7 = (bf16[1024,256]{1,0:T(8,128)(2,1)}, bf16[1024,256]{1,0:T(8,128)(2,1)S(1)}, u32[]{:S(2)}) copy-start(bf16[1024,256]{1,0:T(8,128)(2,1)S(1)} %constant_dynamic-update-slice_fusion.refs_8_.refs_12_.refs_14_) | copy-start | bytes 1572868
  17.8 4.9 %collective-permute-start.3 = (bf16[256,4096]{1,0:T(8,128)(2,1)}, bf16[256,4096]{1,0:T(8,128)(2,1)S(1)}, u32[]{:S(2)}, u32[]{:S(2)}) collective-permute-start(bf16[256,4096]{1,0:T(8,128)(2,1)} %get-tuple-element.58), channel_id=1, source_target_pairs={{0,4},{4,0},{1,5},{5,1},{2,6},{6,2},{3,7},{7,3},{8,12},{12,8},{9,1... | collective-permute-start | bytes 6291464 | tf_op jit(solution)/shard_map/ppermute | solution.py:29
  19.6 18.3 %collective-permute-start.7 = (bf16[1024,256]{1,0:T(8,128)(2,1)S(1)}, bf16[1024,256]{1,0:T(8,128)(2,1)}, u32[]{:S(2)}, u32[]{:S(2)}) collective-permute-start(bf16[1024,256]{1,0:T(8,128)(2,1)S(1)} %constant_dynamic-update-slice_fusion.refs_8_.refs_12_.refs_14_), channel_id=1, source_target_pairs={{0,16},{16,0},{1,17},{17,1},{2,18},{18,2},{3,19},{19,3},{4,20},{20... | collective-permute-start | bytes 1572872 | tf_op jit(solution)/shard_map/ppermute | solution.py:29
  21.2 16.7 %collective-permute-start.8 = (bf16[1024,256]{1,0:T(8,128)(2,1)S(1)}, bf16[1024,256]{1,0:T(8,128)(2,1)}, u32[]{:S(2)}, u32[]{:S(2)}) collective-permute-start(bf16[1024,256]{1,0:T(8,128)(2,1)S(1)} %constant_dynamic-update-slice_fusion.refs_8_.refs_12_.refs_14_), channel_id=1, source_target_pairs={{0,8},{8,0},{1,9},{9,1},{2,10},{10,2},{3,11},{11,3},{4,12},{12,4},... | collective-permute-start | bytes 1572872 | tf_op jit(solution)/shard_map/ppermute | solution.py:29
  24.0 8.3 %collective-permute-start.4 = (bf16[256,256]{1,0:T(8,128)(2,1)S(1)}, bf16[256,256]{1,0:T(8,128)(2,1)S(1)}, u32[]{:S(2)}, u32[]{:S(2)}) collective-permute-start(bf16[256,256]{1,0:T(8,128)(2,1)S(1)} %get-tuple-element.59), channel_id=1, source_target_pairs={{0,1},{1,2},{2,3},{3,0},{4,5},{5,6},{6,7},{7,4},{8,9},{9,10},{10,1... | collective-permute-start | bytes 393224 | tf_op jit(solution)/shard_map/ppermute | solution.py:29
  26.4 11.5 %collective-permute-start.5 = (bf16[256,256]{1,0:T(8,128)(2,1)S(1)}, bf16[256,256]{1,0:T(8,128)(2,1)S(1)}, u32[]{:S(2)}, u32[]{:S(2)}) collective-permute-start(bf16[256,256]{1,0:T(8,128)(2,1)S(1)} %get-tuple-element.59), channel_id=1, source_target_pairs={{0,2},{1,3},{2,0},{3,1},{4,6},{5,7},{6,4},{7,5},{8,10},{9,11},{10,... | collective-permute-start | bytes 393224 | tf_op jit(solution)/shard_map/ppermute | solution.py:29
  28.0 9.8 %collective-permute-start.6 = (bf16[256,256]{1,0:T(8,128)(2,1)S(1)}, bf16[256,256]{1,0:T(8,128)(2,1)S(1)}, u32[]{:S(2)}, u32[]{:S(2)}) collective-permute-start(bf16[256,256]{1,0:T(8,128)(2,1)S(1)} %get-tuple-element.59), channel_id=1, source_target_pairs={{0,3},{1,0},{2,1},{3,2},{4,7},{5,4},{6,5},{7,6},{8,11},{9,8},{10,9... | collective-permute-start | bytes 393224 | tf_op jit(solution)/shard_map/ppermute | solution.py:29
  32.2 16.7 %collective-permute-start.12 = (bf16[256,256]{1,0:T(8,128)(2,1)S(1)}, bf16[256,256]{1,0:T(8,128)(2,1)S(1)}, u32[]{:S(2)}, u32[]{:S(2)}) collective-permute-start(bf16[256,256]{1,0:T(8,128)(2,1)S(1)} %get-tuple-element.63), channel_id=1, source_target_pairs={{0,1},{1,2},{2,3},{3,0},{4,5},{5,6},{6,7},{7,4},{8,9},{9,10},{10,1... | collective-permute-start | bytes 393224 | tf_op jit(solution)/shard_map/ppermute | solution.py:29
  37.9 23.2 %copy-start.4 = (bf16[1024,256]{1,0:T(8,128)(2,1)}, bf16[1024,256]{1,0:T(8,128)(2,1)S(1)}, u32[]{:S(2)}) copy-start(bf16[1024,256]{1,0:T(8,128)(2,1)S(1)} %constant_dynamic-update-slice_fusion.4.refs_6_.refs_3_.refs_5_) | copy-start | bytes 1572868
  37.9 14.1 %collective-permute-start.9 = (bf16[1024,256]{1,0:T(8,128)(2,1)S(1)}, bf16[1024,256]{1,0:T(8,128)(2,1)S(1)}, u32[]{:S(2)}, u32[]{:S(2)}) collective-permute-start(bf16[1024,256]{1,0:T(8,128)(2,1)S(1)} %constant_dynamic-update-slice_fusion.4.refs_6_.refs_3_.refs_5_), channel_id=1, source_target_pairs={{0,16},{16,0},{1,17},{17,1},{2,18},{18,2},{3,19},{19,3},{4,20},{20... | collective-permute-start | bytes 1572872 | tf_op jit(solution)/shard_map/ppermute | solution.py:29
  39.0 13.9 %collective-permute-start.10 = (bf16[1024,256]{1,0:T(8,128)(2,1)}, bf16[1024,256]{1,0:T(8,128)(2,1)S(1)}, u32[]{:S(2)}, u32[]{:S(2)}) collective-permute-start(bf16[1024,256]{1,0:T(8,128)(2,1)} %collective-permute-done.7.refs_10_.refs_14_.refs_16_), channel_id=1, source_target_pairs={{0,8},{8,0},{1,9},{9,1},{2,10},{10,2},{3,11},{11,3},{4,12},{12,4},... | collective-permute-start | bytes 1572872 | tf_op jit(solution)/shard_map/ppermute | solution.py:29
  40.6 8.9 %collective-permute-start.13 = (bf16[256,256]{1,0:T(8,128)(2,1)S(1)}, bf16[256,256]{1,0:T(8,128)(2,1)S(1)}, u32[]{:S(2)}, u32[]{:S(2)}) collective-permute-start(bf16[256,256]{1,0:T(8,128)(2,1)S(1)} %get-tuple-element.63), channel_id=1, source_target_pairs={{0,2},{1,3},{2,0},{3,1},{4,6},{5,7},{6,4},{7,5},{8,10},{9,11},{10,... | collective-permute-start | bytes 393224 | tf_op jit(solution)/shard_map/ppermute | solution.py:29
  45.5 5.9 %collective-permute-start.14 = (bf16[256,256]{1,0:T(8,128)(2,1)S(1)}, bf16[256,256]{1,0:T(8,128)(2,1)S(1)}, u32[]{:S(2)}, u32[]{:S(2)}) collective-permute-start(bf16[256,256]{1,0:T(8,128)(2,1)S(1)} %get-tuple-element.63), channel_id=1, source_target_pairs={{0,3},{1,0},{2,1},{3,2},{4,7},{5,4},{6,5},{7,6},{8,11},{9,8},{10,9... | collective-permute-start | bytes 393224 | tf_op jit(solution)/shard_map/ppermute | solution.py:29
  52.9 21.2 %collective-permute-start.11 = (bf16[1024,256]{1,0:T(8,128)(2,1)S(1)}, bf16[1024,256]{1,0:T(8,128)(2,1)}, u32[]{:S(2)}, u32[]{:S(2)}) collective-permute-start(bf16[1024,256]{1,0:T(8,128)(2,1)S(1)} %constant_dynamic-update-slice_fusion.4.refs_6_.refs_3_.refs_5_), channel_id=1, source_target_pairs={{0,8},{8,0},{1,9},{9,1},{2,10},{10,2},{3,11},{11,3},{4,12},{12,4},... | collective-permute-start | bytes 1572872 | tf_op jit(solution)/shard_map/ppermute | solution.py:29
  54.1 20.0 %collective-permute-start.15 = (bf16[1024,256]{1,0:T(8,128)(2,1)}, bf16[1024,256]{1,0:T(8,128)(2,1)S(1)}, u32[]{:S(2)}, u32[]{:S(2)}) collective-permute-start(bf16[1024,256]{1,0:T(8,128)(2,1)} %constant_dynamic-update-slice_fusion.8.refs_6_.refs_7_.refs_9_), channel_id=1, source_target_pairs={{0,16},{16,0},{1,17},{17,1},{2,18},{18,2},{3,19},{19,3},{4,20},{20... | collective-permute-start | bytes 1572872 | tf_op jit(solution)/shard_map/ppermute | solution.py:29
  61.8 2.4 %collective-permute-start.16 = (f32[256,256]{1,0:T(8,128)S(1)}, f32[256,256]{1,0:T(8,128)}, u32[]{:S(2)}, u32[]{:S(2)}) collective-permute-start(f32[256,256]{1,0:T(8,128)S(1)} %get-tuple-element.66), channel_id=1, source_target_pairs={{0,4},{4,0},{1,5},{5,1},{2,6},{6,2},{3,7},{7,3},{8,12},{12,8},{9,1... | collective-permute-start | bytes 786440 | tf_op jit(solution)/shard_map/ppermute | solution.py:29
  66.1 22.8 %collective-permute-start.19 = (bf16[256,256]{1,0:T(8,128)(2,1)}, bf16[256,256]{1,0:T(8,128)(2,1)S(1)}, u32[]{:S(2)}, u32[]{:S(2)}) collective-permute-start(bf16[256,256]{1,0:T(8,128)(2,1)} %finish_keys.1.refs_7_), channel_id=1, source_target_pairs={{0,1},{1,2},{2,3},{3,0},{4,5},{5,6},{6,7},{7,4},{8,9},{9,10},{10,1... | collective-permute-start | bytes 393224 | tf_op jit(solution)/shard_map/ppermute | solution.py:29
  71.6 17.3 %collective-permute-start.20 = (bf16[256,256]{1,0:T(8,128)(2,1)}, bf16[256,256]{1,0:T(8,128)(2,1)S(1)}, u32[]{:S(2)}, u32[]{:S(2)}) collective-permute-start(bf16[256,256]{1,0:T(8,128)(2,1)} %finish_keys.1.refs_7_), channel_id=1, source_target_pairs={{0,2},{1,3},{2,0},{3,1},{4,6},{5,7},{6,4},{7,5},{8,10},{9,11},{10,... | collective-permute-start | bytes 393224 | tf_op jit(solution)/shard_map/ppermute | solution.py:29
  72.1 16.8 %collective-permute-start.21 = (bf16[256,256]{1,0:T(8,128)(2,1)}, bf16[256,256]{1,0:T(8,128)(2,1)S(1)}, u32[]{:S(2)}, u32[]{:S(2)}) collective-permute-start(bf16[256,256]{1,0:T(8,128)(2,1)} %finish_keys.1.refs_7_), channel_id=1, source_target_pairs={{0,3},{1,0},{2,1},{3,2},{4,7},{5,4},{6,5},{7,6},{8,11},{9,8},{10,9... | collective-permute-start | bytes 393224 | tf_op jit(solution)/shard_map/ppermute | solution.py:29
  74.1 14.0 %collective-permute-start.17 = (bf16[1024,256]{1,0:T(8,128)(2,1)}, bf16[1024,256]{1,0:T(8,128)(2,1)S(1)}, u32[]{:S(2)}, u32[]{:S(2)}) collective-permute-start(bf16[1024,256]{1,0:T(8,128)(2,1)} %collective-permute-done.11.refs_7_.refs_4_.refs_6_), channel_id=1, source_target_pairs={{0,16},{16,0},{1,17},{17,1},{2,18},{18,2},{3,19},{19,3},{4,20},{20... | collective-permute-start | bytes 1572872 | tf_op jit(solution)/shard_map/ppermute | solution.py:29
  75.2 13.7 %collective-permute-start.22 = (bf16[1024,256]{1,0:T(8,128)(2,1)}, bf16[1024,256]{1,0:T(8,128)(2,1)S(1)}, u32[]{:S(2)}, u32[]{:S(2)}) collective-permute-start(bf16[1024,256]{1,0:T(8,128)(2,1)} %constant_dynamic-update-slice_fusion.8.refs_6_.refs_7_.refs_9_), channel_id=1, source_target_pairs={{0,8},{8,0},{1,9},{9,1},{2,10},{10,2},{3,11},{11,3},{4,12},{12,4},... | collective-permute-start | bytes 1572872 | tf_op jit(solution)/shard_map/ppermute | solution.py:29
  88.5 2.2 %collective-permute-start.18 = (f32[256,256]{1,0:T(8,128)S(1)}, f32[256,256]{1,0:T(8,128)S(1)}, u32[]{:S(2)}, u32[]{:S(2)}) collective-permute-start(f32[256,256]{1,0:T(8,128)S(1)} %get-tuple-element.72), channel_id=1, source_target_pairs={{0,4},{4,0},{1,5},{5,1},{2,6},{6,2},{3,7},{7,3},{8,12},{12,8},{9,1... | collective-permute-start | bytes 786440 | tf_op jit(solution)/shard_map/ppermute | solution.py:29
  88.9 8.5 %collective-permute-start.24 = (bf16[512,256]{1,0:T(8,128)(2,1)S(1)}, bf16[512,256]{1,0:T(8,128)(2,1)S(1)}, u32[]{:S(2)}, u32[]{:S(2)}) collective-permute-start(bf16[512,256]{1,0:T(8,128)(2,1)S(1)} %slice.131), channel_id=1, source_target_pairs={{0,16},{16,0},{1,17},{17,1},{2,18},{18,2},{3,19},{19,3},{4,20},{20... | collective-permute-start | bytes 786440 | tf_op jit(solution)/shard_map/ppermute | solution.py:29
  90.0 8.3 %collective-permute-start.23 = (bf16[512,256]{1,0:T(8,128)(2,1)S(1)}, bf16[512,256]{1,0:T(8,128)(2,1)S(1)}, u32[]{:S(2)}, u32[]{:S(2)}) collective-permute-start(bf16[512,256]{1,0:T(8,128)(2,1)S(1)} %slice.130), channel_id=1, source_target_pairs={{0,8},{8,0},{1,9},{9,1},{2,10},{10,2},{3,11},{11,3},{4,12},{12,4},... | collective-permute-start | bytes 786440 | tf_op jit(solution)/shard_map/ppermute | solution.py:29
  90.7 28.8 %copy-start.37 = (bf16[512,4096]{1,0:T(8,128)(2,1)}, bf16[512,4096]{1,0:T(8,128)(2,1)S(1)}, u32[]{:S(2)}) copy-start(bf16[512,4096]{1,0:T(8,128)(2,1)S(1)} %constant_dynamic-update-slice_fusion.12) | copy-start | bytes 12582916
  94.0 4.8 %collective-permute-start.25 = (bf16[256,256]{1,0:T(8,128)(2,1)S(1)}, bf16[256,256]{1,0:T(8,128)(2,1)S(1)}, u32[]{:S(2)}, u32[]{:S(2)}) collective-permute-start(bf16[256,256]{1,0:T(8,128)(2,1)S(1)} %get-tuple-element.83.refs_2_), channel_id=1, source_target_pairs={{0,4},{4,0},{1,5},{5,1},{2,6},{6,2},{3,7},{7,3},{8,12},{12,8},{9,1... | collective-permute-start | bytes 393224 | tf_op jit(solution)/shard_map/ppermute | solution.py:29
  98.7 1.6 collective-permute-start.26
  98.8 20.7 %copy-start.43 = (bf16[512,256]{1,0:T(8,128)(2,1)}, bf16[512,256]{1,0:T(8,128)(2,1)S(1)}, u32[]{:S(2)}) copy-start(bf16[512,256]{1,0:T(8,128)(2,1)S(1)} %constant_dynamic-update-slice_fusion.14) | copy-start | bytes 786436
  103.2 4.9 %collective-permute-start.28 = (bf16[256,256]{1,0:T(8,128)(2,1)S(1)}, bf16[256,256]{1,0:T(8,128)(2,1)S(1)}, u32[]{:S(2)}, u32[]{:S(2)}) collective-permute-start(bf16[256,256]{1,0:T(8,128)(2,1)S(1)} %get-tuple-element.87.refs_3_), channel_id=1, source_target_pairs={{0,4},{4,0},{1,5},{5,1},{2,6},{6,2},{3,7},{7,3},{8,12},{12,8},{9,1... | collective-permute-start | bytes 393224 | tf_op jit(solution)/shard_map/ppermute | solution.py:29
  104.6 14.9 %collective-permute-start.27 = (bf16[1024,256]{1,0:T(8,128)(2,1)S(1)}, bf16[1024,256]{1,0:T(8,128)(2,1)S(1)}, u32[]{:S(2)}, u32[]{:S(2)}) collective-permute-start(bf16[1024,256]{1,0:T(8,128)(2,1)S(1)} %convolution_convert_fusion.3), channel_id=1, source_target_pairs={{0,8},{8,0},{1,9},{9,1},{2,10},{10,2},{3,11},{11,3},{4,12},{12,4},... | collective-permute-start | bytes 1572872 | tf_op jit(solution)/shard_map/ppermute | solution.py:29
  105.2 5.6 %collective-permute-start.30 = (bf16[256,256]{1,0:T(8,128)(2,1)S(1)}, bf16[256,256]{1,0:T(8,128)(2,1)S(1)}, u32[]{:S(2)}, u32[]{:S(2)}) collective-permute-start(bf16[256,256]{1,0:T(8,128)(2,1)S(1)} %get-tuple-element.89), channel_id=1, source_target_pairs={{0,3},{1,0},{2,1},{3,2},{4,7},{5,4},{6,5},{7,6},{8,11},{9,8},{10,9... | collective-permute-start | bytes 393224 | tf_op jit(solution)/shard_map/ppermute | solution.py:29
  106.9 12.6 %collective-permute-start.31 = (bf16[256,256]{1,0:T(8,128)(2,1)S(1)}, bf16[256,256]{1,0:T(8,128)(2,1)S(1)}, u32[]{:S(2)}, u32[]{:S(2)}) collective-permute-start(bf16[256,256]{1,0:T(8,128)(2,1)S(1)} %get-tuple-element.90), channel_id=1, source_target_pairs={{0,2},{1,3},{2,0},{3,1},{4,6},{5,7},{6,4},{7,5},{8,10},{9,11},{10,... | collective-permute-start | bytes 393224 | tf_op jit(solution)/shard_map/ppermute | solution.py:29
  107.6 11.9 %collective-permute-start.32 = (bf16[256,256]{1,0:T(8,128)(2,1)S(1)}, bf16[256,256]{1,0:T(8,128)(2,1)S(1)}, u32[]{:S(2)}, u32[]{:S(2)}) collective-permute-start(bf16[256,256]{1,0:T(8,128)(2,1)S(1)} %get-tuple-element.91), channel_id=1, source_target_pairs={{0,1},{1,2},{2,3},{3,0},{4,5},{5,6},{6,7},{7,4},{8,9},{9,10},{10,1... | collective-permute-start | bytes 393224 | tf_op jit(solution)/shard_map/ppermute | solution.py:29
  108.6 13.8 %collective-permute-start.29 = (bf16[1024,256]{1,0:T(8,128)(2,1)S(1)}, bf16[1024,256]{1,0:T(8,128)(2,1)}, u32[]{:S(2)}, u32[]{:S(2)}) collective-permute-start(bf16[1024,256]{1,0:T(8,128)(2,1)S(1)} %convolution_convert_fusion.2), channel_id=1, source_target_pairs={{0,16},{16,0},{1,17},{17,1},{2,18},{18,2},{3,19},{19,3},{4,20},{20... | collective-permute-start | bytes 1572872 | tf_op jit(solution)/shard_map/ppermute | solution.py:29
  120.9 15.2 %collective-permute-start.38 = (bf16[1024,256]{1,0:T(8,128)(2,1)}, bf16[1024,256]{1,0:T(8,128)(2,1)}, u32[]{:S(2)}, u32[]{:S(2)}) collective-permute-start(bf16[1024,256]{1,0:T(8,128)(2,1)} %convolution_convert_fusion.1), channel_id=1, source_target_pairs={{0,8},{8,0},{1,9},{9,1},{2,10},{10,2},{3,11},{11,3},{4,12},{12,4},... | collective-permute-start | bytes 1572872 | tf_op jit(solution)/shard_map/ppermute | solution.py:29
  121.4 15.2 %collective-permute-start.37 = (bf16[1024,256]{1,0:T(8,128)(2,1)}, bf16[1024,256]{1,0:T(8,128)(2,1)}, u32[]{:S(2)}, u32[]{:S(2)}) collective-permute-start(bf16[1024,256]{1,0:T(8,128)(2,1)} %fusion.3), channel_id=1, source_target_pairs={{0,16},{16,0},{1,17},{17,1},{2,18},{18,2},{3,19},{19,3},{4,20},{20... | collective-permute-start | bytes 1572872 | tf_op jit(solution)/shard_map/ppermute | solution.py:29
  124.3 2.1 %collective-permute-start.33 = (bf16[256,256]{1,0:T(8,128)(2,1)}, bf16[256,256]{1,0:T(8,128)(2,1)S(1)}, u32[]{:S(2)}, u32[]{:S(2)}) collective-permute-start(bf16[256,256]{1,0:T(8,128)(2,1)} %undo_keys.1.refs_4_), channel_id=1, source_target_pairs={{0,4},{4,0},{1,5},{5,1},{2,6},{6,2},{3,7},{7,3},{8,12},{12,8},{9,1... | collective-permute-start | bytes 393224 | tf_op jit(solution)/shard_map/ppermute | solution.py:29
  127.8 12.6 %collective-permute-start.35 = (bf16[512,256]{1,0:T(8,128)(2,1)S(1)}, bf16[512,256]{1,0:T(8,128)(2,1)S(1)}, u32[]{:S(2)}, u32[]{:S(2)}) collective-permute-start(bf16[512,256]{1,0:T(8,128)(2,1)S(1)} %convolution_convert_fusion.6), channel_id=1, source_target_pairs={{0,16},{16,0},{1,17},{17,1},{2,18},{18,2},{3,19},{19,3},{4,20},{20... | collective-permute-start | bytes 786440 | tf_op jit(solution)/shard_map/ppermute | solution.py:29
  129.5 10.9 %collective-permute-start.34 = (bf16[512,256]{1,0:T(8,128)(2,1)S(1)}, bf16[512,256]{1,0:T(8,128)(2,1)S(1)}, u32[]{:S(2)}, u32[]{:S(2)}) collective-permute-start(bf16[512,256]{1,0:T(8,128)(2,1)S(1)} %convolution_convert_fusion.7), channel_id=1, source_target_pairs={{0,8},{8,0},{1,9},{9,1},{2,10},{10,2},{3,11},{11,3},{4,12},{12,4},... | collective-permute-start | bytes 786440 | tf_op jit(solution)/shard_map/ppermute | solution.py:29
  140.4 12.2 %collective-permute-start.39 = (bf16[1024,256]{1,0:T(8,128)(2,1)S(1)}, bf16[1024,256]{1,0:T(8,128)(2,1)S(1)}, u32[]{:S(2)}, u32[]{:S(2)}) collective-permute-start(bf16[1024,256]{1,0:T(8,128)(2,1)S(1)} %copy-done.48), channel_id=1, source_target_pairs={{0,16},{16,0},{1,17},{17,1},{2,18},{18,2},{3,19},{19,3},{4,20},{20... | collective-permute-start | bytes 1572872 | tf_op jit(solution)/shard_map/ppermute | solution.py:29
  141.2 12.7 %collective-permute-start.40 = (bf16[1024,256]{1,0:T(8,128)(2,1)S(1)}, bf16[1024,256]{1,0:T(8,128)(2,1)S(1)}, u32[]{:S(2)}, u32[]{:S(2)}) collective-permute-start(bf16[1024,256]{1,0:T(8,128)(2,1)S(1)} %fusion.5), channel_id=1, source_target_pairs={{0,8},{8,0},{1,9},{9,1},{2,10},{10,2},{3,11},{11,3},{4,12},{12,4},... | collective-permute-start | bytes 1572872 | tf_op jit(solution)/shard_map/ppermute | solution.py:29
  142.4 11.4 %collective-permute-start.41 = (bf16[256,256]{1,0:T(8,128)(2,1)S(1)}, bf16[256,256]{1,0:T(8,128)(2,1)S(1)}, u32[]{:S(2)}, u32[]{:S(2)}) collective-permute-start(bf16[256,256]{1,0:T(8,128)(2,1)S(1)} %get-tuple-element.114), channel_id=1, source_target_pairs={{0,3},{1,0},{2,1},{3,2},{4,7},{5,4},{6,5},{7,6},{8,11},{9,8},{10,9... | collective-permute-start | bytes 393224 | tf_op jit(solution)/shard_map/ppermute | solution.py:29
  144.0 9.8 %collective-permute-start.42 = (bf16[256,256]{1,0:T(8,128)(2,1)S(1)}, bf16[256,256]{1,0:T(8,128)(2,1)S(1)}, u32[]{:S(2)}, u32[]{:S(2)}) collective-permute-start(bf16[256,256]{1,0:T(8,128)(2,1)S(1)} %get-tuple-element.113), channel_id=1, source_target_pairs={{0,2},{1,3},{2,0},{3,1},{4,6},{5,7},{6,4},{7,5},{8,10},{9,11},{10,... | collective-permute-start | bytes 393224 | tf_op jit(solution)/shard_map/ppermute | solution.py:29
  148.3 33.1 %collective-permute-start.36 = (bf16[256,4096]{1,0:T(8,128)(2,1)S(1)}, bf16[256,4096]{1,0:T(8,128)(2,1)S(1)}, u32[]{:S(2)}, u32[]{:S(2)}) collective-permute-start(bf16[256,4096]{1,0:T(8,128)(2,1)S(1)} %grad_columns.1), channel_id=1, source_target_pairs={{0,4},{4,0},{1,5},{5,1},{2,6},{6,2},{3,7},{7,3},{8,12},{12,8},{9,1... | collective-permute-start | bytes 6291464 | tf_op jit(solution)/shard_map/ppermute | solution.py:29
  149.1 20.6 %copy-start.32 = (bf16[256,256]{1,0:T(8,128)(2,1)S(1)}, bf16[256,256]{1,0:T(8,128)(2,1)}, u32[]{:S(2)}) copy-start(bf16[256,256]{1,0:T(8,128)(2,1)} %copy-done.31) | copy-start | bytes 393220
  149.1 20.6 %copy-start.34 = (bf16[256,256]{1,0:T(8,128)(2,1)S(1)}, bf16[256,256]{1,0:T(8,128)(2,1)}, u32[]{:S(2)}) copy-start(bf16[256,256]{1,0:T(8,128)(2,1)} %copy-done.33) | copy-start | bytes 393220
  152.6 6.8 %collective-permute-start.43 = (bf16[256,256]{1,0:T(8,128)(2,1)S(1)}, bf16[256,256]{1,0:T(8,128)(2,1)S(1)}, u32[]{:S(2)}, u32[]{:S(2)}) collective-permute-start(bf16[256,256]{1,0:T(8,128)(2,1)S(1)} %get-tuple-element.112), channel_id=1, source_target_pairs={{0,1},{1,2},{2,3},{3,0},{4,5},{5,6},{6,7},{7,4},{8,9},{9,10},{10,1... | collective-permute-start | bytes 393224 | tf_op jit(solution)/shard_map/ppermute | solution.py:29
  159.5 10.2 %collective-permute-start.45 = (bf16[1024,256]{1,0:T(8,128)(2,1)S(1)}, bf16[1024,256]{1,0:T(8,128)(2,1)S(1)}, u32[]{:S(2)}, u32[]{:S(2)}) collective-permute-start(bf16[1024,256]{1,0:T(8,128)(2,1)S(1)} %pad_maximum_fusion.1), channel_id=1, source_target_pairs={{0,8},{8,0},{1,9},{9,1},{2,10},{10,2},{3,11},{11,3},{4,12},{12,4},... | collective-permute-start | bytes 1572872 | tf_op jit(solution)/shard_map/ppermute | solution.py:29
  160.3 10.1 %collective-permute-start.44 = (bf16[1024,256]{1,0:T(8,128)(2,1)S(1)}, bf16[1024,256]{1,0:T(8,128)(2,1)S(1)}, u32[]{:S(2)}, u32[]{:S(2)}) collective-permute-start(bf16[1024,256]{1,0:T(8,128)(2,1)S(1)} %pad_maximum_fusion), channel_id=1, source_target_pairs={{0,16},{16,0},{1,17},{17,1},{2,18},{18,2},{3,19},{19,3},{4,20},{20... | collective-permute-start | bytes 1572872 | tf_op jit(solution)/shard_map/ppermute | solution.py:29
  162.0 19.4 %copy-start.22 = (bf16[256,256]{1,0:T(8,128)(2,1)S(1)}, bf16[256,256]{1,0:T(8,128)(2,1)}, u32[]{:S(2)}) copy-start(bf16[256,256]{1,0:T(8,128)(2,1)} %copy-done.21) | copy-start | bytes 393220
  162.0 19.4 %copy-start.35 = (s32[2,4]{1,0:T(2,128)S(1)}, s32[2,4]{1,0:T(2,128)}, u32[]{:S(2)}) copy-start(s32[2,4]{1,0:T(2,128)} %pad_add_fusion.1.piece_ref.refs_1_) | copy-start | bytes 100
  162.0 19.4 %copy-start.36 = (s32[4]{0:T(128)S(1)}, s32[4]{0:T(128)}, u32[]{:S(2)}) copy-start(s32[4]{0:T(128)} %fusion.26.slab_ref.refs_0_) | copy-start | bytes 52
  162.1 8.3 %collective-permute-start.46 = (bf16[256,256]{1,0:T(8,128)(2,1)S(1)}, bf16[256,256]{1,0:T(8,128)(2,1)S(1)}, u32[]{:S(2)}, u32[]{:S(2)}) collective-permute-start(bf16[256,256]{1,0:T(8,128)(2,1)S(1)} %get-tuple-element.118), channel_id=1, source_target_pairs={{0,3},{1,0},{2,1},{3,2},{4,7},{5,4},{6,5},{7,6},{8,11},{9,8},{10,9... | collective-permute-start | bytes 393224 | tf_op jit(solution)/shard_map/ppermute | solution.py:29
  162.1 8.3 %collective-permute-start.47 = (bf16[256,256]{1,0:T(8,128)(2,1)S(1)}, bf16[256,256]{1,0:T(8,128)(2,1)S(1)}, u32[]{:S(2)}, u32[]{:S(2)}) collective-permute-start(bf16[256,256]{1,0:T(8,128)(2,1)S(1)} %get-tuple-element.117), channel_id=1, source_target_pairs={{0,2},{1,3},{2,0},{3,1},{4,6},{5,7},{6,4},{7,5},{8,10},{9,11},{10,... | collective-permute-start | bytes 393224 | tf_op jit(solution)/shard_map/ppermute | solution.py:29
  169.7 8.2 %collective-permute-start.48 = (bf16[256,256]{1,0:T(8,128)(2,1)S(1)}, bf16[256,256]{1,0:T(8,128)(2,1)S(1)}, u32[]{:S(2)}, u32[]{:S(2)}) collective-permute-start(bf16[256,256]{1,0:T(8,128)(2,1)S(1)} %get-tuple-element.116), channel_id=1, source_target_pairs={{0,1},{1,2},{2,3},{3,0},{4,5},{5,6},{6,7},{7,4},{8,9},{9,10},{10,1... | collective-permute-start | bytes 393224 | tf_op jit(solution)/shard_map/ppermute | solution.py:29
  178.4 9.1 %collective-permute-start.49 = (bf16[256,256]{1,0:T(8,128)(2,1)S(1)}, bf16[256,256]{1,0:T(8,128)(2,1)S(1)}, u32[]{:S(2)}, u32[]{:S(2)}) collective-permute-start(bf16[256,256]{1,0:T(8,128)(2,1)S(1)} %get-tuple-element.110), channel_id=1, source_target_pairs={{0,3},{1,0},{2,1},{3,2},{4,7},{5,4},{6,5},{7,6},{8,11},{9,8},{10,9... | collective-permute-start | bytes 393224 | tf_op jit(solution)/shard_map/ppermute | solution.py:29
  178.5 9.1 %collective-permute-start.50 = (bf16[256,256]{1,0:T(8,128)(2,1)S(1)}, bf16[256,256]{1,0:T(8,128)(2,1)S(1)}, u32[]{:S(2)}, u32[]{:S(2)}) collective-permute-start(bf16[256,256]{1,0:T(8,128)(2,1)S(1)} %get-tuple-element.109), channel_id=1, source_target_pairs={{0,2},{1,3},{2,0},{3,1},{4,6},{5,7},{6,4},{7,5},{8,10},{9,11},{10,... | collective-permute-start | bytes 393224 | tf_op jit(solution)/shard_map/ppermute | solution.py:29
  178.6 9.0 %collective-permute-start.51 = (bf16[256,256]{1,0:T(8,128)(2,1)S(1)}, bf16[256,256]{1,0:T(8,128)(2,1)S(1)}, u32[]{:S(2)}, u32[]{:S(2)}) collective-permute-start(bf16[256,256]{1,0:T(8,128)(2,1)S(1)} %get-tuple-element.108), channel_id=1, source_target_pairs={{0,1},{1,2},{2,3},{3,0},{4,5},{5,6},{6,7},{7,4},{8,9},{9,10},{10,1... | collective-permute-start | bytes 393224 | tf_op jit(solution)/shard_map/ppermute | solution.py:29
  (37 other events, 275.2 us)

commit v5 on v4

--- a/solution.py
+++ b/solution.py
@@ -113,12 +113,18 @@
     return arrived, went
 
 
-def reduce_line(term, last=()):
+def send_line(term):
     size = lax.axis_size("ctx")
     rows = term.shape[0] // size
-    total = after(term[:rows], *last).astype(jnp.float32)
-    for k in range(1, size):
-        total = total + shift(term[k * rows : (k + 1) * rows], "ctx", -k).astype(jnp.float32)
+    return [term[:rows]] + [
+        shift(term[k * rows : (k + 1) * rows], "ctx", -k) for k in range(1, size)
+    ]
+
+
+def add_line(pieces, last=()):
+    total = after(pieces[0], *last).astype(jnp.float32)
+    for piece in pieces[1:]:
+        total = total + piece.astype(jnp.float32)
     return total
 
 
@@ -475,8 +481,12 @@
 
     q_local = [after(local, theirs) for local in q_local]
     q_line = [jnp.concatenate(gather_line(local), axis=0) for local in q_local]
+    positions = after(positions, kv_line)
+    own_positions = lax.dynamic_slice_in_dim(positions, place * rows, rows)
+    cos_table, sin_table = rope_tables(own_positions, head_dim)
+    sin_table = jnp.where(jnp.arange(head_dim) < head_dim // 2, -sin_table, sin_table)
     kv_sides = along(kv_line, "a"), along(kv_line, "b")
-    stage = kv_sides[0] + kv_sides[1] + q_line[:1]
+    stage = kv_sides[0] + kv_sides[1] + q_line[:1] + [cos_table, sin_table]
     kv_corners = gather_corners(*kv_sides, "b", *stage)
     q0_a = along(after(q_line[0], *stage), "a")
     stage = q0_a + [piece for corner in kv_corners.values() for piece in corner]
@@ -484,10 +494,6 @@
     q0_b = along(after(q_line[0], *stage), "b")
     kv_slabs = in_order(kv_line, *kv_sides, kv_corners)
 
-    positions = after(positions, kv_line)
-    own_positions = lax.dynamic_slice_in_dim(positions, place * rows, rows)
-    cos_table, sin_table = rope_tables(own_positions, head_dim)
-    sin_table = jnp.where(jnp.arange(head_dim) < head_dim // 2, -sin_table, sin_table)
     key_positions = jnp.concatenate(
         [
             lax.dynamic_slice_in_dim(positions, ((place + ctx - k) % ctx) * rows, rows)
@@ -526,8 +532,9 @@
     q0_corners = gather_corners(q0_a, q0_b, "a", *stage)
     q1_b = along(after(q_line[1], *stage), "b")
     part = project_early(in_order(q_line[0], q0_a, q0_b, q0_corners))
-    key_values = gather_line(key_value)
-    stage = q1_b + key_values + [piece for corner in q0_corners.values() for piece in corner]
+    corners = [piece for corner in q0_corners.values() for piece in corner]
+    key_values = gather_line(after(key_value, *corners))
+    stage = q1_b + [piece for corner in q0_corners.values() for piece in corner]
     q1_corners = gather_corners(q1_a, q1_b, "both", *stage)
     q_slabs = [
         in_order(q_line[0], q0_a, q0_b, q0_corners),
@@ -574,10 +581,11 @@
     third = [*came[2][0].values(), *came[2][1].values()]
     sides1, went1 = reduce_sides(made[1], came[1], "a", mid, *sides0, *third)
     line0 = after(made[0](0, slice(None), sides0), *went1)
-    q_grads = [reduce_line(line0, sides1)]
+    sent0 = send_line(line0)
+    q_grads = [add_line(sent0, sides1)]
     line1 = made[1](0, slice(None), sides1)
-    kv_sides, _ = reduce_sides(made[2], came[2], "both", mid, *sides1, q_grads[0])
-    q_grads.append(reduce_line(line1, kv_sides))
+    kv_sides, _ = reduce_sides(made[2], came[2], "both", mid, *sides1, *sent0[1:-1])
+    q_grads.append(add_line(send_line(line1), kv_sides))
 
     weights = [*q_slabs, kv_slabs]
     grad_theirs = grad_columns(
@@ -587,8 +595,8 @@
     grad_input = grad_place(
         [gradients[0][0], gradients[1][0], gradients[2][0]], weights, grad_theirs, slabs, pieces, block
     )
-    kv_line = after(made[2](0, slice(None), kv_sides), q_grads[1])
-    kv_wgrad = reduce_line(kv_line, (grad_input,))
+    kv_term = after(made[2](0, slice(None), kv_sides), *q_grads)
+    kv_wgrad = add_line(send_line(kv_term), (grad_input,))
 
     query_grad = jnp.concatenate(q_grads, axis=1)
     key_grad = kv_wgrad[:, :head_dim]

time: 189 us -> 191 us (1.011)
  Pallas kernels: 32.4 us -> 35.3 us
  starting transfers between devices: 58.7 us -> 61 us
  waiting for transfers between devices: 61.5 us -> 59.2 us
    pallas_call x5, Pallas kernels: 7.97 us -> 11.2 us  [project_rows(): pl.pallas_call(functools.partial(project_kernel, counts=[len(slab) for sl...]
    ppermute x52, starting transfers between devices: 58.7 us -> 61 us  [shift(): lax.ppermute(block, axis, [(i, (i + step) % size) for i in range(size)])]
    ppermute x52, waiting for transfers between devices: 61.5 us -> 59.2 us  [shift(): lax.ppermute(block, axis, [(i, (i + step) % size) for i in range(size)])]
    unnamed x110 -> x104, local copies, waits for them, and re-layouts: 9.58 us -> 7.52 us
  transfers between devices with their start and end apart: 52 -> 52, of which waited for: 17 -> 23; matrix products, arithmetic and copies ran while one was open for 13% -> 14% of each run, Pallas kernels for 16% -> 19%
where the time goes in v5:
time: 191 us; the launch traced here: 190 us
  starting transfers between devices  61 us (32%)
  waiting for transfers between devices  59.2 us (31%)
  Pallas kernels  35.3 us (18%)
  local copies, waits for them, and re-layouts  13 us (7%)
  matrix products  12.8 us (7%)
  other arithmetic  6.97 us (4%)
    ppermute x52, starting transfers between devices, shift(): lax.ppermute(block, axis, [(i, (i + step) % size) for i in range(size)])  61 us
    ppermute x52, waiting for transfers between devices, shift(): lax.ppermute(block, axis, [(i, (i + step) % size) for i in range(size)])  59.2 us
    dot_general x15, matrix products, mm(): lax.dot_general(a, b, (dims, ((), ())), preferred_element_type=jnp.float32)  12.8 us
    pallas_call x5, Pallas kernels, project_rows(): pl.pallas_call(functools.partial(project_kernel, counts=[len(slab) for sl...  11.2 us
    unnamed x104, local copies, waits for them, and re-layouts  7.52 us
    pallas_call x1, Pallas kernels, grad_place(): pl.pallas_call(functools.partial(grad_place_kernel, shape=shape, plane=pl...  5.98 us
    pallas_call x1, Pallas kernels, pick_columns(): pl.pallas_call(functools.partial(pick_kernel, block=block), grid_spec=plt...  5.62 us
    pallas_call x2, Pallas kernels, attend(): pl.pallas_call(functools.partial(attend_kernel, group=group, parts=parts,...  5.45 us
  transfers between devices with their start and end apart: 52, of which 23 were waited for; matrix products, arithmetic and copies ran while one was open for 14% of the time, Pallas kernels for 19%

profile of v5, /device:TPU:0, one launch (start us, length us, event | category | flops | bytes accessed | tf_op | source)
XLA Modules:
  0.0 190.0 jit_solution(1892161172584575239)
XLA Ops:
  2.6 3.1 %collective-permute-start = (bf16[256,256]{1,0:T(8,128)(2,1)S(1)}, bf16[256,256]{1,0:T(8,128)(2,1)}, u32[]{:S(2)}, u32[]{:S(2)}) collective-permute-start(bf16[256,256]{1,0:T(8,128)(2,1)S(1)} %pad_maximum_fusion.4), channel_id=1, source_target_pairs={{0,1},{1,2},{2,3},{3,0},{4,5},{5,6},{6,7},{7,4},{8,9},{9,10},{10,1... | collective-permute-start | bytes 393224 | tf_op jit(solution)/shard_map/ppermute | solution.py:29
  5.6 2.6 %collective-permute-start.1 = (bf16[256,256]{1,0:T(8,128)(2,1)S(1)}, bf16[256,256]{1,0:T(8,128)(2,1)S(1)}, u32[]{:S(2)}, u32[]{:S(2)}) collective-permute-start(bf16[256,256]{1,0:T(8,128)(2,1)S(1)} %pad_maximum_fusion.4), channel_id=1, source_target_pairs={{0,2},{1,3},{2,0},{3,1},{4,6},{5,7},{6,4},{7,5},{8,10},{9,11},{10,... | collective-permute-start | bytes 393224 | tf_op jit(solution)/shard_map/ppermute | solution.py:29
  8.2 1.3 collective-permute-start.2
  11.0 5.6 %pick_columns.1 = (bf16[256,4096]{1,0:T(8,128)(2,1)}, bf16[256,4096]{1,0:T(8,128)(2,1)}) custom-call(s32[4]{0:T(128)} %fusion.26.slab_ref.refs_0_, s32[2,4]{1,0:T(2,128)} %pad_add_fusion.1.piece_ref.refs_1_, bf16[256,8192]{1,0:T(8,128)(2,1)} %bitcast.17), custom_call_target="tpu_custom_call" | custom-call | bytes 8388608 | tf_op jit(solution)/shard_map/pick_columns/pallas_call | solution.py:211
  16.6 1.1 constant_dynamic-update-slice_fusion.2
  18.0 1.6 collective-permute-start.7
  19.6 1.5 collective-permute-start.8
  22.3 2.4 %collective-permute-start.4 = (bf16[256,256]{1,0:T(8,128)(2,1)S(1)}, bf16[256,256]{1,0:T(8,128)(2,1)S(1)}, u32[]{:S(2)}, u32[]{:S(2)}) collective-permute-start(bf16[256,256]{1,0:T(8,128)(2,1)S(1)} %get-tuple-element.60), channel_id=1, source_target_pairs={{0,1},{1,2},{2,3},{3,0},{4,5},{5,6},{6,7},{7,4},{8,9},{9,10},{10,1... | collective-permute-start | bytes 393224 | tf_op jit(solution)/shard_map/ppermute | solution.py:29
  24.7 1.3 negate_select_fusion
  26.0 1.7 collective-permute-start.5
  28.6 1.7 collective-permute-done.4
  30.3 5.1 %collective-permute-done.5 = bf16[256,256]{1,0:T(8,128)(2,1)S(1)} collective-permute-done((bf16[256,256]{1,0:T(8,128)(2,1)S(1)}, bf16[256,256]{1,0:T(8,128)(2,1)S(1)}, u32[]{:S(2)}, u32[]{:S(2)}) %collective-permute-start.5) | collective-permute-done | bytes 131104 | tf_op jit(solution)/shard_map/ppermute | solution.py:29
  35.7 1.6 collective-permute-start.9
  37.3 1.5 collective-permute-start.10
  38.8 3.1 %collective-permute-start.12 = (bf16[256,256]{1,0:T(8,128)(2,1)S(1)}, bf16[256,256]{1,0:T(8,128)(2,1)S(1)}, u32[]{:S(2)}, u32[]{:S(2)}) collective-permute-start(bf16[256,256]{1,0:T(8,128)(2,1)S(1)} %get-tuple-element.65), channel_id=1, source_target_pairs={{0,1},{1,2},{2,3},{3,0},{4,5},{5,6},{6,7},{7,4},{8,9},{9,10},{10,1... | collective-permute-start | bytes 393224 | tf_op jit(solution)/shard_map/ppermute | solution.py:29
  41.8 1.3 collective-permute-start.13
  43.8 1.1 collective-permute-start.14
  44.9 2.1 %collective-permute-done.12 = bf16[256,256]{1,0:T(8,128)(2,1)S(1)} collective-permute-done((bf16[256,256]{1,0:T(8,128)(2,1)S(1)}, bf16[256,256]{1,0:T(8,128)(2,1)S(1)}, u32[]{:S(2)}, u32[]{:S(2)}) %collective-permute-start.12) | collective-permute-done | bytes 131104 | tf_op jit(solution)/shard_map/ppermute | solution.py:29
  47.6 3.6 %collective-permute-done.13 = bf16[256,256]{1,0:T(8,128)(2,1)S(1)} collective-permute-done((bf16[256,256]{1,0:T(8,128)(2,1)S(1)}, bf16[256,256]{1,0:T(8,128)(2,1)S(1)}, u32[]{:S(2)}, u32[]{:S(2)}) %collective-permute-start.13) | collective-permute-done | bytes 131104 | tf_op jit(solution)/shard_map/ppermute | solution.py:29
  54.5 1.0 copy-done.5
  55.5 2.8 %project_rows.5 = (f32[256,256]{1,0:T(8,128)S(1)}, f32[256,256]{1,0:T(8,128)S(1)}) custom-call(bf16[256,4096]{1,0:T(8,128)(2,1)S(1)} %copy-done, bf16[256,4096]{1,0:T(8,128)(2,1)} %collective-permute-done.3.refs_1_.refs_3_.refs_5_.refs_7_, bf16[256,4096]{1,0:T(8,128)(2,1)S(1)} %copy-done, ...), custom_call_target="tpu_custom_call" | custom-call | flops 1073741824 | bytes 6291456 | tf_op jit(solution)/shard_map/project_rows/pallas_call | solution.py:312
  59.9 1.5 collective-permute-done.16.other
  62.1 1.9 finish_keys.1.refs_7_
  64.0 3.3 %collective-permute-done.11.refs_7_.refs_4_.refs_6_ = bf16[1024,256]{1,0:T(8,128)(2,1)} collective-permute-done((bf16[1024,256]{1,0:T(8,128)(2,1)S(1)}, bf16[1024,256]{1,0:T(8,128)(2,1)}, u32[]{:S(2)}, u32[]{:S(2)}) %collective-permute-start.11) | collective-permute-done | bytes 524320 | tf_op jit(solution)/shard_map/ppermute | solution.py:29
  68.2 1.7 fusion.37
  70.0 1.6 collective-permute-start.22
  71.6 9.1 %collective-permute-done.17.refs_2_.refs_6_.refs_8_ = bf16[1024,256]{1,0:T(8,128)(2,1)} collective-permute-done((bf16[1024,256]{1,0:T(8,128)(2,1)}, bf16[1024,256]{1,0:T(8,128)(2,1)}, u32[]{:S(2)}, u32[]{:S(2)}) %collective-permute-start.17) | collective-permute-done | bytes 524320 | tf_op jit(solution)/shard_map/ppermute | solution.py:29
  80.7 2.8 %collective-permute-start.19 = (bf16[256,256]{1,0:T(8,128)(2,1)}, bf16[256,256]{1,0:T(8,128)(2,1)S(1)}, u32[]{:S(2)}, u32[]{:S(2)}) collective-permute-start(bf16[256,256]{1,0:T(8,128)(2,1)} %finish_keys.1.refs_7_), channel_id=1, source_target_pairs={{0,1},{1,2},{2,3},{3,0},{4,5},{5,6},{6,7},{7,4},{8,9},{9,10},{10,1... | collective-permute-start | bytes 393224 | tf_op jit(solution)/shard_map/ppermute | solution.py:29
  83.7 2.6 %project_rows.6 = (f32[256,256]{1,0:T(8,128)S(1)}, f32[256,256]{1,0:T(8,128)S(1)}) custom-call(bf16[256,4096]{1,0:T(8,128)(2,1)S(1)} %copy-done, bf16[256,4096]{1,0:T(8,128)(2,1)} %collective-permute-done.3.refs_1_.refs_3_.refs_5_.refs_7_, bf16[256,4096]{1,0:T(8,128)(2,1)S(1)} %copy-done, ...), custom_call_target="tpu_custom_call" | custom-call | flops 805306368 | bytes 4718592 | tf_op jit(solution)/shard_map/project_rows/pallas_call | solution.py:312
  86.5 2.3 %collective-permute-start.21 = (bf16[256,256]{1,0:T(8,128)(2,1)S(1)}, bf16[256,256]{1,0:T(8,128)(2,1)S(1)}, u32[]{:S(2)}, u32[]{:S(2)}) collective-permute-start(bf16[256,256]{1,0:T(8,128)(2,1)S(1)} %copy-done.27), channel_id=1, source_target_pairs={{0,3},{1,0},{2,1},{3,2},{4,7},{5,4},{6,5},{7,6},{8,11},{9,8},{10,9... | collective-permute-start | bytes 393224 | tf_op jit(solution)/shard_map/ppermute | solution.py:29
  88.8 1.7 project_rows.7
  91.2 1.4 collective-permute-start.23
  92.6 1.8 constant_dynamic-update-slice_fusion.12
  94.7 2.6 %attend.2 = (bf16[256,256]{1,0:T(8,128)(2,1)S(1)}, bf16[256,256]{1,0:T(8,128)(2,1)S(1)}, f32[1024,256]{1,0:T(8,128)S(1)}) custom-call(f32[256,256]{1,0:T(8,128)S(1)} %get-tuple-element.72.refs_0_, f32[256,256]{1,0:T(8,128)S(1)} %collective-permute-done.18.refs_1_, bf16[256,256]{1,0:T(8,128)(2,1)S(1)} %copy-done.29, f32[256,128]{1,0:T(8,128)S(1)} %copy-done.19, ...), custom_call_target="tpu_custom_call" | custom-call | flops 939524096 | bytes 2097152 | tf_op jit(solution)/shard_map/attend/pallas_call | solution.py:395
  97.4 2.5 %project_rows.8 = (f32[256,256]{1,0:T(8,128)S(1)}, f32[256,256]{1,0:T(8,128)S(1)}) custom-call(bf16[256,4096]{1,0:T(8,128)(2,1)S(1)} %copy-done, bf16[256,4096]{1,0:T(8,128)(2,1)} %collective-permute-done.3.refs_1_.refs_3_.refs_5_.refs_7_, bf16[256,4096]{1,0:T(8,128)(2,1)S(1)} %copy-done, ...), custom_call_target="tpu_custom_call" | custom-call | flops 805306368 | bytes 4718592 | tf_op jit(solution)/shard_map/project_rows/pallas_call | solution.py:312
  100.0 1.6 project_rows.9
  102.7 1.5 collective-permute-start.27
  104.2 1.3 convolution_convert_fusion.1
  105.5 2.9 %attend.3 = (bf16[256,256]{1,0:T(8,128)(2,1)S(1)}, bf16[256,256]{1,0:T(8,128)(2,1)S(1)}, f32[256,256]{1,0:T(8,128)S(1)}, bf16[256,256]{1,0:T(8,128)(2,1)S(1)}, b...) custom-call(f32[256,256]{1,0:T(8,128)S(1)} %get-tuple-element.86.refs_0_, ...), custom_call_target="tpu_custom_call" | custom-call | flops 939524096 | bytes 2097152 | tf_op jit(solution)/shard_map/attend/pallas_call | solution.py:395
  108.5 2.8 %collective-permute-start.30 = (bf16[256,256]{1,0:T(8,128)(2,1)S(1)}, bf16[256,256]{1,0:T(8,128)(2,1)S(1)}, u32[]{:S(2)}, u32[]{:S(2)}) collective-permute-start(bf16[256,256]{1,0:T(8,128)(2,1)S(1)} %get-tuple-element.91), channel_id=1, source_target_pairs={{0,3},{1,0},{2,1},{3,2},{4,7},{5,4},{6,5},{7,6},{8,11},{9,8},{10,9... | collective-permute-start | bytes 393224 | tf_op jit(solution)/shard_map/ppermute | solution.py:29
  113.8 1.3 convolution_convert_fusion
  115.1 9.1 %collective-permute-done.31.refs_2_ = bf16[256,256]{1,0:T(8,128)(2,1)S(1)} collective-permute-done((bf16[256,256]{1,0:T(8,128)(2,1)S(1)}, bf16[256,256]{1,0:T(8,128)(2,1)S(1)}, u32[]{:S(2)}, u32[]{:S(2)}) %collective-permute-start.31) | collective-permute-done | bytes 131104 | tf_op jit(solution)/shard_map/ppermute | solution.py:29
  124.3 1.3 fusion.3
  127.1 2.0 %undo_keys.1.refs_4_ = bf16[256,256]{1,0:T(8,128)(2,1)} custom-call(f32[256,256]{1,0:T(8,128)} %copy-done.26, bf16[256,256]{1,0:T(8,128)(2,1)} %copy-done.36, bf16[256,256]{1,0:T(8,128)(2,1)} %copy-done.37, bf16[256,256]{1,0:T(8,128)(2,1)} %copy-done.38, f32[256,128]{1,0:T(8,128)} %get-tuple-element.128.cos_ref.refs_3_.refs_4_, ...), custom_call_target="tpu_custom_call" | custom-call | tf_op jit(solution)/shard_map/undo_keys/pallas_call | solution.py:446
  129.2 2.0 %fusion.5 = bf16[1024,256]{1,0:T(8,128)(2,1)S(1)} fusion(bf16[512,256]{1,0:T(8,128)(2,1)S(1)} %constant_dynamic-update-slice_fusion.16, bf16[1024,256]{1,0:T(8,128)(2,1)} %collective-permute-done.29, bf16[512,4096]{1,0:T(8,128)(2,1)} %copy-done.32), kind=kOutput, calls=%fused_computation.14 | convolution fusion | flops 269221888 | bytes 2359296 | tf_op jit(solution)/shard_map/dot_general | solution.py:24
  131.2 1.4 convolution_convert_fusion.6
  132.7 1.2 collective-permute-start.35
  134.3 1.5 collective-permute-start.34
  136.5 4.3 %collective-permute-done.38 = bf16[1024,256]{1,0:T(8,128)(2,1)} collective-permute-done((bf16[1024,256]{1,0:T(8,128)(2,1)}, bf16[1024,256]{1,0:T(8,128)(2,1)}, u32[]{:S(2)}, u32[]{:S(2)}) %collective-permute-start.38) | collective-permute-done | bytes 524320 | tf_op jit(solution)/shard_map/ppermute | solution.py:29
  141.4 1.7 fusion.4
  143.1 2.2 %collective-permute-done.35 = bf16[512,256]{1,0:T(8,128)(2,1)S(1)} collective-permute-done((bf16[512,256]{1,0:T(8,128)(2,1)S(1)}, bf16[512,256]{1,0:T(8,128)(2,1)S(1)}, u32[]{:S(2)}, u32[]{:S(2)}) %collective-permute-start.35) | collective-permute-done | bytes 262176 | tf_op jit(solution)/shard_map/ppermute | solution.py:29
  145.8 1.5 collective-permute-start.40
  147.3 1.8 collective-permute-start.41
  149.3 3.2 %grad_columns.1 = bf16[256,4096]{1,0:T(8,128)(2,1)S(1)} custom-call(bf16[256,256]{1,0:T(8,128)(2,1)S(1)} %copy-done.23, bf16[256,256]{1,0:T(8,128)(2,1)S(1)} %collective-permute-done.28.refs_1_, bf16[256,256]{1,0:T(8,128)(2,1)S(1)} %collective-permute-done.33.refs_2_, bf16[1024,256]{1,0:T(8,128)(2,1)S(1)} %copy-done.3, ...), custom_call_target="tpu_custom_call" | custom-call | flops 1610612736 | bytes 8388608 | tf_op jit(solution)/shard_map/grad_columns/pallas_call | solution.py:233
  153.4 3.2 %collective-permute-start.43 = (bf16[256,256]{1,0:T(8,128)(2,1)S(1)}, bf16[256,256]{1,0:T(8,128)(2,1)S(1)}, u32[]{:S(2)}, u32[]{:S(2)}) collective-permute-start(bf16[256,256]{1,0:T(8,128)(2,1)S(1)} %get-tuple-element.114), channel_id=1, source_target_pairs={{0,1},{1,2},{2,3},{3,0},{4,5},{5,6},{6,7},{7,4},{8,9},{9,10},{10,1... | collective-permute-start | bytes 393224 | tf_op jit(solution)/shard_map/ppermute | solution.py:29
  157.9 1.4 collective-permute-start.45
  159.3 1.5 collective-permute-start.44
  161.4 1.7 collective-permute-start.46
  164.0 6.0 %collective-permute-done.45 = bf16[1024,256]{1,0:T(8,128)(2,1)S(1)} collective-permute-done((bf16[1024,256]{1,0:T(8,128)(2,1)S(1)}, bf16[1024,256]{1,0:T(8,128)(2,1)S(1)}, u32[]{:S(2)}, u32[]{:S(2)}) %collective-permute-start.45) | collective-permute-done | bytes 524320 | tf_op jit(solution)/shard_map/ppermute | solution.py:29
  170.0 2.0 %collective-permute-start.48 = (bf16[256,256]{1,0:T(8,128)(2,1)S(1)}, bf16[256,256]{1,0:T(8,128)(2,1)S(1)}, u32[]{:S(2)}, u32[]{:S(2)}) collective-permute-start(bf16[256,256]{1,0:T(8,128)(2,1)S(1)} %get-tuple-element.118), channel_id=1, source_target_pairs={{0,1},{1,2},{2,3},{3,0},{4,5},{5,6},{6,7},{7,4},{8,9},{9,10},{10,1... | collective-permute-start | bytes 393224 | tf_op jit(solution)/shard_map/ppermute | solution.py:29
  172.1 4.8 %collective-permute-done.48 = bf16[256,256]{1,0:T(8,128)(2,1)S(1)} collective-permute-done((bf16[256,256]{1,0:T(8,128)(2,1)S(1)}, bf16[256,256]{1,0:T(8,128)(2,1)S(1)}, u32[]{:S(2)}, u32[]{:S(2)}) %collective-permute-start.48) | collective-permute-done | bytes 131104 | tf_op jit(solution)/shard_map/ppermute | solution.py:29
  177.4 1.6 collective-permute-start.49
  180.6 6.0 %grad_place.1 = bf16[256,8192]{1,0:T(8,128)(2,1)} custom-call(s32[4]{0:T(128)S(1)} %copy-done.31, s32[2,4]{1,0:T(2,128)S(1)} %copy-done.30, bf16[256,256]{1,0:T(8,128)(2,1)S(1)} %copy-done.21, bf16[256,256]{1,0:T(8,128)(2,1)S(1)} %get-tuple-element.89.refs_3_, bf16[256,256]{1,0:T(8,128)(2,1)S(1)} %copy-done.24, bf16[1024,256]{1,0:T(8,128)(2,1)S(1)} %copy-done.3, ...), custom_call_target="tpu_custom_call" | custom-call | flops 1610612736 | bytes 12582912 | tf_op jit(solution)/shard_map/grad_place/pallas_call | solution.py:257
  186.5 2.7 %collective-permute-done.50 = bf16[256,256]{1,0:T(8,128)(2,1)S(1)} collective-permute-done((bf16[256,256]{1,0:T(8,128)(2,1)S(1)}, bf16[256,256]{1,0:T(8,128)(2,1)S(1)}, u32[]{:S(2)}, u32[]{:S(2)}) %collective-permute-start.50) | collective-permute-done | bytes 131104 | tf_op jit(solution)/shard_map/ppermute | solution.py:29
  (212 shorter events, 29.2 us)
Async XLA Ops:
  0.6 17.3 %copy-start.34 = (f32[256,512]{1,0:T(8,128)S(1)}, f32[256,512]{1,0:T(8,128)}, u32[]{:S(2)}) copy-start(f32[256,512]{1,0:T(8,128)} %param.8) | copy-start | bytes 1572868
  0.6 20.5 %copy-start.43 = (s32[1024]{0:T(1024)S(1)}, s32[1024]{0:T(1024)}, u32[]{:S(2)}) copy-start(s32[1024]{0:T(1024)} %param.7) | copy-start | bytes 12292
  2.6 14.1 %collective-permute-start = (bf16[256,256]{1,0:T(8,128)(2,1)S(1)}, bf16[256,256]{1,0:T(8,128)(2,1)}, u32[]{:S(2)}, u32[]{:S(2)}) collective-permute-start(bf16[256,256]{1,0:T(8,128)(2,1)S(1)} %pad_maximum_fusion.4), channel_id=1, source_target_pairs={{0,1},{1,2},{2,3},{3,0},{4,5},{5,6},{6,7},{7,4},{8,9},{9,10},{10,1... | collective-permute-start | bytes 393224 | tf_op jit(solution)/shard_map/ppermute | solution.py:29
  5.6 12.1 %collective-permute-start.1 = (bf16[256,256]{1,0:T(8,128)(2,1)S(1)}, bf16[256,256]{1,0:T(8,128)(2,1)S(1)}, u32[]{:S(2)}, u32[]{:S(2)}) collective-permute-start(bf16[256,256]{1,0:T(8,128)(2,1)S(1)} %pad_maximum_fusion.4), channel_id=1, source_target_pairs={{0,2},{1,3},{2,0},{3,1},{4,6},{5,7},{6,4},{7,5},{8,10},{9,11},{10,... | collective-permute-start | bytes 393224 | tf_op jit(solution)/shard_map/ppermute | solution.py:29
  8.2 9.5 %collective-permute-start.2 = (bf16[256,256]{1,0:T(8,128)(2,1)S(1)}, bf16[256,256]{1,0:T(8,128)(2,1)S(1)}, u32[]{:S(2)}, u32[]{:S(2)}) collective-permute-start(bf16[256,256]{1,0:T(8,128)(2,1)S(1)} %pad_maximum_fusion.4), channel_id=1, source_target_pairs={{0,3},{1,0},{2,1},{3,2},{4,7},{5,4},{6,5},{7,6},{8,11},{9,8},{10,9... | collective-permute-start | bytes 393224 | tf_op jit(solution)/shard_map/ppermute | solution.py:29
  16.6 37.9 %copy-start = (bf16[256,4096]{1,0:T(8,128)(2,1)S(1)}, bf16[256,4096]{1,0:T(8,128)(2,1)}, u32[]{:S(2)}) copy-start(bf16[256,4096]{1,0:T(8,128)(2,1)} %get-tuple-element.84.refs_0_.refs_2_.refs_4_.refs_6_) | copy-start | bytes 6291460
  17.7 35.6 %copy-start.4 = (bf16[1024,256]{1,0:T(8,128)(2,1)}, bf16[1024,256]{1,0:T(8,128)(2,1)S(1)}, u32[]{:S(2)}) copy-start(bf16[1024,256]{1,0:T(8,128)(2,1)S(1)} %constant_dynamic-update-slice_fusion.refs_8_.refs_12_.refs_14_) | copy-start | bytes 1572868
  17.8 4.6 %collective-permute-start.3 = (bf16[256,4096]{1,0:T(8,128)(2,1)}, bf16[256,4096]{1,0:T(8,128)(2,1)}, u32[]{:S(2)}, u32[]{:S(2)}) collective-permute-start(bf16[256,4096]{1,0:T(8,128)(2,1)} %get-tuple-element.59), channel_id=1, source_target_pairs={{0,4},{4,0},{1,5},{5,1},{2,6},{6,2},{3,7},{7,3},{8,12},{12,8},{9,1... | collective-permute-start | bytes 6291464 | tf_op jit(solution)/shard_map/ppermute | solution.py:29
  18.0 17.6 %collective-permute-start.7 = (bf16[1024,256]{1,0:T(8,128)(2,1)S(1)}, bf16[1024,256]{1,0:T(8,128)(2,1)S(1)}, u32[]{:S(2)}, u32[]{:S(2)}) collective-permute-start(bf16[1024,256]{1,0:T(8,128)(2,1)S(1)} %constant_dynamic-update-slice_fusion.refs_8_.refs_12_.refs_14_), channel_id=1, source_target_pairs={{0,16},{16,0},{1,17},{17,1},{2,18},{18,2},{3,19},{19,3},{4,20},{20... | collective-permute-start | bytes 1572872 | tf_op jit(solution)/shard_map/ppermute | solution.py:29
  19.6 16.1 %collective-permute-start.8 = (bf16[1024,256]{1,0:T(8,128)(2,1)S(1)}, bf16[1024,256]{1,0:T(8,128)(2,1)S(1)}, u32[]{:S(2)}, u32[]{:S(2)}) collective-permute-start(bf16[1024,256]{1,0:T(8,128)(2,1)S(1)} %constant_dynamic-update-slice_fusion.refs_8_.refs_12_.refs_14_), channel_id=1, source_target_pairs={{0,8},{8,0},{1,9},{9,1},{2,10},{10,2},{3,11},{11,3},{4,12},{12,4},... | collective-permute-start | bytes 1572872 | tf_op jit(solution)/shard_map/ppermute | solution.py:29
  22.3 8.0 %collective-permute-start.4 = (bf16[256,256]{1,0:T(8,128)(2,1)S(1)}, bf16[256,256]{1,0:T(8,128)(2,1)S(1)}, u32[]{:S(2)}, u32[]{:S(2)}) collective-permute-start(bf16[256,256]{1,0:T(8,128)(2,1)S(1)} %get-tuple-element.60), channel_id=1, source_target_pairs={{0,1},{1,2},{2,3},{3,0},{4,5},{5,6},{6,7},{7,4},{8,9},{9,10},{10,1... | collective-permute-start | bytes 393224 | tf_op jit(solution)/shard_map/ppermute | solution.py:29
  26.0 9.4 %collective-permute-start.5 = (bf16[256,256]{1,0:T(8,128)(2,1)S(1)}, bf16[256,256]{1,0:T(8,128)(2,1)S(1)}, u32[]{:S(2)}, u32[]{:S(2)}) collective-permute-start(bf16[256,256]{1,0:T(8,128)(2,1)S(1)} %get-tuple-element.60), channel_id=1, source_target_pairs={{0,2},{1,3},{2,0},{3,1},{4,6},{5,7},{6,4},{7,5},{8,10},{9,11},{10,... | collective-permute-start | bytes 393224 | tf_op jit(solution)/shard_map/ppermute | solution.py:29
  27.7 8.0 %collective-permute-start.6 = (bf16[256,256]{1,0:T(8,128)(2,1)S(1)}, bf16[256,256]{1,0:T(8,128)(2,1)S(1)}, u32[]{:S(2)}, u32[]{:S(2)}) collective-permute-start(bf16[256,256]{1,0:T(8,128)(2,1)S(1)} %get-tuple-element.60), channel_id=1, source_target_pairs={{0,3},{1,0},{2,1},{3,2},{4,7},{5,4},{6,5},{7,6},{8,11},{9,8},{10,9... | collective-permute-start | bytes 393224 | tf_op jit(solution)/shard_map/ppermute | solution.py:29
  35.7 22.7 %copy-start.1 = (bf16[1024,256]{1,0:T(8,128)(2,1)}, bf16[1024,256]{1,0:T(8,128)(2,1)S(1)}, u32[]{:S(2)}) copy-start(bf16[1024,256]{1,0:T(8,128)(2,1)S(1)} %constant_dynamic-update-slice_fusion.4.refs_6_.refs_3_.refs_5_) | copy-start | bytes 1572868
  35.7 22.7 %copy-start.10 = (bf16[1024,256]{1,0:T(8,128)(2,1)}, bf16[1024,256]{1,0:T(8,128)(2,1)S(1)}, u32[]{:S(2)}) copy-start(bf16[1024,256]{1,0:T(8,128)(2,1)S(1)} %collective-permute-done.7.refs_10_.refs_14_.refs_16_) | copy-start | bytes 1572868
  35.7 16.9 %collective-permute-start.9 = (bf16[1024,256]{1,0:T(8,128)(2,1)S(1)}, bf16[1024,256]{1,0:T(8,128)(2,1)S(1)}, u32[]{:S(2)}, u32[]{:S(2)}) collective-permute-start(bf16[1024,256]{1,0:T(8,128)(2,1)S(1)} %constant_dynamic-update-slice_fusion.4.refs_6_.refs_3_.refs_5_), channel_id=1, source_target_pairs={{0,16},{16,0},{1,17},{17,1},{2,18},{18,2},{3,19},{19,3},{4,20},{20... | collective-permute-start | bytes 1572872 | tf_op jit(solution)/shard_map/ppermute | solution.py:29
  37.3 16.1 %collective-permute-start.10 = (bf16[1024,256]{1,0:T(8,128)(2,1)S(1)}, bf16[1024,256]{1,0:T(8,128)(2,1)S(1)}, u32[]{:S(2)}, u32[]{:S(2)}) collective-permute-start(bf16[1024,256]{1,0:T(8,128)(2,1)S(1)} %collective-permute-done.7.refs_10_.refs_14_.refs_16_), channel_id=1, source_target_pairs={{0,8},{8,0},{1,9},{9,1},{2,10},{10,2},{3,11},{11,3},{4,12},{12,4},... | collective-permute-start | bytes 1572872 | tf_op jit(solution)/shard_map/ppermute | solution.py:29
  38.8 8.2 %collective-permute-start.12 = (bf16[256,256]{1,0:T(8,128)(2,1)S(1)}, bf16[256,256]{1,0:T(8,128)(2,1)S(1)}, u32[]{:S(2)}, u32[]{:S(2)}) collective-permute-start(bf16[256,256]{1,0:T(8,128)(2,1)S(1)} %get-tuple-element.65), channel_id=1, source_target_pairs={{0,1},{1,2},{2,3},{3,0},{4,5},{5,6},{6,7},{7,4},{8,9},{9,10},{10,1... | collective-permute-start | bytes 393224 | tf_op jit(solution)/shard_map/ppermute | solution.py:29
  41.8 9.4 %collective-permute-start.13 = (bf16[256,256]{1,0:T(8,128)(2,1)S(1)}, bf16[256,256]{1,0:T(8,128)(2,1)S(1)}, u32[]{:S(2)}, u32[]{:S(2)}) collective-permute-start(bf16[256,256]{1,0:T(8,128)(2,1)S(1)} %get-tuple-element.65), channel_id=1, source_target_pairs={{0,2},{1,3},{2,0},{3,1},{4,6},{5,7},{6,4},{7,5},{8,10},{9,11},{10,... | collective-permute-start | bytes 393224 | tf_op jit(solution)/shard_map/ppermute | solution.py:29
  43.8 8.2 %collective-permute-start.14 = (bf16[256,256]{1,0:T(8,128)(2,1)S(1)}, bf16[256,256]{1,0:T(8,128)(2,1)S(1)}, u32[]{:S(2)}, u32[]{:S(2)}) collective-permute-start(bf16[256,256]{1,0:T(8,128)(2,1)S(1)} %get-tuple-element.65), channel_id=1, source_target_pairs={{0,3},{1,0},{2,1},{3,2},{4,7},{5,4},{6,5},{7,6},{8,11},{9,8},{10,9... | collective-permute-start | bytes 393224 | tf_op jit(solution)/shard_map/ppermute | solution.py:29
  51.9 18.1 %copy-start.44 = (s32[256]{0:T(256)S(1)}, s32[256]{0:T(256)}, u32[]{:S(2)}) copy-start(s32[256]{0:T(256)} %get-tuple-element.131) | copy-start | bytes 3076
  53.4 13.9 %collective-permute-start.11 = (bf16[1024,256]{1,0:T(8,128)(2,1)S(1)}, bf16[1024,256]{1,0:T(8,128)(2,1)}, u32[]{:S(2)}, u32[]{:S(2)}) collective-permute-start(bf16[1024,256]{1,0:T(8,128)(2,1)S(1)} %constant_dynamic-update-slice_fusion.4.refs_6_.refs_3_.refs_5_), channel_id=1, source_target_pairs={{0,8},{8,0},{1,9},{9,1},{2,10},{10,2},{3,11},{11,3},{4,12},{12,4},... | collective-permute-start | bytes 1572872 | tf_op jit(solution)/shard_map/ppermute | solution.py:29
  54.0 13.7 %collective-permute-start.15 = (bf16[1024,256]{1,0:T(8,128)(2,1)}, bf16[1024,256]{1,0:T(8,128)(2,1)S(1)}, u32[]{:S(2)}, u32[]{:S(2)}) collective-permute-start(bf16[1024,256]{1,0:T(8,128)(2,1)} %constant_dynamic-update-slice_fusion.8.refs_6_.refs_7_.refs_9_), channel_id=1, source_target_pairs={{0,16},{16,0},{1,17},{17,1},{2,18},{18,2},{3,19},{19,3},{4,20},{20... | collective-permute-start | bytes 1572872 | tf_op jit(solution)/shard_map/ppermute | solution.py:29
  59.9 1.5 collective-permute-start.16
  67.7 13.0 %collective-permute-start.17 = (bf16[1024,256]{1,0:T(8,128)(2,1)}, bf16[1024,256]{1,0:T(8,128)(2,1)}, u32[]{:S(2)}, u32[]{:S(2)}) collective-permute-start(bf16[1024,256]{1,0:T(8,128)(2,1)} %collective-permute-done.11.refs_7_.refs_4_.refs_6_), channel_id=1, source_target_pairs={{0,16},{16,0},{1,17},{17,1},{2,18},{18,2},{3,19},{19,3},{4,20},{20... | collective-permute-start | bytes 1572872 | tf_op jit(solution)/shard_map/ppermute | solution.py:29
  70.0 20.5 %collective-permute-start.22 = (bf16[1024,256]{1,0:T(8,128)(2,1)}, bf16[1024,256]{1,0:T(8,128)(2,1)S(1)}, u32[]{:S(2)}, u32[]{:S(2)}) collective-permute-start(bf16[1024,256]{1,0:T(8,128)(2,1)} %constant_dynamic-update-slice_fusion.8.refs_6_.refs_7_.refs_9_), channel_id=1, source_target_pairs={{0,8},{8,0},{1,9},{9,1},{2,10},{10,2},{3,11},{11,3},{4,12},{12,4},... | collective-permute-start | bytes 1572872 | tf_op jit(solution)/shard_map/ppermute | solution.py:29
  80.7 10.5 %collective-permute-start.19 = (bf16[256,256]{1,0:T(8,128)(2,1)}, bf16[256,256]{1,0:T(8,128)(2,1)S(1)}, u32[]{:S(2)}, u32[]{:S(2)}) collective-permute-start(bf16[256,256]{1,0:T(8,128)(2,1)} %finish_keys.1.refs_7_), channel_id=1, source_target_pairs={{0,1},{1,2},{2,3},{3,0},{4,5},{5,6},{6,7},{7,4},{8,9},{9,10},{10,1... | collective-permute-start | bytes 393224 | tf_op jit(solution)/shard_map/ppermute | solution.py:29
  86.3 8.3 %collective-permute-start.20 = (bf16[256,256]{1,0:T(8,128)(2,1)S(1)}, bf16[256,256]{1,0:T(8,128)(2,1)S(1)}, u32[]{:S(2)}, u32[]{:S(2)}) collective-permute-start(bf16[256,256]{1,0:T(8,128)(2,1)S(1)} %copy-done.27), channel_id=1, source_target_pairs={{0,2},{1,3},{2,0},{3,1},{4,6},{5,7},{6,4},{7,5},{8,10},{9,11},{10,... | collective-permute-start | bytes 393224 | tf_op jit(solution)/shard_map/ppermute | solution.py:29
  86.5 8.2 %collective-permute-start.21 = (bf16[256,256]{1,0:T(8,128)(2,1)S(1)}, bf16[256,256]{1,0:T(8,128)(2,1)S(1)}, u32[]{:S(2)}, u32[]{:S(2)}) collective-permute-start(bf16[256,256]{1,0:T(8,128)(2,1)S(1)} %copy-done.27), channel_id=1, source_target_pairs={{0,3},{1,0},{2,1},{3,2},{4,7},{5,4},{6,5},{7,6},{8,11},{9,8},{10,9... | collective-permute-start | bytes 393224 | tf_op jit(solution)/shard_map/ppermute | solution.py:29
  90.5 4.2 %collective-permute-start.18 = (f32[256,256]{1,0:T(8,128)S(1)}, f32[256,256]{1,0:T(8,128)S(1)}, u32[]{:S(2)}, u32[]{:S(2)}) collective-permute-start(f32[256,256]{1,0:T(8,128)S(1)} %get-tuple-element.73), channel_id=1, source_target_pairs={{0,4},{4,0},{1,5},{5,1},{2,6},{6,2},{3,7},{7,3},{8,12},{12,8},{9,1... | collective-permute-start | bytes 786440 | tf_op jit(solution)/shard_map/ppermute | solution.py:29
  90.6 9.3 %collective-permute-start.24 = (bf16[512,256]{1,0:T(8,128)(2,1)S(1)}, bf16[512,256]{1,0:T(8,128)(2,1)S(1)}, u32[]{:S(2)}, u32[]{:S(2)}) collective-permute-start(bf16[512,256]{1,0:T(8,128)(2,1)S(1)} %slice.131), channel_id=1, source_target_pairs={{0,16},{16,0},{1,17},{17,1},{2,18},{18,2},{3,19},{19,3},{4,20},{20... | collective-permute-start | bytes 786440 | tf_op jit(solution)/shard_map/ppermute | solution.py:29
  91.2 8.7 %collective-permute-start.23 = (bf16[512,256]{1,0:T(8,128)(2,1)S(1)}, bf16[512,256]{1,0:T(8,128)(2,1)S(1)}, u32[]{:S(2)}, u32[]{:S(2)}) collective-permute-start(bf16[512,256]{1,0:T(8,128)(2,1)S(1)} %slice.130), channel_id=1, source_target_pairs={{0,8},{8,0},{1,9},{9,1},{2,10},{10,2},{3,11},{11,3},{4,12},{12,4},... | collective-permute-start | bytes 786440 | tf_op jit(solution)/shard_map/ppermute | solution.py:29
  94.4 29.9 %copy-start.32 = (bf16[512,4096]{1,0:T(8,128)(2,1)}, bf16[512,4096]{1,0:T(8,128)(2,1)S(1)}, u32[]{:S(2)}) copy-start(bf16[512,4096]{1,0:T(8,128)(2,1)S(1)} %constant_dynamic-update-slice_fusion.12) | copy-start | bytes 12582916
  97.3 4.8 %collective-permute-start.25 = (bf16[256,256]{1,0:T(8,128)(2,1)S(1)}, bf16[256,256]{1,0:T(8,128)(2,1)S(1)}, u32[]{:S(2)}, u32[]{:S(2)}) collective-permute-start(bf16[256,256]{1,0:T(8,128)(2,1)S(1)} %get-tuple-element.85.refs_2_), channel_id=1, source_target_pairs={{0,4},{4,0},{1,5},{5,1},{2,6},{6,2},{3,7},{7,3},{8,12},{12,8},{9,1... | collective-permute-start | bytes 393224 | tf_op jit(solution)/shard_map/ppermute | solution.py:29
  101.6 3.9 %collective-permute-start.26 = (f32[256,256]{1,0:T(8,128)S(1)}, f32[256,256]{1,0:T(8,128)S(1)}, u32[]{:S(2)}, u32[]{:S(2)}) collective-permute-start(f32[256,256]{1,0:T(8,128)S(1)} %get-tuple-element.87), channel_id=1, source_target_pairs={{0,4},{4,0},{1,5},{5,1},{2,6},{6,2},{3,7},{7,3},{8,12},{12,8},{9,1... | collective-permute-start | bytes 786440 | tf_op jit(solution)/shard_map/ppermute | solution.py:29
  102.2 22.1 %copy-start.41 = (bf16[512,256]{1,0:T(8,128)(2,1)}, bf16[512,256]{1,0:T(8,128)(2,1)S(1)}, u32[]{:S(2)}) copy-start(bf16[512,256]{1,0:T(8,128)(2,1)S(1)} %constant_dynamic-update-slice_fusion.14) | copy-start | bytes 786436
  102.7 21.6 %collective-permute-start.27 = (bf16[1024,256]{1,0:T(8,128)(2,1)S(1)}, bf16[1024,256]{1,0:T(8,128)(2,1)S(1)}, u32[]{:S(2)}, u32[]{:S(2)}) collective-permute-start(bf16[1024,256]{1,0:T(8,128)(2,1)S(1)} %convolution_convert_fusion.3), channel_id=1, source_target_pairs={{0,8},{8,0},{1,9},{9,1},{2,10},{10,2},{3,11},{11,3},{4,12},{12,4},... | collective-permute-start | bytes 1572872 | tf_op jit(solution)/shard_map/ppermute | solution.py:29
  108.4 4.3 %collective-permute-start.28 = (bf16[256,256]{1,0:T(8,128)(2,1)S(1)}, bf16[256,256]{1,0:T(8,128)(2,1)S(1)}, u32[]{:S(2)}, u32[]{:S(2)}) collective-permute-start(bf16[256,256]{1,0:T(8,128)(2,1)S(1)} %get-tuple-element.89.refs_3_), channel_id=1, source_target_pairs={{0,4},{4,0},{1,5},{5,1},{2,6},{6,2},{3,7},{7,3},{8,12},{12,8},{9,1... | collective-permute-start | bytes 393224 | tf_op jit(solution)/shard_map/ppermute | solution.py:29
  108.5 6.7 %collective-permute-start.30 = (bf16[256,256]{1,0:T(8,128)(2,1)S(1)}, bf16[256,256]{1,0:T(8,128)(2,1)S(1)}, u32[]{:S(2)}, u32[]{:S(2)}) collective-permute-start(bf16[256,256]{1,0:T(8,128)(2,1)S(1)} %get-tuple-element.91), channel_id=1, source_target_pairs={{0,3},{1,0},{2,1},{3,2},{4,7},{5,4},{6,5},{7,6},{8,11},{9,8},{10,9... | collective-permute-start | bytes 393224 | tf_op jit(solution)/shard_map/ppermute | solution.py:29
  111.2 13.0 %collective-permute-start.31 = (bf16[256,256]{1,0:T(8,128)(2,1)S(1)}, bf16[256,256]{1,0:T(8,128)(2,1)S(1)}, u32[]{:S(2)}, u32[]{:S(2)}) collective-permute-start(bf16[256,256]{1,0:T(8,128)(2,1)S(1)} %get-tuple-element.92), channel_id=1, source_target_pairs={{0,2},{1,3},{2,0},{3,1},{4,6},{5,7},{6,4},{7,5},{8,10},{9,11},{10,... | collective-permute-start | bytes 393224 | tf_op jit(solution)/shard_map/ppermute | solution.py:29
  111.9 12.3 %collective-permute-start.32 = (bf16[256,256]{1,0:T(8,128)(2,1)S(1)}, bf16[256,256]{1,0:T(8,128)(2,1)S(1)}, u32[]{:S(2)}, u32[]{:S(2)}) collective-permute-start(bf16[256,256]{1,0:T(8,128)(2,1)S(1)} %get-tuple-element.93), channel_id=1, source_target_pairs={{0,1},{1,2},{2,3},{3,0},{4,5},{5,6},{6,7},{7,4},{8,9},{9,10},{10,1... | collective-permute-start | bytes 393224 | tf_op jit(solution)/shard_map/ppermute | solution.py:29
  113.2 13.9 %collective-permute-start.29 = (bf16[1024,256]{1,0:T(8,128)(2,1)S(1)}, bf16[1024,256]{1,0:T(8,128)(2,1)}, u32[]{:S(2)}, u32[]{:S(2)}) collective-permute-start(bf16[1024,256]{1,0:T(8,128)(2,1)S(1)} %convolution_convert_fusion.2), channel_id=1, source_target_pairs={{0,16},{16,0},{1,17},{17,1},{2,18},{18,2},{3,19},{19,3},{4,20},{20... | collective-permute-start | bytes 1572872 | tf_op jit(solution)/shard_map/ppermute | solution.py:29
  125.6 15.1 %collective-permute-start.38 = (bf16[1024,256]{1,0:T(8,128)(2,1)}, bf16[1024,256]{1,0:T(8,128)(2,1)}, u32[]{:S(2)}, u32[]{:S(2)}) collective-permute-start(bf16[1024,256]{1,0:T(8,128)(2,1)} %convolution_convert_fusion.1), channel_id=1, source_target_pairs={{0,8},{8,0},{1,9},{9,1},{2,10},{10,2},{3,11},{11,3},{4,12},{12,4},... | collective-permute-start | bytes 1572872 | tf_op jit(solution)/shard_map/ppermute | solution.py:29
  126.2 15.2 %collective-permute-start.37 = (bf16[1024,256]{1,0:T(8,128)(2,1)}, bf16[1024,256]{1,0:T(8,128)(2,1)}, u32[]{:S(2)}, u32[]{:S(2)}) collective-permute-start(bf16[1024,256]{1,0:T(8,128)(2,1)} %fusion.3), channel_id=1, source_target_pairs={{0,16},{16,0},{1,17},{17,1},{2,18},{18,2},{3,19},{19,3},{4,20},{20... | collective-permute-start | bytes 1572872 | tf_op jit(solution)/shard_map/ppermute | solution.py:29
  129.1 2.1 %collective-permute-start.33 = (bf16[256,256]{1,0:T(8,128)(2,1)}, bf16[256,256]{1,0:T(8,128)(2,1)S(1)}, u32[]{:S(2)}, u32[]{:S(2)}) collective-permute-start(bf16[256,256]{1,0:T(8,128)(2,1)} %undo_keys.1.refs_4_), channel_id=1, source_target_pairs={{0,4},{4,0},{1,5},{5,1},{2,6},{6,2},{3,7},{7,3},{8,12},{12,8},{9,1... | collective-permute-start | bytes 393224 | tf_op jit(solution)/shard_map/ppermute | solution.py:29
  132.7 12.6 %collective-permute-start.35 = (bf16[512,256]{1,0:T(8,128)(2,1)S(1)}, bf16[512,256]{1,0:T(8,128)(2,1)S(1)}, u32[]{:S(2)}, u32[]{:S(2)}) collective-permute-start(bf16[512,256]{1,0:T(8,128)(2,1)S(1)} %convolution_convert_fusion.6), channel_id=1, source_target_pairs={{0,16},{16,0},{1,17},{17,1},{2,18},{18,2},{3,19},{19,3},{4,20},{20... | collective-permute-start | bytes 786440 | tf_op jit(solution)/shard_map/ppermute | solution.py:29
  134.3 11.0 %collective-permute-start.34 = (bf16[512,256]{1,0:T(8,128)(2,1)S(1)}, bf16[512,256]{1,0:T(8,128)(2,1)S(1)}, u32[]{:S(2)}, u32[]{:S(2)}) collective-permute-start(bf16[512,256]{1,0:T(8,128)(2,1)S(1)} %convolution_convert_fusion.7), channel_id=1, source_target_pairs={{0,8},{8,0},{1,9},{9,1},{2,10},{10,2},{3,11},{11,3},{4,12},{12,4},... | collective-permute-start | bytes 786440 | tf_op jit(solution)/shard_map/ppermute | solution.py:29
  145.3 12.3 %collective-permute-start.39 = (bf16[1024,256]{1,0:T(8,128)(2,1)S(1)}, bf16[1024,256]{1,0:T(8,128)(2,1)S(1)}, u32[]{:S(2)}, u32[]{:S(2)}) collective-permute-start(bf16[1024,256]{1,0:T(8,128)(2,1)S(1)} %copy-done.45), channel_id=1, source_target_pairs={{0,16},{16,0},{1,17},{17,1},{2,18},{18,2},{3,19},{19,3},{4,20},{20... | collective-permute-start | bytes 1572872 | tf_op jit(solution)/shard_map/ppermute | solution.py:29
  145.8 12.1 %collective-permute-start.40 = (bf16[1024,256]{1,0:T(8,128)(2,1)S(1)}, bf16[1024,256]{1,0:T(8,128)(2,1)S(1)}, u32[]{:S(2)}, u32[]{:S(2)}) collective-permute-start(bf16[1024,256]{1,0:T(8,128)(2,1)S(1)} %fusion.5), channel_id=1, source_target_pairs={{0,8},{8,0},{1,9},{9,1},{2,10},{10,2},{3,11},{11,3},{4,12},{12,4},... | collective-permute-start | bytes 1572872 | tf_op jit(solution)/shard_map/ppermute | solution.py:29
  147.3 6.1 %collective-permute-start.41 = (bf16[256,256]{1,0:T(8,128)(2,1)S(1)}, bf16[256,256]{1,0:T(8,128)(2,1)S(1)}, u32[]{:S(2)}, u32[]{:S(2)}) collective-permute-start(bf16[256,256]{1,0:T(8,128)(2,1)S(1)} %get-tuple-element.116), channel_id=1, source_target_pairs={{0,3},{1,0},{2,1},{3,2},{4,7},{5,4},{6,5},{7,6},{8,11},{9,8},{10,9... | collective-permute-start | bytes 393224 | tf_op jit(solution)/shard_map/ppermute | solution.py:29
  149.1 8.3 %collective-permute-start.42 = (bf16[256,256]{1,0:T(8,128)(2,1)S(1)}, bf16[256,256]{1,0:T(8,128)(2,1)S(1)}, u32[]{:S(2)}, u32[]{:S(2)}) collective-permute-start(bf16[256,256]{1,0:T(8,128)(2,1)S(1)} %get-tuple-element.115), channel_id=1, source_target_pairs={{0,2},{1,3},{2,0},{3,1},{4,6},{5,7},{6,4},{7,5},{8,10},{9,11},{10,... | collective-permute-start | bytes 393224 | tf_op jit(solution)/shard_map/ppermute | solution.py:29
  152.5 28.0 %collective-permute-start.36 = (bf16[256,4096]{1,0:T(8,128)(2,1)S(1)}, bf16[256,4096]{1,0:T(8,128)(2,1)S(1)}, u32[]{:S(2)}, u32[]{:S(2)}) collective-permute-start(bf16[256,4096]{1,0:T(8,128)(2,1)S(1)} %grad_columns.1), channel_id=1, source_target_pairs={{0,4},{4,0},{1,5},{5,1},{2,6},{6,2},{3,7},{7,3},{8,12},{12,8},{9,1... | collective-permute-start | bytes 6291464 | tf_op jit(solution)/shard_map/ppermute | solution.py:29
  153.4 9.8 %collective-permute-start.43 = (bf16[256,256]{1,0:T(8,128)(2,1)S(1)}, bf16[256,256]{1,0:T(8,128)(2,1)S(1)}, u32[]{:S(2)}, u32[]{:S(2)}) collective-permute-start(bf16[256,256]{1,0:T(8,128)(2,1)S(1)} %get-tuple-element.114), channel_id=1, source_target_pairs={{0,1},{1,2},{2,3},{3,0},{4,5},{5,6},{6,7},{7,4},{8,9},{9,10},{10,1... | collective-permute-start | bytes 393224 | tf_op jit(solution)/shard_map/ppermute | solution.py:29
  157.9 12.1 %collective-permute-start.45 = (bf16[1024,256]{1,0:T(8,128)(2,1)S(1)}, bf16[1024,256]{1,0:T(8,128)(2,1)S(1)}, u32[]{:S(2)}, u32[]{:S(2)}) collective-permute-start(bf16[1024,256]{1,0:T(8,128)(2,1)S(1)} %pad_maximum_fusion.1), channel_id=1, source_target_pairs={{0,8},{8,0},{1,9},{9,1},{2,10},{10,2},{3,11},{11,3},{4,12},{12,4},... | collective-permute-start | bytes 1572872 | tf_op jit(solution)/shard_map/ppermute | solution.py:29
  159.3 12.7 %collective-permute-start.44 = (bf16[1024,256]{1,0:T(8,128)(2,1)S(1)}, bf16[1024,256]{1,0:T(8,128)(2,1)S(1)}, u32[]{:S(2)}, u32[]{:S(2)}) collective-permute-start(bf16[1024,256]{1,0:T(8,128)(2,1)S(1)} %pad_maximum_fusion), channel_id=1, source_target_pairs={{0,16},{16,0},{1,17},{17,1},{2,18},{18,2},{3,19},{19,3},{4,20},{20... | collective-permute-start | bytes 1572872 | tf_op jit(solution)/shard_map/ppermute | solution.py:29
  161.4 19.2 %copy-start.21 = (bf16[256,256]{1,0:T(8,128)(2,1)S(1)}, bf16[256,256]{1,0:T(8,128)(2,1)}, u32[]{:S(2)}) copy-start(bf16[256,256]{1,0:T(8,128)(2,1)} %copy-done.20) | copy-start | bytes 393220
  161.4 19.2 %copy-start.30 = (s32[2,4]{1,0:T(2,128)S(1)}, s32[2,4]{1,0:T(2,128)}, u32[]{:S(2)}) copy-start(s32[2,4]{1,0:T(2,128)} %pad_add_fusion.1.piece_ref.refs_1_) | copy-start | bytes 100
  161.4 19.2 %copy-start.31 = (s32[4]{0:T(128)S(1)}, s32[4]{0:T(128)}, u32[]{:S(2)}) copy-start(s32[4]{0:T(128)} %fusion.26.slab_ref.refs_0_) | copy-start | bytes 52
  161.4 10.6 %collective-permute-start.46 = (bf16[256,256]{1,0:T(8,128)(2,1)S(1)}, bf16[256,256]{1,0:T(8,128)(2,1)S(1)}, u32[]{:S(2)}, u32[]{:S(2)}) collective-permute-start(bf16[256,256]{1,0:T(8,128)(2,1)S(1)} %get-tuple-element.120), channel_id=1, source_target_pairs={{0,3},{1,0},{2,1},{3,2},{4,7},{5,4},{6,5},{7,6},{8,11},{9,8},{10,9... | collective-permute-start | bytes 393224 | tf_op jit(solution)/shard_map/ppermute | solution.py:29
  163.2 8.9 %collective-permute-start.47 = (bf16[256,256]{1,0:T(8,128)(2,1)S(1)}, bf16[256,256]{1,0:T(8,128)(2,1)S(1)}, u32[]{:S(2)}, u32[]{:S(2)}) collective-permute-start(bf16[256,256]{1,0:T(8,128)(2,1)S(1)} %get-tuple-element.119), channel_id=1, source_target_pairs={{0,2},{1,3},{2,0},{3,1},{4,6},{5,7},{6,4},{7,5},{8,10},{9,11},{10,... | collective-permute-start | bytes 393224 | tf_op jit(solution)/shard_map/ppermute | solution.py:29
  170.0 6.8 %collective-permute-start.48 = (bf16[256,256]{1,0:T(8,128)(2,1)S(1)}, bf16[256,256]{1,0:T(8,128)(2,1)S(1)}, u32[]{:S(2)}, u32[]{:S(2)}) collective-permute-start(bf16[256,256]{1,0:T(8,128)(2,1)S(1)} %get-tuple-element.118), channel_id=1, source_target_pairs={{0,1},{1,2},{2,3},{3,0},{4,5},{5,6},{6,7},{7,4},{8,9},{9,10},{10,1... | collective-permute-start | bytes 393224 | tf_op jit(solution)/shard_map/ppermute | solution.py:29
  177.4 9.1 %collective-permute-start.49 = (bf16[256,256]{1,0:T(8,128)(2,1)S(1)}, bf16[256,256]{1,0:T(8,128)(2,1)S(1)}, u32[]{:S(2)}, u32[]{:S(2)}) collective-permute-start(bf16[256,256]{1,0:T(8,128)(2,1)S(1)} %get-tuple-element.112), channel_id=1, source_target_pairs={{0,3},{1,0},{2,1},{3,2},{4,7},{5,4},{6,5},{7,6},{8,11},{9,8},{10,9... | collective-permute-start | bytes 393224 | tf_op jit(solution)/shard_map/ppermute | solution.py:29
  179.0 10.2 %collective-permute-start.50 = (bf16[256,256]{1,0:T(8,128)(2,1)S(1)}, bf16[256,256]{1,0:T(8,128)(2,1)S(1)}, u32[]{:S(2)}, u32[]{:S(2)}) collective-permute-start(bf16[256,256]{1,0:T(8,128)(2,1)S(1)} %get-tuple-element.111), channel_id=1, source_target_pairs={{0,2},{1,3},{2,0},{3,1},{4,6},{5,7},{6,4},{7,5},{8,10},{9,11},{10,... | collective-permute-start | bytes 393224 | tf_op jit(solution)/shard_map/ppermute | solution.py:29
  179.1 10.1 %collective-permute-start.51 = (bf16[256,256]{1,0:T(8,128)(2,1)S(1)}, bf16[256,256]{1,0:T(8,128)(2,1)S(1)}, u32[]{:S(2)}, u32[]{:S(2)}) collective-permute-start(bf16[256,256]{1,0:T(8,128)(2,1)S(1)} %get-tuple-element.110), channel_id=1, source_target_pairs={{0,1},{1,2},{2,3},{3,0},{4,5},{5,6},{6,7},{7,4},{8,9},{9,10},{10,1... | collective-permute-start | bytes 393224 | tf_op jit(solution)/shard_map/ppermute | solution.py:29
  (34 other events, 288.8 us)

commit v6 on v5

--- a/solution.py
+++ b/solution.py
@@ -532,9 +532,8 @@
     q0_corners = gather_corners(q0_a, q0_b, "a", *stage)
     q1_b = along(after(q_line[1], *stage), "b")
     part = project_early(in_order(q_line[0], q0_a, q0_b, q0_corners))
-    corners = [piece for corner in q0_corners.values() for piece in corner]
-    key_values = gather_line(after(key_value, *corners))
-    stage = q1_b + [piece for corner in q0_corners.values() for piece in corner]
+    key_values = gather_line(key_value)
+    stage = q1_b + key_values + [piece for corner in q0_corners.values() for piece in corner]
     q1_corners = gather_corners(q1_a, q1_b, "both", *stage)
     q_slabs = [
         in_order(q_line[0], q0_a, q0_b, q0_corners),
@@ -571,7 +570,7 @@
     summed = [terms[0]] + [shift(terms[k], "ctx", -k) for k in range(1, ctx)]
     first = [*came[0][0].values(), *came[0][1].values()]
     second = [*came[1][0].values(), *came[1][1].values()]
-    sides0, went0 = reduce_sides(made[0], came[0], "b", mid, *first, *summed[1:])
+    sides0, went0 = reduce_sides(made[0], came[0], "b", mid, *first, *summed[1:-1])
     grad_kv = undo_keys(
         [after(summed[0], *first, *second, *went0), *summed[1:]], cos_table, sin_table
     )
@@ -579,7 +578,7 @@
     made.append(terms_of(*gradients[2]))
     came.append(reduce_corners(made[2], "both", mid))
     third = [*came[2][0].values(), *came[2][1].values()]
-    sides1, went1 = reduce_sides(made[1], came[1], "a", mid, *sides0, *third)
+    sides1, went1 = reduce_sides(made[1], came[1], "a", mid, *sides0)
     line0 = after(made[0](0, slice(None), sides0), *went1)
     sent0 = send_line(line0)
     q_grads = [add_line(sent0, sides1)]

time: 191 us -> 183 us (0.958)
  waiting for transfers between devices: 59.2 us -> 48.4 us
  starting transfers between devices: 61 us -> 64.6 us
    ppermute x52, waiting for transfers between devices: 59.2 us -> 48.4 us  [shift(): lax.ppermute(block, axis, [(i, (i + step) % size) for i in range(size)])]
    ppermute x52, starting transfers between devices: 61 us -> 64.6 us  [shift(): lax.ppermute(block, axis, [(i, (i + step) % size) for i in range(size)])]
    unnamed x104 -> x108, local copies, waits for them, and re-layouts: 7.52 us -> 8.33 us
  transfers between devices with their start and end apart: 52 -> 52, of which waited for: 23 -> 18; matrix products, arithmetic and copies ran while one was open for 14% -> 14% of each run, Pallas kernels for 19% -> 19%
where the time goes in v6:
time: 183 us
  starting transfers between devices  64.6 us (35%)
  waiting for transfers between devices  48.4 us (26%)
  Pallas kernels  35 us (19%)
  local copies, waits for them, and re-layouts  12.8 us (7%)
  matrix products  12.8 us (7%)
  other arithmetic  7.5 us (4%)
    ppermute x52, starting transfers between devices, shift(): lax.ppermute(block, axis, [(i, (i + step) % size) for i in range(size)])  64.6 us
    ppermute x52, waiting for transfers between devices, shift(): lax.ppermute(block, axis, [(i, (i + step) % size) for i in range(size)])  48.4 us
    dot_general x15, matrix products, mm(): lax.dot_general(a, b, (dims, ((), ())), preferred_element_type=jnp.float32)  12.8 us
    pallas_call x5, Pallas kernels, project_rows(): pl.pallas_call(functools.partial(project_kernel, counts=[len(slab) for sl...  11.2 us
    unnamed x108, local copies, waits for them, and re-layouts  8.33 us
    pallas_call x1, Pallas kernels, grad_place(): pl.pallas_call(functools.partial(grad_place_kernel, shape=shape, plane=pl...  5.84 us
    pallas_call x1, Pallas kernels, pick_columns(): pl.pallas_call(functools.partial(pick_kernel, block=block), grid_spec=plt...  5.62 us
    pallas_call x2, Pallas kernels, attend(): pl.pallas_call(functools.partial(attend_kernel, group=group, parts=parts,...  5.4 us
  transfers between devices with their start and end apart: 52, of which 18 were waited for; matrix products, arithmetic and copies ran while one was open for 14% of the time, Pallas kernels for 19%

profile of v6, /device:TPU:0, one launch (start us, length us, event | category | flops | bytes accessed | tf_op | source)
XLA Modules:
  0.0 182.8 jit_solution(2753425809471552284)
XLA Ops:
  2.6 3.1 %collective-permute-start = (bf16[256,256]{1,0:T(8,128)(2,1)S(1)}, bf16[256,256]{1,0:T(8,128)(2,1)}, u32[]{:S(2)}, u32[]{:S(2)}) collective-permute-start(bf16[256,256]{1,0:T(8,128)(2,1)S(1)} %pad_maximum_fusion.4), channel_id=1, source_target_pairs={{0,1},{1,2},{2,3},{3,0},{4,5},{5,6},{6,7},{7,4},{8,9},{9,10},{10,1... | collective-permute-start | bytes 393224 | tf_op jit(solution)/shard_map/ppermute | solution.py:29
  5.6 2.6 %collective-permute-start.1 = (bf16[256,256]{1,0:T(8,128)(2,1)S(1)}, bf16[256,256]{1,0:T(8,128)(2,1)S(1)}, u32[]{:S(2)}, u32[]{:S(2)}) collective-permute-start(bf16[256,256]{1,0:T(8,128)(2,1)S(1)} %pad_maximum_fusion.4), channel_id=1, source_target_pairs={{0,2},{1,3},{2,0},{3,1},{4,6},{5,7},{6,4},{7,5},{8,10},{9,11},{10,... | collective-permute-start | bytes 393224 | tf_op jit(solution)/shard_map/ppermute | solution.py:29
  8.2 1.3 collective-permute-start.2
  10.9 5.6 %pick_columns.1 = (bf16[256,4096]{1,0:T(8,128)(2,1)}, bf16[256,4096]{1,0:T(8,128)(2,1)}) custom-call(s32[4]{0:T(128)} %fusion.26.slab_ref.refs_0_, s32[2,4]{1,0:T(2,128)} %pad_add_fusion.1.piece_ref.refs_1_, bf16[256,8192]{1,0:T(8,128)(2,1)} %bitcast.17), custom_call_target="tpu_custom_call" | custom-call | bytes 8388608 | tf_op jit(solution)/shard_map/pick_columns/pallas_call | solution.py:211
  16.6 1.1 constant_dynamic-update-slice_fusion.2
  18.0 1.6 collective-permute-start.7
  19.5 1.5 collective-permute-start.8
  22.3 2.5 %collective-permute-start.4 = (bf16[256,256]{1,0:T(8,128)(2,1)S(1)}, bf16[256,256]{1,0:T(8,128)(2,1)S(1)}, u32[]{:S(2)}, u32[]{:S(2)}) collective-permute-start(bf16[256,256]{1,0:T(8,128)(2,1)S(1)} %get-tuple-element.59), channel_id=1, source_target_pairs={{0,1},{1,2},{2,3},{3,0},{4,5},{5,6},{6,7},{7,4},{8,9},{9,10},{10,1... | collective-permute-start | bytes 393224 | tf_op jit(solution)/shard_map/ppermute | solution.py:29
  24.7 1.3 negate_select_fusion
  26.0 1.7 collective-permute-start.5
  28.6 1.6 collective-permute-done.4
  30.2 5.2 %collective-permute-done.5 = bf16[256,256]{1,0:T(8,128)(2,1)S(1)} collective-permute-done((bf16[256,256]{1,0:T(8,128)(2,1)S(1)}, bf16[256,256]{1,0:T(8,128)(2,1)S(1)}, u32[]{:S(2)}, u32[]{:S(2)}) %collective-permute-start.5) | collective-permute-done | bytes 131104 | tf_op jit(solution)/shard_map/ppermute | solution.py:29
  35.7 1.6 collective-permute-start.9
  37.2 1.5 collective-permute-start.10
  38.7 3.1 %collective-permute-start.12 = (bf16[256,256]{1,0:T(8,128)(2,1)S(1)}, bf16[256,256]{1,0:T(8,128)(2,1)S(1)}, u32[]{:S(2)}, u32[]{:S(2)}) collective-permute-start(bf16[256,256]{1,0:T(8,128)(2,1)S(1)} %get-tuple-element.64), channel_id=1, source_target_pairs={{0,1},{1,2},{2,3},{3,0},{4,5},{5,6},{6,7},{7,4},{8,9},{9,10},{10,1... | collective-permute-start | bytes 393224 | tf_op jit(solution)/shard_map/ppermute | solution.py:29
  41.8 1.3 collective-permute-start.13
  43.7 1.1 collective-permute-start.14
  44.8 2.1 %collective-permute-done.12 = bf16[256,256]{1,0:T(8,128)(2,1)S(1)} collective-permute-done((bf16[256,256]{1,0:T(8,128)(2,1)S(1)}, bf16[256,256]{1,0:T(8,128)(2,1)S(1)}, u32[]{:S(2)}, u32[]{:S(2)}) %collective-permute-start.12) | collective-permute-done | bytes 131104 | tf_op jit(solution)/shard_map/ppermute | solution.py:29
  47.6 3.6 %collective-permute-done.13 = bf16[256,256]{1,0:T(8,128)(2,1)S(1)} collective-permute-done((bf16[256,256]{1,0:T(8,128)(2,1)S(1)}, bf16[256,256]{1,0:T(8,128)(2,1)S(1)}, u32[]{:S(2)}, u32[]{:S(2)}) %collective-permute-start.13) | collective-permute-done | bytes 131104 | tf_op jit(solution)/shard_map/ppermute | solution.py:29
  54.5 1.0 copy-done.5
  55.5 2.8 %project_rows.5 = (f32[256,256]{1,0:T(8,128)S(1)}, f32[256,256]{1,0:T(8,128)S(1)}) custom-call(bf16[256,4096]{1,0:T(8,128)(2,1)S(1)} %copy-done, bf16[256,4096]{1,0:T(8,128)(2,1)} %collective-permute-done.3.refs_1_.refs_3_.refs_5_.refs_7_, bf16[256,4096]{1,0:T(8,128)(2,1)S(1)} %copy-done, ...), custom_call_target="tpu_custom_call" | custom-call | flops 1073741824 | bytes 6291456 | tf_op jit(solution)/shard_map/project_rows/pallas_call | solution.py:312
  61.5 1.8 %finish_keys.1.refs_7_ = bf16[256,256]{1,0:T(8,128)(2,1)} custom-call(f32[256,256]{1,0:T(8,128)} %copy-done.27, f32[256,256]{1,0:T(8,128)} %collective-permute-done.16.other, f32[256,128]{1,0:T(8,128)} %get-tuple-element.126.cos_ref.refs_3_.refs_4_, f32[256,128]{1,0:T(8,128)} %get-tuple-element.125.sin_ref.refs_4_.refs_5_), custom_call_target="tpu_custom_call" | custom-call | tf_op jit(solution)/shard_map/finish_keys/pallas_call | solution.py:424
  63.4 2.6 %collective-permute-start.19 = (bf16[256,256]{1,0:T(8,128)(2,1)}, bf16[256,256]{1,0:T(8,128)(2,1)S(1)}, u32[]{:S(2)}, u32[]{:S(2)}) collective-permute-start(bf16[256,256]{1,0:T(8,128)(2,1)} %finish_keys.1.refs_7_), channel_id=1, source_target_pairs={{0,1},{1,2},{2,3},{3,0},{4,5},{5,6},{6,7},{7,4},{8,9},{9,10},{10,1... | collective-permute-start | bytes 393224 | tf_op jit(solution)/shard_map/ppermute | solution.py:29
  66.0 2.4 %collective-permute-start.20 = (bf16[256,256]{1,0:T(8,128)(2,1)}, bf16[256,256]{1,0:T(8,128)(2,1)S(1)}, u32[]{:S(2)}, u32[]{:S(2)}) collective-permute-start(bf16[256,256]{1,0:T(8,128)(2,1)} %finish_keys.1.refs_7_), channel_id=1, source_target_pairs={{0,2},{1,3},{2,0},{3,1},{4,6},{5,7},{6,4},{7,5},{8,10},{9,11},{10,... | collective-permute-start | bytes 393224 | tf_op jit(solution)/shard_map/ppermute | solution.py:29
  69.0 1.5 collective-permute-start.17
  70.5 1.5 collective-permute-start.22
  72.3 2.5 %project_rows.6 = (f32[256,256]{1,0:T(8,128)S(1)}, f32[256,256]{1,0:T(8,128)S(1)}) custom-call(bf16[256,4096]{1,0:T(8,128)(2,1)S(1)} %copy-done, bf16[256,4096]{1,0:T(8,128)(2,1)} %collective-permute-done.3.refs_1_.refs_3_.refs_5_.refs_7_, bf16[256,4096]{1,0:T(8,128)(2,1)S(1)} %copy-done, ...), custom_call_target="tpu_custom_call" | custom-call | flops 805306368 | bytes 4718592 | tf_op jit(solution)/shard_map/project_rows/pallas_call | solution.py:312
  74.8 7.7 %collective-permute-done.17.refs_2_.refs_6_.refs_8_ = bf16[1024,256]{1,0:T(8,128)(2,1)S(1)} collective-permute-done((bf16[1024,256]{1,0:T(8,128)(2,1)}, bf16[1024,256]{1,0:T(8,128)(2,1)S(1)}, u32[]{:S(2)}, u32[]{:S(2)}) %collective-permute-start.17) | collective-permute-done | bytes 524320 | tf_op jit(solution)/shard_map/ppermute | solution.py:29
  82.6 1.8 project_rows.7
  84.5 1.6 collective-permute-start.24
  86.1 1.5 collective-permute-start.23
  87.6 1.8 constant_dynamic-update-slice_fusion.12
  89.5 2.6 %attend.2 = (bf16[256,256]{1,0:T(8,128)(2,1)S(1)}, bf16[256,256]{1,0:T(8,128)(2,1)S(1)}, f32[1024,256]{1,0:T(8,128)S(1)}) custom-call(f32[256,256]{1,0:T(8,128)S(1)} %get-tuple-element.71.refs_0_, f32[256,256]{1,0:T(8,128)S(1)} %collective-permute-done.18.refs_1_, bf16[256,256]{1,0:T(8,128)(2,1)S(1)} %copy-done.31, f32[256,128]{1,0:T(8,128)S(1)} %copy-done.21, ...), custom_call_target="tpu_custom_call" | custom-call | flops 939524096 | bytes 2097152 | tf_op jit(solution)/shard_map/attend/pallas_call | solution.py:395
  92.1 2.5 %project_rows.8 = (f32[256,256]{1,0:T(8,128)S(1)}, f32[256,256]{1,0:T(8,128)S(1)}) custom-call(bf16[256,4096]{1,0:T(8,128)(2,1)S(1)} %copy-done, bf16[256,4096]{1,0:T(8,128)(2,1)} %collective-permute-done.3.refs_1_.refs_3_.refs_5_.refs_7_, bf16[256,4096]{1,0:T(8,128)(2,1)S(1)} %copy-done, ...), custom_call_target="tpu_custom_call" | custom-call | flops 805306368 | bytes 4718592 | tf_op jit(solution)/shard_map/project_rows/pallas_call | solution.py:312
  94.7 1.6 project_rows.9
  98.3 1.3 convolution_convert_fusion.1
  99.7 2.8 %attend.3 = (bf16[256,256]{1,0:T(8,128)(2,1)S(1)}, bf16[256,256]{1,0:T(8,128)(2,1)S(1)}, f32[256,256]{1,0:T(8,128)S(1)}, bf16[256,256]{1,0:T(8,128)(2,1)S(1)}, b...) custom-call(f32[256,256]{1,0:T(8,128)S(1)} %get-tuple-element.84.refs_0_, ...), custom_call_target="tpu_custom_call" | custom-call | flops 939524096 | bytes 2097152 | tf_op jit(solution)/shard_map/attend/pallas_call | solution.py:395
  102.8 1.4 collective-permute-start.30
  104.2 1.5 collective-permute-start.31
  107.9 1.3 convolution_convert_fusion
  109.2 2.2 %collective-permute-done.27 = bf16[1024,256]{1,0:T(8,128)(2,1)S(1)} collective-permute-done((bf16[1024,256]{1,0:T(8,128)(2,1)S(1)}, bf16[1024,256]{1,0:T(8,128)(2,1)S(1)}, u32[]{:S(2)}, u32[]{:S(2)}) %collective-permute-start.27) | collective-permute-done | bytes 524320 | tf_op jit(solution)/shard_map/ppermute | solution.py:29
  111.4 1.3 fusion.3
  112.7 5.2 %collective-permute-done.31.refs_2_ = bf16[256,256]{1,0:T(8,128)(2,1)S(1)} collective-permute-done((bf16[256,256]{1,0:T(8,128)(2,1)S(1)}, bf16[256,256]{1,0:T(8,128)(2,1)S(1)}, u32[]{:S(2)}, u32[]{:S(2)}) %collective-permute-start.31) | collective-permute-done | bytes 131104 | tf_op jit(solution)/shard_map/ppermute | solution.py:29
  117.9 1.2 collective-permute-start.38
  119.5 1.2 collective-permute-done.29
  122.2 2.0 %undo_keys.1.refs_4_ = bf16[256,256]{1,0:T(8,128)(2,1)} custom-call(f32[256,256]{1,0:T(8,128)} %copy-done.28, bf16[256,256]{1,0:T(8,128)(2,1)} %copy-done.38, bf16[256,256]{1,0:T(8,128)(2,1)} %copy-done.39, bf16[256,256]{1,0:T(8,128)(2,1)} %copy-done.40, f32[256,128]{1,0:T(8,128)} %get-tuple-element.126.cos_ref.refs_3_.refs_4_, ...), custom_call_target="tpu_custom_call" | custom-call | tf_op jit(solution)/shard_map/undo_keys/pallas_call | solution.py:446
  124.3 2.0 %fusion.5 = bf16[1024,256]{1,0:T(8,128)(2,1)S(1)} fusion(bf16[512,256]{1,0:T(8,128)(2,1)S(1)} %constant_dynamic-update-slice_fusion.16, bf16[1024,256]{1,0:T(8,128)(2,1)} %copy-done.47, bf16[512,4096]{1,0:T(8,128)(2,1)} %copy-done.34), kind=kOutput, calls=%fused_computation.14 | convolution fusion | flops 269221888 | bytes 2359296 | tf_op jit(solution)/shard_map/dot_general | solution.py:24
  126.3 1.4 convolution_convert_fusion.6
  128.8 1.2 collective-permute-start.34
  131.5 2.7 %collective-permute-done.37 = bf16[1024,256]{1,0:T(8,128)(2,1)} collective-permute-done((bf16[1024,256]{1,0:T(8,128)(2,1)}, bf16[1024,256]{1,0:T(8,128)(2,1)}, u32[]{:S(2)}, u32[]{:S(2)}) %collective-permute-start.37) | collective-permute-done | bytes 524320 | tf_op jit(solution)/shard_map/ppermute | solution.py:29
  135.0 1.7 fusion.4
  136.7 3.3 %collective-permute-start.41 = (bf16[256,256]{1,0:T(8,128)(2,1)S(1)}, bf16[256,256]{1,0:T(8,128)(2,1)S(1)}, u32[]{:S(2)}, u32[]{:S(2)}) collective-permute-start(bf16[256,256]{1,0:T(8,128)(2,1)S(1)} %get-tuple-element.114), channel_id=1, source_target_pairs={{0,3},{1,0},{2,1},{3,2},{4,7},{5,4},{6,5},{7,6},{8,11},{9,8},{10,9... | collective-permute-start | bytes 393224 | tf_op jit(solution)/shard_map/ppermute | solution.py:29
  140.2 3.0 %grad_columns.1 = bf16[256,4096]{1,0:T(8,128)(2,1)S(1)} custom-call(bf16[256,256]{1,0:T(8,128)(2,1)S(1)} %copy-done.25, bf16[256,256]{1,0:T(8,128)(2,1)S(1)} %collective-permute-done.28.refs_1_, bf16[256,256]{1,0:T(8,128)(2,1)S(1)} %collective-permute-done.33.refs_2_, bf16[1024,256]{1,0:T(8,128)(2,1)S(1)} %copy-done.3, ...), custom_call_target="tpu_custom_call" | custom-call | flops 1610612736 | bytes 8388608 | tf_op jit(solution)/shard_map/grad_columns/pallas_call | solution.py:233
  144.2 2.4 %collective-permute-start.43 = (bf16[256,256]{1,0:T(8,128)(2,1)S(1)}, bf16[256,256]{1,0:T(8,128)(2,1)S(1)}, u32[]{:S(2)}, u32[]{:S(2)}) collective-permute-start(bf16[256,256]{1,0:T(8,128)(2,1)S(1)} %get-tuple-element.112), channel_id=1, source_target_pairs={{0,1},{1,2},{2,3},{3,0},{4,5},{5,6},{6,7},{7,4},{8,9},{9,10},{10,1... | collective-permute-start | bytes 393224 | tf_op jit(solution)/shard_map/ppermute | solution.py:29
  146.6 1.6 collective-permute-done.42
  148.2 1.2 collective-permute-done.39
  150.0 1.0 collective-permute-start.44
  151.6 4.9 %collective-permute-start.46 = (bf16[256,256]{1,0:T(8,128)(2,1)S(1)}, bf16[256,256]{1,0:T(8,128)(2,1)S(1)}, u32[]{:S(2)}, u32[]{:S(2)}) collective-permute-start(bf16[256,256]{1,0:T(8,128)(2,1)S(1)} %get-tuple-element.118), channel_id=1, source_target_pairs={{0,3},{1,0},{2,1},{3,2},{4,7},{5,4},{6,5},{7,6},{8,11},{9,8},{10,9... | collective-permute-start | bytes 393224 | tf_op jit(solution)/shard_map/ppermute | solution.py:29
  156.5 5.2 %collective-permute-done.45 = bf16[1024,256]{1,0:T(8,128)(2,1)S(1)} collective-permute-done((bf16[1024,256]{1,0:T(8,128)(2,1)S(1)}, bf16[1024,256]{1,0:T(8,128)(2,1)S(1)}, u32[]{:S(2)}, u32[]{:S(2)}) %collective-permute-start.45) | collective-permute-done | bytes 524320 | tf_op jit(solution)/shard_map/ppermute | solution.py:29
  161.7 2.8 %collective-permute-start.48 = (bf16[256,256]{1,0:T(8,128)(2,1)S(1)}, bf16[256,256]{1,0:T(8,128)(2,1)S(1)}, u32[]{:S(2)}, u32[]{:S(2)}) collective-permute-start(bf16[256,256]{1,0:T(8,128)(2,1)S(1)} %get-tuple-element.116), channel_id=1, source_target_pairs={{0,1},{1,2},{2,3},{3,0},{4,5},{5,6},{6,7},{7,4},{8,9},{9,10},{10,1... | collective-permute-start | bytes 393224 | tf_op jit(solution)/shard_map/ppermute | solution.py:29
  164.6 4.8 %collective-permute-done.48 = bf16[256,256]{1,0:T(8,128)(2,1)S(1)} collective-permute-done((bf16[256,256]{1,0:T(8,128)(2,1)S(1)}, bf16[256,256]{1,0:T(8,128)(2,1)S(1)}, u32[]{:S(2)}, u32[]{:S(2)}) %collective-permute-start.48) | collective-permute-done | bytes 131104 | tf_op jit(solution)/shard_map/ppermute | solution.py:29
  170.0 2.1 %collective-permute-start.49 = (bf16[256,256]{1,0:T(8,128)(2,1)S(1)}, bf16[256,256]{1,0:T(8,128)(2,1)S(1)}, u32[]{:S(2)}, u32[]{:S(2)}) collective-permute-start(bf16[256,256]{1,0:T(8,128)(2,1)S(1)} %get-tuple-element.110), channel_id=1, source_target_pairs={{0,3},{1,0},{2,1},{3,2},{4,7},{5,4},{6,5},{7,6},{8,11},{9,8},{10,9... | collective-permute-start | bytes 393224 | tf_op jit(solution)/shard_map/ppermute | solution.py:29
  173.6 5.8 %grad_place.1 = bf16[256,8192]{1,0:T(8,128)(2,1)} custom-call(s32[4]{0:T(128)S(1)} %copy-done.33, s32[2,4]{1,0:T(2,128)S(1)} %copy-done.32, bf16[256,256]{1,0:T(8,128)(2,1)S(1)} %copy-done.23, bf16[256,256]{1,0:T(8,128)(2,1)S(1)} %get-tuple-element.87.refs_3_, bf16[256,256]{1,0:T(8,128)(2,1)S(1)} %copy-done.26, bf16[1024,256]{1,0:T(8,128)(2,1)S(1)} %copy-done.3, ...), custom_call_target="tpu_custom_call" | custom-call | flops 1610612736 | bytes 12582912 | tf_op jit(solution)/shard_map/grad_place/pallas_call | solution.py:257
  179.4 2.5 %collective-permute-done.50 = bf16[256,256]{1,0:T(8,128)(2,1)S(1)} collective-permute-done((bf16[256,256]{1,0:T(8,128)(2,1)S(1)}, bf16[256,256]{1,0:T(8,128)(2,1)S(1)}, u32[]{:S(2)}, u32[]{:S(2)}) %collective-permute-start.50) | collective-permute-done | bytes 131104 | tf_op jit(solution)/shard_map/ppermute | solution.py:29
  (216 shorter events, 29.5 us)
Async XLA Ops:
  0.6 17.2 %copy-start.36 = (f32[256,512]{1,0:T(8,128)S(1)}, f32[256,512]{1,0:T(8,128)}, u32[]{:S(2)}) copy-start(f32[256,512]{1,0:T(8,128)} %param.8) | copy-start | bytes 1572868
  0.6 20.4 %copy-start.45 = (s32[1024]{0:T(1024)S(1)}, s32[1024]{0:T(1024)}, u32[]{:S(2)}) copy-start(s32[1024]{0:T(1024)} %param.7) | copy-start | bytes 12292
  2.6 14.0 %collective-permute-start = (bf16[256,256]{1,0:T(8,128)(2,1)S(1)}, bf16[256,256]{1,0:T(8,128)(2,1)}, u32[]{:S(2)}, u32[]{:S(2)}) collective-permute-start(bf16[256,256]{1,0:T(8,128)(2,1)S(1)} %pad_maximum_fusion.4), channel_id=1, source_target_pairs={{0,1},{1,2},{2,3},{3,0},{4,5},{5,6},{6,7},{7,4},{8,9},{9,10},{10,1... | collective-permute-start | bytes 393224 | tf_op jit(solution)/shard_map/ppermute | solution.py:29
  5.6 12.0 %collective-permute-start.1 = (bf16[256,256]{1,0:T(8,128)(2,1)S(1)}, bf16[256,256]{1,0:T(8,128)(2,1)S(1)}, u32[]{:S(2)}, u32[]{:S(2)}) collective-permute-start(bf16[256,256]{1,0:T(8,128)(2,1)S(1)} %pad_maximum_fusion.4), channel_id=1, source_target_pairs={{0,2},{1,3},{2,0},{3,1},{4,6},{5,7},{6,4},{7,5},{8,10},{9,11},{10,... | collective-permute-start | bytes 393224 | tf_op jit(solution)/shard_map/ppermute | solution.py:29
  8.2 9.4 %collective-permute-start.2 = (bf16[256,256]{1,0:T(8,128)(2,1)S(1)}, bf16[256,256]{1,0:T(8,128)(2,1)S(1)}, u32[]{:S(2)}, u32[]{:S(2)}) collective-permute-start(bf16[256,256]{1,0:T(8,128)(2,1)S(1)} %pad_maximum_fusion.4), channel_id=1, source_target_pairs={{0,3},{1,0},{2,1},{3,2},{4,7},{5,4},{6,5},{7,6},{8,11},{9,8},{10,9... | collective-permute-start | bytes 393224 | tf_op jit(solution)/shard_map/ppermute | solution.py:29
  16.5 37.9 %copy-start = (bf16[256,4096]{1,0:T(8,128)(2,1)S(1)}, bf16[256,4096]{1,0:T(8,128)(2,1)}, u32[]{:S(2)}) copy-start(bf16[256,4096]{1,0:T(8,128)(2,1)} %get-tuple-element.82.refs_0_.refs_2_.refs_4_.refs_6_) | copy-start | bytes 6291460
  17.7 35.7 %copy-start.4 = (bf16[1024,256]{1,0:T(8,128)(2,1)}, bf16[1024,256]{1,0:T(8,128)(2,1)S(1)}, u32[]{:S(2)}) copy-start(bf16[1024,256]{1,0:T(8,128)(2,1)S(1)} %constant_dynamic-update-slice_fusion.refs_8_.refs_12_.refs_14_) | copy-start | bytes 1572868
  17.7 4.6 %collective-permute-start.3 = (bf16[256,4096]{1,0:T(8,128)(2,1)}, bf16[256,4096]{1,0:T(8,128)(2,1)}, u32[]{:S(2)}, u32[]{:S(2)}) collective-permute-start(bf16[256,4096]{1,0:T(8,128)(2,1)} %get-tuple-element.58), channel_id=1, source_target_pairs={{0,4},{4,0},{1,5},{5,1},{2,6},{6,2},{3,7},{7,3},{8,12},{12,8},{9,1... | collective-permute-start | bytes 6291464 | tf_op jit(solution)/shard_map/ppermute | solution.py:29
  18.0 17.7 %collective-permute-start.7 = (bf16[1024,256]{1,0:T(8,128)(2,1)S(1)}, bf16[1024,256]{1,0:T(8,128)(2,1)S(1)}, u32[]{:S(2)}, u32[]{:S(2)}) collective-permute-start(bf16[1024,256]{1,0:T(8,128)(2,1)S(1)} %constant_dynamic-update-slice_fusion.refs_8_.refs_12_.refs_14_), channel_id=1, source_target_pairs={{0,16},{16,0},{1,17},{17,1},{2,18},{18,2},{3,19},{19,3},{4,20},{20... | collective-permute-start | bytes 1572872 | tf_op jit(solution)/shard_map/ppermute | solution.py:29
  19.5 16.1 %collective-permute-start.8 = (bf16[1024,256]{1,0:T(8,128)(2,1)S(1)}, bf16[1024,256]{1,0:T(8,128)(2,1)S(1)}, u32[]{:S(2)}, u32[]{:S(2)}) collective-permute-start(bf16[1024,256]{1,0:T(8,128)(2,1)S(1)} %constant_dynamic-update-slice_fusion.refs_8_.refs_12_.refs_14_), channel_id=1, source_target_pairs={{0,8},{8,0},{1,9},{9,1},{2,10},{10,2},{3,11},{11,3},{4,12},{12,4},... | collective-permute-start | bytes 1572872 | tf_op jit(solution)/shard_map/ppermute | solution.py:29
  22.3 7.9 %collective-permute-start.4 = (bf16[256,256]{1,0:T(8,128)(2,1)S(1)}, bf16[256,256]{1,0:T(8,128)(2,1)S(1)}, u32[]{:S(2)}, u32[]{:S(2)}) collective-permute-start(bf16[256,256]{1,0:T(8,128)(2,1)S(1)} %get-tuple-element.59), channel_id=1, source_target_pairs={{0,1},{1,2},{2,3},{3,0},{4,5},{5,6},{6,7},{7,4},{8,9},{9,10},{10,1... | collective-permute-start | bytes 393224 | tf_op jit(solution)/shard_map/ppermute | solution.py:29
  26.0 9.4 %collective-permute-start.5 = (bf16[256,256]{1,0:T(8,128)(2,1)S(1)}, bf16[256,256]{1,0:T(8,128)(2,1)S(1)}, u32[]{:S(2)}, u32[]{:S(2)}) collective-permute-start(bf16[256,256]{1,0:T(8,128)(2,1)S(1)} %get-tuple-element.59), channel_id=1, source_target_pairs={{0,2},{1,3},{2,0},{3,1},{4,6},{5,7},{6,4},{7,5},{8,10},{9,11},{10,... | collective-permute-start | bytes 393224 | tf_op jit(solution)/shard_map/ppermute | solution.py:29
  27.7 7.9 %collective-permute-start.6 = (bf16[256,256]{1,0:T(8,128)(2,1)S(1)}, bf16[256,256]{1,0:T(8,128)(2,1)S(1)}, u32[]{:S(2)}, u32[]{:S(2)}) collective-permute-start(bf16[256,256]{1,0:T(8,128)(2,1)S(1)} %get-tuple-element.59), channel_id=1, source_target_pairs={{0,3},{1,0},{2,1},{3,2},{4,7},{5,4},{6,5},{7,6},{8,11},{9,8},{10,9... | collective-permute-start | bytes 393224 | tf_op jit(solution)/shard_map/ppermute | solution.py:29
  35.6 22.7 %copy-start.1 = (bf16[1024,256]{1,0:T(8,128)(2,1)}, bf16[1024,256]{1,0:T(8,128)(2,1)S(1)}, u32[]{:S(2)}) copy-start(bf16[1024,256]{1,0:T(8,128)(2,1)S(1)} %constant_dynamic-update-slice_fusion.4.refs_6_.refs_3_.refs_5_) | copy-start | bytes 1572868
  35.6 22.7 %copy-start.10 = (bf16[1024,256]{1,0:T(8,128)(2,1)}, bf16[1024,256]{1,0:T(8,128)(2,1)S(1)}, u32[]{:S(2)}) copy-start(bf16[1024,256]{1,0:T(8,128)(2,1)S(1)} %collective-permute-done.7.refs_10_.refs_14_.refs_16_) | copy-start | bytes 1572868
  35.7 16.9 %collective-permute-start.9 = (bf16[1024,256]{1,0:T(8,128)(2,1)S(1)}, bf16[1024,256]{1,0:T(8,128)(2,1)S(1)}, u32[]{:S(2)}, u32[]{:S(2)}) collective-permute-start(bf16[1024,256]{1,0:T(8,128)(2,1)S(1)} %constant_dynamic-update-slice_fusion.4.refs_6_.refs_3_.refs_5_), channel_id=1, source_target_pairs={{0,16},{16,0},{1,17},{17,1},{2,18},{18,2},{3,19},{19,3},{4,20},{20... | collective-permute-start | bytes 1572872 | tf_op jit(solution)/shard_map/ppermute | solution.py:29
  37.2 16.1 %collective-permute-start.10 = (bf16[1024,256]{1,0:T(8,128)(2,1)S(1)}, bf16[1024,256]{1,0:T(8,128)(2,1)S(1)}, u32[]{:S(2)}, u32[]{:S(2)}) collective-permute-start(bf16[1024,256]{1,0:T(8,128)(2,1)S(1)} %collective-permute-done.7.refs_10_.refs_14_.refs_16_), channel_id=1, source_target_pairs={{0,8},{8,0},{1,9},{9,1},{2,10},{10,2},{3,11},{11,3},{4,12},{12,4},... | collective-permute-start | bytes 1572872 | tf_op jit(solution)/shard_map/ppermute | solution.py:29
  38.7 8.2 %collective-permute-start.12 = (bf16[256,256]{1,0:T(8,128)(2,1)S(1)}, bf16[256,256]{1,0:T(8,128)(2,1)S(1)}, u32[]{:S(2)}, u32[]{:S(2)}) collective-permute-start(bf16[256,256]{1,0:T(8,128)(2,1)S(1)} %get-tuple-element.64), channel_id=1, source_target_pairs={{0,1},{1,2},{2,3},{3,0},{4,5},{5,6},{6,7},{7,4},{8,9},{9,10},{10,1... | collective-permute-start | bytes 393224 | tf_op jit(solution)/shard_map/ppermute | solution.py:29
  41.8 9.4 %collective-permute-start.13 = (bf16[256,256]{1,0:T(8,128)(2,1)S(1)}, bf16[256,256]{1,0:T(8,128)(2,1)S(1)}, u32[]{:S(2)}, u32[]{:S(2)}) collective-permute-start(bf16[256,256]{1,0:T(8,128)(2,1)S(1)} %get-tuple-element.64), channel_id=1, source_target_pairs={{0,2},{1,3},{2,0},{3,1},{4,6},{5,7},{6,4},{7,5},{8,10},{9,11},{10,... | collective-permute-start | bytes 393224 | tf_op jit(solution)/shard_map/ppermute | solution.py:29
  43.7 8.1 %collective-permute-start.14 = (bf16[256,256]{1,0:T(8,128)(2,1)S(1)}, bf16[256,256]{1,0:T(8,128)(2,1)S(1)}, u32[]{:S(2)}, u32[]{:S(2)}) collective-permute-start(bf16[256,256]{1,0:T(8,128)(2,1)S(1)} %get-tuple-element.64), channel_id=1, source_target_pairs={{0,3},{1,0},{2,1},{3,2},{4,7},{5,4},{6,5},{7,6},{8,11},{9,8},{10,9... | collective-permute-start | bytes 393224 | tf_op jit(solution)/shard_map/ppermute | solution.py:29
  53.4 15.7 %collective-permute-start.11 = (bf16[1024,256]{1,0:T(8,128)(2,1)S(1)}, bf16[1024,256]{1,0:T(8,128)(2,1)}, u32[]{:S(2)}, u32[]{:S(2)}) collective-permute-start(bf16[1024,256]{1,0:T(8,128)(2,1)S(1)} %constant_dynamic-update-slice_fusion.4.refs_6_.refs_3_.refs_5_), channel_id=1, source_target_pairs={{0,8},{8,0},{1,9},{9,1},{2,10},{10,2},{3,11},{11,3},{4,12},{12,4},... | collective-permute-start | bytes 1572872 | tf_op jit(solution)/shard_map/ppermute | solution.py:29
  53.9 15.1 %collective-permute-start.15 = (bf16[1024,256]{1,0:T(8,128)(2,1)}, bf16[1024,256]{1,0:T(8,128)(2,1)S(1)}, u32[]{:S(2)}, u32[]{:S(2)}) collective-permute-start(bf16[1024,256]{1,0:T(8,128)(2,1)} %constant_dynamic-update-slice_fusion.8.refs_6_.refs_7_.refs_9_), channel_id=1, source_target_pairs={{0,16},{16,0},{1,17},{17,1},{2,18},{18,2},{3,19},{19,3},{4,20},{20... | collective-permute-start | bytes 1572872 | tf_op jit(solution)/shard_map/ppermute | solution.py:29
  59.8 1.7 collective-permute-start.16
  63.4 21.1 %collective-permute-start.19 = (bf16[256,256]{1,0:T(8,128)(2,1)}, bf16[256,256]{1,0:T(8,128)(2,1)S(1)}, u32[]{:S(2)}, u32[]{:S(2)}) collective-permute-start(bf16[256,256]{1,0:T(8,128)(2,1)} %finish_keys.1.refs_7_), channel_id=1, source_target_pairs={{0,1},{1,2},{2,3},{3,0},{4,5},{5,6},{6,7},{7,4},{8,9},{9,10},{10,1... | collective-permute-start | bytes 393224 | tf_op jit(solution)/shard_map/ppermute | solution.py:29
  66.0 18.5 %collective-permute-start.20 = (bf16[256,256]{1,0:T(8,128)(2,1)}, bf16[256,256]{1,0:T(8,128)(2,1)S(1)}, u32[]{:S(2)}, u32[]{:S(2)}) collective-permute-start(bf16[256,256]{1,0:T(8,128)(2,1)} %finish_keys.1.refs_7_), channel_id=1, source_target_pairs={{0,2},{1,3},{2,0},{3,1},{4,6},{5,7},{6,4},{7,5},{8,10},{9,11},{10,... | collective-permute-start | bytes 393224 | tf_op jit(solution)/shard_map/ppermute | solution.py:29
  68.4 16.1 %collective-permute-start.21 = (bf16[256,256]{1,0:T(8,128)(2,1)}, bf16[256,256]{1,0:T(8,128)(2,1)S(1)}, u32[]{:S(2)}, u32[]{:S(2)}) collective-permute-start(bf16[256,256]{1,0:T(8,128)(2,1)} %finish_keys.1.refs_7_), channel_id=1, source_target_pairs={{0,3},{1,0},{2,1},{3,2},{4,7},{5,4},{6,5},{7,6},{8,11},{9,8},{10,9... | collective-permute-start | bytes 393224 | tf_op jit(solution)/shard_map/ppermute | solution.py:29
  69.0 13.5 %collective-permute-start.17 = (bf16[1024,256]{1,0:T(8,128)(2,1)}, bf16[1024,256]{1,0:T(8,128)(2,1)S(1)}, u32[]{:S(2)}, u32[]{:S(2)}) collective-permute-start(bf16[1024,256]{1,0:T(8,128)(2,1)} %collective-permute-done.11.refs_7_.refs_4_.refs_6_), channel_id=1, source_target_pairs={{0,16},{16,0},{1,17},{17,1},{2,18},{18,2},{3,19},{19,3},{4,20},{20... | collective-permute-start | bytes 1572872 | tf_op jit(solution)/shard_map/ppermute | solution.py:29
  70.5 13.9 %collective-permute-start.22 = (bf16[1024,256]{1,0:T(8,128)(2,1)}, bf16[1024,256]{1,0:T(8,128)(2,1)S(1)}, u32[]{:S(2)}, u32[]{:S(2)}) collective-permute-start(bf16[1024,256]{1,0:T(8,128)(2,1)} %constant_dynamic-update-slice_fusion.8.refs_6_.refs_7_.refs_9_), channel_id=1, source_target_pairs={{0,8},{8,0},{1,9},{9,1},{2,10},{10,2},{3,11},{11,3},{4,12},{12,4},... | collective-permute-start | bytes 1572872 | tf_op jit(solution)/shard_map/ppermute | solution.py:29
  84.4 5.1 %collective-permute-start.18 = (f32[256,256]{1,0:T(8,128)S(1)}, f32[256,256]{1,0:T(8,128)S(1)}, u32[]{:S(2)}, u32[]{:S(2)}) collective-permute-start(f32[256,256]{1,0:T(8,128)S(1)} %get-tuple-element.72), channel_id=1, source_target_pairs={{0,4},{4,0},{1,5},{5,1},{2,6},{6,2},{3,7},{7,3},{8,12},{12,8},{9,1... | collective-permute-start | bytes 786440 | tf_op jit(solution)/shard_map/ppermute | solution.py:29
  84.5 10.2 %collective-permute-start.24 = (bf16[512,256]{1,0:T(8,128)(2,1)S(1)}, bf16[512,256]{1,0:T(8,128)(2,1)S(1)}, u32[]{:S(2)}, u32[]{:S(2)}) collective-permute-start(bf16[512,256]{1,0:T(8,128)(2,1)S(1)} %slice.131), channel_id=1, source_target_pairs={{0,16},{16,0},{1,17},{17,1},{2,18},{18,2},{3,19},{19,3},{4,20},{20... | collective-permute-start | bytes 786440 | tf_op jit(solution)/shard_map/ppermute | solution.py:29
  86.1 8.6 %collective-permute-start.23 = (bf16[512,256]{1,0:T(8,128)(2,1)S(1)}, bf16[512,256]{1,0:T(8,128)(2,1)S(1)}, u32[]{:S(2)}, u32[]{:S(2)}) collective-permute-start(bf16[512,256]{1,0:T(8,128)(2,1)S(1)} %slice.130), channel_id=1, source_target_pairs={{0,8},{8,0},{1,9},{9,1},{2,10},{10,2},{3,11},{11,3},{4,12},{12,4},... | collective-permute-start | bytes 786440 | tf_op jit(solution)/shard_map/ppermute | solution.py:29
  89.4 22.0 %copy-start.34 = (bf16[512,4096]{1,0:T(8,128)(2,1)}, bf16[512,4096]{1,0:T(8,128)(2,1)S(1)}, u32[]{:S(2)}) copy-start(bf16[512,4096]{1,0:T(8,128)(2,1)S(1)} %constant_dynamic-update-slice_fusion.12) | copy-start | bytes 12582916
  92.0 4.8 %collective-permute-start.25 = (bf16[256,256]{1,0:T(8,128)(2,1)S(1)}, bf16[256,256]{1,0:T(8,128)(2,1)S(1)}, u32[]{:S(2)}, u32[]{:S(2)}) collective-permute-start(bf16[256,256]{1,0:T(8,128)(2,1)S(1)} %get-tuple-element.83.refs_2_), channel_id=1, source_target_pairs={{0,4},{4,0},{1,5},{5,1},{2,6},{6,2},{3,7},{7,3},{8,12},{12,8},{9,1... | collective-permute-start | bytes 393224 | tf_op jit(solution)/shard_map/ppermute | solution.py:29
  96.3 3.3 %collective-permute-start.26 = (f32[256,256]{1,0:T(8,128)S(1)}, f32[256,256]{1,0:T(8,128)S(1)}, u32[]{:S(2)}, u32[]{:S(2)}) collective-permute-start(f32[256,256]{1,0:T(8,128)S(1)} %get-tuple-element.85), channel_id=1, source_target_pairs={{0,4},{4,0},{1,5},{5,1},{2,6},{6,2},{3,7},{7,3},{8,12},{12,8},{9,1... | collective-permute-start | bytes 786440 | tf_op jit(solution)/shard_map/ppermute | solution.py:29
  96.9 14.4 %copy-start.43 = (bf16[512,256]{1,0:T(8,128)(2,1)}, bf16[512,256]{1,0:T(8,128)(2,1)S(1)}, u32[]{:S(2)}) copy-start(bf16[512,256]{1,0:T(8,128)(2,1)S(1)} %constant_dynamic-update-slice_fusion.14) | copy-start | bytes 786436
  97.4 13.9 %collective-permute-start.27 = (bf16[1024,256]{1,0:T(8,128)(2,1)S(1)}, bf16[1024,256]{1,0:T(8,128)(2,1)S(1)}, u32[]{:S(2)}, u32[]{:S(2)}) collective-permute-start(bf16[1024,256]{1,0:T(8,128)(2,1)S(1)} %convolution_convert_fusion.3), channel_id=1, source_target_pairs={{0,8},{8,0},{1,9},{9,1},{2,10},{10,2},{3,11},{11,3},{4,12},{12,4},... | collective-permute-start | bytes 1572872 | tf_op jit(solution)/shard_map/ppermute | solution.py:29
  102.5 4.3 %collective-permute-start.28 = (bf16[256,256]{1,0:T(8,128)(2,1)S(1)}, bf16[256,256]{1,0:T(8,128)(2,1)S(1)}, u32[]{:S(2)}, u32[]{:S(2)}) collective-permute-start(bf16[256,256]{1,0:T(8,128)(2,1)S(1)} %get-tuple-element.87.refs_3_), channel_id=1, source_target_pairs={{0,4},{4,0},{1,5},{5,1},{2,6},{6,2},{3,7},{7,3},{8,12},{12,8},{9,1... | collective-permute-start | bytes 393224 | tf_op jit(solution)/shard_map/ppermute | solution.py:29
  102.8 9.9 %collective-permute-start.30 = (bf16[256,256]{1,0:T(8,128)(2,1)S(1)}, bf16[256,256]{1,0:T(8,128)(2,1)S(1)}, u32[]{:S(2)}, u32[]{:S(2)}) collective-permute-start(bf16[256,256]{1,0:T(8,128)(2,1)S(1)} %get-tuple-element.89), channel_id=1, source_target_pairs={{0,3},{1,0},{2,1},{3,2},{4,7},{5,4},{6,5},{7,6},{8,11},{9,8},{10,9... | collective-permute-start | bytes 393224 | tf_op jit(solution)/shard_map/ppermute | solution.py:29
  104.2 13.7 %collective-permute-start.31 = (bf16[256,256]{1,0:T(8,128)(2,1)S(1)}, bf16[256,256]{1,0:T(8,128)(2,1)S(1)}, u32[]{:S(2)}, u32[]{:S(2)}) collective-permute-start(bf16[256,256]{1,0:T(8,128)(2,1)S(1)} %get-tuple-element.90), channel_id=1, source_target_pairs={{0,2},{1,3},{2,0},{3,1},{4,6},{5,7},{6,4},{7,5},{8,10},{9,11},{10,... | collective-permute-start | bytes 393224 | tf_op jit(solution)/shard_map/ppermute | solution.py:29
  105.7 15.8 %collective-permute-start.32 = (bf16[256,256]{1,0:T(8,128)(2,1)S(1)}, bf16[256,256]{1,0:T(8,128)(2,1)S(1)}, u32[]{:S(2)}, u32[]{:S(2)}) collective-permute-start(bf16[256,256]{1,0:T(8,128)(2,1)S(1)} %get-tuple-element.94), channel_id=1, source_target_pairs={{0,1},{1,2},{2,3},{3,0},{4,5},{5,6},{6,7},{7,4},{8,9},{9,10},{10,1... | collective-permute-start | bytes 393224 | tf_op jit(solution)/shard_map/ppermute | solution.py:29
  106.8 17.4 %copy-start.41 = (bf16[512,256]{1,0:T(8,128)(2,1)}, bf16[512,256]{1,0:T(8,128)(2,1)S(1)}, u32[]{:S(2)}) copy-start(bf16[512,256]{1,0:T(8,128)(2,1)S(1)} %constant_dynamic-update-slice_fusion.16) | copy-start | bytes 786436
  107.3 13.4 %collective-permute-start.29 = (bf16[1024,256]{1,0:T(8,128)(2,1)S(1)}, bf16[1024,256]{1,0:T(8,128)(2,1)S(1)}, u32[]{:S(2)}, u32[]{:S(2)}) collective-permute-start(bf16[1024,256]{1,0:T(8,128)(2,1)S(1)} %convolution_convert_fusion.2), channel_id=1, source_target_pairs={{0,16},{16,0},{1,17},{17,1},{2,18},{18,2},{3,19},{19,3},{4,20},{20... | collective-permute-start | bytes 1572872 | tf_op jit(solution)/shard_map/ppermute | solution.py:29
  117.9 13.7 %collective-permute-start.38 = (bf16[1024,256]{1,0:T(8,128)(2,1)}, bf16[1024,256]{1,0:T(8,128)(2,1)}, u32[]{:S(2)}, u32[]{:S(2)}) collective-permute-start(bf16[1024,256]{1,0:T(8,128)(2,1)} %convolution_convert_fusion.1), channel_id=1, source_target_pairs={{0,8},{8,0},{1,9},{9,1},{2,10},{10,2},{3,11},{11,3},{4,12},{12,4},... | collective-permute-start | bytes 1572872 | tf_op jit(solution)/shard_map/ppermute | solution.py:29
  119.0 15.2 %collective-permute-start.37 = (bf16[1024,256]{1,0:T(8,128)(2,1)}, bf16[1024,256]{1,0:T(8,128)(2,1)}, u32[]{:S(2)}, u32[]{:S(2)}) collective-permute-start(bf16[1024,256]{1,0:T(8,128)(2,1)} %fusion.3), channel_id=1, source_target_pairs={{0,16},{16,0},{1,17},{17,1},{2,18},{18,2},{3,19},{19,3},{4,20},{20... | collective-permute-start | bytes 1572872 | tf_op jit(solution)/shard_map/ppermute | solution.py:29
  124.2 2.1 %collective-permute-start.33 = (bf16[256,256]{1,0:T(8,128)(2,1)}, bf16[256,256]{1,0:T(8,128)(2,1)S(1)}, u32[]{:S(2)}, u32[]{:S(2)}) collective-permute-start(bf16[256,256]{1,0:T(8,128)(2,1)} %undo_keys.1.refs_4_), channel_id=1, source_target_pairs={{0,4},{4,0},{1,5},{5,1},{2,6},{6,2},{3,7},{7,3},{8,12},{12,8},{9,1... | collective-permute-start | bytes 393224 | tf_op jit(solution)/shard_map/ppermute | solution.py:29
  127.7 12.3 %collective-permute-start.35 = (bf16[512,256]{1,0:T(8,128)(2,1)S(1)}, bf16[512,256]{1,0:T(8,128)(2,1)S(1)}, u32[]{:S(2)}, u32[]{:S(2)}) collective-permute-start(bf16[512,256]{1,0:T(8,128)(2,1)S(1)} %convolution_convert_fusion.6), channel_id=1, source_target_pairs={{0,16},{16,0},{1,17},{17,1},{2,18},{18,2},{3,19},{19,3},{4,20},{20... | collective-permute-start | bytes 786440 | tf_op jit(solution)/shard_map/ppermute | solution.py:29
  128.8 11.4 %collective-permute-start.34 = (bf16[512,256]{1,0:T(8,128)(2,1)S(1)}, bf16[512,256]{1,0:T(8,128)(2,1)S(1)}, u32[]{:S(2)}, u32[]{:S(2)}) collective-permute-start(bf16[512,256]{1,0:T(8,128)(2,1)S(1)} %convolution_convert_fusion.7), channel_id=1, source_target_pairs={{0,8},{8,0},{1,9},{9,1},{2,10},{10,2},{3,11},{11,3},{4,12},{12,4},... | collective-permute-start | bytes 786440 | tf_op jit(solution)/shard_map/ppermute | solution.py:29
  134.2 15.1 %collective-permute-start.39 = (bf16[1024,256]{1,0:T(8,128)(2,1)S(1)}, bf16[1024,256]{1,0:T(8,128)(2,1)S(1)}, u32[]{:S(2)}, u32[]{:S(2)}) collective-permute-start(bf16[1024,256]{1,0:T(8,128)(2,1)S(1)} %copy-done.46), channel_id=1, source_target_pairs={{0,16},{16,0},{1,17},{17,1},{2,18},{18,2},{3,19},{19,3},{4,20},{20... | collective-permute-start | bytes 1572872 | tf_op jit(solution)/shard_map/ppermute | solution.py:29
  134.7 14.6 %collective-permute-start.40 = (bf16[1024,256]{1,0:T(8,128)(2,1)S(1)}, bf16[1024,256]{1,0:T(8,128)(2,1)S(1)}, u32[]{:S(2)}, u32[]{:S(2)}) collective-permute-start(bf16[1024,256]{1,0:T(8,128)(2,1)S(1)} %fusion.5), channel_id=1, source_target_pairs={{0,8},{8,0},{1,9},{9,1},{2,10},{10,2},{3,11},{11,3},{4,12},{12,4},... | collective-permute-start | bytes 1572872 | tf_op jit(solution)/shard_map/ppermute | solution.py:29
  136.7 7.5 %collective-permute-start.41 = (bf16[256,256]{1,0:T(8,128)(2,1)S(1)}, bf16[256,256]{1,0:T(8,128)(2,1)S(1)}, u32[]{:S(2)}, u32[]{:S(2)}) collective-permute-start(bf16[256,256]{1,0:T(8,128)(2,1)S(1)} %get-tuple-element.114), channel_id=1, source_target_pairs={{0,3},{1,0},{2,1},{3,2},{4,7},{5,4},{6,5},{7,6},{8,11},{9,8},{10,9... | collective-permute-start | bytes 393224 | tf_op jit(solution)/shard_map/ppermute | solution.py:29
  140.0 8.1 %collective-permute-start.42 = (bf16[256,256]{1,0:T(8,128)(2,1)S(1)}, bf16[256,256]{1,0:T(8,128)(2,1)S(1)}, u32[]{:S(2)}, u32[]{:S(2)}) collective-permute-start(bf16[256,256]{1,0:T(8,128)(2,1)S(1)} %get-tuple-element.113), channel_id=1, source_target_pairs={{0,2},{1,3},{2,0},{3,1},{4,6},{5,7},{6,4},{7,5},{8,10},{9,11},{10,... | collective-permute-start | bytes 393224 | tf_op jit(solution)/shard_map/ppermute | solution.py:29
  143.3 30.3 %collective-permute-start.36 = (bf16[256,4096]{1,0:T(8,128)(2,1)S(1)}, bf16[256,4096]{1,0:T(8,128)(2,1)S(1)}, u32[]{:S(2)}, u32[]{:S(2)}) collective-permute-start(bf16[256,4096]{1,0:T(8,128)(2,1)S(1)} %grad_columns.1), channel_id=1, source_target_pairs={{0,4},{4,0},{1,5},{5,1},{2,6},{6,2},{3,7},{7,3},{8,12},{12,8},{9,1... | collective-permute-start | bytes 6291464 | tf_op jit(solution)/shard_map/ppermute | solution.py:29
  144.2 12.3 %collective-permute-start.43 = (bf16[256,256]{1,0:T(8,128)(2,1)S(1)}, bf16[256,256]{1,0:T(8,128)(2,1)S(1)}, u32[]{:S(2)}, u32[]{:S(2)}) collective-permute-start(bf16[256,256]{1,0:T(8,128)(2,1)S(1)} %get-tuple-element.112), channel_id=1, source_target_pairs={{0,1},{1,2},{2,3},{3,0},{4,5},{5,6},{6,7},{7,4},{8,9},{9,10},{10,1... | collective-permute-start | bytes 393224 | tf_op jit(solution)/shard_map/ppermute | solution.py:29
  149.4 12.3 %collective-permute-start.45 = (bf16[1024,256]{1,0:T(8,128)(2,1)S(1)}, bf16[1024,256]{1,0:T(8,128)(2,1)S(1)}, u32[]{:S(2)}, u32[]{:S(2)}) collective-permute-start(bf16[1024,256]{1,0:T(8,128)(2,1)S(1)} %pad_maximum_fusion.1), channel_id=1, source_target_pairs={{0,8},{8,0},{1,9},{9,1},{2,10},{10,2},{3,11},{11,3},{4,12},{12,4},... | collective-permute-start | bytes 1572872 | tf_op jit(solution)/shard_map/ppermute | solution.py:29
  150.0 14.6 %collective-permute-start.44 = (bf16[1024,256]{1,0:T(8,128)(2,1)S(1)}, bf16[1024,256]{1,0:T(8,128)(2,1)S(1)}, u32[]{:S(2)}, u32[]{:S(2)}) collective-permute-start(bf16[1024,256]{1,0:T(8,128)(2,1)S(1)} %pad_maximum_fusion), channel_id=1, source_target_pairs={{0,16},{16,0},{1,17},{17,1},{2,18},{18,2},{3,19},{19,3},{4,20},{20... | collective-permute-start | bytes 1572872 | tf_op jit(solution)/shard_map/ppermute | solution.py:29
  151.5 22.1 %copy-start.23 = (bf16[256,256]{1,0:T(8,128)(2,1)S(1)}, bf16[256,256]{1,0:T(8,128)(2,1)}, u32[]{:S(2)}) copy-start(bf16[256,256]{1,0:T(8,128)(2,1)} %copy-done.22) | copy-start | bytes 393220
  151.5 22.1 %copy-start.32 = (s32[2,4]{1,0:T(2,128)S(1)}, s32[2,4]{1,0:T(2,128)}, u32[]{:S(2)}) copy-start(s32[2,4]{1,0:T(2,128)} %pad_add_fusion.1.piece_ref.refs_1_) | copy-start | bytes 100
  151.6 22.0 %copy-start.33 = (s32[4]{0:T(128)S(1)}, s32[4]{0:T(128)}, u32[]{:S(2)}) copy-start(s32[4]{0:T(128)} %fusion.26.slab_ref.refs_0_) | copy-start | bytes 52
  151.6 13.0 %collective-permute-start.46 = (bf16[256,256]{1,0:T(8,128)(2,1)S(1)}, bf16[256,256]{1,0:T(8,128)(2,1)S(1)}, u32[]{:S(2)}, u32[]{:S(2)}) collective-permute-start(bf16[256,256]{1,0:T(8,128)(2,1)S(1)} %get-tuple-element.118), channel_id=1, source_target_pairs={{0,3},{1,0},{2,1},{3,2},{4,7},{5,4},{6,5},{7,6},{8,11},{9,8},{10,9... | collective-permute-start | bytes 393224 | tf_op jit(solution)/shard_map/ppermute | solution.py:29
  156.5 8.1 %collective-permute-start.47 = (bf16[256,256]{1,0:T(8,128)(2,1)S(1)}, bf16[256,256]{1,0:T(8,128)(2,1)S(1)}, u32[]{:S(2)}, u32[]{:S(2)}) collective-permute-start(bf16[256,256]{1,0:T(8,128)(2,1)S(1)} %get-tuple-element.117), channel_id=1, source_target_pairs={{0,2},{1,3},{2,0},{3,1},{4,6},{5,7},{6,4},{7,5},{8,10},{9,11},{10,... | collective-permute-start | bytes 393224 | tf_op jit(solution)/shard_map/ppermute | solution.py:29
  161.7 7.7 %collective-permute-start.48 = (bf16[256,256]{1,0:T(8,128)(2,1)S(1)}, bf16[256,256]{1,0:T(8,128)(2,1)S(1)}, u32[]{:S(2)}, u32[]{:S(2)}) collective-permute-start(bf16[256,256]{1,0:T(8,128)(2,1)S(1)} %get-tuple-element.116), channel_id=1, source_target_pairs={{0,1},{1,2},{2,3},{3,0},{4,5},{5,6},{6,7},{7,4},{8,9},{9,10},{10,1... | collective-permute-start | bytes 393224 | tf_op jit(solution)/shard_map/ppermute | solution.py:29
  170.0 9.4 %collective-permute-start.49 = (bf16[256,256]{1,0:T(8,128)(2,1)S(1)}, bf16[256,256]{1,0:T(8,128)(2,1)S(1)}, u32[]{:S(2)}, u32[]{:S(2)}) collective-permute-start(bf16[256,256]{1,0:T(8,128)(2,1)S(1)} %get-tuple-element.110), channel_id=1, source_target_pairs={{0,3},{1,0},{2,1},{3,2},{4,7},{5,4},{6,5},{7,6},{8,11},{9,8},{10,9... | collective-permute-start | bytes 393224 | tf_op jit(solution)/shard_map/ppermute | solution.py:29
  172.1 9.9 %collective-permute-start.50 = (bf16[256,256]{1,0:T(8,128)(2,1)S(1)}, bf16[256,256]{1,0:T(8,128)(2,1)S(1)}, u32[]{:S(2)}, u32[]{:S(2)}) collective-permute-start(bf16[256,256]{1,0:T(8,128)(2,1)S(1)} %get-tuple-element.109), channel_id=1, source_target_pairs={{0,2},{1,3},{2,0},{3,1},{4,6},{5,7},{6,4},{7,5},{8,10},{9,11},{10,... | collective-permute-start | bytes 393224 | tf_op jit(solution)/shard_map/ppermute | solution.py:29
  172.1 9.9 %collective-permute-start.51 = (bf16[256,256]{1,0:T(8,128)(2,1)S(1)}, bf16[256,256]{1,0:T(8,128)(2,1)S(1)}, u32[]{:S(2)}, u32[]{:S(2)}) collective-permute-start(bf16[256,256]{1,0:T(8,128)(2,1)S(1)} %get-tuple-element.108), channel_id=1, source_target_pairs={{0,1},{1,2},{2,3},{3,0},{4,5},{5,6},{6,7},{7,4},{8,9},{9,10},{10,1... | collective-permute-start | bytes 393224 | tf_op jit(solution)/shard_map/ppermute | solution.py:29
  (36 other events, 249.5 us)

commit v7 on v6

--- a/solution.py
+++ b/solution.py
@@ -570,7 +570,7 @@
     summed = [terms[0]] + [shift(terms[k], "ctx", -k) for k in range(1, ctx)]
     first = [*came[0][0].values(), *came[0][1].values()]
     second = [*came[1][0].values(), *came[1][1].values()]
-    sides0, went0 = reduce_sides(made[0], came[0], "b", mid, *first, *summed[1:-1])
+    sides0, went0 = reduce_sides(made[0], came[0], "b", mid, *first, *summed[1:2])
     grad_kv = undo_keys(
         [after(summed[0], *first, *second, *went0), *summed[1:]], cos_table, sin_table
     )
@@ -584,7 +584,7 @@
     q_grads = [add_line(sent0, sides1)]
     line1 = made[1](0, slice(None), sides1)
     kv_sides, _ = reduce_sides(made[2], came[2], "both", mid, *sides1, *sent0[1:-1])
-    q_grads.append(add_line(send_line(line1), kv_sides))
+    sent1 = send_line(line1)
 
     weights = [*q_slabs, kv_slabs]
     grad_theirs = grad_columns(
@@ -594,7 +594,8 @@
     grad_input = grad_place(
         [gradients[0][0], gradients[1][0], gradients[2][0]], weights, grad_theirs, slabs, pieces, block
     )
-    kv_term = after(made[2](0, slice(None), kv_sides), *q_grads)
+    kv_term = after(made[2](0, slice(None), kv_sides), q_grads[0], *sent1[1:-1])
+    q_grads.append(add_line(sent1, (grad_input,)))
     kv_wgrad = add_line(send_line(kv_term), (grad_input,))
 
     query_grad = jnp.concatenate(q_grads, axis=1)

time: 183 us -> 191 us (1.044)
  waiting for transfers between devices: 48.4 us -> 61.1 us
  starting transfers between devices: 64.6 us -> 58.9 us
    ppermute x52, waiting for transfers between devices: 48.4 us -> 61.1 us  [shift(): lax.ppermute(block, axis, [(i, (i + step) % size) for i in range(size)])]
    ppermute x52, starting transfers between devices: 64.6 us -> 58.9 us  [shift(): lax.ppermute(block, axis, [(i, (i + step) % size) for i in range(size)])]
  transfers between devices with their start and end apart: 52 -> 52, of which waited for: 18 -> 17; matrix products, arithmetic and copies ran while one was open for 14% -> 13% of each run, Pallas kernels for 19% -> 18%
where the time goes in v7:
time: 191 us
  waiting for transfers between devices  61.1 us (32%)
  starting transfers between devices  58.9 us (31%)
  Pallas kernels  35 us (18%)
  local copies, waits for them, and re-layouts  13.5 us (7%)
  matrix products  12.8 us (7%)
  other arithmetic  7.51 us (4%)
    ppermute x52, waiting for transfers between devices, shift(): lax.ppermute(block, axis, [(i, (i + step) % size) for i in range(size)])  61.1 us
    ppermute x52, starting transfers between devices, shift(): lax.ppermute(block, axis, [(i, (i + step) % size) for i in range(size)])  58.9 us
    dot_general x15, matrix products, mm(): lax.dot_general(a, b, (dims, ((), ())), preferred_element_type=jnp.float32)  12.8 us
    pallas_call x5, Pallas kernels, project_rows(): pl.pallas_call(functools.partial(project_kernel, counts=[len(slab) for sl...  11.2 us
    unnamed x108, local copies, waits for them, and re-layouts  8.99 us
    pallas_call x1, Pallas kernels, grad_place(): pl.pallas_call(functools.partial(grad_place_kernel, shape=shape, plane=pl...  5.84 us
    pallas_call x1, Pallas kernels, pick_columns(): pl.pallas_call(functools.partial(pick_kernel, block=block), grid_spec=plt...  5.62 us
    pallas_call x2, Pallas kernels, attend(): pl.pallas_call(functools.partial(attend_kernel, group=group, parts=parts,...  5.41 us
  transfers between devices with their start and end apart: 52, of which 17 were waited for; matrix products, arithmetic and copies ran while one was open for 13% of the time, Pallas kernels for 18%

profile of v7, /device:TPU:0, one launch (start us, length us, event | category | flops | bytes accessed | tf_op | source)
XLA Modules:
  0.0 190.5 jit_solution(11861635923191399199)
XLA Ops:
  0.7 1.0 convert.10
  1.6 0.9 convert.11
  2.6 3.1 %collective-permute-start = (bf16[256,256]{1,0:T(8,128)(2,1)S(1)}, bf16[256,256]{1,0:T(8,128)(2,1)}, u32[]{:S(2)}, u32[]{:S(2)}) collective-permute-start(bf16[256,256]{1,0:T(8,128)(2,1)S(1)} %pad_maximum_fusion.4), channel_id=1, source_target_pairs={{0,1},{1,2},{2,3},{3,0},{4,5},{5,6},{6,7},{7,4},{8,9},{9,10},{10,1... | collective-permute-start | bytes 393224 | tf_op jit(solution)/shard_map/ppermute | solution.py:29
  5.6 2.6 %collective-permute-start.1 = (bf16[256,256]{1,0:T(8,128)(2,1)S(1)}, bf16[256,256]{1,0:T(8,128)(2,1)S(1)}, u32[]{:S(2)}, u32[]{:S(2)}) collective-permute-start(bf16[256,256]{1,0:T(8,128)(2,1)S(1)} %pad_maximum_fusion.4), channel_id=1, source_target_pairs={{0,2},{1,3},{2,0},{3,1},{4,6},{5,7},{6,4},{7,5},{8,10},{9,11},{10,... | collective-permute-start | bytes 393224 | tf_op jit(solution)/shard_map/ppermute | solution.py:29
  8.2 1.3 collective-permute-start.2
  10.9 5.6 %pick_columns.1 = (bf16[256,4096]{1,0:T(8,128)(2,1)}, bf16[256,4096]{1,0:T(8,128)(2,1)}) custom-call(s32[4]{0:T(128)} %fusion.26.slab_ref.refs_0_, s32[2,4]{1,0:T(2,128)} %pad_add_fusion.1.piece_ref.refs_1_, bf16[256,8192]{1,0:T(8,128)(2,1)} %bitcast.17), custom_call_target="tpu_custom_call" | custom-call | bytes 8388608 | tf_op jit(solution)/shard_map/pick_columns/pallas_call | solution.py:211
  16.6 1.1 constant_dynamic-update-slice_fusion.2
  18.0 1.6 collective-permute-start.7
  19.5 1.5 collective-permute-start.8
  22.3 2.5 %collective-permute-start.4 = (bf16[256,256]{1,0:T(8,128)(2,1)S(1)}, bf16[256,256]{1,0:T(8,128)(2,1)S(1)}, u32[]{:S(2)}, u32[]{:S(2)}) collective-permute-start(bf16[256,256]{1,0:T(8,128)(2,1)S(1)} %get-tuple-element.59), channel_id=1, source_target_pairs={{0,1},{1,2},{2,3},{3,0},{4,5},{5,6},{6,7},{7,4},{8,9},{9,10},{10,1... | collective-permute-start | bytes 393224 | tf_op jit(solution)/shard_map/ppermute | solution.py:29
  24.7 1.3 negate_select_fusion
  26.0 1.7 collective-permute-start.5
  28.6 1.6 collective-permute-done.4
  30.2 5.2 %collective-permute-done.5 = bf16[256,256]{1,0:T(8,128)(2,1)S(1)} collective-permute-done((bf16[256,256]{1,0:T(8,128)(2,1)S(1)}, bf16[256,256]{1,0:T(8,128)(2,1)S(1)}, u32[]{:S(2)}, u32[]{:S(2)}) %collective-permute-start.5) | collective-permute-done | bytes 131104 | tf_op jit(solution)/shard_map/ppermute | solution.py:29
  35.6 1.6 collective-permute-start.9
  37.2 1.5 collective-permute-start.10
  38.7 3.1 %collective-permute-start.12 = (bf16[256,256]{1,0:T(8,128)(2,1)S(1)}, bf16[256,256]{1,0:T(8,128)(2,1)S(1)}, u32[]{:S(2)}, u32[]{:S(2)}) collective-permute-start(bf16[256,256]{1,0:T(8,128)(2,1)S(1)} %get-tuple-element.64), channel_id=1, source_target_pairs={{0,1},{1,2},{2,3},{3,0},{4,5},{5,6},{6,7},{7,4},{8,9},{9,10},{10,1... | collective-permute-start | bytes 393224 | tf_op jit(solution)/shard_map/ppermute | solution.py:29
  41.8 1.3 collective-permute-start.13
  43.8 1.1 collective-permute-start.14
  44.8 2.1 %collective-permute-done.12 = bf16[256,256]{1,0:T(8,128)(2,1)S(1)} collective-permute-done((bf16[256,256]{1,0:T(8,128)(2,1)S(1)}, bf16[256,256]{1,0:T(8,128)(2,1)S(1)}, u32[]{:S(2)}, u32[]{:S(2)}) %collective-permute-start.12) | collective-permute-done | bytes 131104 | tf_op jit(solution)/shard_map/ppermute | solution.py:29
  47.6 3.6 %collective-permute-done.13 = bf16[256,256]{1,0:T(8,128)(2,1)S(1)} collective-permute-done((bf16[256,256]{1,0:T(8,128)(2,1)S(1)}, bf16[256,256]{1,0:T(8,128)(2,1)S(1)}, u32[]{:S(2)}, u32[]{:S(2)}) %collective-permute-start.13) | collective-permute-done | bytes 131104 | tf_op jit(solution)/shard_map/ppermute | solution.py:29
  54.5 1.0 copy-done.5
  55.5 2.8 %project_rows.5 = (f32[256,256]{1,0:T(8,128)S(1)}, f32[256,256]{1,0:T(8,128)S(1)}) custom-call(bf16[256,4096]{1,0:T(8,128)(2,1)S(1)} %copy-done, bf16[256,4096]{1,0:T(8,128)(2,1)} %collective-permute-done.3.refs_1_.refs_3_.refs_5_.refs_7_, bf16[256,4096]{1,0:T(8,128)(2,1)S(1)} %copy-done, ...), custom_call_target="tpu_custom_call" | custom-call | flops 1073741824 | bytes 6291456 | tf_op jit(solution)/shard_map/project_rows/pallas_call | solution.py:312
  61.5 1.9 finish_keys.1.refs_7_
  63.4 2.6 %collective-permute-start.19 = (bf16[256,256]{1,0:T(8,128)(2,1)}, bf16[256,256]{1,0:T(8,128)(2,1)S(1)}, u32[]{:S(2)}, u32[]{:S(2)}) collective-permute-start(bf16[256,256]{1,0:T(8,128)(2,1)} %finish_keys.1.refs_7_), channel_id=1, source_target_pairs={{0,1},{1,2},{2,3},{3,0},{4,5},{5,6},{6,7},{7,4},{8,9},{9,10},{10,1... | collective-permute-start | bytes 393224 | tf_op jit(solution)/shard_map/ppermute | solution.py:29
  66.0 2.4 %collective-permute-start.20 = (bf16[256,256]{1,0:T(8,128)(2,1)}, bf16[256,256]{1,0:T(8,128)(2,1)S(1)}, u32[]{:S(2)}, u32[]{:S(2)}) collective-permute-start(bf16[256,256]{1,0:T(8,128)(2,1)} %finish_keys.1.refs_7_), channel_id=1, source_target_pairs={{0,2},{1,3},{2,0},{3,1},{4,6},{5,7},{6,4},{7,5},{8,10},{9,11},{10,... | collective-permute-start | bytes 393224 | tf_op jit(solution)/shard_map/ppermute | solution.py:29
  69.0 1.5 collective-permute-start.17
  70.6 1.5 collective-permute-start.22
  72.3 2.5 %project_rows.6 = (f32[256,256]{1,0:T(8,128)S(1)}, f32[256,256]{1,0:T(8,128)S(1)}) custom-call(bf16[256,4096]{1,0:T(8,128)(2,1)S(1)} %copy-done, bf16[256,4096]{1,0:T(8,128)(2,1)} %collective-permute-done.3.refs_1_.refs_3_.refs_5_.refs_7_, bf16[256,4096]{1,0:T(8,128)(2,1)S(1)} %copy-done, ...), custom_call_target="tpu_custom_call" | custom-call | flops 805306368 | bytes 4718592 | tf_op jit(solution)/shard_map/project_rows/pallas_call | solution.py:312
  74.9 7.7 %collective-permute-done.17.refs_2_.refs_6_.refs_8_ = bf16[1024,256]{1,0:T(8,128)(2,1)S(1)} collective-permute-done((bf16[1024,256]{1,0:T(8,128)(2,1)}, bf16[1024,256]{1,0:T(8,128)(2,1)S(1)}, u32[]{:S(2)}, u32[]{:S(2)}) %collective-permute-start.17) | collective-permute-done | bytes 524320 | tf_op jit(solution)/shard_map/ppermute | solution.py:29
  82.6 1.8 project_rows.7
  84.5 1.6 collective-permute-start.24
  86.1 1.5 collective-permute-start.23
  87.6 1.8 constant_dynamic-update-slice_fusion.12
  89.5 2.6 %attend.2 = (bf16[256,256]{1,0:T(8,128)(2,1)S(1)}, bf16[256,256]{1,0:T(8,128)(2,1)S(1)}, f32[1024,256]{1,0:T(8,128)S(1)}) custom-call(f32[256,256]{1,0:T(8,128)S(1)} %get-tuple-element.71.refs_0_, f32[256,256]{1,0:T(8,128)S(1)} %collective-permute-done.18.refs_1_, bf16[256,256]{1,0:T(8,128)(2,1)S(1)} %copy-done.31, f32[256,128]{1,0:T(8,128)S(1)} %copy-done.21, ...), custom_call_target="tpu_custom_call" | custom-call | flops 939524096 | bytes 2097152 | tf_op jit(solution)/shard_map/attend/pallas_call | solution.py:395
  92.2 2.5 %project_rows.8 = (f32[256,256]{1,0:T(8,128)S(1)}, f32[256,256]{1,0:T(8,128)S(1)}) custom-call(bf16[256,4096]{1,0:T(8,128)(2,1)S(1)} %copy-done, bf16[256,4096]{1,0:T(8,128)(2,1)} %collective-permute-done.3.refs_1_.refs_3_.refs_5_.refs_7_, bf16[256,4096]{1,0:T(8,128)(2,1)S(1)} %copy-done, ...), custom_call_target="tpu_custom_call" | custom-call | flops 805306368 | bytes 4718592 | tf_op jit(solution)/shard_map/project_rows/pallas_call | solution.py:312
  94.7 1.6 project_rows.9
  98.4 1.3 convolution_convert_fusion.1
  99.7 2.8 %attend.3 = (bf16[256,256]{1,0:T(8,128)(2,1)S(1)}, bf16[256,256]{1,0:T(8,128)(2,1)S(1)}, f32[256,256]{1,0:T(8,128)S(1)}, bf16[256,256]{1,0:T(8,128)(2,1)S(1)}, b...) custom-call(f32[256,256]{1,0:T(8,128)S(1)} %get-tuple-element.84.refs_0_, ...), custom_call_target="tpu_custom_call" | custom-call | flops 939524096 | bytes 2097152 | tf_op jit(solution)/shard_map/attend/pallas_call | solution.py:395
  102.8 1.4 collective-permute-start.30
  104.3 1.5 collective-permute-start.31
  108.0 1.3 convolution_convert_fusion
  109.2 2.1 %collective-permute-done.27 = bf16[1024,256]{1,0:T(8,128)(2,1)S(1)} collective-permute-done((bf16[1024,256]{1,0:T(8,128)(2,1)S(1)}, bf16[1024,256]{1,0:T(8,128)(2,1)S(1)}, u32[]{:S(2)}, u32[]{:S(2)}) %collective-permute-start.27) | collective-permute-done | bytes 524320 | tf_op jit(solution)/shard_map/ppermute | solution.py:29
  111.4 1.3 fusion.3
  112.7 1.3 collective-permute-start.38
  114.6 7.7 %collective-permute-done.29 = bf16[1024,256]{1,0:T(8,128)(2,1)S(1)} collective-permute-done((bf16[1024,256]{1,0:T(8,128)(2,1)S(1)}, bf16[1024,256]{1,0:T(8,128)(2,1)S(1)}, u32[]{:S(2)}, u32[]{:S(2)}) %collective-permute-start.29) | collective-permute-done | bytes 524320 | tf_op jit(solution)/shard_map/ppermute | solution.py:29
  124.5 2.0 %undo_keys.1.refs_4_ = bf16[256,256]{1,0:T(8,128)(2,1)} custom-call(f32[256,256]{1,0:T(8,128)} %copy-done.28, bf16[256,256]{1,0:T(8,128)(2,1)} %copy-done.38, bf16[256,256]{1,0:T(8,128)(2,1)} %copy-done.39, bf16[256,256]{1,0:T(8,128)(2,1)} %copy-done.40, f32[256,128]{1,0:T(8,128)} %get-tuple-element.126.cos_ref.refs_3_.refs_4_, ...), custom_call_target="tpu_custom_call" | custom-call | tf_op jit(solution)/shard_map/undo_keys/pallas_call | solution.py:446
  126.6 2.0 %fusion.5 = bf16[1024,256]{1,0:T(8,128)(2,1)S(1)} fusion(bf16[512,256]{1,0:T(8,128)(2,1)S(1)} %constant_dynamic-update-slice_fusion.16, bf16[1024,256]{1,0:T(8,128)(2,1)} %copy-done.47, bf16[512,4096]{1,0:T(8,128)(2,1)} %copy-done.34), kind=kOutput, calls=%fused_computation.14 | convolution fusion | flops 269221888 | bytes 2359296 | tf_op jit(solution)/shard_map/dot_general | solution.py:24
  128.6 1.4 convolution_convert_fusion.7
  130.1 1.0 collective-permute-start.34
  132.8 1.6 collective-permute-start.39
  134.4 1.1 collective-permute-start.40
  135.5 1.7 fusion.4
  137.2 2.1 %collective-permute-done.34 = bf16[512,256]{1,0:T(8,128)(2,1)S(1)} collective-permute-done((bf16[512,256]{1,0:T(8,128)(2,1)S(1)}, bf16[512,256]{1,0:T(8,128)(2,1)S(1)}, u32[]{:S(2)}, u32[]{:S(2)}) %collective-permute-start.34) | collective-permute-done | bytes 262176 | tf_op jit(solution)/shard_map/ppermute | solution.py:29
  139.3 1.4 collective-permute-done.35
  140.8 3.0 %grad_columns.1 = bf16[256,4096]{1,0:T(8,128)(2,1)S(1)} custom-call(bf16[256,256]{1,0:T(8,128)(2,1)S(1)} %copy-done.25, bf16[256,256]{1,0:T(8,128)(2,1)S(1)} %collective-permute-done.28.refs_1_, bf16[256,256]{1,0:T(8,128)(2,1)S(1)} %collective-permute-done.33.refs_2_, bf16[1024,256]{1,0:T(8,128)(2,1)S(1)} %copy-done.3, ...), custom_call_target="tpu_custom_call" | custom-call | flops 1610612736 | bytes 8388608 | tf_op jit(solution)/shard_map/grad_columns/pallas_call | solution.py:233
  144.0 3.5 %collective-permute-start.41 = (bf16[256,256]{1,0:T(8,128)(2,1)S(1)}, bf16[256,256]{1,0:T(8,128)(2,1)S(1)}, u32[]{:S(2)}, u32[]{:S(2)}) collective-permute-start(bf16[256,256]{1,0:T(8,128)(2,1)S(1)} %get-tuple-element.114), channel_id=1, source_target_pairs={{0,3},{1,0},{2,1},{3,2},{4,7},{5,4},{6,5},{7,6},{8,11},{9,8},{10,9... | collective-permute-start | bytes 393224 | tf_op jit(solution)/shard_map/ppermute | solution.py:29
  148.3 3.0 %collective-permute-done.41 = bf16[256,256]{1,0:T(8,128)(2,1)S(1)} collective-permute-done((bf16[256,256]{1,0:T(8,128)(2,1)S(1)}, bf16[256,256]{1,0:T(8,128)(2,1)S(1)}, u32[]{:S(2)}, u32[]{:S(2)}) %collective-permute-start.41) | collective-permute-done | bytes 131104 | tf_op jit(solution)/shard_map/ppermute | solution.py:29
  151.5 8.1 %collective-permute-done.42 = bf16[256,256]{1,0:T(8,128)(2,1)S(1)} collective-permute-done((bf16[256,256]{1,0:T(8,128)(2,1)S(1)}, bf16[256,256]{1,0:T(8,128)(2,1)S(1)}, u32[]{:S(2)}, u32[]{:S(2)}) %collective-permute-start.42) | collective-permute-done | bytes 131104 | tf_op jit(solution)/shard_map/ppermute | solution.py:29
  160.1 1.1 collective-permute-start.48
  162.7 10.4 %collective-permute-done.47 = bf16[1024,256]{1,0:T(8,128)(2,1)S(1)} collective-permute-done((bf16[1024,256]{1,0:T(8,128)(2,1)S(1)}, bf16[1024,256]{1,0:T(8,128)(2,1)S(1)}, u32[]{:S(2)}, u32[]{:S(2)}) %collective-permute-start.47) | collective-permute-done | bytes 524320 | tf_op jit(solution)/shard_map/ppermute | solution.py:29
  173.9 3.6 %collective-permute-start.49 = (bf16[256,256]{1,0:T(8,128)(2,1)S(1)}, bf16[256,256]{1,0:T(8,128)(2,1)S(1)}, u32[]{:S(2)}, u32[]{:S(2)}) collective-permute-start(bf16[256,256]{1,0:T(8,128)(2,1)S(1)} %get-tuple-element.110), channel_id=1, source_target_pairs={{0,3},{1,0},{2,1},{3,2},{4,7},{5,4},{6,5},{7,6},{8,11},{9,8},{10,9... | collective-permute-start | bytes 393224 | tf_op jit(solution)/shard_map/ppermute | solution.py:29
  178.2 5.8 %grad_place.1 = bf16[256,8192]{1,0:T(8,128)(2,1)} custom-call(s32[4]{0:T(128)S(1)} %copy-done.33, s32[2,4]{1,0:T(2,128)S(1)} %copy-done.32, bf16[256,256]{1,0:T(8,128)(2,1)S(1)} %copy-done.23, bf16[256,256]{1,0:T(8,128)(2,1)S(1)} %get-tuple-element.87.refs_3_, bf16[256,256]{1,0:T(8,128)(2,1)S(1)} %copy-done.26, bf16[1024,256]{1,0:T(8,128)(2,1)S(1)} %copy-done.3, ...), custom_call_target="tpu_custom_call" | custom-call | flops 1610612736 | bytes 12582912 | tf_op jit(solution)/shard_map/grad_place/pallas_call | solution.py:257
  184.0 4.8 %collective-permute-done.50 = bf16[256,256]{1,0:T(8,128)(2,1)S(1)} collective-permute-done((bf16[256,256]{1,0:T(8,128)(2,1)S(1)}, bf16[256,256]{1,0:T(8,128)(2,1)S(1)}, u32[]{:S(2)}, u32[]{:S(2)}) %collective-permute-start.50) | collective-permute-done | bytes 131104 | tf_op jit(solution)/shard_map/ppermute | solution.py:29
  (216 shorter events, 27.7 us)
Async XLA Ops:
  0.6 17.2 %copy-start.36 = (f32[256,512]{1,0:T(8,128)S(1)}, f32[256,512]{1,0:T(8,128)}, u32[]{:S(2)}) copy-start(f32[256,512]{1,0:T(8,128)} %param.8) | copy-start | bytes 1572868
  0.6 20.4 %copy-start.45 = (s32[1024]{0:T(1024)S(1)}, s32[1024]{0:T(1024)}, u32[]{:S(2)}) copy-start(s32[1024]{0:T(1024)} %param.7) | copy-start | bytes 12292
  2.6 14.0 %collective-permute-start = (bf16[256,256]{1,0:T(8,128)(2,1)S(1)}, bf16[256,256]{1,0:T(8,128)(2,1)}, u32[]{:S(2)}, u32[]{:S(2)}) collective-permute-start(bf16[256,256]{1,0:T(8,128)(2,1)S(1)} %pad_maximum_fusion.4), channel_id=1, source_target_pairs={{0,1},{1,2},{2,3},{3,0},{4,5},{5,6},{6,7},{7,4},{8,9},{9,10},{10,1... | collective-permute-start | bytes 393224 | tf_op jit(solution)/shard_map/ppermute | solution.py:29
  5.6 12.0 %collective-permute-start.1 = (bf16[256,256]{1,0:T(8,128)(2,1)S(1)}, bf16[256,256]{1,0:T(8,128)(2,1)S(1)}, u32[]{:S(2)}, u32[]{:S(2)}) collective-permute-start(bf16[256,256]{1,0:T(8,128)(2,1)S(1)} %pad_maximum_fusion.4), channel_id=1, source_target_pairs={{0,2},{1,3},{2,0},{3,1},{4,6},{5,7},{6,4},{7,5},{8,10},{9,11},{10,... | collective-permute-start | bytes 393224 | tf_op jit(solution)/shard_map/ppermute | solution.py:29
  8.2 9.4 %collective-permute-start.2 = (bf16[256,256]{1,0:T(8,128)(2,1)S(1)}, bf16[256,256]{1,0:T(8,128)(2,1)S(1)}, u32[]{:S(2)}, u32[]{:S(2)}) collective-permute-start(bf16[256,256]{1,0:T(8,128)(2,1)S(1)} %pad_maximum_fusion.4), channel_id=1, source_target_pairs={{0,3},{1,0},{2,1},{3,2},{4,7},{5,4},{6,5},{7,6},{8,11},{9,8},{10,9... | collective-permute-start | bytes 393224 | tf_op jit(solution)/shard_map/ppermute | solution.py:29
  16.5 37.9 %copy-start = (bf16[256,4096]{1,0:T(8,128)(2,1)S(1)}, bf16[256,4096]{1,0:T(8,128)(2,1)}, u32[]{:S(2)}) copy-start(bf16[256,4096]{1,0:T(8,128)(2,1)} %get-tuple-element.82.refs_0_.refs_2_.refs_4_.refs_6_) | copy-start | bytes 6291460
  17.7 35.7 %copy-start.4 = (bf16[1024,256]{1,0:T(8,128)(2,1)}, bf16[1024,256]{1,0:T(8,128)(2,1)S(1)}, u32[]{:S(2)}) copy-start(bf16[1024,256]{1,0:T(8,128)(2,1)S(1)} %constant_dynamic-update-slice_fusion.refs_8_.refs_12_.refs_14_) | copy-start | bytes 1572868
  17.7 4.6 %collective-permute-start.3 = (bf16[256,4096]{1,0:T(8,128)(2,1)}, bf16[256,4096]{1,0:T(8,128)(2,1)}, u32[]{:S(2)}, u32[]{:S(2)}) collective-permute-start(bf16[256,4096]{1,0:T(8,128)(2,1)} %get-tuple-element.58), channel_id=1, source_target_pairs={{0,4},{4,0},{1,5},{5,1},{2,6},{6,2},{3,7},{7,3},{8,12},{12,8},{9,1... | collective-permute-start | bytes 6291464 | tf_op jit(solution)/shard_map/ppermute | solution.py:29
  18.0 17.7 %collective-permute-start.7 = (bf16[1024,256]{1,0:T(8,128)(2,1)S(1)}, bf16[1024,256]{1,0:T(8,128)(2,1)S(1)}, u32[]{:S(2)}, u32[]{:S(2)}) collective-permute-start(bf16[1024,256]{1,0:T(8,128)(2,1)S(1)} %constant_dynamic-update-slice_fusion.refs_8_.refs_12_.refs_14_), channel_id=1, source_target_pairs={{0,16},{16,0},{1,17},{17,1},{2,18},{18,2},{3,19},{19,3},{4,20},{20... | collective-permute-start | bytes 1572872 | tf_op jit(solution)/shard_map/ppermute | solution.py:29
  19.5 16.1 %collective-permute-start.8 = (bf16[1024,256]{1,0:T(8,128)(2,1)S(1)}, bf16[1024,256]{1,0:T(8,128)(2,1)S(1)}, u32[]{:S(2)}, u32[]{:S(2)}) collective-permute-start(bf16[1024,256]{1,0:T(8,128)(2,1)S(1)} %constant_dynamic-update-slice_fusion.refs_8_.refs_12_.refs_14_), channel_id=1, source_target_pairs={{0,8},{8,0},{1,9},{9,1},{2,10},{10,2},{3,11},{11,3},{4,12},{12,4},... | collective-permute-start | bytes 1572872 | tf_op jit(solution)/shard_map/ppermute | solution.py:29
  22.3 7.9 %collective-permute-start.4 = (bf16[256,256]{1,0:T(8,128)(2,1)S(1)}, bf16[256,256]{1,0:T(8,128)(2,1)S(1)}, u32[]{:S(2)}, u32[]{:S(2)}) collective-permute-start(bf16[256,256]{1,0:T(8,128)(2,1)S(1)} %get-tuple-element.59), channel_id=1, source_target_pairs={{0,1},{1,2},{2,3},{3,0},{4,5},{5,6},{6,7},{7,4},{8,9},{9,10},{10,1... | collective-permute-start | bytes 393224 | tf_op jit(solution)/shard_map/ppermute | solution.py:29
  26.0 9.4 %collective-permute-start.5 = (bf16[256,256]{1,0:T(8,128)(2,1)S(1)}, bf16[256,256]{1,0:T(8,128)(2,1)S(1)}, u32[]{:S(2)}, u32[]{:S(2)}) collective-permute-start(bf16[256,256]{1,0:T(8,128)(2,1)S(1)} %get-tuple-element.59), channel_id=1, source_target_pairs={{0,2},{1,3},{2,0},{3,1},{4,6},{5,7},{6,4},{7,5},{8,10},{9,11},{10,... | collective-permute-start | bytes 393224 | tf_op jit(solution)/shard_map/ppermute | solution.py:29
  27.7 7.9 %collective-permute-start.6 = (bf16[256,256]{1,0:T(8,128)(2,1)S(1)}, bf16[256,256]{1,0:T(8,128)(2,1)S(1)}, u32[]{:S(2)}, u32[]{:S(2)}) collective-permute-start(bf16[256,256]{1,0:T(8,128)(2,1)S(1)} %get-tuple-element.59), channel_id=1, source_target_pairs={{0,3},{1,0},{2,1},{3,2},{4,7},{5,4},{6,5},{7,6},{8,11},{9,8},{10,9... | collective-permute-start | bytes 393224 | tf_op jit(solution)/shard_map/ppermute | solution.py:29
  35.6 22.7 %copy-start.1 = (bf16[1024,256]{1,0:T(8,128)(2,1)}, bf16[1024,256]{1,0:T(8,128)(2,1)S(1)}, u32[]{:S(2)}) copy-start(bf16[1024,256]{1,0:T(8,128)(2,1)S(1)} %constant_dynamic-update-slice_fusion.4.refs_6_.refs_3_.refs_5_) | copy-start | bytes 1572868
  35.6 22.7 %copy-start.10 = (bf16[1024,256]{1,0:T(8,128)(2,1)}, bf16[1024,256]{1,0:T(8,128)(2,1)S(1)}, u32[]{:S(2)}) copy-start(bf16[1024,256]{1,0:T(8,128)(2,1)S(1)} %collective-permute-done.7.refs_10_.refs_14_.refs_16_) | copy-start | bytes 1572868
  35.6 16.9 %collective-permute-start.9 = (bf16[1024,256]{1,0:T(8,128)(2,1)S(1)}, bf16[1024,256]{1,0:T(8,128)(2,1)S(1)}, u32[]{:S(2)}, u32[]{:S(2)}) collective-permute-start(bf16[1024,256]{1,0:T(8,128)(2,1)S(1)} %constant_dynamic-update-slice_fusion.4.refs_6_.refs_3_.refs_5_), channel_id=1, source_target_pairs={{0,16},{16,0},{1,17},{17,1},{2,18},{18,2},{3,19},{19,3},{4,20},{20... | collective-permute-start | bytes 1572872 | tf_op jit(solution)/shard_map/ppermute | solution.py:29
  37.2 16.1 %collective-permute-start.10 = (bf16[1024,256]{1,0:T(8,128)(2,1)S(1)}, bf16[1024,256]{1,0:T(8,128)(2,1)S(1)}, u32[]{:S(2)}, u32[]{:S(2)}) collective-permute-start(bf16[1024,256]{1,0:T(8,128)(2,1)S(1)} %collective-permute-done.7.refs_10_.refs_14_.refs_16_), channel_id=1, source_target_pairs={{0,8},{8,0},{1,9},{9,1},{2,10},{10,2},{3,11},{11,3},{4,12},{12,4},... | collective-permute-start | bytes 1572872 | tf_op jit(solution)/shard_map/ppermute | solution.py:29
  38.7 8.2 %collective-permute-start.12 = (bf16[256,256]{1,0:T(8,128)(2,1)S(1)}, bf16[256,256]{1,0:T(8,128)(2,1)S(1)}, u32[]{:S(2)}, u32[]{:S(2)}) collective-permute-start(bf16[256,256]{1,0:T(8,128)(2,1)S(1)} %get-tuple-element.64), channel_id=1, source_target_pairs={{0,1},{1,2},{2,3},{3,0},{4,5},{5,6},{6,7},{7,4},{8,9},{9,10},{10,1... | collective-permute-start | bytes 393224 | tf_op jit(solution)/shard_map/ppermute | solution.py:29
  41.8 9.4 %collective-permute-start.13 = (bf16[256,256]{1,0:T(8,128)(2,1)S(1)}, bf16[256,256]{1,0:T(8,128)(2,1)S(1)}, u32[]{:S(2)}, u32[]{:S(2)}) collective-permute-start(bf16[256,256]{1,0:T(8,128)(2,1)S(1)} %get-tuple-element.64), channel_id=1, source_target_pairs={{0,2},{1,3},{2,0},{3,1},{4,6},{5,7},{6,4},{7,5},{8,10},{9,11},{10,... | collective-permute-start | bytes 393224 | tf_op jit(solution)/shard_map/ppermute | solution.py:29
  43.8 8.1 %collective-permute-start.14 = (bf16[256,256]{1,0:T(8,128)(2,1)S(1)}, bf16[256,256]{1,0:T(8,128)(2,1)S(1)}, u32[]{:S(2)}, u32[]{:S(2)}) collective-permute-start(bf16[256,256]{1,0:T(8,128)(2,1)S(1)} %get-tuple-element.64), channel_id=1, source_target_pairs={{0,3},{1,0},{2,1},{3,2},{4,7},{5,4},{6,5},{7,6},{8,11},{9,8},{10,9... | collective-permute-start | bytes 393224 | tf_op jit(solution)/shard_map/ppermute | solution.py:29
  53.3 15.7 %collective-permute-start.11 = (bf16[1024,256]{1,0:T(8,128)(2,1)S(1)}, bf16[1024,256]{1,0:T(8,128)(2,1)}, u32[]{:S(2)}, u32[]{:S(2)}) collective-permute-start(bf16[1024,256]{1,0:T(8,128)(2,1)S(1)} %constant_dynamic-update-slice_fusion.4.refs_6_.refs_3_.refs_5_), channel_id=1, source_target_pairs={{0,8},{8,0},{1,9},{9,1},{2,10},{10,2},{3,11},{11,3},{4,12},{12,4},... | collective-permute-start | bytes 1572872 | tf_op jit(solution)/shard_map/ppermute | solution.py:29
  53.9 15.1 %collective-permute-start.15 = (bf16[1024,256]{1,0:T(8,128)(2,1)}, bf16[1024,256]{1,0:T(8,128)(2,1)S(1)}, u32[]{:S(2)}, u32[]{:S(2)}) collective-permute-start(bf16[1024,256]{1,0:T(8,128)(2,1)} %constant_dynamic-update-slice_fusion.8.refs_6_.refs_7_.refs_9_), channel_id=1, source_target_pairs={{0,16},{16,0},{1,17},{17,1},{2,18},{18,2},{3,19},{19,3},{4,20},{20... | collective-permute-start | bytes 1572872 | tf_op jit(solution)/shard_map/ppermute | solution.py:29
  59.9 1.7 collective-permute-start.16
  63.4 21.1 %collective-permute-start.19 = (bf16[256,256]{1,0:T(8,128)(2,1)}, bf16[256,256]{1,0:T(8,128)(2,1)S(1)}, u32[]{:S(2)}, u32[]{:S(2)}) collective-permute-start(bf16[256,256]{1,0:T(8,128)(2,1)} %finish_keys.1.refs_7_), channel_id=1, source_target_pairs={{0,1},{1,2},{2,3},{3,0},{4,5},{5,6},{6,7},{7,4},{8,9},{9,10},{10,1... | collective-permute-start | bytes 393224 | tf_op jit(solution)/shard_map/ppermute | solution.py:29
  66.0 18.5 %collective-permute-start.20 = (bf16[256,256]{1,0:T(8,128)(2,1)}, bf16[256,256]{1,0:T(8,128)(2,1)S(1)}, u32[]{:S(2)}, u32[]{:S(2)}) collective-permute-start(bf16[256,256]{1,0:T(8,128)(2,1)} %finish_keys.1.refs_7_), channel_id=1, source_target_pairs={{0,2},{1,3},{2,0},{3,1},{4,6},{5,7},{6,4},{7,5},{8,10},{9,11},{10,... | collective-permute-start | bytes 393224 | tf_op jit(solution)/shard_map/ppermute | solution.py:29
  68.5 16.1 %collective-permute-start.21 = (bf16[256,256]{1,0:T(8,128)(2,1)}, bf16[256,256]{1,0:T(8,128)(2,1)S(1)}, u32[]{:S(2)}, u32[]{:S(2)}) collective-permute-start(bf16[256,256]{1,0:T(8,128)(2,1)} %finish_keys.1.refs_7_), channel_id=1, source_target_pairs={{0,3},{1,0},{2,1},{3,2},{4,7},{5,4},{6,5},{7,6},{8,11},{9,8},{10,9... | collective-permute-start | bytes 393224 | tf_op jit(solution)/shard_map/ppermute | solution.py:29
  69.0 13.6 %collective-permute-start.17 = (bf16[1024,256]{1,0:T(8,128)(2,1)}, bf16[1024,256]{1,0:T(8,128)(2,1)S(1)}, u32[]{:S(2)}, u32[]{:S(2)}) collective-permute-start(bf16[1024,256]{1,0:T(8,128)(2,1)} %collective-permute-done.11.refs_7_.refs_4_.refs_6_), channel_id=1, source_target_pairs={{0,16},{16,0},{1,17},{17,1},{2,18},{18,2},{3,19},{19,3},{4,20},{20... | collective-permute-start | bytes 1572872 | tf_op jit(solution)/shard_map/ppermute | solution.py:29
  70.6 13.9 %collective-permute-start.22 = (bf16[1024,256]{1,0:T(8,128)(2,1)}, bf16[1024,256]{1,0:T(8,128)(2,1)S(1)}, u32[]{:S(2)}, u32[]{:S(2)}) collective-permute-start(bf16[1024,256]{1,0:T(8,128)(2,1)} %constant_dynamic-update-slice_fusion.8.refs_6_.refs_7_.refs_9_), channel_id=1, source_target_pairs={{0,8},{8,0},{1,9},{9,1},{2,10},{10,2},{3,11},{11,3},{4,12},{12,4},... | collective-permute-start | bytes 1572872 | tf_op jit(solution)/shard_map/ppermute | solution.py:29
  84.4 5.1 %collective-permute-start.18 = (f32[256,256]{1,0:T(8,128)S(1)}, f32[256,256]{1,0:T(8,128)S(1)}, u32[]{:S(2)}, u32[]{:S(2)}) collective-permute-start(f32[256,256]{1,0:T(8,128)S(1)} %get-tuple-element.72), channel_id=1, source_target_pairs={{0,4},{4,0},{1,5},{5,1},{2,6},{6,2},{3,7},{7,3},{8,12},{12,8},{9,1... | collective-permute-start | bytes 786440 | tf_op jit(solution)/shard_map/ppermute | solution.py:29
  84.5 10.2 %collective-permute-start.24 = (bf16[512,256]{1,0:T(8,128)(2,1)S(1)}, bf16[512,256]{1,0:T(8,128)(2,1)S(1)}, u32[]{:S(2)}, u32[]{:S(2)}) collective-permute-start(bf16[512,256]{1,0:T(8,128)(2,1)S(1)} %slice.131), channel_id=1, source_target_pairs={{0,16},{16,0},{1,17},{17,1},{2,18},{18,2},{3,19},{19,3},{4,20},{20... | collective-permute-start | bytes 786440 | tf_op jit(solution)/shard_map/ppermute | solution.py:29
  86.1 8.6 %collective-permute-start.23 = (bf16[512,256]{1,0:T(8,128)(2,1)S(1)}, bf16[512,256]{1,0:T(8,128)(2,1)S(1)}, u32[]{:S(2)}, u32[]{:S(2)}) collective-permute-start(bf16[512,256]{1,0:T(8,128)(2,1)S(1)} %slice.130), channel_id=1, source_target_pairs={{0,8},{8,0},{1,9},{9,1},{2,10},{10,2},{3,11},{11,3},{4,12},{12,4},... | collective-permute-start | bytes 786440 | tf_op jit(solution)/shard_map/ppermute | solution.py:29
  89.4 22.0 %copy-start.34 = (bf16[512,4096]{1,0:T(8,128)(2,1)}, bf16[512,4096]{1,0:T(8,128)(2,1)S(1)}, u32[]{:S(2)}) copy-start(bf16[512,4096]{1,0:T(8,128)(2,1)S(1)} %constant_dynamic-update-slice_fusion.12) | copy-start | bytes 12582916
  92.1 4.8 %collective-permute-start.25 = (bf16[256,256]{1,0:T(8,128)(2,1)S(1)}, bf16[256,256]{1,0:T(8,128)(2,1)S(1)}, u32[]{:S(2)}, u32[]{:S(2)}) collective-permute-start(bf16[256,256]{1,0:T(8,128)(2,1)S(1)} %get-tuple-element.83.refs_2_), channel_id=1, source_target_pairs={{0,4},{4,0},{1,5},{5,1},{2,6},{6,2},{3,7},{7,3},{8,12},{12,8},{9,1... | collective-permute-start | bytes 393224 | tf_op jit(solution)/shard_map/ppermute | solution.py:29
  96.3 3.3 %collective-permute-start.26 = (f32[256,256]{1,0:T(8,128)S(1)}, f32[256,256]{1,0:T(8,128)S(1)}, u32[]{:S(2)}, u32[]{:S(2)}) collective-permute-start(f32[256,256]{1,0:T(8,128)S(1)} %get-tuple-element.85), channel_id=1, source_target_pairs={{0,4},{4,0},{1,5},{5,1},{2,6},{6,2},{3,7},{7,3},{8,12},{12,8},{9,1... | collective-permute-start | bytes 786440 | tf_op jit(solution)/shard_map/ppermute | solution.py:29
  97.5 13.9 %collective-permute-start.27 = (bf16[1024,256]{1,0:T(8,128)(2,1)S(1)}, bf16[1024,256]{1,0:T(8,128)(2,1)S(1)}, u32[]{:S(2)}, u32[]{:S(2)}) collective-permute-start(bf16[1024,256]{1,0:T(8,128)(2,1)S(1)} %convolution_convert_fusion.3), channel_id=1, source_target_pairs={{0,8},{8,0},{1,9},{9,1},{2,10},{10,2},{3,11},{11,3},{4,12},{12,4},... | collective-permute-start | bytes 1572872 | tf_op jit(solution)/shard_map/ppermute | solution.py:29
  102.6 4.3 %collective-permute-start.28 = (bf16[256,256]{1,0:T(8,128)(2,1)S(1)}, bf16[256,256]{1,0:T(8,128)(2,1)S(1)}, u32[]{:S(2)}, u32[]{:S(2)}) collective-permute-start(bf16[256,256]{1,0:T(8,128)(2,1)S(1)} %get-tuple-element.87.refs_3_), channel_id=1, source_target_pairs={{0,4},{4,0},{1,5},{5,1},{2,6},{6,2},{3,7},{7,3},{8,12},{12,8},{9,1... | collective-permute-start | bytes 393224 | tf_op jit(solution)/shard_map/ppermute | solution.py:29
  102.8 9.9 %collective-permute-start.30 = (bf16[256,256]{1,0:T(8,128)(2,1)S(1)}, bf16[256,256]{1,0:T(8,128)(2,1)S(1)}, u32[]{:S(2)}, u32[]{:S(2)}) collective-permute-start(bf16[256,256]{1,0:T(8,128)(2,1)S(1)} %get-tuple-element.89), channel_id=1, source_target_pairs={{0,3},{1,0},{2,1},{3,2},{4,7},{5,4},{6,5},{7,6},{8,11},{9,8},{10,9... | collective-permute-start | bytes 393224 | tf_op jit(solution)/shard_map/ppermute | solution.py:29
  104.3 18.1 %collective-permute-start.31 = (bf16[256,256]{1,0:T(8,128)(2,1)S(1)}, bf16[256,256]{1,0:T(8,128)(2,1)S(1)}, u32[]{:S(2)}, u32[]{:S(2)}) collective-permute-start(bf16[256,256]{1,0:T(8,128)(2,1)S(1)} %get-tuple-element.93), channel_id=1, source_target_pairs={{0,2},{1,3},{2,0},{3,1},{4,6},{5,7},{6,4},{7,5},{8,10},{9,11},{10,... | collective-permute-start | bytes 393224 | tf_op jit(solution)/shard_map/ppermute | solution.py:29
  105.8 17.4 %collective-permute-start.32 = (bf16[256,256]{1,0:T(8,128)(2,1)S(1)}, bf16[256,256]{1,0:T(8,128)(2,1)S(1)}, u32[]{:S(2)}, u32[]{:S(2)}) collective-permute-start(bf16[256,256]{1,0:T(8,128)(2,1)S(1)} %get-tuple-element.94), channel_id=1, source_target_pairs={{0,1},{1,2},{2,3},{3,0},{4,5},{5,6},{6,7},{7,4},{8,9},{9,10},{10,1... | collective-permute-start | bytes 393224 | tf_op jit(solution)/shard_map/ppermute | solution.py:29
  106.9 19.7 %copy-start.41 = (bf16[512,256]{1,0:T(8,128)(2,1)}, bf16[512,256]{1,0:T(8,128)(2,1)S(1)}, u32[]{:S(2)}) copy-start(bf16[512,256]{1,0:T(8,128)(2,1)S(1)} %constant_dynamic-update-slice_fusion.16) | copy-start | bytes 786436
  107.4 14.9 %collective-permute-start.29 = (bf16[1024,256]{1,0:T(8,128)(2,1)S(1)}, bf16[1024,256]{1,0:T(8,128)(2,1)S(1)}, u32[]{:S(2)}, u32[]{:S(2)}) collective-permute-start(bf16[1024,256]{1,0:T(8,128)(2,1)S(1)} %convolution_convert_fusion.2), channel_id=1, source_target_pairs={{0,16},{16,0},{1,17},{17,1},{2,18},{18,2},{3,19},{19,3},{4,20},{20... | collective-permute-start | bytes 1572872 | tf_op jit(solution)/shard_map/ppermute | solution.py:29
  112.7 20.1 %collective-permute-start.38 = (bf16[1024,256]{1,0:T(8,128)(2,1)}, bf16[1024,256]{1,0:T(8,128)(2,1)}, u32[]{:S(2)}, u32[]{:S(2)}) collective-permute-start(bf16[1024,256]{1,0:T(8,128)(2,1)} %convolution_convert_fusion.1), channel_id=1, source_target_pairs={{0,8},{8,0},{1,9},{9,1},{2,10},{10,2},{3,11},{11,3},{4,12},{12,4},... | collective-permute-start | bytes 1572872 | tf_op jit(solution)/shard_map/ppermute | solution.py:29
  114.1 18.7 %collective-permute-start.37 = (bf16[1024,256]{1,0:T(8,128)(2,1)}, bf16[1024,256]{1,0:T(8,128)(2,1)}, u32[]{:S(2)}, u32[]{:S(2)}) collective-permute-start(bf16[1024,256]{1,0:T(8,128)(2,1)} %fusion.3), channel_id=1, source_target_pairs={{0,16},{16,0},{1,17},{17,1},{2,18},{18,2},{3,19},{19,3},{4,20},{20... | collective-permute-start | bytes 1572872 | tf_op jit(solution)/shard_map/ppermute | solution.py:29
  126.5 2.1 %collective-permute-start.33 = (bf16[256,256]{1,0:T(8,128)(2,1)}, bf16[256,256]{1,0:T(8,128)(2,1)S(1)}, u32[]{:S(2)}, u32[]{:S(2)}) collective-permute-start(bf16[256,256]{1,0:T(8,128)(2,1)} %undo_keys.1.refs_4_), channel_id=1, source_target_pairs={{0,4},{4,0},{1,5},{5,1},{2,6},{6,2},{3,7},{7,3},{8,12},{12,8},{9,1... | collective-permute-start | bytes 393224 | tf_op jit(solution)/shard_map/ppermute | solution.py:29
  130.1 9.2 %collective-permute-start.34 = (bf16[512,256]{1,0:T(8,128)(2,1)S(1)}, bf16[512,256]{1,0:T(8,128)(2,1)S(1)}, u32[]{:S(2)}, u32[]{:S(2)}) collective-permute-start(bf16[512,256]{1,0:T(8,128)(2,1)S(1)} %convolution_convert_fusion.7), channel_id=1, source_target_pairs={{0,8},{8,0},{1,9},{9,1},{2,10},{10,2},{3,11},{11,3},{4,12},{12,4},... | collective-permute-start | bytes 786440 | tf_op jit(solution)/shard_map/ppermute | solution.py:29
  131.5 9.2 %collective-permute-start.35 = (bf16[512,256]{1,0:T(8,128)(2,1)S(1)}, bf16[512,256]{1,0:T(8,128)(2,1)S(1)}, u32[]{:S(2)}, u32[]{:S(2)}) collective-permute-start(bf16[512,256]{1,0:T(8,128)(2,1)S(1)} %convolution_convert_fusion.6), channel_id=1, source_target_pairs={{0,16},{16,0},{1,17},{17,1},{2,18},{18,2},{3,19},{19,3},{4,20},{20... | collective-permute-start | bytes 786440 | tf_op jit(solution)/shard_map/ppermute | solution.py:29
  132.8 26.8 %collective-permute-start.39 = (bf16[1024,256]{1,0:T(8,128)(2,1)S(1)}, bf16[1024,256]{1,0:T(8,128)(2,1)S(1)}, u32[]{:S(2)}, u32[]{:S(2)}) collective-permute-start(bf16[1024,256]{1,0:T(8,128)(2,1)S(1)} %copy-done.46), channel_id=1, source_target_pairs={{0,16},{16,0},{1,17},{17,1},{2,18},{18,2},{3,19},{19,3},{4,20},{20... | collective-permute-start | bytes 1572872 | tf_op jit(solution)/shard_map/ppermute | solution.py:29
  134.4 25.2 %collective-permute-start.40 = (bf16[1024,256]{1,0:T(8,128)(2,1)S(1)}, bf16[1024,256]{1,0:T(8,128)(2,1)S(1)}, u32[]{:S(2)}, u32[]{:S(2)}) collective-permute-start(bf16[1024,256]{1,0:T(8,128)(2,1)S(1)} %fusion.5), channel_id=1, source_target_pairs={{0,8},{8,0},{1,9},{9,1},{2,10},{10,2},{3,11},{11,3},{4,12},{12,4},... | collective-permute-start | bytes 1572872 | tf_op jit(solution)/shard_map/ppermute | solution.py:29
  143.8 17.4 %copy-start.42 = (bf16[512,256]{1,0:T(8,128)(2,1)S(1)}, bf16[512,256]{1,0:T(8,128)(2,1)}, u32[]{:S(2)}) copy-start(bf16[512,256]{1,0:T(8,128)(2,1)} %copy-done.41) | copy-start | bytes 786436
  143.8 34.3 %collective-permute-start.36 = (bf16[256,4096]{1,0:T(8,128)(2,1)S(1)}, bf16[256,4096]{1,0:T(8,128)(2,1)S(1)}, u32[]{:S(2)}, u32[]{:S(2)}) collective-permute-start(bf16[256,4096]{1,0:T(8,128)(2,1)S(1)} %grad_columns.1), channel_id=1, source_target_pairs={{0,4},{4,0},{1,5},{5,1},{2,6},{6,2},{3,7},{7,3},{8,12},{12,8},{9,1... | collective-permute-start | bytes 6291464 | tf_op jit(solution)/shard_map/ppermute | solution.py:29
  144.0 7.4 %collective-permute-start.41 = (bf16[256,256]{1,0:T(8,128)(2,1)S(1)}, bf16[256,256]{1,0:T(8,128)(2,1)S(1)}, u32[]{:S(2)}, u32[]{:S(2)}) collective-permute-start(bf16[256,256]{1,0:T(8,128)(2,1)S(1)} %get-tuple-element.114), channel_id=1, source_target_pairs={{0,3},{1,0},{2,1},{3,2},{4,7},{5,4},{6,5},{7,6},{8,11},{9,8},{10,9... | collective-permute-start | bytes 393224 | tf_op jit(solution)/shard_map/ppermute | solution.py:29
  147.5 12.1 %collective-permute-start.42 = (bf16[256,256]{1,0:T(8,128)(2,1)S(1)}, bf16[256,256]{1,0:T(8,128)(2,1)S(1)}, u32[]{:S(2)}, u32[]{:S(2)}) collective-permute-start(bf16[256,256]{1,0:T(8,128)(2,1)S(1)} %get-tuple-element.113), channel_id=1, source_target_pairs={{0,2},{1,3},{2,0},{3,1},{4,6},{5,7},{6,4},{7,5},{8,10},{9,11},{10,... | collective-permute-start | bytes 393224 | tf_op jit(solution)/shard_map/ppermute | solution.py:29
  151.4 11.3 %collective-permute-start.43 = (bf16[256,256]{1,0:T(8,128)(2,1)S(1)}, bf16[256,256]{1,0:T(8,128)(2,1)S(1)}, u32[]{:S(2)}, u32[]{:S(2)}) collective-permute-start(bf16[256,256]{1,0:T(8,128)(2,1)S(1)} %get-tuple-element.112), channel_id=1, source_target_pairs={{0,1},{1,2},{2,3},{3,0},{4,5},{5,6},{6,7},{7,4},{8,9},{9,10},{10,1... | collective-permute-start | bytes 393224 | tf_op jit(solution)/shard_map/ppermute | solution.py:29
  159.6 13.4 %collective-permute-start.47 = (bf16[1024,256]{1,0:T(8,128)(2,1)S(1)}, bf16[1024,256]{1,0:T(8,128)(2,1)S(1)}, u32[]{:S(2)}, u32[]{:S(2)}) collective-permute-start(bf16[1024,256]{1,0:T(8,128)(2,1)S(1)} %pad_maximum_fusion.1), channel_id=1, source_target_pairs={{0,16},{16,0},{1,17},{17,1},{2,18},{18,2},{3,19},{19,3},{4,20},{20... | collective-permute-start | bytes 1572872 | tf_op jit(solution)/shard_map/ppermute | solution.py:29
  160.1 13.2 %collective-permute-start.48 = (bf16[1024,256]{1,0:T(8,128)(2,1)S(1)}, bf16[1024,256]{1,0:T(8,128)(2,1)S(1)}, u32[]{:S(2)}, u32[]{:S(2)}) collective-permute-start(bf16[1024,256]{1,0:T(8,128)(2,1)S(1)} %pad_maximum_fusion.2), channel_id=1, source_target_pairs={{0,8},{8,0},{1,9},{9,1},{2,10},{10,2},{3,11},{11,3},{4,12},{12,4},... | collective-permute-start | bytes 1572872 | tf_op jit(solution)/shard_map/ppermute | solution.py:29
  161.7 16.5 %copy-start.23 = (bf16[256,256]{1,0:T(8,128)(2,1)S(1)}, bf16[256,256]{1,0:T(8,128)(2,1)}, u32[]{:S(2)}) copy-start(bf16[256,256]{1,0:T(8,128)(2,1)} %copy-done.22) | copy-start | bytes 393220
  161.7 16.5 %copy-start.32 = (s32[2,4]{1,0:T(2,128)S(1)}, s32[2,4]{1,0:T(2,128)}, u32[]{:S(2)}) copy-start(s32[2,4]{1,0:T(2,128)} %pad_add_fusion.1.piece_ref.refs_1_) | copy-start | bytes 100
  161.7 16.5 %copy-start.33 = (s32[4]{0:T(128)S(1)}, s32[4]{0:T(128)}, u32[]{:S(2)}) copy-start(s32[4]{0:T(128)} %fusion.26.slab_ref.refs_0_) | copy-start | bytes 52
  161.8 12.0 %collective-permute-start.44 = (bf16[256,256]{1,0:T(8,128)(2,1)S(1)}, bf16[256,256]{1,0:T(8,128)(2,1)S(1)}, u32[]{:S(2)}, u32[]{:S(2)}) collective-permute-start(bf16[256,256]{1,0:T(8,128)(2,1)S(1)} %get-tuple-element.118), channel_id=1, source_target_pairs={{0,3},{1,0},{2,1},{3,2},{4,7},{5,4},{6,5},{7,6},{8,11},{9,8},{10,9... | collective-permute-start | bytes 393224 | tf_op jit(solution)/shard_map/ppermute | solution.py:29
  162.6 11.2 %collective-permute-start.45 = (bf16[256,256]{1,0:T(8,128)(2,1)S(1)}, bf16[256,256]{1,0:T(8,128)(2,1)S(1)}, u32[]{:S(2)}, u32[]{:S(2)}) collective-permute-start(bf16[256,256]{1,0:T(8,128)(2,1)S(1)} %get-tuple-element.117), channel_id=1, source_target_pairs={{0,2},{1,3},{2,0},{3,1},{4,6},{5,7},{6,4},{7,5},{8,10},{9,11},{10,... | collective-permute-start | bytes 393224 | tf_op jit(solution)/shard_map/ppermute | solution.py:29
  173.1 16.5 %collective-permute-start.46 = (bf16[256,256]{1,0:T(8,128)(2,1)S(1)}, bf16[256,256]{1,0:T(8,128)(2,1)S(1)}, u32[]{:S(2)}, u32[]{:S(2)}) collective-permute-start(bf16[256,256]{1,0:T(8,128)(2,1)S(1)} %get-tuple-element.116), channel_id=1, source_target_pairs={{0,1},{1,2},{2,3},{3,0},{4,5},{5,6},{6,7},{7,4},{8,9},{9,10},{10,1... | collective-permute-start | bytes 393224 | tf_op jit(solution)/shard_map/ppermute | solution.py:29
  173.9 10.2 %collective-permute-start.49 = (bf16[256,256]{1,0:T(8,128)(2,1)S(1)}, bf16[256,256]{1,0:T(8,128)(2,1)S(1)}, u32[]{:S(2)}, u32[]{:S(2)}) collective-permute-start(bf16[256,256]{1,0:T(8,128)(2,1)S(1)} %get-tuple-element.110), channel_id=1, source_target_pairs={{0,3},{1,0},{2,1},{3,2},{4,7},{5,4},{6,5},{7,6},{8,11},{9,8},{10,9... | collective-permute-start | bytes 393224 | tf_op jit(solution)/shard_map/ppermute | solution.py:29
  177.5 11.3 %collective-permute-start.50 = (bf16[256,256]{1,0:T(8,128)(2,1)S(1)}, bf16[256,256]{1,0:T(8,128)(2,1)S(1)}, u32[]{:S(2)}, u32[]{:S(2)}) collective-permute-start(bf16[256,256]{1,0:T(8,128)(2,1)S(1)} %get-tuple-element.109), channel_id=1, source_target_pairs={{0,2},{1,3},{2,0},{3,1},{4,6},{5,7},{6,4},{7,5},{8,10},{9,11},{10,... | collective-permute-start | bytes 393224 | tf_op jit(solution)/shard_map/ppermute | solution.py:29
  177.5 11.3 %collective-permute-start.51 = (bf16[256,256]{1,0:T(8,128)(2,1)S(1)}, bf16[256,256]{1,0:T(8,128)(2,1)S(1)}, u32[]{:S(2)}, u32[]{:S(2)}) collective-permute-start(bf16[256,256]{1,0:T(8,128)(2,1)S(1)} %get-tuple-element.108), channel_id=1, source_target_pairs={{0,1},{1,2},{2,3},{3,0},{4,5},{5,6},{6,7},{7,4},{8,9},{9,10},{10,1... | collective-permute-start | bytes 393224 | tf_op jit(solution)/shard_map/ppermute | solution.py:29
  (36 other events, 243.3 us)

commit v8 on v7

--- a/solution.py
+++ b/solution.py
@@ -570,7 +570,7 @@
     summed = [terms[0]] + [shift(terms[k], "ctx", -k) for k in range(1, ctx)]
     first = [*came[0][0].values(), *came[0][1].values()]
     second = [*came[1][0].values(), *came[1][1].values()]
-    sides0, went0 = reduce_sides(made[0], came[0], "b", mid, *first, *summed[1:2])
+    sides0, went0 = reduce_sides(made[0], came[0], "b", mid, *first, *summed[1:-1])
     grad_kv = undo_keys(
         [after(summed[0], *first, *second, *went0), *summed[1:]], cos_table, sin_table
     )
@@ -585,6 +585,7 @@
     line1 = made[1](0, slice(None), sides1)
     kv_sides, _ = reduce_sides(made[2], came[2], "both", mid, *sides1, *sent0[1:-1])
     sent1 = send_line(line1)
+    q_grads.append(add_line(sent1, kv_sides))
 
     weights = [*q_slabs, kv_slabs]
     grad_theirs = grad_columns(
@@ -595,7 +596,6 @@
         [gradients[0][0], gradients[1][0], gradients[2][0]], weights, grad_theirs, slabs, pieces, block
     )
     kv_term = after(made[2](0, slice(None), kv_sides), q_grads[0], *sent1[1:-1])
-    q_grads.append(add_line(sent1, (grad_input,)))
     kv_wgrad = add_line(send_line(kv_term), (grad_input,))
 
     query_grad = jnp.concatenate(q_grads, axis=1)

time: 191 us -> 181 us (0.948)
  waiting for transfers between devices: 61.1 us -> 44.4 us
  starting transfers between devices: 58.9 us -> 66.4 us
    ppermute x52, waiting for transfers between devices: 61.1 us -> 44.4 us  [shift(): lax.ppermute(block, axis, [(i, (i + step) % size) for i in range(size)])]
    ppermute x52, starting transfers between devices: 58.9 us -> 66.4 us  [shift(): lax.ppermute(block, axis, [(i, (i + step) % size) for i in range(size)])]
  transfers between devices with their start and end apart: 52 -> 52, of which waited for: 17 -> 18; matrix products, arithmetic and copies ran while one was open for 13% -> 14% of each run, Pallas kernels for 18% -> 19%
where the time goes in v8:
time: 181 us
  starting transfers between devices  66.4 us (37%)
  waiting for transfers between devices  44.4 us (25%)
  Pallas kernels  35 us (19%)
  local copies, waits for them, and re-layouts  12.8 us (7%)
  matrix products  12.8 us (7%)
  other arithmetic  7.49 us (4%)
    ppermute x52, starting transfers between devices, shift(): lax.ppermute(block, axis, [(i, (i + step) % size) for i in range(size)])  66.4 us
    ppermute x52, waiting for transfers between devices, shift(): lax.ppermute(block, axis, [(i, (i + step) % size) for i in range(size)])  44.4 us
    dot_general x15, matrix products, mm(): lax.dot_general(a, b, (dims, ((), ())), preferred_element_type=jnp.float32)  12.8 us
    pallas_call x5, Pallas kernels, project_rows(): pl.pallas_call(functools.partial(project_kernel, counts=[len(slab) for sl...  11.2 us
    unnamed x108, local copies, waits for them, and re-layouts  8.33 us
    pallas_call x1, Pallas kernels, grad_place(): pl.pallas_call(functools.partial(grad_place_kernel, shape=shape, plane=pl...  5.84 us
    pallas_call x1, Pallas kernels, pick_columns(): pl.pallas_call(functools.partial(pick_kernel, block=block), grid_spec=plt...  5.62 us
    pallas_call x2, Pallas kernels, attend(): pl.pallas_call(functools.partial(attend_kernel, group=group, parts=parts,...  5.4 us
  transfers between devices with their start and end apart: 52, of which 18 were waited for; matrix products, arithmetic and copies ran while one was open for 14% of the time, Pallas kernels for 19%

profile of v8, /device:TPU:0, one launch (start us, length us, event | category | flops | bytes accessed | tf_op | source)
XLA Modules:
  0.0 180.6 jit_solution(6700532534295097651)
XLA Ops:
  2.6 3.1 %collective-permute-start = (bf16[256,256]{1,0:T(8,128)(2,1)S(1)}, bf16[256,256]{1,0:T(8,128)(2,1)}, u32[]{:S(2)}, u32[]{:S(2)}) collective-permute-start(bf16[256,256]{1,0:T(8,128)(2,1)S(1)} %pad_maximum_fusion.4), channel_id=1, source_target_pairs={{0,1},{1,2},{2,3},{3,0},{4,5},{5,6},{6,7},{7,4},{8,9},{9,10},{10,1... | collective-permute-start | bytes 393224 | tf_op jit(solution)/shard_map/ppermute | solution.py:29
  5.6 2.6 %collective-permute-start.1 = (bf16[256,256]{1,0:T(8,128)(2,1)S(1)}, bf16[256,256]{1,0:T(8,128)(2,1)S(1)}, u32[]{:S(2)}, u32[]{:S(2)}) collective-permute-start(bf16[256,256]{1,0:T(8,128)(2,1)S(1)} %pad_maximum_fusion.4), channel_id=1, source_target_pairs={{0,2},{1,3},{2,0},{3,1},{4,6},{5,7},{6,4},{7,5},{8,10},{9,11},{10,... | collective-permute-start | bytes 393224 | tf_op jit(solution)/shard_map/ppermute | solution.py:29
  8.2 1.3 collective-permute-start.2
  10.9 5.6 %pick_columns.1 = (bf16[256,4096]{1,0:T(8,128)(2,1)}, bf16[256,4096]{1,0:T(8,128)(2,1)}) custom-call(s32[4]{0:T(128)} %fusion.26.slab_ref.refs_0_, s32[2,4]{1,0:T(2,128)} %pad_add_fusion.1.piece_ref.refs_1_, bf16[256,8192]{1,0:T(8,128)(2,1)} %bitcast.17), custom_call_target="tpu_custom_call" | custom-call | bytes 8388608 | tf_op jit(solution)/shard_map/pick_columns/pallas_call | solution.py:211
  16.6 1.1 constant_dynamic-update-slice_fusion.2
  18.0 1.6 collective-permute-start.7
  19.5 1.5 collective-permute-start.8
  22.3 2.5 %collective-permute-start.4 = (bf16[256,256]{1,0:T(8,128)(2,1)S(1)}, bf16[256,256]{1,0:T(8,128)(2,1)S(1)}, u32[]{:S(2)}, u32[]{:S(2)}) collective-permute-start(bf16[256,256]{1,0:T(8,128)(2,1)S(1)} %get-tuple-element.59), channel_id=1, source_target_pairs={{0,1},{1,2},{2,3},{3,0},{4,5},{5,6},{6,7},{7,4},{8,9},{9,10},{10,1... | collective-permute-start | bytes 393224 | tf_op jit(solution)/shard_map/ppermute | solution.py:29
  24.7 1.3 negate_select_fusion
  26.0 1.7 collective-permute-start.5
  28.6 1.6 collective-permute-done.4
  30.2 5.2 %collective-permute-done.5 = bf16[256,256]{1,0:T(8,128)(2,1)S(1)} collective-permute-done((bf16[256,256]{1,0:T(8,128)(2,1)S(1)}, bf16[256,256]{1,0:T(8,128)(2,1)S(1)}, u32[]{:S(2)}, u32[]{:S(2)}) %collective-permute-start.5) | collective-permute-done | bytes 131104 | tf_op jit(solution)/shard_map/ppermute | solution.py:29
  35.7 1.6 collective-permute-start.9
  37.2 1.5 collective-permute-start.10
  38.7 3.1 %collective-permute-start.12 = (bf16[256,256]{1,0:T(8,128)(2,1)S(1)}, bf16[256,256]{1,0:T(8,128)(2,1)S(1)}, u32[]{:S(2)}, u32[]{:S(2)}) collective-permute-start(bf16[256,256]{1,0:T(8,128)(2,1)S(1)} %get-tuple-element.64), channel_id=1, source_target_pairs={{0,1},{1,2},{2,3},{3,0},{4,5},{5,6},{6,7},{7,4},{8,9},{9,10},{10,1... | collective-permute-start | bytes 393224 | tf_op jit(solution)/shard_map/ppermute | solution.py:29
  41.8 1.3 collective-permute-start.13
  43.7 1.1 collective-permute-start.14
  44.8 2.1 %collective-permute-done.12 = bf16[256,256]{1,0:T(8,128)(2,1)S(1)} collective-permute-done((bf16[256,256]{1,0:T(8,128)(2,1)S(1)}, bf16[256,256]{1,0:T(8,128)(2,1)S(1)}, u32[]{:S(2)}, u32[]{:S(2)}) %collective-permute-start.12) | collective-permute-done | bytes 131104 | tf_op jit(solution)/shard_map/ppermute | solution.py:29
  47.6 3.6 %collective-permute-done.13 = bf16[256,256]{1,0:T(8,128)(2,1)S(1)} collective-permute-done((bf16[256,256]{1,0:T(8,128)(2,1)S(1)}, bf16[256,256]{1,0:T(8,128)(2,1)S(1)}, u32[]{:S(2)}, u32[]{:S(2)}) %collective-permute-start.13) | collective-permute-done | bytes 131104 | tf_op jit(solution)/shard_map/ppermute | solution.py:29
  54.5 1.0 copy-done.5
  55.5 2.8 %project_rows.5 = (f32[256,256]{1,0:T(8,128)S(1)}, f32[256,256]{1,0:T(8,128)S(1)}) custom-call(bf16[256,4096]{1,0:T(8,128)(2,1)S(1)} %copy-done, bf16[256,4096]{1,0:T(8,128)(2,1)} %collective-permute-done.3.refs_1_.refs_3_.refs_5_.refs_7_, bf16[256,4096]{1,0:T(8,128)(2,1)S(1)} %copy-done, ...), custom_call_target="tpu_custom_call" | custom-call | flops 1073741824 | bytes 6291456 | tf_op jit(solution)/shard_map/project_rows/pallas_call | solution.py:312
  61.5 1.8 %finish_keys.1.refs_7_ = bf16[256,256]{1,0:T(8,128)(2,1)} custom-call(f32[256,256]{1,0:T(8,128)} %copy-done.27, f32[256,256]{1,0:T(8,128)} %collective-permute-done.16.other, f32[256,128]{1,0:T(8,128)} %get-tuple-element.126.cos_ref.refs_3_.refs_4_, f32[256,128]{1,0:T(8,128)} %get-tuple-element.125.sin_ref.refs_4_.refs_5_), custom_call_target="tpu_custom_call" | custom-call | tf_op jit(solution)/shard_map/finish_keys/pallas_call | solution.py:424
  63.4 2.6 %collective-permute-start.19 = (bf16[256,256]{1,0:T(8,128)(2,1)}, bf16[256,256]{1,0:T(8,128)(2,1)S(1)}, u32[]{:S(2)}, u32[]{:S(2)}) collective-permute-start(bf16[256,256]{1,0:T(8,128)(2,1)} %finish_keys.1.refs_7_), channel_id=1, source_target_pairs={{0,1},{1,2},{2,3},{3,0},{4,5},{5,6},{6,7},{7,4},{8,9},{9,10},{10,1... | collective-permute-start | bytes 393224 | tf_op jit(solution)/shard_map/ppermute | solution.py:29
  66.0 2.4 %collective-permute-start.20 = (bf16[256,256]{1,0:T(8,128)(2,1)}, bf16[256,256]{1,0:T(8,128)(2,1)S(1)}, u32[]{:S(2)}, u32[]{:S(2)}) collective-permute-start(bf16[256,256]{1,0:T(8,128)(2,1)} %finish_keys.1.refs_7_), channel_id=1, source_target_pairs={{0,2},{1,3},{2,0},{3,1},{4,6},{5,7},{6,4},{7,5},{8,10},{9,11},{10,... | collective-permute-start | bytes 393224 | tf_op jit(solution)/shard_map/ppermute | solution.py:29
  69.0 1.5 collective-permute-start.17
  70.5 1.5 collective-permute-start.22
  72.3 2.5 %project_rows.6 = (f32[256,256]{1,0:T(8,128)S(1)}, f32[256,256]{1,0:T(8,128)S(1)}) custom-call(bf16[256,4096]{1,0:T(8,128)(2,1)S(1)} %copy-done, bf16[256,4096]{1,0:T(8,128)(2,1)} %collective-permute-done.3.refs_1_.refs_3_.refs_5_.refs_7_, bf16[256,4096]{1,0:T(8,128)(2,1)S(1)} %copy-done, ...), custom_call_target="tpu_custom_call" | custom-call | flops 805306368 | bytes 4718592 | tf_op jit(solution)/shard_map/project_rows/pallas_call | solution.py:312
  74.8 7.7 %collective-permute-done.17.refs_2_.refs_6_.refs_8_ = bf16[1024,256]{1,0:T(8,128)(2,1)S(1)} collective-permute-done((bf16[1024,256]{1,0:T(8,128)(2,1)}, bf16[1024,256]{1,0:T(8,128)(2,1)S(1)}, u32[]{:S(2)}, u32[]{:S(2)}) %collective-permute-start.17) | collective-permute-done | bytes 524320 | tf_op jit(solution)/shard_map/ppermute | solution.py:29
  82.6 1.8 project_rows.7
  84.5 1.6 collective-permute-start.24
  86.1 1.5 collective-permute-start.23
  87.6 1.8 constant_dynamic-update-slice_fusion.12
  89.5 2.6 %attend.2 = (bf16[256,256]{1,0:T(8,128)(2,1)S(1)}, bf16[256,256]{1,0:T(8,128)(2,1)S(1)}, f32[1024,256]{1,0:T(8,128)S(1)}) custom-call(f32[256,256]{1,0:T(8,128)S(1)} %get-tuple-element.71.refs_0_, f32[256,256]{1,0:T(8,128)S(1)} %collective-permute-done.18.refs_1_, bf16[256,256]{1,0:T(8,128)(2,1)S(1)} %copy-done.31, f32[256,128]{1,0:T(8,128)S(1)} %copy-done.21, ...), custom_call_target="tpu_custom_call" | custom-call | flops 939524096 | bytes 2097152 | tf_op jit(solution)/shard_map/attend/pallas_call | solution.py:395
  92.1 2.5 %project_rows.8 = (f32[256,256]{1,0:T(8,128)S(1)}, f32[256,256]{1,0:T(8,128)S(1)}) custom-call(bf16[256,4096]{1,0:T(8,128)(2,1)S(1)} %copy-done, bf16[256,4096]{1,0:T(8,128)(2,1)} %collective-permute-done.3.refs_1_.refs_3_.refs_5_.refs_7_, bf16[256,4096]{1,0:T(8,128)(2,1)S(1)} %copy-done, ...), custom_call_target="tpu_custom_call" | custom-call | flops 805306368 | bytes 4718592 | tf_op jit(solution)/shard_map/project_rows/pallas_call | solution.py:312
  94.7 1.6 project_rows.9
  98.3 1.3 convolution_convert_fusion.1
  99.7 2.8 %attend.3 = (bf16[256,256]{1,0:T(8,128)(2,1)S(1)}, bf16[256,256]{1,0:T(8,128)(2,1)S(1)}, f32[256,256]{1,0:T(8,128)S(1)}, bf16[256,256]{1,0:T(8,128)(2,1)S(1)}, b...) custom-call(f32[256,256]{1,0:T(8,128)S(1)} %get-tuple-element.84.refs_0_, ...), custom_call_target="tpu_custom_call" | custom-call | flops 939524096 | bytes 2097152 | tf_op jit(solution)/shard_map/attend/pallas_call | solution.py:395
  102.8 1.4 collective-permute-start.30
  104.2 1.5 collective-permute-start.31
  107.9 1.3 convolution_convert_fusion
  109.2 2.2 %collective-permute-done.27 = bf16[1024,256]{1,0:T(8,128)(2,1)S(1)} collective-permute-done((bf16[1024,256]{1,0:T(8,128)(2,1)S(1)}, bf16[1024,256]{1,0:T(8,128)(2,1)S(1)}, u32[]{:S(2)}, u32[]{:S(2)}) %collective-permute-start.27) | collective-permute-done | bytes 524320 | tf_op jit(solution)/shard_map/ppermute | solution.py:29
  111.4 1.3 fusion.3
  112.7 5.2 %collective-permute-done.31.refs_2_ = bf16[256,256]{1,0:T(8,128)(2,1)S(1)} collective-permute-done((bf16[256,256]{1,0:T(8,128)(2,1)S(1)}, bf16[256,256]{1,0:T(8,128)(2,1)S(1)}, u32[]{:S(2)}, u32[]{:S(2)}) %collective-permute-start.31) | collective-permute-done | bytes 131104 | tf_op jit(solution)/shard_map/ppermute | solution.py:29
  117.9 1.2 collective-permute-start.38
  119.5 1.2 collective-permute-done.29
  122.2 2.0 %undo_keys.1.refs_4_ = bf16[256,256]{1,0:T(8,128)(2,1)} custom-call(f32[256,256]{1,0:T(8,128)} %copy-done.28, bf16[256,256]{1,0:T(8,128)(2,1)} %copy-done.38, bf16[256,256]{1,0:T(8,128)(2,1)} %copy-done.39, bf16[256,256]{1,0:T(8,128)(2,1)} %copy-done.40, f32[256,128]{1,0:T(8,128)} %get-tuple-element.126.cos_ref.refs_3_.refs_4_, ...), custom_call_target="tpu_custom_call" | custom-call | tf_op jit(solution)/shard_map/undo_keys/pallas_call | solution.py:446
  124.3 2.0 %fusion.5 = bf16[1024,256]{1,0:T(8,128)(2,1)S(1)} fusion(bf16[512,256]{1,0:T(8,128)(2,1)S(1)} %constant_dynamic-update-slice_fusion.16, bf16[1024,256]{1,0:T(8,128)(2,1)} %copy-done.47, bf16[512,4096]{1,0:T(8,128)(2,1)} %copy-done.34), kind=kOutput, calls=%fused_computation.14 | convolution fusion | flops 269221888 | bytes 2359296 | tf_op jit(solution)/shard_map/dot_general | solution.py:24
  126.3 1.4 convolution_convert_fusion.6
  128.8 1.2 collective-permute-start.34
  131.5 2.7 %collective-permute-done.37 = bf16[1024,256]{1,0:T(8,128)(2,1)} collective-permute-done((bf16[1024,256]{1,0:T(8,128)(2,1)}, bf16[1024,256]{1,0:T(8,128)(2,1)}, u32[]{:S(2)}, u32[]{:S(2)}) %collective-permute-start.37) | collective-permute-done | bytes 524320 | tf_op jit(solution)/shard_map/ppermute | solution.py:29
  135.0 1.7 fusion.4
  136.7 3.3 %collective-permute-start.41 = (bf16[256,256]{1,0:T(8,128)(2,1)S(1)}, bf16[256,256]{1,0:T(8,128)(2,1)S(1)}, u32[]{:S(2)}, u32[]{:S(2)}) collective-permute-start(bf16[256,256]{1,0:T(8,128)(2,1)S(1)} %get-tuple-element.114), channel_id=1, source_target_pairs={{0,3},{1,0},{2,1},{3,2},{4,7},{5,4},{6,5},{7,6},{8,11},{9,8},{10,9... | collective-permute-start | bytes 393224 | tf_op jit(solution)/shard_map/ppermute | solution.py:29
  140.2 3.0 %grad_columns.1 = bf16[256,4096]{1,0:T(8,128)(2,1)S(1)} custom-call(bf16[256,256]{1,0:T(8,128)(2,1)S(1)} %copy-done.25, bf16[256,256]{1,0:T(8,128)(2,1)S(1)} %collective-permute-done.28.refs_1_, bf16[256,256]{1,0:T(8,128)(2,1)S(1)} %collective-permute-done.33.refs_2_, bf16[1024,256]{1,0:T(8,128)(2,1)S(1)} %copy-done.3, ...), custom_call_target="tpu_custom_call" | custom-call | flops 1610612736 | bytes 8388608 | tf_op jit(solution)/shard_map/grad_columns/pallas_call | solution.py:233
  144.2 2.4 %collective-permute-start.43 = (bf16[256,256]{1,0:T(8,128)(2,1)S(1)}, bf16[256,256]{1,0:T(8,128)(2,1)S(1)}, u32[]{:S(2)}, u32[]{:S(2)}) collective-permute-start(bf16[256,256]{1,0:T(8,128)(2,1)S(1)} %get-tuple-element.112), channel_id=1, source_target_pairs={{0,1},{1,2},{2,3},{3,0},{4,5},{5,6},{6,7},{7,4},{8,9},{9,10},{10,1... | collective-permute-start | bytes 393224 | tf_op jit(solution)/shard_map/ppermute | solution.py:29
  146.6 1.6 collective-permute-done.42
  148.2 1.2 collective-permute-done.39
  151.6 4.9 %collective-permute-start.46 = (bf16[256,256]{1,0:T(8,128)(2,1)S(1)}, bf16[256,256]{1,0:T(8,128)(2,1)S(1)}, u32[]{:S(2)}, u32[]{:S(2)}) collective-permute-start(bf16[256,256]{1,0:T(8,128)(2,1)S(1)} %get-tuple-element.118), channel_id=1, source_target_pairs={{0,3},{1,0},{2,1},{3,2},{4,7},{5,4},{6,5},{7,6},{8,11},{9,8},{10,9... | collective-permute-start | bytes 393224 | tf_op jit(solution)/shard_map/ppermute | solution.py:29
  156.6 5.1 %collective-permute-done.45 = bf16[1024,256]{1,0:T(8,128)(2,1)S(1)} collective-permute-done((bf16[1024,256]{1,0:T(8,128)(2,1)S(1)}, bf16[1024,256]{1,0:T(8,128)(2,1)S(1)}, u32[]{:S(2)}, u32[]{:S(2)}) %collective-permute-start.45) | collective-permute-done | bytes 524320 | tf_op jit(solution)/shard_map/ppermute | solution.py:29
  161.7 2.8 %collective-permute-start.48 = (bf16[256,256]{1,0:T(8,128)(2,1)S(1)}, bf16[256,256]{1,0:T(8,128)(2,1)S(1)}, u32[]{:S(2)}, u32[]{:S(2)}) collective-permute-start(bf16[256,256]{1,0:T(8,128)(2,1)S(1)} %get-tuple-element.116), channel_id=1, source_target_pairs={{0,1},{1,2},{2,3},{3,0},{4,5},{5,6},{6,7},{7,4},{8,9},{9,10},{10,1... | collective-permute-start | bytes 393224 | tf_op jit(solution)/shard_map/ppermute | solution.py:29
  165.1 2.9 %collective-permute-start.49 = (bf16[256,256]{1,0:T(8,128)(2,1)S(1)}, bf16[256,256]{1,0:T(8,128)(2,1)S(1)}, u32[]{:S(2)}, u32[]{:S(2)}) collective-permute-start(bf16[256,256]{1,0:T(8,128)(2,1)S(1)} %get-tuple-element.110), channel_id=1, source_target_pairs={{0,3},{1,0},{2,1},{3,2},{4,7},{5,4},{6,5},{7,6},{8,11},{9,8},{10,9... | collective-permute-start | bytes 393224 | tf_op jit(solution)/shard_map/ppermute | solution.py:29
  168.0 1.7 collective-permute-start.51
  169.6 1.2 collective-permute-done.48
  171.8 5.8 %grad_place.1 = bf16[256,8192]{1,0:T(8,128)(2,1)} custom-call(s32[4]{0:T(128)S(1)} %copy-done.33, s32[2,4]{1,0:T(2,128)S(1)} %copy-done.32, bf16[256,256]{1,0:T(8,128)(2,1)S(1)} %copy-done.23, bf16[256,256]{1,0:T(8,128)(2,1)S(1)} %get-tuple-element.87.refs_3_, bf16[256,256]{1,0:T(8,128)(2,1)S(1)} %copy-done.26, bf16[1024,256]{1,0:T(8,128)(2,1)S(1)} %copy-done.3, ...), custom_call_target="tpu_custom_call" | custom-call | flops 1610612736 | bytes 12582912 | tf_op jit(solution)/shard_map/grad_place/pallas_call | solution.py:257
  177.7 2.1 %collective-permute-done.50 = bf16[256,256]{1,0:T(8,128)(2,1)S(1)} collective-permute-done((bf16[256,256]{1,0:T(8,128)(2,1)S(1)}, bf16[256,256]{1,0:T(8,128)(2,1)S(1)}, u32[]{:S(2)}, u32[]{:S(2)}) %collective-permute-start.50) | collective-permute-done | bytes 131104 | tf_op jit(solution)/shard_map/ppermute | solution.py:29
  (216 shorter events, 29.8 us)
Async XLA Ops:
  0.6 17.2 %copy-start.36 = (f32[256,512]{1,0:T(8,128)S(1)}, f32[256,512]{1,0:T(8,128)}, u32[]{:S(2)}) copy-start(f32[256,512]{1,0:T(8,128)} %param.8) | copy-start | bytes 1572868
  0.6 20.4 %copy-start.45 = (s32[1024]{0:T(1024)S(1)}, s32[1024]{0:T(1024)}, u32[]{:S(2)}) copy-start(s32[1024]{0:T(1024)} %param.7) | copy-start | bytes 12292
  2.6 14.0 %collective-permute-start = (bf16[256,256]{1,0:T(8,128)(2,1)S(1)}, bf16[256,256]{1,0:T(8,128)(2,1)}, u32[]{:S(2)}, u32[]{:S(2)}) collective-permute-start(bf16[256,256]{1,0:T(8,128)(2,1)S(1)} %pad_maximum_fusion.4), channel_id=1, source_target_pairs={{0,1},{1,2},{2,3},{3,0},{4,5},{5,6},{6,7},{7,4},{8,9},{9,10},{10,1... | collective-permute-start | bytes 393224 | tf_op jit(solution)/shard_map/ppermute | solution.py:29
  5.6 12.0 %collective-permute-start.1 = (bf16[256,256]{1,0:T(8,128)(2,1)S(1)}, bf16[256,256]{1,0:T(8,128)(2,1)S(1)}, u32[]{:S(2)}, u32[]{:S(2)}) collective-permute-start(bf16[256,256]{1,0:T(8,128)(2,1)S(1)} %pad_maximum_fusion.4), channel_id=1, source_target_pairs={{0,2},{1,3},{2,0},{3,1},{4,6},{5,7},{6,4},{7,5},{8,10},{9,11},{10,... | collective-permute-start | bytes 393224 | tf_op jit(solution)/shard_map/ppermute | solution.py:29
  8.2 9.4 %collective-permute-start.2 = (bf16[256,256]{1,0:T(8,128)(2,1)S(1)}, bf16[256,256]{1,0:T(8,128)(2,1)S(1)}, u32[]{:S(2)}, u32[]{:S(2)}) collective-permute-start(bf16[256,256]{1,0:T(8,128)(2,1)S(1)} %pad_maximum_fusion.4), channel_id=1, source_target_pairs={{0,3},{1,0},{2,1},{3,2},{4,7},{5,4},{6,5},{7,6},{8,11},{9,8},{10,9... | collective-permute-start | bytes 393224 | tf_op jit(solution)/shard_map/ppermute | solution.py:29
  16.5 37.9 %copy-start = (bf16[256,4096]{1,0:T(8,128)(2,1)S(1)}, bf16[256,4096]{1,0:T(8,128)(2,1)}, u32[]{:S(2)}) copy-start(bf16[256,4096]{1,0:T(8,128)(2,1)} %get-tuple-element.82.refs_0_.refs_2_.refs_4_.refs_6_) | copy-start | bytes 6291460
  17.7 35.7 %copy-start.4 = (bf16[1024,256]{1,0:T(8,128)(2,1)}, bf16[1024,256]{1,0:T(8,128)(2,1)S(1)}, u32[]{:S(2)}) copy-start(bf16[1024,256]{1,0:T(8,128)(2,1)S(1)} %constant_dynamic-update-slice_fusion.refs_8_.refs_12_.refs_14_) | copy-start | bytes 1572868
  17.7 4.6 %collective-permute-start.3 = (bf16[256,4096]{1,0:T(8,128)(2,1)}, bf16[256,4096]{1,0:T(8,128)(2,1)}, u32[]{:S(2)}, u32[]{:S(2)}) collective-permute-start(bf16[256,4096]{1,0:T(8,128)(2,1)} %get-tuple-element.58), channel_id=1, source_target_pairs={{0,4},{4,0},{1,5},{5,1},{2,6},{6,2},{3,7},{7,3},{8,12},{12,8},{9,1... | collective-permute-start | bytes 6291464 | tf_op jit(solution)/shard_map/ppermute | solution.py:29
  18.0 17.7 %collective-permute-start.7 = (bf16[1024,256]{1,0:T(8,128)(2,1)S(1)}, bf16[1024,256]{1,0:T(8,128)(2,1)S(1)}, u32[]{:S(2)}, u32[]{:S(2)}) collective-permute-start(bf16[1024,256]{1,0:T(8,128)(2,1)S(1)} %constant_dynamic-update-slice_fusion.refs_8_.refs_12_.refs_14_), channel_id=1, source_target_pairs={{0,16},{16,0},{1,17},{17,1},{2,18},{18,2},{3,19},{19,3},{4,20},{20... | collective-permute-start | bytes 1572872 | tf_op jit(solution)/shard_map/ppermute | solution.py:29
  19.5 16.1 %collective-permute-start.8 = (bf16[1024,256]{1,0:T(8,128)(2,1)S(1)}, bf16[1024,256]{1,0:T(8,128)(2,1)S(1)}, u32[]{:S(2)}, u32[]{:S(2)}) collective-permute-start(bf16[1024,256]{1,0:T(8,128)(2,1)S(1)} %constant_dynamic-update-slice_fusion.refs_8_.refs_12_.refs_14_), channel_id=1, source_target_pairs={{0,8},{8,0},{1,9},{9,1},{2,10},{10,2},{3,11},{11,3},{4,12},{12,4},... | collective-permute-start | bytes 1572872 | tf_op jit(solution)/shard_map/ppermute | solution.py:29
  22.3 7.9 %collective-permute-start.4 = (bf16[256,256]{1,0:T(8,128)(2,1)S(1)}, bf16[256,256]{1,0:T(8,128)(2,1)S(1)}, u32[]{:S(2)}, u32[]{:S(2)}) collective-permute-start(bf16[256,256]{1,0:T(8,128)(2,1)S(1)} %get-tuple-element.59), channel_id=1, source_target_pairs={{0,1},{1,2},{2,3},{3,0},{4,5},{5,6},{6,7},{7,4},{8,9},{9,10},{10,1... | collective-permute-start | bytes 393224 | tf_op jit(solution)/shard_map/ppermute | solution.py:29
  26.0 9.4 %collective-permute-start.5 = (bf16[256,256]{1,0:T(8,128)(2,1)S(1)}, bf16[256,256]{1,0:T(8,128)(2,1)S(1)}, u32[]{:S(2)}, u32[]{:S(2)}) collective-permute-start(bf16[256,256]{1,0:T(8,128)(2,1)S(1)} %get-tuple-element.59), channel_id=1, source_target_pairs={{0,2},{1,3},{2,0},{3,1},{4,6},{5,7},{6,4},{7,5},{8,10},{9,11},{10,... | collective-permute-start | bytes 393224 | tf_op jit(solution)/shard_map/ppermute | solution.py:29
  27.7 7.9 %collective-permute-start.6 = (bf16[256,256]{1,0:T(8,128)(2,1)S(1)}, bf16[256,256]{1,0:T(8,128)(2,1)S(1)}, u32[]{:S(2)}, u32[]{:S(2)}) collective-permute-start(bf16[256,256]{1,0:T(8,128)(2,1)S(1)} %get-tuple-element.59), channel_id=1, source_target_pairs={{0,3},{1,0},{2,1},{3,2},{4,7},{5,4},{6,5},{7,6},{8,11},{9,8},{10,9... | collective-permute-start | bytes 393224 | tf_op jit(solution)/shard_map/ppermute | solution.py:29
  35.6 22.7 %copy-start.1 = (bf16[1024,256]{1,0:T(8,128)(2,1)}, bf16[1024,256]{1,0:T(8,128)(2,1)S(1)}, u32[]{:S(2)}) copy-start(bf16[1024,256]{1,0:T(8,128)(2,1)S(1)} %constant_dynamic-update-slice_fusion.4.refs_6_.refs_3_.refs_5_) | copy-start | bytes 1572868
  35.6 22.7 %copy-start.10 = (bf16[1024,256]{1,0:T(8,128)(2,1)}, bf16[1024,256]{1,0:T(8,128)(2,1)S(1)}, u32[]{:S(2)}) copy-start(bf16[1024,256]{1,0:T(8,128)(2,1)S(1)} %collective-permute-done.7.refs_10_.refs_14_.refs_16_) | copy-start | bytes 1572868
  35.7 16.9 %collective-permute-start.9 = (bf16[1024,256]{1,0:T(8,128)(2,1)S(1)}, bf16[1024,256]{1,0:T(8,128)(2,1)S(1)}, u32[]{:S(2)}, u32[]{:S(2)}) collective-permute-start(bf16[1024,256]{1,0:T(8,128)(2,1)S(1)} %constant_dynamic-update-slice_fusion.4.refs_6_.refs_3_.refs_5_), channel_id=1, source_target_pairs={{0,16},{16,0},{1,17},{17,1},{2,18},{18,2},{3,19},{19,3},{4,20},{20... | collective-permute-start | bytes 1572872 | tf_op jit(solution)/shard_map/ppermute | solution.py:29
  37.2 16.1 %collective-permute-start.10 = (bf16[1024,256]{1,0:T(8,128)(2,1)S(1)}, bf16[1024,256]{1,0:T(8,128)(2,1)S(1)}, u32[]{:S(2)}, u32[]{:S(2)}) collective-permute-start(bf16[1024,256]{1,0:T(8,128)(2,1)S(1)} %collective-permute-done.7.refs_10_.refs_14_.refs_16_), channel_id=1, source_target_pairs={{0,8},{8,0},{1,9},{9,1},{2,10},{10,2},{3,11},{11,3},{4,12},{12,4},... | collective-permute-start | bytes 1572872 | tf_op jit(solution)/shard_map/ppermute | solution.py:29
  38.7 8.2 %collective-permute-start.12 = (bf16[256,256]{1,0:T(8,128)(2,1)S(1)}, bf16[256,256]{1,0:T(8,128)(2,1)S(1)}, u32[]{:S(2)}, u32[]{:S(2)}) collective-permute-start(bf16[256,256]{1,0:T(8,128)(2,1)S(1)} %get-tuple-element.64), channel_id=1, source_target_pairs={{0,1},{1,2},{2,3},{3,0},{4,5},{5,6},{6,7},{7,4},{8,9},{9,10},{10,1... | collective-permute-start | bytes 393224 | tf_op jit(solution)/shard_map/ppermute | solution.py:29
  41.8 9.4 %collective-permute-start.13 = (bf16[256,256]{1,0:T(8,128)(2,1)S(1)}, bf16[256,256]{1,0:T(8,128)(2,1)S(1)}, u32[]{:S(2)}, u32[]{:S(2)}) collective-permute-start(bf16[256,256]{1,0:T(8,128)(2,1)S(1)} %get-tuple-element.64), channel_id=1, source_target_pairs={{0,2},{1,3},{2,0},{3,1},{4,6},{5,7},{6,4},{7,5},{8,10},{9,11},{10,... | collective-permute-start | bytes 393224 | tf_op jit(solution)/shard_map/ppermute | solution.py:29
  43.7 8.1 %collective-permute-start.14 = (bf16[256,256]{1,0:T(8,128)(2,1)S(1)}, bf16[256,256]{1,0:T(8,128)(2,1)S(1)}, u32[]{:S(2)}, u32[]{:S(2)}) collective-permute-start(bf16[256,256]{1,0:T(8,128)(2,1)S(1)} %get-tuple-element.64), channel_id=1, source_target_pairs={{0,3},{1,0},{2,1},{3,2},{4,7},{5,4},{6,5},{7,6},{8,11},{9,8},{10,9... | collective-permute-start | bytes 393224 | tf_op jit(solution)/shard_map/ppermute | solution.py:29
  53.4 15.7 %collective-permute-start.11 = (bf16[1024,256]{1,0:T(8,128)(2,1)S(1)}, bf16[1024,256]{1,0:T(8,128)(2,1)}, u32[]{:S(2)}, u32[]{:S(2)}) collective-permute-start(bf16[1024,256]{1,0:T(8,128)(2,1)S(1)} %constant_dynamic-update-slice_fusion.4.refs_6_.refs_3_.refs_5_), channel_id=1, source_target_pairs={{0,8},{8,0},{1,9},{9,1},{2,10},{10,2},{3,11},{11,3},{4,12},{12,4},... | collective-permute-start | bytes 1572872 | tf_op jit(solution)/shard_map/ppermute | solution.py:29
  53.9 15.1 %collective-permute-start.15 = (bf16[1024,256]{1,0:T(8,128)(2,1)}, bf16[1024,256]{1,0:T(8,128)(2,1)S(1)}, u32[]{:S(2)}, u32[]{:S(2)}) collective-permute-start(bf16[1024,256]{1,0:T(8,128)(2,1)} %constant_dynamic-update-slice_fusion.8.refs_6_.refs_7_.refs_9_), channel_id=1, source_target_pairs={{0,16},{16,0},{1,17},{17,1},{2,18},{18,2},{3,19},{19,3},{4,20},{20... | collective-permute-start | bytes 1572872 | tf_op jit(solution)/shard_map/ppermute | solution.py:29
  59.8 1.7 collective-permute-start.16
  63.4 21.1 %collective-permute-start.19 = (bf16[256,256]{1,0:T(8,128)(2,1)}, bf16[256,256]{1,0:T(8,128)(2,1)S(1)}, u32[]{:S(2)}, u32[]{:S(2)}) collective-permute-start(bf16[256,256]{1,0:T(8,128)(2,1)} %finish_keys.1.refs_7_), channel_id=1, source_target_pairs={{0,1},{1,2},{2,3},{3,0},{4,5},{5,6},{6,7},{7,4},{8,9},{9,10},{10,1... | collective-permute-start | bytes 393224 | tf_op jit(solution)/shard_map/ppermute | solution.py:29
  66.0 18.5 %collective-permute-start.20 = (bf16[256,256]{1,0:T(8,128)(2,1)}, bf16[256,256]{1,0:T(8,128)(2,1)S(1)}, u32[]{:S(2)}, u32[]{:S(2)}) collective-permute-start(bf16[256,256]{1,0:T(8,128)(2,1)} %finish_keys.1.refs_7_), channel_id=1, source_target_pairs={{0,2},{1,3},{2,0},{3,1},{4,6},{5,7},{6,4},{7,5},{8,10},{9,11},{10,... | collective-permute-start | bytes 393224 | tf_op jit(solution)/shard_map/ppermute | solution.py:29
  68.4 16.1 %collective-permute-start.21 = (bf16[256,256]{1,0:T(8,128)(2,1)}, bf16[256,256]{1,0:T(8,128)(2,1)S(1)}, u32[]{:S(2)}, u32[]{:S(2)}) collective-permute-start(bf16[256,256]{1,0:T(8,128)(2,1)} %finish_keys.1.refs_7_), channel_id=1, source_target_pairs={{0,3},{1,0},{2,1},{3,2},{4,7},{5,4},{6,5},{7,6},{8,11},{9,8},{10,9... | collective-permute-start | bytes 393224 | tf_op jit(solution)/shard_map/ppermute | solution.py:29
  69.0 13.5 %collective-permute-start.17 = (bf16[1024,256]{1,0:T(8,128)(2,1)}, bf16[1024,256]{1,0:T(8,128)(2,1)S(1)}, u32[]{:S(2)}, u32[]{:S(2)}) collective-permute-start(bf16[1024,256]{1,0:T(8,128)(2,1)} %collective-permute-done.11.refs_7_.refs_4_.refs_6_), channel_id=1, source_target_pairs={{0,16},{16,0},{1,17},{17,1},{2,18},{18,2},{3,19},{19,3},{4,20},{20... | collective-permute-start | bytes 1572872 | tf_op jit(solution)/shard_map/ppermute | solution.py:29
  70.5 13.9 %collective-permute-start.22 = (bf16[1024,256]{1,0:T(8,128)(2,1)}, bf16[1024,256]{1,0:T(8,128)(2,1)S(1)}, u32[]{:S(2)}, u32[]{:S(2)}) collective-permute-start(bf16[1024,256]{1,0:T(8,128)(2,1)} %constant_dynamic-update-slice_fusion.8.refs_6_.refs_7_.refs_9_), channel_id=1, source_target_pairs={{0,8},{8,0},{1,9},{9,1},{2,10},{10,2},{3,11},{11,3},{4,12},{12,4},... | collective-permute-start | bytes 1572872 | tf_op jit(solution)/shard_map/ppermute | solution.py:29
  84.4 5.1 %collective-permute-start.18 = (f32[256,256]{1,0:T(8,128)S(1)}, f32[256,256]{1,0:T(8,128)S(1)}, u32[]{:S(2)}, u32[]{:S(2)}) collective-permute-start(f32[256,256]{1,0:T(8,128)S(1)} %get-tuple-element.72), channel_id=1, source_target_pairs={{0,4},{4,0},{1,5},{5,1},{2,6},{6,2},{3,7},{7,3},{8,12},{12,8},{9,1... | collective-permute-start | bytes 786440 | tf_op jit(solution)/shard_map/ppermute | solution.py:29
  84.5 10.2 %collective-permute-start.24 = (bf16[512,256]{1,0:T(8,128)(2,1)S(1)}, bf16[512,256]{1,0:T(8,128)(2,1)S(1)}, u32[]{:S(2)}, u32[]{:S(2)}) collective-permute-start(bf16[512,256]{1,0:T(8,128)(2,1)S(1)} %slice.131), channel_id=1, source_target_pairs={{0,16},{16,0},{1,17},{17,1},{2,18},{18,2},{3,19},{19,3},{4,20},{20... | collective-permute-start | bytes 786440 | tf_op jit(solution)/shard_map/ppermute | solution.py:29
  86.1 8.6 %collective-permute-start.23 = (bf16[512,256]{1,0:T(8,128)(2,1)S(1)}, bf16[512,256]{1,0:T(8,128)(2,1)S(1)}, u32[]{:S(2)}, u32[]{:S(2)}) collective-permute-start(bf16[512,256]{1,0:T(8,128)(2,1)S(1)} %slice.130), channel_id=1, source_target_pairs={{0,8},{8,0},{1,9},{9,1},{2,10},{10,2},{3,11},{11,3},{4,12},{12,4},... | collective-permute-start | bytes 786440 | tf_op jit(solution)/shard_map/ppermute | solution.py:29
  89.4 22.0 %copy-start.34 = (bf16[512,4096]{1,0:T(8,128)(2,1)}, bf16[512,4096]{1,0:T(8,128)(2,1)S(1)}, u32[]{:S(2)}) copy-start(bf16[512,4096]{1,0:T(8,128)(2,1)S(1)} %constant_dynamic-update-slice_fusion.12) | copy-start | bytes 12582916
  92.0 4.8 %collective-permute-start.25 = (bf16[256,256]{1,0:T(8,128)(2,1)S(1)}, bf16[256,256]{1,0:T(8,128)(2,1)S(1)}, u32[]{:S(2)}, u32[]{:S(2)}) collective-permute-start(bf16[256,256]{1,0:T(8,128)(2,1)S(1)} %get-tuple-element.83.refs_2_), channel_id=1, source_target_pairs={{0,4},{4,0},{1,5},{5,1},{2,6},{6,2},{3,7},{7,3},{8,12},{12,8},{9,1... | collective-permute-start | bytes 393224 | tf_op jit(solution)/shard_map/ppermute | solution.py:29
  96.3 3.3 %collective-permute-start.26 = (f32[256,256]{1,0:T(8,128)S(1)}, f32[256,256]{1,0:T(8,128)S(1)}, u32[]{:S(2)}, u32[]{:S(2)}) collective-permute-start(f32[256,256]{1,0:T(8,128)S(1)} %get-tuple-element.85), channel_id=1, source_target_pairs={{0,4},{4,0},{1,5},{5,1},{2,6},{6,2},{3,7},{7,3},{8,12},{12,8},{9,1... | collective-permute-start | bytes 786440 | tf_op jit(solution)/shard_map/ppermute | solution.py:29
  96.9 14.4 %copy-start.43 = (bf16[512,256]{1,0:T(8,128)(2,1)}, bf16[512,256]{1,0:T(8,128)(2,1)S(1)}, u32[]{:S(2)}) copy-start(bf16[512,256]{1,0:T(8,128)(2,1)S(1)} %constant_dynamic-update-slice_fusion.14) | copy-start | bytes 786436
  97.4 13.9 %collective-permute-start.27 = (bf16[1024,256]{1,0:T(8,128)(2,1)S(1)}, bf16[1024,256]{1,0:T(8,128)(2,1)S(1)}, u32[]{:S(2)}, u32[]{:S(2)}) collective-permute-start(bf16[1024,256]{1,0:T(8,128)(2,1)S(1)} %convolution_convert_fusion.3), channel_id=1, source_target_pairs={{0,8},{8,0},{1,9},{9,1},{2,10},{10,2},{3,11},{11,3},{4,12},{12,4},... | collective-permute-start | bytes 1572872 | tf_op jit(solution)/shard_map/ppermute | solution.py:29
  102.5 4.3 %collective-permute-start.28 = (bf16[256,256]{1,0:T(8,128)(2,1)S(1)}, bf16[256,256]{1,0:T(8,128)(2,1)S(1)}, u32[]{:S(2)}, u32[]{:S(2)}) collective-permute-start(bf16[256,256]{1,0:T(8,128)(2,1)S(1)} %get-tuple-element.87.refs_3_), channel_id=1, source_target_pairs={{0,4},{4,0},{1,5},{5,1},{2,6},{6,2},{3,7},{7,3},{8,12},{12,8},{9,1... | collective-permute-start | bytes 393224 | tf_op jit(solution)/shard_map/ppermute | solution.py:29
  102.8 9.9 %collective-permute-start.30 = (bf16[256,256]{1,0:T(8,128)(2,1)S(1)}, bf16[256,256]{1,0:T(8,128)(2,1)S(1)}, u32[]{:S(2)}, u32[]{:S(2)}) collective-permute-start(bf16[256,256]{1,0:T(8,128)(2,1)S(1)} %get-tuple-element.89), channel_id=1, source_target_pairs={{0,3},{1,0},{2,1},{3,2},{4,7},{5,4},{6,5},{7,6},{8,11},{9,8},{10,9... | collective-permute-start | bytes 393224 | tf_op jit(solution)/shard_map/ppermute | solution.py:29
  104.2 13.7 %collective-permute-start.31 = (bf16[256,256]{1,0:T(8,128)(2,1)S(1)}, bf16[256,256]{1,0:T(8,128)(2,1)S(1)}, u32[]{:S(2)}, u32[]{:S(2)}) collective-permute-start(bf16[256,256]{1,0:T(8,128)(2,1)S(1)} %get-tuple-element.90), channel_id=1, source_target_pairs={{0,2},{1,3},{2,0},{3,1},{4,6},{5,7},{6,4},{7,5},{8,10},{9,11},{10,... | collective-permute-start | bytes 393224 | tf_op jit(solution)/shard_map/ppermute | solution.py:29
  105.7 15.8 %collective-permute-start.32 = (bf16[256,256]{1,0:T(8,128)(2,1)S(1)}, bf16[256,256]{1,0:T(8,128)(2,1)S(1)}, u32[]{:S(2)}, u32[]{:S(2)}) collective-permute-start(bf16[256,256]{1,0:T(8,128)(2,1)S(1)} %get-tuple-element.94), channel_id=1, source_target_pairs={{0,1},{1,2},{2,3},{3,0},{4,5},{5,6},{6,7},{7,4},{8,9},{9,10},{10,1... | collective-permute-start | bytes 393224 | tf_op jit(solution)/shard_map/ppermute | solution.py:29
  106.8 17.4 %copy-start.41 = (bf16[512,256]{1,0:T(8,128)(2,1)}, bf16[512,256]{1,0:T(8,128)(2,1)S(1)}, u32[]{:S(2)}) copy-start(bf16[512,256]{1,0:T(8,128)(2,1)S(1)} %constant_dynamic-update-slice_fusion.16) | copy-start | bytes 786436
  107.3 13.4 %collective-permute-start.29 = (bf16[1024,256]{1,0:T(8,128)(2,1)S(1)}, bf16[1024,256]{1,0:T(8,128)(2,1)S(1)}, u32[]{:S(2)}, u32[]{:S(2)}) collective-permute-start(bf16[1024,256]{1,0:T(8,128)(2,1)S(1)} %convolution_convert_fusion.2), channel_id=1, source_target_pairs={{0,16},{16,0},{1,17},{17,1},{2,18},{18,2},{3,19},{19,3},{4,20},{20... | collective-permute-start | bytes 1572872 | tf_op jit(solution)/shard_map/ppermute | solution.py:29
  117.9 13.7 %collective-permute-start.38 = (bf16[1024,256]{1,0:T(8,128)(2,1)}, bf16[1024,256]{1,0:T(8,128)(2,1)}, u32[]{:S(2)}, u32[]{:S(2)}) collective-permute-start(bf16[1024,256]{1,0:T(8,128)(2,1)} %convolution_convert_fusion.1), channel_id=1, source_target_pairs={{0,8},{8,0},{1,9},{9,1},{2,10},{10,2},{3,11},{11,3},{4,12},{12,4},... | collective-permute-start | bytes 1572872 | tf_op jit(solution)/shard_map/ppermute | solution.py:29
  119.0 15.2 %collective-permute-start.37 = (bf16[1024,256]{1,0:T(8,128)(2,1)}, bf16[1024,256]{1,0:T(8,128)(2,1)}, u32[]{:S(2)}, u32[]{:S(2)}) collective-permute-start(bf16[1024,256]{1,0:T(8,128)(2,1)} %fusion.3), channel_id=1, source_target_pairs={{0,16},{16,0},{1,17},{17,1},{2,18},{18,2},{3,19},{19,3},{4,20},{20... | collective-permute-start | bytes 1572872 | tf_op jit(solution)/shard_map/ppermute | solution.py:29
  124.2 2.1 %collective-permute-start.33 = (bf16[256,256]{1,0:T(8,128)(2,1)}, bf16[256,256]{1,0:T(8,128)(2,1)S(1)}, u32[]{:S(2)}, u32[]{:S(2)}) collective-permute-start(bf16[256,256]{1,0:T(8,128)(2,1)} %undo_keys.1.refs_4_), channel_id=1, source_target_pairs={{0,4},{4,0},{1,5},{5,1},{2,6},{6,2},{3,7},{7,3},{8,12},{12,8},{9,1... | collective-permute-start | bytes 393224 | tf_op jit(solution)/shard_map/ppermute | solution.py:29
  127.7 12.3 %collective-permute-start.35 = (bf16[512,256]{1,0:T(8,128)(2,1)S(1)}, bf16[512,256]{1,0:T(8,128)(2,1)S(1)}, u32[]{:S(2)}, u32[]{:S(2)}) collective-permute-start(bf16[512,256]{1,0:T(8,128)(2,1)S(1)} %convolution_convert_fusion.6), channel_id=1, source_target_pairs={{0,16},{16,0},{1,17},{17,1},{2,18},{18,2},{3,19},{19,3},{4,20},{20... | collective-permute-start | bytes 786440 | tf_op jit(solution)/shard_map/ppermute | solution.py:29
  128.8 11.4 %collective-permute-start.34 = (bf16[512,256]{1,0:T(8,128)(2,1)S(1)}, bf16[512,256]{1,0:T(8,128)(2,1)S(1)}, u32[]{:S(2)}, u32[]{:S(2)}) collective-permute-start(bf16[512,256]{1,0:T(8,128)(2,1)S(1)} %convolution_convert_fusion.7), channel_id=1, source_target_pairs={{0,8},{8,0},{1,9},{9,1},{2,10},{10,2},{3,11},{11,3},{4,12},{12,4},... | collective-permute-start | bytes 786440 | tf_op jit(solution)/shard_map/ppermute | solution.py:29
  134.2 15.1 %collective-permute-start.39 = (bf16[1024,256]{1,0:T(8,128)(2,1)S(1)}, bf16[1024,256]{1,0:T(8,128)(2,1)S(1)}, u32[]{:S(2)}, u32[]{:S(2)}) collective-permute-start(bf16[1024,256]{1,0:T(8,128)(2,1)S(1)} %copy-done.46), channel_id=1, source_target_pairs={{0,16},{16,0},{1,17},{17,1},{2,18},{18,2},{3,19},{19,3},{4,20},{20... | collective-permute-start | bytes 1572872 | tf_op jit(solution)/shard_map/ppermute | solution.py:29
  134.7 14.6 %collective-permute-start.40 = (bf16[1024,256]{1,0:T(8,128)(2,1)S(1)}, bf16[1024,256]{1,0:T(8,128)(2,1)S(1)}, u32[]{:S(2)}, u32[]{:S(2)}) collective-permute-start(bf16[1024,256]{1,0:T(8,128)(2,1)S(1)} %fusion.5), channel_id=1, source_target_pairs={{0,8},{8,0},{1,9},{9,1},{2,10},{10,2},{3,11},{11,3},{4,12},{12,4},... | collective-permute-start | bytes 1572872 | tf_op jit(solution)/shard_map/ppermute | solution.py:29
  136.7 7.5 %collective-permute-start.41 = (bf16[256,256]{1,0:T(8,128)(2,1)S(1)}, bf16[256,256]{1,0:T(8,128)(2,1)S(1)}, u32[]{:S(2)}, u32[]{:S(2)}) collective-permute-start(bf16[256,256]{1,0:T(8,128)(2,1)S(1)} %get-tuple-element.114), channel_id=1, source_target_pairs={{0,3},{1,0},{2,1},{3,2},{4,7},{5,4},{6,5},{7,6},{8,11},{9,8},{10,9... | collective-permute-start | bytes 393224 | tf_op jit(solution)/shard_map/ppermute | solution.py:29
  140.0 8.1 %collective-permute-start.42 = (bf16[256,256]{1,0:T(8,128)(2,1)S(1)}, bf16[256,256]{1,0:T(8,128)(2,1)S(1)}, u32[]{:S(2)}, u32[]{:S(2)}) collective-permute-start(bf16[256,256]{1,0:T(8,128)(2,1)S(1)} %get-tuple-element.113), channel_id=1, source_target_pairs={{0,2},{1,3},{2,0},{3,1},{4,6},{5,7},{6,4},{7,5},{8,10},{9,11},{10,... | collective-permute-start | bytes 393224 | tf_op jit(solution)/shard_map/ppermute | solution.py:29
  143.3 28.5 %collective-permute-start.36 = (bf16[256,4096]{1,0:T(8,128)(2,1)S(1)}, bf16[256,4096]{1,0:T(8,128)(2,1)S(1)}, u32[]{:S(2)}, u32[]{:S(2)}) collective-permute-start(bf16[256,4096]{1,0:T(8,128)(2,1)S(1)} %grad_columns.1), channel_id=1, source_target_pairs={{0,4},{4,0},{1,5},{5,1},{2,6},{6,2},{3,7},{7,3},{8,12},{12,8},{9,1... | collective-permute-start | bytes 6291464 | tf_op jit(solution)/shard_map/ppermute | solution.py:29
  144.2 12.3 %collective-permute-start.43 = (bf16[256,256]{1,0:T(8,128)(2,1)S(1)}, bf16[256,256]{1,0:T(8,128)(2,1)S(1)}, u32[]{:S(2)}, u32[]{:S(2)}) collective-permute-start(bf16[256,256]{1,0:T(8,128)(2,1)S(1)} %get-tuple-element.112), channel_id=1, source_target_pairs={{0,1},{1,2},{2,3},{3,0},{4,5},{5,6},{6,7},{7,4},{8,9},{9,10},{10,1... | collective-permute-start | bytes 393224 | tf_op jit(solution)/shard_map/ppermute | solution.py:29
  149.4 12.3 %collective-permute-start.45 = (bf16[1024,256]{1,0:T(8,128)(2,1)S(1)}, bf16[1024,256]{1,0:T(8,128)(2,1)S(1)}, u32[]{:S(2)}, u32[]{:S(2)}) collective-permute-start(bf16[1024,256]{1,0:T(8,128)(2,1)S(1)} %pad_maximum_fusion.1), channel_id=1, source_target_pairs={{0,8},{8,0},{1,9},{9,1},{2,10},{10,2},{3,11},{11,3},{4,12},{12,4},... | collective-permute-start | bytes 1572872 | tf_op jit(solution)/shard_map/ppermute | solution.py:29
  150.0 14.5 %collective-permute-start.44 = (bf16[1024,256]{1,0:T(8,128)(2,1)S(1)}, bf16[1024,256]{1,0:T(8,128)(2,1)S(1)}, u32[]{:S(2)}, u32[]{:S(2)}) collective-permute-start(bf16[1024,256]{1,0:T(8,128)(2,1)S(1)} %pad_maximum_fusion), channel_id=1, source_target_pairs={{0,16},{16,0},{1,17},{17,1},{2,18},{18,2},{3,19},{19,3},{4,20},{20... | collective-permute-start | bytes 1572872 | tf_op jit(solution)/shard_map/ppermute | solution.py:29
  151.5 20.3 %copy-start.23 = (bf16[256,256]{1,0:T(8,128)(2,1)S(1)}, bf16[256,256]{1,0:T(8,128)(2,1)}, u32[]{:S(2)}) copy-start(bf16[256,256]{1,0:T(8,128)(2,1)} %copy-done.22) | copy-start | bytes 393220
  151.5 20.3 %copy-start.32 = (s32[2,4]{1,0:T(2,128)S(1)}, s32[2,4]{1,0:T(2,128)}, u32[]{:S(2)}) copy-start(s32[2,4]{1,0:T(2,128)} %pad_add_fusion.1.piece_ref.refs_1_) | copy-start | bytes 100
  151.6 20.3 %copy-start.33 = (s32[4]{0:T(128)S(1)}, s32[4]{0:T(128)}, u32[]{:S(2)}) copy-start(s32[4]{0:T(128)} %fusion.26.slab_ref.refs_0_) | copy-start | bytes 52
  151.6 13.4 %collective-permute-start.46 = (bf16[256,256]{1,0:T(8,128)(2,1)S(1)}, bf16[256,256]{1,0:T(8,128)(2,1)S(1)}, u32[]{:S(2)}, u32[]{:S(2)}) collective-permute-start(bf16[256,256]{1,0:T(8,128)(2,1)S(1)} %get-tuple-element.118), channel_id=1, source_target_pairs={{0,3},{1,0},{2,1},{3,2},{4,7},{5,4},{6,5},{7,6},{8,11},{9,8},{10,9... | collective-permute-start | bytes 393224 | tf_op jit(solution)/shard_map/ppermute | solution.py:29
  156.5 8.5 %collective-permute-start.47 = (bf16[256,256]{1,0:T(8,128)(2,1)S(1)}, bf16[256,256]{1,0:T(8,128)(2,1)S(1)}, u32[]{:S(2)}, u32[]{:S(2)}) collective-permute-start(bf16[256,256]{1,0:T(8,128)(2,1)S(1)} %get-tuple-element.117), channel_id=1, source_target_pairs={{0,2},{1,3},{2,0},{3,1},{4,6},{5,7},{6,4},{7,5},{8,10},{9,11},{10,... | collective-permute-start | bytes 393224 | tf_op jit(solution)/shard_map/ppermute | solution.py:29
  161.7 9.2 %collective-permute-start.48 = (bf16[256,256]{1,0:T(8,128)(2,1)S(1)}, bf16[256,256]{1,0:T(8,128)(2,1)S(1)}, u32[]{:S(2)}, u32[]{:S(2)}) collective-permute-start(bf16[256,256]{1,0:T(8,128)(2,1)S(1)} %get-tuple-element.116), channel_id=1, source_target_pairs={{0,1},{1,2},{2,3},{3,0},{4,5},{5,6},{6,7},{7,4},{8,9},{9,10},{10,1... | collective-permute-start | bytes 393224 | tf_op jit(solution)/shard_map/ppermute | solution.py:29
  165.1 12.6 %collective-permute-start.49 = (bf16[256,256]{1,0:T(8,128)(2,1)S(1)}, bf16[256,256]{1,0:T(8,128)(2,1)S(1)}, u32[]{:S(2)}, u32[]{:S(2)}) collective-permute-start(bf16[256,256]{1,0:T(8,128)(2,1)S(1)} %get-tuple-element.110), channel_id=1, source_target_pairs={{0,3},{1,0},{2,1},{3,2},{4,7},{5,4},{6,5},{7,6},{8,11},{9,8},{10,9... | collective-permute-start | bytes 393224 | tf_op jit(solution)/shard_map/ppermute | solution.py:29
  168.0 11.8 %collective-permute-start.50 = (bf16[256,256]{1,0:T(8,128)(2,1)S(1)}, bf16[256,256]{1,0:T(8,128)(2,1)S(1)}, u32[]{:S(2)}, u32[]{:S(2)}) collective-permute-start(bf16[256,256]{1,0:T(8,128)(2,1)S(1)} %get-tuple-element.109), channel_id=1, source_target_pairs={{0,2},{1,3},{2,0},{3,1},{4,6},{5,7},{6,4},{7,5},{8,10},{9,11},{10,... | collective-permute-start | bytes 393224 | tf_op jit(solution)/shard_map/ppermute | solution.py:29
  168.0 11.8 %collective-permute-start.51 = (bf16[256,256]{1,0:T(8,128)(2,1)S(1)}, bf16[256,256]{1,0:T(8,128)(2,1)S(1)}, u32[]{:S(2)}, u32[]{:S(2)}) collective-permute-start(bf16[256,256]{1,0:T(8,128)(2,1)S(1)} %get-tuple-element.108), channel_id=1, source_target_pairs={{0,1},{1,2},{2,3},{3,0},{4,5},{5,6},{6,7},{7,4},{8,9},{9,10},{10,1... | collective-permute-start | bytes 393224 | tf_op jit(solution)/shard_map/ppermute | solution.py:29
  (36 other events, 249.5 us)
